TPU v7x, 32 devices: a whole 2x2x4 slice. The times are simulated.
32 devices in a mesh: grp: 4 (over x, core), freq: 8 (over z, y).
Axes of the slice: x: 2, y: 2, z: 4, core: 2. Of those that a mesh axis runs over, the one named last changes fastest.
Arguments:
- spectra: float32 [32, 2, 4096], P('grp', None, 'freq'), may hold values from -6 to 6
- station_mask: int32 [32], P('grp'), may hold values 0 or 1
- owners: int32 [4, 2, 64, 1], P('grp'), may hold values from 0 to 3; in each aligned block of 64 rows (0 to 63, 64 to 127, ..., all dimensions but the last counted through in order) at most 32 rows name the same one
Outputs:
- inbox: float32 [4, 2, 4, 32, 4096], P('grp', None, None, None, 'freq')
Inputs may be any that keep to these rules, and one draw needn't show every extreme that they name: `owners`: in each round, no owner is named by more than 32 of one group's 64 pairs, a bound that some block reaches; every group owns some pair.
All inputs are finite; a program needn't handle non-finite values. No bound on the sum of `station_mask` on one device may be relied on, other than what follows from the above.
Results may differ from a plain program's by a relative error of at most 0.0003.
Values sent between devices are 32-bit elements; how exact they have to be, the bound alone decides.
No kernel may reach another device: no remote copies, remote signals or barrier semaphores. Data moves between devices by JAX's collectives and lax.ppermute only.
A program may use at most 128 MiB of HBM per device.

v0:
```python
import math

import jax
import jax.numpy as jnp
from jax import lax
from jax.sharding import PartitionSpec as P

LAGS = 4096


def passed_along(block, axis, distance):
    devices = range(lax.axis_size(axis))
    route = [((i - distance) % len(devices), i) for i in devices]
    return lax.ppermute(block, axis, route)


def phase_table(bin_ids, lag_count, bin_total):
    lag_ids = jnp.arange(lag_count, dtype=jnp.int32) - lag_count // 2
    phase_turns = jnp.mod(bin_ids[:, None] * lag_ids[None, :], 2 * bin_total)
    angles = phase_turns.astype(jnp.float32) * (math.pi / bin_total)
    return (jnp.cos(angles), jnp.sin(angles))


def per_device(spectra, station_mask, owners):
    station_count = spectra.shape[0]
    band_bins = spectra.shape[2]
    groups = lax.axis_size("grp")
    shards = lax.axis_size("freq")
    round_count = min(2, groups - 1)
    bin_total = band_bins * shards
    pair_count = station_count * station_count
    capacity = (2 * pair_count + groups - 1) // groups
    lag_band = LAGS // shards
    norm_scale = 1.0 / math.sqrt(bin_total)
    own_weight = station_mask.astype(jnp.float32)
    pair_ids = jnp.arange(pair_count, dtype=jnp.int32)
    earlier = pair_ids[None, :] < pair_ids[:, None]
    slot_ids = jnp.arange(groups * capacity, dtype=jnp.int32)
    base_cos, base_sin = phase_table(jnp.arange(band_bins, dtype=jnp.int32), LAGS, bin_total)
    base_table = jnp.concatenate(
        [
            jnp.concatenate([base_cos, base_sin], axis=1),
            jnp.concatenate([-base_sin, base_cos], axis=1),
        ],
        axis=0,
    )
    twist_cos, twist_sin = phase_table(
        jnp.arange(shards, dtype=jnp.int32) * band_bins, LAGS, bin_total
    )
    held_spectra = spectra
    held_weight = own_weight
    buffers = []
    for round_index in range(round_count):
        held_spectra, held_weight = passed_along((spectra, own_weight), "grp", round_index + 1)
        pair_weight = (own_weight[:, None] * held_weight[None, :])[..., None]
        cross_real = (
            spectra[:, None, 0] * held_spectra[None, :, 0]
            + spectra[:, None, 1] * held_spectra[None, :, 1]
        ) * pair_weight
        cross_imag = (
            spectra[:, None, 1] * held_spectra[None, :, 0]
            - spectra[:, None, 0] * held_spectra[None, :, 1]
        ) * pair_weight
        cross_real = cross_real.reshape(pair_count, band_bins)
        cross_imag = cross_imag.reshape(pair_count, band_bins)
        crossed = jnp.stack([cross_real, cross_imag], axis=1)
        crossed = crossed.reshape(shards, pair_count // shards, 2, band_bins)
        piece = lax.all_to_all(crossed, "freq", split_axis=0, concat_axis=3, tiled=True)
        item_count = piece.shape[1]
        blocks = piece.reshape(item_count, 2, shards, band_bins).transpose(0, 2, 1, 3)
        blocks = blocks.reshape(item_count * shards, 2 * band_bins)
        spread = jnp.dot(blocks, base_table, precision=lax.Precision.HIGHEST)
        spread = spread.reshape(item_count, shards, 2, LAGS)
        folded = jnp.einsum(
            "nbl,bl->ln", spread[:, :, 0], twist_cos, precision=lax.Precision.HIGHEST
        )
        folded = folded - jnp.einsum(
            "nbl,bl->ln", spread[:, :, 1], twist_sin, precision=lax.Precision.HIGHEST
        )
        lagged = folded * norm_scale
        correlation = lax.all_to_all(lagged, "freq", split_axis=0, concat_axis=1, tiled=True)
        owner_ids = owners[0, round_index, :, 0]
        same_owner = (owner_ids[:, None] == owner_ids[None, :]) & earlier
        pair_rank = jnp.sum(same_owner.astype(jnp.int32), axis=1)
        placing = ((owner_ids * capacity + pair_rank)[:, None] == slot_ids[None, :]).astype(
            jnp.float32
        )
        buffers.append(
            jnp.einsum("lp,px->xl", correlation, placing, precision=lax.Precision.HIGHEST)
        )
    outgoing = jnp.stack(buffers, axis=0).reshape(round_count, groups, capacity, lag_band)
    incoming = lax.all_to_all(outgoing, "grp", split_axis=1, concat_axis=1, tiled=True)
    return incoming.reshape(1, round_count, groups, capacity, lag_band)


def solution(mesh):
    placed = (P("grp", None, "freq"), P("grp"), P("grp", None, None, None))
    return jax.shard_map(
        per_device,
        mesh=mesh,
        in_specs=placed,
        out_specs=P("grp", None, None, None, "freq"),
        check_vma=False,
    )
```

profile of v0, /device:TPU:0, one launch (start us, length us, event | category | flops | bytes accessed | tf_op | source)
XLA Modules:
  0.0 205.7 jit_solution(4710102604300017127)
XLA Ops:
  0.0 0.7 convert_element_type.30
  0.7 0.5 collective-permute-start.1
  1.1 2.5 %collective-permute-start.3 = (f32[8]{0:T(128)S(1)}, f32[8]{0:T(128)S(1)}, u32[]{:S(2)}, u32[]{:S(2)}) collective-permute-start(f32[8]{0:T(128)S(1)} %convert_element_type.30), channel_id=1, source_target_pairs={{16,0},{24,8},{0,16},{8,24},{17,1},{25,9},{1,17},{9,25},{18,2},{26... | collective-permute-start | bytes 104 | tf_op jit(solution)/shard_map/ppermute | solution.py:14
  3.6 0.8 copy.16
  4.4 0.1 collective-permute-start
  4.5 1.7 collective-permute-start.2
  6.2 35.6 %fusion.6 = (f32[512,4096]{0,1:T(8,128)S(1)}, f32[512,4096]{0,1:T(8,128)S(1)}, f32[512,4096]{0,1:T(8,128)}) fusion(s32[4096]{0:T(1024)S(1)} %iota_add_fusion), kind=kLoop, calls=%fused_computation.10 | loop fusion | flops 31457280 | bytes 25182208 | tf_op jit(solution)/shard_map/sin | solution.py:21
  41.8 0.0 copy-start
  41.8 25.2 %maximum_maximum_fusion = f32[1024,8192]{0,1:T(8,128)} fusion(f32[512,4096]{0,1:T(8,128)} %get-tuple-element.27, f32[512,4096]{0,1:T(8,128)S(1)} %get-tuple-element.26, f32[512,4096]{0,1:T(8,128)S(1)} %get-tuple-element.25), kind=kLoop, calls=%fused_computation | loop fusion | flops 25165824 | bytes 58720256 | tf_op jit(solution)/shard_map/concatenate | solution.py:40
  67.0 0.0 collective-permute-done.1
  67.0 0.0 collective-permute-done.3
  67.0 0.1 broadcast_multiply_fusion.1
  67.1 0.0 collective-permute-done
  67.1 0.0 collective-permute-done.2
  67.1 0.6 add_multiply_fusion.1
  67.8 0.9 pad_maximum_fusion.1
  68.7 5.8 %all-to-all-start = ((f32[8,8,2,512]{3,2,1,0:T(2,128)}), f32[8,8,2,512]{3,2,1,0:T(2,128)S(1)}, u32[]{:S(2)}, u32[]{:S(2)}) async-start(f32[8,8,2,512]{3,2,1,0:T(2,128)} %pad_maximum_fusion.1), calls=%async_computation | async-start | bytes 524288 | tf_op jit(solution)/shard_map/all_to_all | solution.py:68
  74.6 0.6 cosine_bitcast_fusion
  75.1 0.9 pad_maximum_fusion.2
  76.1 7.6 %all-to-all-done = f32[8,8,2,512]{3,2,1,0:T(2,128)S(1)} async-done(((f32[8,8,2,512]{3,2,1,0:T(2,128)}), f32[8,8,2,512]{3,2,1,0:T(2,128)S(1)}, u32[]{:S(2)}, u32[]{:S(2)}) %all-to-all-start) | async-done | bytes 262176 | tf_op jit(solution)/shard_map/all_to_all | solution.py:68
  83.7 3.6 %all-to-all-start.2 = ((f32[8,8,2,512]{3,2,1,0:T(2,128)}), f32[8,8,2,512]{3,2,1,0:T(2,128)S(1)}, u32[]{:S(2)}, u32[]{:S(2)}) async-start(f32[8,8,2,512]{3,2,1,0:T(2,128)} %pad_maximum_fusion.2), calls=%async_computation.2 | async-start | bytes 524288 | tf_op jit(solution)/shard_map/all_to_all | solution.py:68
  87.3 0.0 copy-done
  87.3 0.2 convert_reduce_fusion
  87.5 0.2 copy.19
  87.6 8.2 %all-to-all-done.2 = f32[8,8,2,512]{3,2,1,0:T(2,128)S(1)} async-done(((f32[8,8,2,512]{3,2,1,0:T(2,128)}), f32[8,8,2,512]{3,2,1,0:T(2,128)S(1)}, u32[]{:S(2)}, u32[]{:S(2)}) %all-to-all-start.2) | async-done | bytes 262176 | tf_op jit(solution)/shard_map/all_to_all | solution.py:68
  95.8 0.2 copy.21
  96.0 35.3 %fusion.30 = f32[8,8,2,4096]{3,1,2,0:T(8,128)S(1)} fusion(f32[8,8,1024,1]{2,1,3,0:T(8,128)S(1)} %bitcast.115, f32[2,4096,1024,1]{2,1,0,3:T(8,128)} %bitcast.112), kind=kOutput, calls=%fused_computation.74 | convolution fusion | flops 6442450944 | bytes 35913728 | tf_op jit(solution)/shard_map/dot_general | solution.py:72
  131.3 36.7 %fusion.31 = f32[8,8,2,4096]{3,1,2,0:T(8,128)} fusion(f32[8,8,1024,1]{2,1,3,0:T(8,128)S(1)} %bitcast.116, f32[2,4096,1024,1]{2,1,0,3:T(8,128)} %bitcast.113), kind=kOutput, calls=%fused_computation.75 | convolution fusion | flops 6442450944 | bytes 35913728 | tf_op jit(solution)/shard_map/dot_general | solution.py:72
  168.1 2.9 %fusion.10 = (f32[4096,8]{0,1:T(8,128)S(1)}, f32[4096,8]{0,1:T(8,128)S(1)}, f32[4096,8]{0,1:T(8,128)S(1)}, f32[4096,8]{0,1:T(8,128)S(1)}) fusion(f32[8,8,2,4096]{3,1,2,0:T(8,128)} %fusion.31, f32[4096,8]{0,1:T(8,128)S(1)} %get-tuple-element.24, f32[4096,8]{0,1:T(8,128)S(1)} %get-tuple-element.23, f32[8,8,2,4096]{3,1,2,0:T(8,128)S(1)} %fusion.30), kind=kLoop, calls=%fused_computation.17 | loop fusion | flops 1966080 | bytes 4980736 | tf_op jit(solution)/shard_map/nbl,bl->ln/dot_general | solution.py:77
  170.9 0.7 subtract_multiply_fusion.2
  171.6 3.6 %all-to-all-start.1 = ((f32[8,512,8]{1,2,0:T(8,128)}), f32[8,512,8]{1,2,0:T(8,128)S(1)}, u32[]{:S(2)}, u32[]{:S(2)}) async-start(f32[8,512,8]{1,2,0:T(8,128)} %bitcast.27), calls=%async_computation.1 | async-start | bytes 262144 | tf_op jit(solution)/shard_map/all_to_all | solution.py:81
  175.2 0.7 subtract_multiply_fusion
  175.9 6.7 %all-to-all-done.1 = f32[8,512,8]{1,2,0:T(8,128)S(1)} async-done(((f32[8,512,8]{1,2,0:T(8,128)}), f32[8,512,8]{1,2,0:T(8,128)S(1)}, u32[]{:S(2)}, u32[]{:S(2)}) %all-to-all-start.1) | async-done | bytes 131104 | tf_op jit(solution)/shard_map/all_to_all | solution.py:81
  182.5 3.4 %all-to-all-start.3 = ((f32[8,512,8]{1,2,0:T(8,128)}), f32[8,512,8]{1,2,0:T(8,128)S(1)}, u32[]{:S(2)}, u32[]{:S(2)}) async-start(f32[8,512,8]{1,2,0:T(8,128)} %bitcast.48), calls=%async_computation.3 | async-start | bytes 262144 | tf_op jit(solution)/shard_map/all_to_all | solution.py:81
  185.9 0.3 convolution_bitcast_fusion.1
  186.2 6.9 %all-to-all-done.3 = f32[8,512,8]{1,2,0:T(8,128)S(1)} async-done(((f32[8,512,8]{1,2,0:T(8,128)}), f32[8,512,8]{1,2,0:T(8,128)S(1)}, u32[]{:S(2)}, u32[]{:S(2)}) %all-to-all-start.3) | async-done | bytes 131104 | tf_op jit(solution)/shard_map/all_to_all | solution.py:81
  193.2 0.3 convolution_bitcast_fusion
  193.6 11.2 %all_to_all.73 = f32[2,4,32,512]{3,2,0,1:T(8,128)S(1)} all-to-all(f32[2,4,32,512]{3,2,0,1:T(8,128)S(1)} %copy.22), channel_id=1, replica_groups=mesh['grp'=4,'freq'=8] {'grp'}, dimensions={1} | all-to-all | bytes 1048576 | tf_op jit(solution)/shard_map/all_to_all | solution.py:92
  204.8 0.8 copy.23
  (10 shorter events, 0.1 us)
Async XLA Ops:
  0.7 66.4 %collective-permute-start.1 = (f32[8]{0:T(128)S(1)}, f32[8]{0:T(128)S(1)}, u32[]{:S(2)}, u32[]{:S(2)}) collective-permute-start(f32[8]{0:T(128)S(1)} %convert_element_type.30), channel_id=1, source_target_pairs={{24,0},{0,8},{8,16},{16,24},{25,1},{1,9},{9,17},{17,25},{26,2},{2,... | collective-permute-start | bytes 104 | tf_op jit(solution)/shard_map/ppermute | solution.py:14
  1.1 65.9 %collective-permute-start.3 = (f32[8]{0:T(128)S(1)}, f32[8]{0:T(128)S(1)}, u32[]{:S(2)}, u32[]{:S(2)}) collective-permute-start(f32[8]{0:T(128)S(1)} %convert_element_type.30), channel_id=1, source_target_pairs={{16,0},{24,8},{0,16},{8,24},{17,1},{25,9},{1,17},{9,25},{18,2},{26... | collective-permute-start | bytes 104 | tf_op jit(solution)/shard_map/ppermute | solution.py:14
  4.4 62.7 %collective-permute-start = (f32[8,2,512]{2,0,1:T(8,128)S(1)}, f32[8,2,512]{2,0,1:T(8,128)S(1)}, u32[]{:S(2)}, u32[]{:S(2)}) collective-permute-start(f32[8,2,512]{2,0,1:T(8,128)S(1)} %copy.16), channel_id=1, source_target_pairs={{24,0},{0,8},{8,16},{16,24},{25,1},{1,9},{9,17},{17,25},{26,2},{2,... | collective-permute-start | bytes 98312 | tf_op jit(solution)/shard_map/ppermute | solution.py:14
  4.5 62.6 %collective-permute-start.2 = (f32[8,2,512]{2,0,1:T(8,128)S(1)}, f32[8,2,512]{2,0,1:T(8,128)S(1)}, u32[]{:S(2)}, u32[]{:S(2)}) collective-permute-start(f32[8,2,512]{2,0,1:T(8,128)S(1)} %copy.16), channel_id=1, source_target_pairs={{16,0},{24,8},{0,16},{8,24},{17,1},{25,9},{1,17},{9,25},{18,2},{26... | collective-permute-start | bytes 98312 | tf_op jit(solution)/shard_map/ppermute | solution.py:14
  41.8 45.4 %copy-start = (s32[1,2,64,1]{2,3,1,0:T(1,128)S(1)}, s32[1,2,64,1]{2,3,1,0:T(1,128)}, u32[]{:S(2)}) copy-start(s32[1,2,64,1]{2,3,1,0:T(1,128)} %param.5) | copy-start | bytes 1540
  68.7 15.0 %all-to-all-start = ((f32[8,8,2,512]{3,2,1,0:T(2,128)}), f32[8,8,2,512]{3,2,1,0:T(2,128)S(1)}, u32[]{:S(2)}, u32[]{:S(2)}) async-start(f32[8,8,2,512]{3,2,1,0:T(2,128)} %pad_maximum_fusion.1), calls=%async_computation | async-start | bytes 524288 | tf_op jit(solution)/shard_map/all_to_all | solution.py:68
  83.7 12.2 %all-to-all-start.2 = ((f32[8,8,2,512]{3,2,1,0:T(2,128)}), f32[8,8,2,512]{3,2,1,0:T(2,128)S(1)}, u32[]{:S(2)}, u32[]{:S(2)}) async-start(f32[8,8,2,512]{3,2,1,0:T(2,128)} %pad_maximum_fusion.2), calls=%async_computation.2 | async-start | bytes 524288 | tf_op jit(solution)/shard_map/all_to_all | solution.py:68
  171.6 10.9 %all-to-all-start.1 = ((f32[8,512,8]{1,2,0:T(8,128)}), f32[8,512,8]{1,2,0:T(8,128)S(1)}, u32[]{:S(2)}, u32[]{:S(2)}) async-start(f32[8,512,8]{1,2,0:T(8,128)} %bitcast.27), calls=%async_computation.1 | async-start | bytes 262144 | tf_op jit(solution)/shard_map/all_to_all | solution.py:81
  182.5 10.7 %all-to-all-start.3 = ((f32[8,512,8]{1,2,0:T(8,128)}), f32[8,512,8]{1,2,0:T(8,128)S(1)}, u32[]{:S(2)}, u32[]{:S(2)}) async-start(f32[8,512,8]{1,2,0:T(8,128)} %bitcast.48), calls=%async_computation.3 | async-start | bytes 262144 | tf_op jit(solution)/shard_map/all_to_all | solution.py:81
where the time goes:
time: 207 us; the launch traced here: 206 us
  matrix products  72.7 us (35%)
  other arithmetic  69 us (33%)
  waiting for transfers between devices  29.4 us (14%)
  starting transfers between devices  21.2 us (10%)
  blocking collectives  11.2 us (5%)
    dot_general x2, matrix products, per_device(): spread = jnp.dot(blocks, base_table, precision=lax.Precision.HIGHEST)  72.1 us
    sin x1, other arithmetic, phase_table(): return (jnp.cos(angles), jnp.sin(angles))  35.6 us
    concatenate x1, other arithmetic, per_device(): jnp.concatenate([jnp.concatenate([base_cos, base_sin], axis=1), jnp.conca...  25.2 us
    all_to_all x2, waiting for transfers between devices, per_device(): lax.all_to_all(crossed, 'freq', split_axis=0, concat_axis=3, tiled=True)  15.8 us
    all_to_all x2, waiting for transfers between devices, per_device(): lax.all_to_all(lagged, 'freq', split_axis=0, concat_axis=1, tiled=True)  13.6 us
    all_to_all x1, blocking collectives, per_device(): lax.all_to_all(outgoing, 'grp', split_axis=1, concat_axis=1, tiled=True)  11.2 us
    all_to_all x2, starting transfers between devices, per_device(): lax.all_to_all(crossed, 'freq', split_axis=0, concat_axis=3, tiled=True)  9.43 us
    all_to_all x2, starting transfers between devices, per_device(): lax.all_to_all(lagged, 'freq', split_axis=0, concat_axis=1, tiled=True)  6.97 us
  transfers between devices with their start and end apart: 8, of which 4 were waited for; matrix products, arithmetic and copies ran while one was open for 31% of the time, Pallas kernels for 0%

commit v1 on v0

v1 whole, which is shorter than its diff:
```python
import functools
import math

import jax
import jax.numpy as jnp
import numpy as np
from jax import lax
from jax.experimental import pallas as pl
from jax.experimental.pallas import tpu as pltpu
from jax.sharding import PartitionSpec as P

LAGS = 4096
LANES = 128
SUBLANES = 8
PARTS = 3


def split_bf16(values, parts):
    pieces = []
    for _ in range(parts - 1):
        piece = values.astype(jnp.bfloat16)
        pieces.append(piece)
        values = values - piece.astype(jnp.float32)
    pieces.append(values.astype(jnp.bfloat16))
    return pieces


def dft_tables(bin_total, half_band):
    turns = (np.arange(bin_total)[:, None] * (2 * np.arange(half_band) + 1)[None, :]) % (4 * bin_total)
    angles = turns * (math.pi / (2 * bin_total))
    tables = []
    for exact in (np.cos(angles), np.sin(angles)):
        high = exact.astype(jnp.bfloat16)
        low = (exact - high.astype(np.float64)).astype(jnp.bfloat16)
        tables += [high, low]
    return tables


def iota(shape, axis):
    return lax.broadcasted_iota(jnp.int32, shape, axis)


def dot(left, right):
    return jnp.dot(left, right, preferred_element_type=jnp.float32)


def pick_matrices(owner_ids, me, groups, stations, rounds, capacity):
    pairs = stations * stations
    listed = rounds * pairs
    rows = rounds * groups * capacity
    mine = owner_ids == me
    before = (iota((listed, listed), 0) < iota((listed, listed), 1)) & (
        iota((listed, listed), 0) // pairs == iota((listed, listed), 1) // pairs
    )
    rank = dot(mine.astype(jnp.bfloat16), before.astype(jnp.bfloat16))
    marked = jnp.where(mine, rank, -1.0).astype(jnp.bfloat16)
    of_group = (iota((rows, groups), 0) // capacity) % groups == iota((rows, groups), 1)
    held = dot(of_group.astype(jnp.bfloat16), marked)
    row_id = iota((rows, listed), 0)
    lane_id = iota((rows, listed), 1)
    chosen = (held == (row_id % capacity).astype(jnp.float32)) & (
        row_id // (groups * capacity) == lane_id // pairs
    )
    chosen = chosen.astype(jnp.bfloat16)
    columns = PARTS * groups * stations
    pair_id = iota((listed, columns), 0) % pairs
    station = iota((listed, columns), 1) % stations
    first = dot(chosen, (pair_id // stations == station).astype(jnp.bfloat16))
    second = dot(chosen, (pair_id % stations == station).astype(jnp.bfloat16))
    row_id = iota((rows, columns), 0)
    row_group = (row_id // capacity) % groups
    row_round = row_id // (groups * capacity)
    column_group = (iota((rows, columns), 1) // stations) % groups
    partner = (row_group + groups - 1 - row_round) % groups
    first = jnp.where(column_group == row_group, first, 0.0)
    second = jnp.where(column_group == partner, second, 0.0)
    return first.astype(jnp.bfloat16), second.astype(jnp.bfloat16)


def stack_kernel(
    sizes, me_ref, block_ref, owners_ref, twist_ref, ch_ref, cl_ref, sh_ref, sl_ref, out_ref,
    pick_a, pick_b, even, odd,
):
    groups, stations, rounds, capacity, band_bins = sizes
    step = pl.program_id(0)
    chunks = band_bins // LANES
    held = groups * stations

    @pl.when(step == 0)
    def _():
        first, second = pick_matrices(
            owners_ref[...], me_ref[0], groups, stations, rounds, capacity
        )
        pick_a[...] = first
        pick_b[...] = second
        even[...] = jnp.zeros_like(even)
        odd[...] = jnp.zeros_like(odd)

    def band(part):
        tiles = [
            block_ref[:, 0, pl.ds((part * chunks + q) * stations, stations), :].reshape(held, LANES)
            for q in range(chunks)
        ]
        return jnp.concatenate(tiles, axis=1)

    real, imag = band(0), band(1)
    turn_cos, turn_sin = twist_ref[0, 0:1, :], twist_ref[0, 1:2, :]
    turned_real = real * turn_cos + imag * turn_sin
    turned_imag = imag * turn_cos - real * turn_sin

    def picked(pick, values):
        return dot(pick[...], jnp.concatenate(split_bf16(values, PARTS), axis=0))

    a_real, a_imag = picked(pick_a, real), picked(pick_a, imag)
    b_real, b_imag = picked(pick_b, turned_real), picked(pick_b, turned_imag)
    cross_real = a_real * b_real + a_imag * b_imag
    cross_imag = a_imag * b_real - a_real * b_imag
    high, low = split_bf16(cross_real, 2)
    even[...] += dot(high, ch_ref[...]) + (dot(high, cl_ref[...]) + dot(low, ch_ref[...]))
    high, low = split_bf16(cross_imag, 2)
    odd[...] += dot(high, sh_ref[...]) + (dot(high, sl_ref[...]) + dot(low, sh_ref[...]))

    @pl.when(step == pl.num_programs(0) - 1)
    def _():
        half = even.shape[1]
        total = even[...] + odd[...]
        mirror = (iota((half, half), 0) + iota((half, half), 1) == half - 1).astype(jnp.bfloat16)
        pieces = [dot(piece, mirror) for piece in split_bf16(total, 3)]
        below = pieces[0] + (pieces[1] + pieces[2])
        out_ref[...] = jnp.concatenate([below, even[...] - odd[...]], axis=1)


def per_device(spectra, station_mask, owners):
    stations, _, band_bins = spectra.shape
    groups = lax.axis_size("grp")
    shards = lax.axis_size("freq")
    rounds = owners.shape[1]
    pairs = stations * stations
    bin_total = band_bins * shards
    capacity = (2 * pairs + groups - 1) // groups
    lag_band = LAGS // shards
    half_band = lag_band // 2
    chunks = band_bins // LANES
    rows = rounds * groups * capacity

    masked = spectra * station_mask.astype(jnp.float32)[:, None, None]
    tiles = masked.reshape(stations, 2, chunks, LANES).transpose(1, 2, 0, 3)
    tiles = tiles.reshape(2 * chunks * stations, LANES)
    listed = owners[0, :, :, 0].reshape(1, rounds * pairs).astype(jnp.float32)
    listed = jnp.broadcast_to(listed, (SUBLANES, rounds * pairs))
    payload = jnp.concatenate([tiles, listed], axis=0)
    gathered = lax.all_gather(payload, ("grp", "freq"), axis=0, tiled=False)
    depth = payload.shape[0]
    gathered = gathered.reshape(groups, shards, depth, LANES)
    owner_ids = gathered[:, 0, depth - SUBLANES, :].astype(jnp.int32)

    me = lax.axis_index("grp").astype(jnp.int32).reshape(1)
    centre = lag_band * (2 * lax.axis_index("freq") + 1) - 1 - LAGS
    turns = jnp.mod(jnp.arange(bin_total, dtype=jnp.int32) * centre, 4 * bin_total)
    angles = turns.astype(jnp.float32) * (math.pi / (2 * bin_total))
    norm = 1.0 / math.sqrt(bin_total)
    twist = jnp.stack([jnp.cos(angles) * norm, jnp.sin(angles) * norm])
    twist = twist.reshape(2, shards, band_bins).transpose(1, 0, 2)
    tables = [jnp.asarray(table) for table in dft_tables(bin_total, half_band)]

    table_spec = pl.BlockSpec((band_bins, half_band), lambda f: (f, 0))
    columns = PARTS * groups * stations
    out = pl.pallas_call(
        functools.partial(stack_kernel, (groups, stations, rounds, capacity, band_bins)),
        grid=(shards,),
        out_shape=jax.ShapeDtypeStruct((rows, lag_band), jnp.float32),
        in_specs=[
            pl.BlockSpec(memory_space=pltpu.SMEM),
            pl.BlockSpec((groups, 1, depth, LANES), lambda f: (0, f, 0, 0)),
            pl.BlockSpec((groups, LANES), lambda f: (0, 0)),
            pl.BlockSpec((1, 2, band_bins), lambda f: (f, 0, 0)),
            table_spec,
            table_spec,
            table_spec,
            table_spec,
        ],
        out_specs=pl.BlockSpec((rows, lag_band), lambda f: (0, 0)),
        scratch_shapes=[
            pltpu.VMEM((rows, columns), jnp.bfloat16),
            pltpu.VMEM((rows, columns), jnp.bfloat16),
            pltpu.VMEM((rows, half_band), jnp.float32),
            pltpu.VMEM((rows, half_band), jnp.float32),
        ],
        compiler_params=pltpu.CompilerParams(
            dimension_semantics=("arbitrary",), vmem_limit_bytes=32 * 1024 * 1024
        ),
        name="owned_stacks",
    )(me, gathered, owner_ids, twist, *tables)
    return out.reshape(1, rounds, groups, capacity, lag_band)


def solution(mesh):
    placed = (P("grp", None, "freq"), P("grp"), P("grp", None, None, None))
    return jax.shard_map(
        per_device,
        mesh=mesh,
        in_specs=placed,
        out_specs=P("grp", None, None, None, "freq"),
        check_vma=False,
    )
```

time: 207 us -> 92.8 us (0.45)
  matrix products: 72.7 us -> 0 us
  other arithmetic: 69 us -> 3.34 us
  waiting for transfers between devices: 29.4 us -> 57.1 us
  starting transfers between devices: 21.2 us -> 0.01 us
  between operations: 0.14 us -> 13.4 us
  blocking collectives: 11.2 us -> 0 us
  Pallas kernels: 0 us -> 9.94 us
  local copies, waits for them, and re-layouts: 1.97 us -> 8.48 us
    dot_general x4 -> x0, matrix products: 72.7 us -> none  [the longest x2 72.1 us: per_device(): spread = jnp.dot(blocks, base_table, precision=lax.Precision.HIGHEST)]
    all_gather x0 -> x1, waiting for transfers between devices: none -> 57.1 us  [per_device(): gathered = lax.all_gather(payload, ('grp', 'freq'), axis=0, tiled=False)]
    sin x1 -> x0, other arithmetic: 35.6 us -> none  [phase_table(): return (jnp.cos(angles), jnp.sin(angles))]
    all_to_all x4 -> x0, waiting for transfers between devices: 29.4 us -> none  [the longest x2 15.8 us: per_device(): lax.all_to_all(crossed, 'freq', split_axis=0, concat_axis=3, tiled=True)]
    concatenate x1, other arithmetic: 25.2 us -> 0.62 us  [per_device(): payload = jnp.concatenate([tiles, listed], axis=0)]
    all_to_all x4 -> x0, starting transfers between devices: 16.4 us -> none  [the longest x2 9.43 us: per_device(): lax.all_to_all(crossed, 'freq', split_axis=0, concat_axis=3, tiled=True)]
    all_to_all x1 -> x0, blocking collectives: 11.2 us -> none  [per_device(): lax.all_to_all(outgoing, 'grp', split_axis=1, concat_axis=1, tiled=True)]
    pallas_call x0 -> x1, Pallas kernels: none -> 9.94 us  [per_device(): pl.pallas_call(functools.partial(stack_kernel, (groups, stations, rounds,...]
  transfers between devices with their start and end apart: 8 -> 1, of which waited for: 4 -> 1; matrix products, arithmetic and copies ran while one was open for 31% -> 1% of each run, Pallas kernels for 0% -> 0%
where the time goes in v1:
time: 92.8 us; the launch traced here: 92.3 us
  waiting for transfers between devices  57.1 us (62%)
  between operations  13.4 us (14%)
  Pallas kernels  9.94 us (11%)
  local copies, waits for them, and re-layouts  8.48 us (9%)
  other arithmetic  3.34 us (4%)
    all_gather x1, waiting for transfers between devices, per_device(): gathered = lax.all_gather(payload, ('grp', 'freq'), axis=0, tiled=False)  57.1 us
    pallas_call x1, Pallas kernels, per_device(): pl.pallas_call(functools.partial(stack_kernel, (groups, stations, rounds,...  9.94 us
    unnamed x10, local copies, waits for them, and re-layouts  7.63 us
  transfers between devices with their start and end apart: 1, of which 1 were waited for; matrix products, arithmetic and copies ran while one was open for 1% of the time, Pallas kernels for 0%

profile of v1, /device:TPU:0, one launch (start us, length us, event | category | flops | bytes accessed | tf_op | source)
XLA Modules:
  0.0 92.3 jit_solution(14617270633131948530)
XLA Ops:
  6.5 0.0 all-gather.3.cloned.1.call-start
  6.5 0.7 convert_element_type.35
  7.2 0.7 convert_reduce_fusion
  7.9 0.1 convert_element_type.37
  8.0 0.8 broadcast_multiply_fusion
  8.9 0.6 pad_maximum_fusion
  9.5 0.0 all-gather.3.cloned.1.call-update
  9.6 0.5 cosine_multiply_fusion
  10.1 57.1 %all-gather.3.cloned.1.call-done = f32[2304,128]{1,0:T(8,128)} async-done(((f32[72,128]{1,0:T(8,128)}), f32[2304,128]{1,0:T(8,128)}) %all-gather.3.cloned.1.call-update) | async-done | bytes 1179664 | tf_op jit(solution)/shard_map/all_gather | solution.py:152
  67.2 0.7 slice.4
  67.9 0.0 copy-start
  67.9 1.6 %copy-done = bf16[4096,256]{1,0:T(8,128)(2,1)S(1)} copy-done((bf16[4096,256]{1,0:T(8,128)(2,1)S(1)}, bf16[4096,256]{1,0:T(8,128)(2,1)}, u32[]{:S(2)}) %copy-start) | copy-done | bytes 2097176
  69.5 0.0 copy-start.1
  69.5 1.6 %copy-done.1 = bf16[4096,256]{1,0:T(8,128)(2,1)S(1)} copy-done((bf16[4096,256]{1,0:T(8,128)(2,1)S(1)}, bf16[4096,256]{1,0:T(8,128)(2,1)}, u32[]{:S(2)}) %copy-start.1) | copy-done | bytes 2097176
  71.1 0.0 copy-start.2
  71.1 1.6 %copy-done.2 = bf16[4096,256]{1,0:T(8,128)(2,1)S(1)} copy-done((bf16[4096,256]{1,0:T(8,128)(2,1)S(1)}, bf16[4096,256]{1,0:T(8,128)(2,1)}, u32[]{:S(2)}) %copy-start.2) | copy-done | bytes 2097176
  72.7 0.0 copy-start.3
  72.7 1.6 %copy-done.3 = bf16[4096,256]{1,0:T(8,128)(2,1)S(1)} copy-done((bf16[4096,256]{1,0:T(8,128)(2,1)S(1)}, bf16[4096,256]{1,0:T(8,128)(2,1)}, u32[]{:S(2)}) %copy-start.3) | copy-done | bytes 2097176
  74.3 0.0 copy-start.4
  74.3 1.3 %copy-done.4 = f32[2304,128]{1,0:T(8,128)S(1)} copy-done((f32[2304,128]{1,0:T(8,128)S(1)}, f32[2304,128]{1,0:T(8,128)}, u32[]{:S(2)}) %copy-start.4) | copy-done | bytes 1179672
  75.6 9.9 %owned_stacks.1 = f32[256,512]{1,0:T(8,128)} custom-call(s32[1]{0:T(128)} %bitcast.me_ref, f32[4,8,72,128]{3,2,1,0:T(8,128)S(1)} %bitcast.12, s32[4,128]{1,0:T(4,128)S(1)} %convert_bitcast_fusion.owners_ref, f32[8,2,512]{2,1,0:T(2,128)S(1)} %maximum_bitcast_fusion.twist_ref, bf16[4096,256]{1,0:T(8,128)(2,1)S(1)} %copy-done.3, ...), custom_call_target="tpu_custom_call" | custom-call | tf_op jit(solution)/shard_map/owned_stacks/pallas_call | solution.py:168
  (6 shorter events, 0.1 us)
Async XLA Ops:
  6.5 60.7 %all-gather.3.cloned.1.call-start = ((), (), s32[]{:S(2)}) async-start(), calls=%async_computation | async-start | bytes 1216512 | tf_op jit(solution)/shard_map/all_gather | solution.py:152
  67.9 1.6 %copy-start = (bf16[4096,256]{1,0:T(8,128)(2,1)S(1)}, bf16[4096,256]{1,0:T(8,128)(2,1)}, u32[]{:S(2)}) copy-start(bf16[4096,256]{1,0:T(8,128)(2,1)} %constant.51.clone.sl_ref) | copy-start | bytes 6291460
  69.5 1.6 %copy-start.1 = (bf16[4096,256]{1,0:T(8,128)(2,1)S(1)}, bf16[4096,256]{1,0:T(8,128)(2,1)}, u32[]{:S(2)}) copy-start(bf16[4096,256]{1,0:T(8,128)(2,1)} %constant.50.clone.sh_ref) | copy-start | bytes 6291460
  71.1 1.6 %copy-start.2 = (bf16[4096,256]{1,0:T(8,128)(2,1)S(1)}, bf16[4096,256]{1,0:T(8,128)(2,1)}, u32[]{:S(2)}) copy-start(bf16[4096,256]{1,0:T(8,128)(2,1)} %constant.49.clone.cl_ref) | copy-start | bytes 6291460
  72.7 1.6 %copy-start.3 = (bf16[4096,256]{1,0:T(8,128)(2,1)S(1)}, bf16[4096,256]{1,0:T(8,128)(2,1)}, u32[]{:S(2)}) copy-start(bf16[4096,256]{1,0:T(8,128)(2,1)} %constant.48.clone.ch_ref) | copy-start | bytes 6291460
  74.3 1.3 %copy-start.4 = (f32[2304,128]{1,0:T(8,128)S(1)}, f32[2304,128]{1,0:T(8,128)}, u32[]{:S(2)}) copy-start(f32[2304,128]{1,0:T(8,128)} %all-gather.3.cloned.1.call-done) | copy-start | bytes 3538948
Sparse Core Ops, SparseCore 0:
  10.3 56.8 all-gather.2

commit v2 on v1

--- a/solution.py
+++ b/solution.py
@@ -11,7 +11,6 @@
 
 LAGS = 4096
 LANES = 128
-SUBLANES = 8
 PARTS = 3
 
 
@@ -44,7 +43,7 @@
     return jnp.dot(left, right, preferred_element_type=jnp.float32)
 
 
-def pick_matrices(owner_ids, me, groups, stations, rounds, capacity):
+def pick_matrices(owner_ids, column_group, me, groups, stations, rounds, capacity):
     pairs = stations * stations
     listed = rounds * pairs
     rows = rounds * groups * capacity
@@ -70,26 +69,23 @@
     row_id = iota((rows, columns), 0)
     row_group = (row_id // capacity) % groups
     row_round = row_id // (groups * capacity)
-    column_group = (iota((rows, columns), 1) // stations) % groups
     partner = (row_group + groups - 1 - row_round) % groups
     first = jnp.where(column_group == row_group, first, 0.0)
     second = jnp.where(column_group == partner, second, 0.0)
     return first.astype(jnp.bfloat16), second.astype(jnp.bfloat16)
 
 
-def stack_kernel(
-    sizes, me_ref, block_ref, owners_ref, twist_ref, ch_ref, cl_ref, sh_ref, sl_ref, out_ref,
-    pick_a, pick_b, even, odd,
-):
+def stack_kernel(sizes, bands_ref, me_ref, owners_ref, columns_ref, twist_ref, *refs):
     groups, stations, rounds, capacity, band_bins = sizes
+    block_refs, refs = refs[:-9], refs[-9:]
+    ch_ref, cl_ref, sh_ref, sl_ref, out_ref, pick_a, pick_b, even, odd = refs
     step = pl.program_id(0)
     chunks = band_bins // LANES
-    held = groups * stations
 
     @pl.when(step == 0)
     def _():
         first, second = pick_matrices(
-            owners_ref[...], me_ref[0], groups, stations, rounds, capacity
+            owners_ref[...], columns_ref[...], me_ref[0], groups, stations, rounds, capacity
         )
         pick_a[...] = first
         pick_b[...] = second
@@ -97,10 +93,13 @@
         odd[...] = jnp.zeros_like(odd)
 
     def band(part):
-        tiles = [
-            block_ref[:, 0, pl.ds((part * chunks + q) * stations, stations), :].reshape(held, LANES)
-            for q in range(chunks)
-        ]
+        tiles = []
+        for q in range(chunks):
+            rows = pl.ds((part * chunks + q) * stations, stations)
+            held = [
+                ref[group, 0, rows, :] for ref in block_refs for group in range(ref.shape[0])
+            ]
+            tiles.append(jnp.concatenate(held, axis=0))
         return jnp.concatenate(tiles, axis=1)
 
     real, imag = band(0), band(1)
@@ -130,12 +129,46 @@
         out_ref[...] = jnp.concatenate([below, even[...] - odd[...]], axis=1)
 
 
+def swapped(block, axis, mask):
+    route = [(i ^ mask, i) for i in range(lax.axis_size(axis))]
+    return lax.ppermute(block, axis, route)
+
+
+def shifted(block, axis, distance):
+    size = lax.axis_size(axis)
+    return lax.ppermute(block, axis, [((i - distance) % size, i) for i in range(size)])
+
+
+def of_all(block, axis):
+    size = lax.axis_size(axis)
+    me = lax.axis_index(axis)
+    blocks = [block] + [shifted(block, axis, distance) for distance in range(1, size)]
+    places = jnp.stack([(me - distance) % size for distance in range(size)])
+    return blocks, places.astype(jnp.int32)
+
+
+def by_halves(block, axis):
+    size = lax.axis_size(axis)
+    if size & (size - 1):
+        return of_all(block, axis)
+    me = lax.axis_index(axis)
+    blocks, masks = [block], [0]
+    bit = size // 2
+    while bit:
+        blocks += [swapped(held, axis, bit) for held in blocks]
+        masks += [mask ^ bit for mask in masks]
+        bit //= 2
+    places = jnp.stack([me ^ mask for mask in masks])
+    return blocks, places.astype(jnp.int32)
+
+
 def per_device(spectra, station_mask, owners):
     stations, _, band_bins = spectra.shape
     groups = lax.axis_size("grp")
     shards = lax.axis_size("freq")
     rounds = owners.shape[1]
     pairs = stations * stations
+    listed = rounds * pairs
     bin_total = band_bins * shards
     capacity = (2 * pairs + groups - 1) // groups
     lag_band = LAGS // shards
@@ -146,15 +179,16 @@
     masked = spectra * station_mask.astype(jnp.float32)[:, None, None]
     tiles = masked.reshape(stations, 2, chunks, LANES).transpose(1, 2, 0, 3)
     tiles = tiles.reshape(2 * chunks * stations, LANES)
-    listed = owners[0, :, :, 0].reshape(1, rounds * pairs).astype(jnp.float32)
-    listed = jnp.broadcast_to(listed, (SUBLANES, rounds * pairs))
-    payload = jnp.concatenate([tiles, listed], axis=0)
-    gathered = lax.all_gather(payload, ("grp", "freq"), axis=0, tiled=False)
-    depth = payload.shape[0]
-    gathered = gathered.reshape(groups, shards, depth, LANES)
-    owner_ids = gathered[:, 0, depth - SUBLANES, :].astype(jnp.int32)
-
-    me = lax.axis_index("grp").astype(jnp.int32).reshape(1)
+    own_owners = owners[0, :, :, 0].reshape(1, listed)
+    owner_lists, _ = of_all(own_owners, "grp")
+    bands, band_places = of_all(tiles, "freq")
+    blocks, group_places = by_halves(jnp.stack(bands), "grp")
+    blocks = [block[None] for block in blocks]
+
+    me = lax.axis_index("grp").astype(jnp.int32)
+    owner_ids = jnp.concatenate(owner_lists, axis=0)
+    owner_ids = jnp.roll(owner_ids[::-1], me + 1, axis=0)
+    column_group = jnp.tile(jnp.repeat(group_places, stations), PARTS)[None, :]
     centre = lag_band * (2 * lax.axis_index("freq") + 1) - 1 - LAGS
     turns = jnp.mod(jnp.arange(bin_total, dtype=jnp.int32) * centre, 4 * bin_total)
     angles = turns.astype(jnp.float32) * (math.pi / (2 * bin_total))
@@ -163,34 +197,34 @@
     twist = twist.reshape(2, shards, band_bins).transpose(1, 0, 2)
     tables = [jnp.asarray(table) for table in dft_tables(bin_total, half_band)]
 
-    table_spec = pl.BlockSpec((band_bins, half_band), lambda f: (f, 0))
     columns = PARTS * groups * stations
+    depth = tiles.shape[0]
     out = pl.pallas_call(
         functools.partial(stack_kernel, (groups, stations, rounds, capacity, band_bins)),
-        grid=(shards,),
+        grid_spec=pltpu.PrefetchScalarGridSpec(
+            num_scalar_prefetch=2,
+            grid=(shards,),
+            in_specs=[
+                pl.BlockSpec((groups, listed), lambda f, *_: (0, 0)),
+                pl.BlockSpec((1, columns), lambda f, *_: (0, 0)),
+                pl.BlockSpec((1, 2, band_bins), lambda f, places, _: (places[f], 0, 0)),
+            ]
+            + [pl.BlockSpec((1, 1, depth, LANES), lambda f, *_: (0, f, 0, 0))] * len(blocks)
+            + [pl.BlockSpec((band_bins, half_band), lambda f, places, _: (places[f], 0))] * 4,
+            out_specs=pl.BlockSpec((rows, lag_band), lambda f, *_: (0, 0)),
+            scratch_shapes=[
+                pltpu.VMEM((rows, columns), jnp.bfloat16),
+                pltpu.VMEM((rows, columns), jnp.bfloat16),
+                pltpu.VMEM((rows, half_band), jnp.float32),
+                pltpu.VMEM((rows, half_band), jnp.float32),
+            ],
+        ),
         out_shape=jax.ShapeDtypeStruct((rows, lag_band), jnp.float32),
-        in_specs=[
-            pl.BlockSpec(memory_space=pltpu.SMEM),
-            pl.BlockSpec((groups, 1, depth, LANES), lambda f: (0, f, 0, 0)),
-            pl.BlockSpec((groups, LANES), lambda f: (0, 0)),
-            pl.BlockSpec((1, 2, band_bins), lambda f: (f, 0, 0)),
-            table_spec,
-            table_spec,
-            table_spec,
-            table_spec,
-        ],
-        out_specs=pl.BlockSpec((rows, lag_band), lambda f: (0, 0)),
-        scratch_shapes=[
-            pltpu.VMEM((rows, columns), jnp.bfloat16),
-            pltpu.VMEM((rows, columns), jnp.bfloat16),
-            pltpu.VMEM((rows, half_band), jnp.float32),
-            pltpu.VMEM((rows, half_band), jnp.float32),
-        ],
         compiler_params=pltpu.CompilerParams(
-            dimension_semantics=("arbitrary",), vmem_limit_bytes=32 * 1024 * 1024
+            dimension_semantics=("arbitrary",), vmem_limit_bytes=56 * 1024 * 1024
         ),
         name="owned_stacks",
-    )(me, gathered, owner_ids, twist, *tables)
+    )(band_places, me.reshape(1), owner_ids, column_group, twist, *blocks, *tables)
     return out.reshape(1, rounds, groups, capacity, lag_band)
 
 

time: 92.8 us -> 64.7 us (0.70)
  waiting for transfers between devices: 57.1 us -> 33.6 us
  between operations: 13.4 us -> 0.16 us
  starting transfers between devices: 0.01 us -> 10.5 us
  local copies, waits for them, and re-layouts: 8.48 us -> 3.47 us
  Pallas kernels: 9.94 us -> 12.4 us
    all_gather x1 -> x0, waiting for transfers between devices: 57.1 us -> none  [per_device(): gathered = lax.all_gather(payload, ('grp', 'freq'), axis=0, tiled=False)]
    ppermute x0 -> x13, waiting for transfers between devices: none -> 33.6 us  [the longest x10 29.2 us: shifted(): lax.ppermute(block, axis, [((i - distance) % size, i) for i in range(size)])]
    ppermute x0 -> x13, starting transfers between devices: none -> 10.5 us  [the longest x10 9.5 us: shifted(): lax.ppermute(block, axis, [((i - distance) % size, i) for i in range(size)])]
    unnamed x10 -> x16, local copies, waits for them, and re-layouts: 7.63 us -> 1.26 us
    pallas_call x1, Pallas kernels: 9.94 us -> 12.4 us  [per_device(): pl.pallas_call(functools.partial(stack_kernel, (groups, stations, rounds,...]
    another operation x0 -> x6, local copies, waits for them, and re-layouts: none -> 1.47 us  [the longest x3 0.71 us: per_device(): column_group = jnp.tile(jnp.repeat(group_places, stations), PARTS)[None, :]]
    unnamed x0 -> x1, other arithmetic: none -> 1.34 us
  transfers between devices with their start and end apart: 1 -> 13, of which waited for: 1 -> 8; matrix products, arithmetic and copies ran while one was open for 1% -> 8% of each run, Pallas kernels for 0% -> 0%
where the time goes in v2:
time: 64.7 us; the launch traced here: 64.3 us
  waiting for transfers between devices  33.6 us (52%)
  Pallas kernels  12.4 us (19%)
  starting transfers between devices  10.5 us (16%)
  other arithmetic  4.06 us (6%)
  local copies, waits for them, and re-layouts  3.47 us (5%)
    ppermute x10, waiting for transfers between devices, shifted(): lax.ppermute(block, axis, [((i - distance) % size, i) for i in range(size)])  29.2 us
    pallas_call x1, Pallas kernels, per_device(): pl.pallas_call(functools.partial(stack_kernel, (groups, stations, rounds,...  12.4 us
    ppermute x10, starting transfers between devices, shifted(): lax.ppermute(block, axis, [((i - distance) % size, i) for i in range(size)])  9.5 us
    ppermute x3, waiting for transfers between devices, swapped(): return lax.ppermute(block, axis, route)  4.45 us
    unnamed x1, other arithmetic  1.34 us
  transfers between devices with their start and end apart: 13, of which 8 were waited for; matrix products, arithmetic and copies ran while one was open for 8% of the time, Pallas kernels for 0%

profile of v2, /device:TPU:0, one launch (start us, length us, event | category | flops | bytes accessed | tf_op | source)
XLA Modules:
  0.0 64.3 jit_solution(3510862859377418680)
XLA Ops:
  0.0 0.5 broadcast.141
  0.5 1.3 %reduce.3 = s32[2,64]{1,0:T(2,128)S(1)} reduce(s32[1,2,64,1]{2,3,1,0:T(1,128)} %param.9, s32[]{:T(128)} %broadcast.141), dimensions={0,3}, to_apply=%param.9.reduce_sub_computation.3 | reduce | bytes 1028 | tf_op args[2]
  1.9 0.1 reshape_squeeze.3
  1.9 2.4 %collective-permute-start.2 = (s32[1,128]{1,0:T(1,128)S(1)}, s32[1,128]{1,0:T(1,128)S(1)}, u32[]{:S(2)}, u32[]{:S(2)}) collective-permute-start(s32[1,128]{1,0:T(1,128)S(1)} %reshape_squeeze.3), channel_id=1, source_target_pairs={{8,0},{16,8},{24,16},{0,24},{9,1},{17,9},{25,17},{1,25},{10,2},{18... | collective-permute-start | bytes 1544 | tf_op jit(solution)/shard_map/ppermute | solution.py:139
  4.3 0.6 collective-permute-start.1
  4.9 0.2 collective-permute-start
  5.1 0.7 %convert_element_type.20 = f32[8]{0:T(128)S(1)} convert(s32[8]{0:T(128)} %param.8) | non-fusion elementwise | flops 8 | bytes 64 | tf_op jit(solution)/shard_map/convert_element_type | solution.py:179
  5.8 0.8 %broadcast_multiply_fusion = f32[8,2,512]{2,1,0:T(2,128)S(1)} fusion(f32[8,2,512]{2,1,0:T(2,128)} %param.7, f32[8]{0:T(128)S(1)} %convert_element_type.20), kind=kLoop, calls=%fused_computation.12 | loop fusion | flops 8192 | bytes 65568 | tf_op jit(solution)/shard_map/mul | solution.py:179
  6.7 4.6 %collective-permute-start.9 = (f32[64,128]{1,0:T(8,128)S(1)}, f32[64,128]{1,0:T(8,128)S(1)}, u32[]{:S(2)}, u32[]{:S(2)}) collective-permute-start(f32[64,128]{1,0:T(8,128)S(1)} %bitcast.43), channel_id=1, source_target_pairs={{1,0},{2,1},{3,2},{4,3},{5,4},{6,5},{7,6},{0,7},{9,8},{10,9},{11,1... | collective-permute-start | bytes 98312 | tf_op jit(solution)/shard_map/ppermute | solution.py:139
  11.3 0.0 collective-permute-start.3
  11.3 0.1 pad_add_fusion.2
  11.5 0.1 broadcast_in_dim.16
  11.5 0.1 tile.7
  11.6 0.6 broadcast_in_dim_tile.3.columns_ref
  12.2 5.9 %collective-permute-done.3 = f32[64,128]{1,0:T(8,128)S(1)} collective-permute-done((f32[64,128]{1,0:T(8,128)S(1)}, f32[64,128]{1,0:T(8,128)S(1)}, u32[]{:S(2)}, u32[]{:S(2)}) %collective-permute-start.3) | collective-permute-done | bytes 32800 | tf_op jit(solution)/shard_map/ppermute | solution.py:139
  18.1 0.0 collective-permute-start.4
  18.1 5.8 %collective-permute-done.4 = f32[64,128]{1,0:T(8,128)S(1)} collective-permute-done((f32[64,128]{1,0:T(8,128)S(1)}, f32[64,128]{1,0:T(8,128)S(1)}, u32[]{:S(2)}, u32[]{:S(2)}) %collective-permute-start.4) | collective-permute-done | bytes 32800 | tf_op jit(solution)/shard_map/ppermute | solution.py:139
  23.9 0.0 collective-permute-start.5
  23.9 5.7 %collective-permute-done.5 = f32[64,128]{1,0:T(8,128)S(1)} collective-permute-done((f32[64,128]{1,0:T(8,128)S(1)}, f32[64,128]{1,0:T(8,128)S(1)}, u32[]{:S(2)}, u32[]{:S(2)}) %collective-permute-start.5) | collective-permute-done | bytes 32800 | tf_op jit(solution)/shard_map/ppermute | solution.py:139
  29.6 0.0 collective-permute-start.6
  29.6 4.8 %collective-permute-done.6 = f32[64,128]{1,0:T(8,128)S(1)} collective-permute-done((f32[64,128]{1,0:T(8,128)S(1)}, f32[64,128]{1,0:T(8,128)S(1)}, u32[]{:S(2)}, u32[]{:S(2)}) %collective-permute-start.6) | collective-permute-done | bytes 32800 | tf_op jit(solution)/shard_map/ppermute | solution.py:139
  34.4 0.0 collective-permute-start.7
  34.4 4.8 %collective-permute-done.7 = f32[64,128]{1,0:T(8,128)S(1)} collective-permute-done((f32[64,128]{1,0:T(8,128)S(1)}, f32[64,128]{1,0:T(8,128)S(1)}, u32[]{:S(2)}, u32[]{:S(2)}) %collective-permute-start.7) | collective-permute-done | bytes 32800 | tf_op jit(solution)/shard_map/ppermute | solution.py:139
  39.2 1.7 %collective-permute-start.8 = (f32[64,128]{1,0:T(8,128)S(1)}, f32[64,128]{1,0:T(8,128)S(1)}, u32[]{:S(2)}, u32[]{:S(2)}) collective-permute-start(f32[64,128]{1,0:T(8,128)S(1)} %bitcast.50), channel_id=1, source_target_pairs={{2,0},{3,1},{4,2},{5,3},{6,4},{7,5},{0,6},{1,7},{10,8},{11,9},{12,... | collective-permute-start | bytes 98312 | tf_op jit(solution)/shard_map/ppermute | solution.py:139
  41.0 2.2 %collective-permute-done.8 = f32[64,128]{1,0:T(8,128)S(1)} collective-permute-done((f32[64,128]{1,0:T(8,128)S(1)}, f32[64,128]{1,0:T(8,128)S(1)}, u32[]{:S(2)}, u32[]{:S(2)}) %collective-permute-start.8) | collective-permute-done | bytes 32800 | tf_op jit(solution)/shard_map/ppermute | solution.py:139
  43.2 0.0 collective-permute-done.9
  43.2 0.0 copy-start
  43.2 1.0 %collective-permute-start.10 = (f32[8,64,128]{2,1,0:T(8,128)S(1)}, f32[8,64,128]{2,1,0:T(8,128)S(1)}, u32[]{:S(2)}, u32[]{:S(2)}) collective-permute-start(f32[8,64,128]{2,1,0:T(8,128)S(1)} %bitcast_dynamic-update-slice_fusion), channel_id=1, source_target_pairs={{16,0},{24,8},{0,16},{8,24},{17,1},{25,9},{1,17},{9,25},{18,2},{26... | collective-permute-start | bytes 786440 | tf_op jit(solution)/shard_map/ppermute | solution.py:134
  44.2 0.5 cosine_multiply_fusion
  44.7 0.6 maximum_bitcast_fusion.twist_ref
  45.3 0.7 %stack.77.bands_ref = s32[8]{0:T(128)} concatenate(s32[1]{0:T(128)} %bitcast, s32[1]{0:T(128)} %bitcast.1, s32[1]{0:T(128)} %bitcast.2, s32[1]{0:T(128)} %bitcast.3, s32[1]{0:T(128)} %bitcast.4, s32[1]{0:T(128)} %bitcast.5, s32[1]{0:T(128)} %bitcast.6, s32[1]{0:T(128)} %bitcast.7), dimensions={0} | concatenate | bytes 64 | tf_op jit(solution)/shard_map/stack | solution.py:146
  46.0 0.0 collective-permute-start.11
  46.0 3.6 %collective-permute-done.10 = f32[8,64,128]{2,1,0:T(8,128)S(1)} collective-permute-done((f32[8,64,128]{2,1,0:T(8,128)S(1)}, f32[8,64,128]{2,1,0:T(8,128)S(1)}, u32[]{:S(2)}, u32[]{:S(2)}) %collective-permute-start.10) | collective-permute-done | bytes 262176 | tf_op jit(solution)/shard_map/ppermute | solution.py:134
  49.6 0.0 copy-start.1
  49.6 0.0 collective-permute-start.12
  49.6 0.0 collective-permute-done.2
  49.6 0.0 collective-permute-done.1
  49.6 0.0 collective-permute-done
  49.7 0.6 constant_dynamic-slice_fusion.owners_ref
  50.3 0.0 collective-permute-done.11
  50.3 0.0 copy-start.2
  50.3 0.8 %collective-permute-done.12 = f32[8,64,128]{2,1,0:T(8,128)S(1)} collective-permute-done((f32[8,64,128]{2,1,0:T(8,128)S(1)}, f32[8,64,128]{2,1,0:T(8,128)S(1)}, u32[]{:S(2)}, u32[]{:S(2)}) %collective-permute-start.12) | collective-permute-done | bytes 262176 | tf_op jit(solution)/shard_map/ppermute | solution.py:134
  51.2 0.0 copy-start.3
  51.2 0.0 copy-done
  51.2 0.0 copy-done.1
  51.2 0.0 copy-done.2
  51.2 0.7 %copy-done.3 = f32[8,64,128]{2,1,0:T(8,128)} copy-done((f32[8,64,128]{2,1,0:T(8,128)}, f32[8,64,128]{2,1,0:T(8,128)S(1)}, u32[]{:S(2)}) %copy-start.3) | copy-done | bytes 262168
  51.9 12.4 %owned_stacks.1 = f32[256,512]{1,0:T(8,128)} custom-call(s32[8]{0:T(128)} %stack.77.bands_ref, s32[1]{0:T(128)} %bitcast.8.me_ref, s32[4,128]{1,0:T(4,128)} %constant_dynamic-slice_fusion.owners_ref, s32[1,96]{1,0:T(1,128)} %broadcast_in_dim_tile.3.columns_ref, f32[8,2,512]{2,1,0:T(2,128)} %maximum_bitcast_fusion.twist_ref, f32[1,8,64,128]{3,2,1,0:T(8,128)} %bitcast.39, ...), custom_call_target="tpu_custom_call" | custom-call | tf_op jit(solution)/shard_map/owned_stacks/pallas_call | solution.py:202
  (15 shorter events, 0.1 us)
Async XLA Ops:
  1.9 47.7 %collective-permute-start.2 = (s32[1,128]{1,0:T(1,128)S(1)}, s32[1,128]{1,0:T(1,128)S(1)}, u32[]{:S(2)}, u32[]{:S(2)}) collective-permute-start(s32[1,128]{1,0:T(1,128)S(1)} %reshape_squeeze.3), channel_id=1, source_target_pairs={{8,0},{16,8},{24,16},{0,24},{9,1},{17,9},{25,17},{1,25},{10,2},{18... | collective-permute-start | bytes 1544 | tf_op jit(solution)/shard_map/ppermute | solution.py:139
  4.3 45.3 %collective-permute-start.1 = (s32[1,128]{1,0:T(1,128)S(1)}, s32[1,128]{1,0:T(1,128)S(1)}, u32[]{:S(2)}, u32[]{:S(2)}) collective-permute-start(s32[1,128]{1,0:T(1,128)S(1)} %reshape_squeeze.3), channel_id=1, source_target_pairs={{16,0},{24,8},{0,16},{8,24},{17,1},{25,9},{1,17},{9,25},{18,2},{26... | collective-permute-start | bytes 1544 | tf_op jit(solution)/shard_map/ppermute | solution.py:139
  4.9 44.7 %collective-permute-start = (s32[1,128]{1,0:T(1,128)S(1)}, s32[1,128]{1,0:T(1,128)S(1)}, u32[]{:S(2)}, u32[]{:S(2)}) collective-permute-start(s32[1,128]{1,0:T(1,128)S(1)} %reshape_squeeze.3), channel_id=1, source_target_pairs={{24,0},{0,8},{8,16},{16,24},{25,1},{1,9},{9,17},{17,25},{26,2},{2,... | collective-permute-start | bytes 1544 | tf_op jit(solution)/shard_map/ppermute | solution.py:139
  6.7 36.5 %collective-permute-start.9 = (f32[64,128]{1,0:T(8,128)S(1)}, f32[64,128]{1,0:T(8,128)S(1)}, u32[]{:S(2)}, u32[]{:S(2)}) collective-permute-start(f32[64,128]{1,0:T(8,128)S(1)} %bitcast.43), channel_id=1, source_target_pairs={{1,0},{2,1},{3,2},{4,3},{5,4},{6,5},{7,6},{0,7},{9,8},{10,9},{11,1... | collective-permute-start | bytes 98312 | tf_op jit(solution)/shard_map/ppermute | solution.py:139
  11.3 6.9 %collective-permute-start.3 = (f32[64,128]{1,0:T(8,128)S(1)}, f32[64,128]{1,0:T(8,128)S(1)}, u32[]{:S(2)}, u32[]{:S(2)}) collective-permute-start(f32[64,128]{1,0:T(8,128)S(1)} %bitcast.44), channel_id=1, source_target_pairs={{7,0},{0,1},{1,2},{2,3},{3,4},{4,5},{5,6},{6,7},{15,8},{8,9},{9,10... | collective-permute-start | bytes 98312 | tf_op jit(solution)/shard_map/ppermute | solution.py:139
  18.1 5.8 %collective-permute-start.4 = (f32[64,128]{1,0:T(8,128)S(1)}, f32[64,128]{1,0:T(8,128)S(1)}, u32[]{:S(2)}, u32[]{:S(2)}) collective-permute-start(f32[64,128]{1,0:T(8,128)S(1)} %bitcast.46), channel_id=1, source_target_pairs={{6,0},{7,1},{0,2},{1,3},{2,4},{3,5},{4,6},{5,7},{14,8},{15,9},{8,1... | collective-permute-start | bytes 98312 | tf_op jit(solution)/shard_map/ppermute | solution.py:139
  23.9 5.7 %collective-permute-start.5 = (f32[64,128]{1,0:T(8,128)S(1)}, f32[64,128]{1,0:T(8,128)S(1)}, u32[]{:S(2)}, u32[]{:S(2)}) collective-permute-start(f32[64,128]{1,0:T(8,128)S(1)} %bitcast.47), channel_id=1, source_target_pairs={{5,0},{6,1},{7,2},{0,3},{1,4},{2,5},{3,6},{4,7},{13,8},{14,9},{15,... | collective-permute-start | bytes 98312 | tf_op jit(solution)/shard_map/ppermute | solution.py:139
  29.6 4.8 %collective-permute-start.6 = (f32[64,128]{1,0:T(8,128)S(1)}, f32[64,128]{1,0:T(8,128)S(1)}, u32[]{:S(2)}, u32[]{:S(2)}) collective-permute-start(f32[64,128]{1,0:T(8,128)S(1)} %bitcast.48), channel_id=1, source_target_pairs={{4,0},{5,1},{6,2},{7,3},{0,4},{1,5},{2,6},{3,7},{12,8},{13,9},{14,... | collective-permute-start | bytes 98312 | tf_op jit(solution)/shard_map/ppermute | solution.py:139
  34.4 4.8 %collective-permute-start.7 = (f32[64,128]{1,0:T(8,128)S(1)}, f32[64,128]{1,0:T(8,128)S(1)}, u32[]{:S(2)}, u32[]{:S(2)}) collective-permute-start(f32[64,128]{1,0:T(8,128)S(1)} %bitcast.49), channel_id=1, source_target_pairs={{3,0},{4,1},{5,2},{6,3},{7,4},{0,5},{1,6},{2,7},{11,8},{12,9},{13,... | collective-permute-start | bytes 98312 | tf_op jit(solution)/shard_map/ppermute | solution.py:139
  39.2 3.9 %collective-permute-start.8 = (f32[64,128]{1,0:T(8,128)S(1)}, f32[64,128]{1,0:T(8,128)S(1)}, u32[]{:S(2)}, u32[]{:S(2)}) collective-permute-start(f32[64,128]{1,0:T(8,128)S(1)} %bitcast.50), channel_id=1, source_target_pairs={{2,0},{3,1},{4,2},{5,3},{6,4},{7,5},{0,6},{1,7},{10,8},{11,9},{12,... | collective-permute-start | bytes 98312 | tf_op jit(solution)/shard_map/ppermute | solution.py:139
  43.2 8.0 %copy-start = (f32[8,64,128]{2,1,0:T(8,128)}, f32[8,64,128]{2,1,0:T(8,128)S(1)}, u32[]{:S(2)}) copy-start(f32[8,64,128]{2,1,0:T(8,128)S(1)} %bitcast_dynamic-update-slice_fusion) | copy-start | bytes 786436
  43.2 6.4 %collective-permute-start.10 = (f32[8,64,128]{2,1,0:T(8,128)S(1)}, f32[8,64,128]{2,1,0:T(8,128)S(1)}, u32[]{:S(2)}, u32[]{:S(2)}) collective-permute-start(f32[8,64,128]{2,1,0:T(8,128)S(1)} %bitcast_dynamic-update-slice_fusion), channel_id=1, source_target_pairs={{16,0},{24,8},{0,16},{8,24},{17,1},{25,9},{1,17},{9,25},{18,2},{26... | collective-permute-start | bytes 786440 | tf_op jit(solution)/shard_map/ppermute | solution.py:134
  46.0 4.3 %collective-permute-start.11 = (f32[8,64,128]{2,1,0:T(8,128)S(1)}, f32[8,64,128]{2,1,0:T(8,128)S(1)}, u32[]{:S(2)}, u32[]{:S(2)}) collective-permute-start(f32[8,64,128]{2,1,0:T(8,128)S(1)} %bitcast_dynamic-update-slice_fusion), channel_id=1, source_target_pairs={{8,0},{0,8},{24,16},{16,24},{9,1},{1,9},{25,17},{17,25},{10,2},{2,... | collective-permute-start | bytes 786440 | tf_op jit(solution)/shard_map/ppermute | solution.py:134
  49.6 1.5 %copy-start.1 = (f32[8,64,128]{2,1,0:T(8,128)}, f32[8,64,128]{2,1,0:T(8,128)S(1)}, u32[]{:S(2)}) copy-start(f32[8,64,128]{2,1,0:T(8,128)S(1)} %collective-permute-done.10) | copy-start | bytes 786436
  49.6 1.5 %collective-permute-start.12 = (f32[8,64,128]{2,1,0:T(8,128)S(1)}, f32[8,64,128]{2,1,0:T(8,128)S(1)}, u32[]{:S(2)}, u32[]{:S(2)}) collective-permute-start(f32[8,64,128]{2,1,0:T(8,128)S(1)} %collective-permute-done.10), channel_id=1, source_target_pairs={{8,0},{0,8},{24,16},{16,24},{9,1},{1,9},{25,17},{17,25},{10,2},{2,... | collective-permute-start | bytes 786440 | tf_op jit(solution)/shard_map/ppermute | solution.py:134
  50.3 0.9 %copy-start.2 = (f32[8,64,128]{2,1,0:T(8,128)}, f32[8,64,128]{2,1,0:T(8,128)S(1)}, u32[]{:S(2)}) copy-start(f32[8,64,128]{2,1,0:T(8,128)S(1)} %collective-permute-done.11) | copy-start | bytes 786436
  51.2 0.7 %copy-start.3 = (f32[8,64,128]{2,1,0:T(8,128)}, f32[8,64,128]{2,1,0:T(8,128)S(1)}, u32[]{:S(2)}) copy-start(f32[8,64,128]{2,1,0:T(8,128)S(1)} %collective-permute-done.12) | copy-start | bytes 786436

commit v3 on v2

v3 whole, which is shorter than its diff:
```python
import functools
import math

import jax
import jax.numpy as jnp
import numpy as np
from jax import lax
from jax.experimental import pallas as pl
from jax.experimental.pallas import tpu as pltpu
from jax.sharding import PartitionSpec as P

LAGS = 4096
LANES = 128
SUBLANES = 8


def split_bf16(values, parts):
    pieces = []
    for _ in range(parts - 1):
        piece = values.astype(jnp.bfloat16)
        pieces.append(piece)
        values = values - piece.astype(jnp.float32)
    pieces.append(values.astype(jnp.bfloat16))
    return pieces


def dft_tables(bin_total, half_band):
    turns = (np.arange(bin_total)[:, None] * (2 * np.arange(half_band) + 1)[None, :]) % (4 * bin_total)
    angles = turns * (math.pi / (2 * bin_total))
    tables = []
    for exact in (np.cos(angles), np.sin(angles)):
        high = exact.astype(jnp.bfloat16)
        low = (exact - high.astype(np.float64)).astype(jnp.bfloat16)
        tables += [high, low]
    return tables


def iota(shape, axis):
    return lax.broadcasted_iota(jnp.int32, shape, axis)


def dot(left, right):
    return jnp.dot(left, right, preferred_element_type=jnp.float32)


def padded(count, multiple):
    return -(-count // multiple) * multiple


def pick_slots(extras, places, me, stations, rounds, slots):
    groups = len(extras)
    pairs = stations * stations
    listed = rounds * pairs
    rows = rounds * groups * slots
    place = iota((groups, groups), 1)
    held_by = jnp.zeros((groups, groups), jnp.int32)
    for position in range(groups):
        held_by = jnp.where(place == position, places[position], held_by)
    lane = iota((1, listed), 1)

    def by_group(row, shift):
        wanted = (iota((groups, groups), 0) + groups - shift) % groups
        held = jnp.concatenate([extra[row : row + 1, :] for extra in extras], axis=0)
        return dot((held_by == wanted).astype(jnp.bfloat16), held.astype(jnp.bfloat16))

    def of_station(values, number):
        spread = iota((LANES, listed), 0) == number
        return dot(values.astype(jnp.bfloat16), spread.astype(jnp.bfloat16))

    owner_ids = jnp.zeros((groups, listed), jnp.float32)
    partner_mask = jnp.zeros((groups, listed), jnp.float32)
    for index in range(rounds):
        of_round = lane // pairs == index
        owner_ids = jnp.where(of_round, by_group(index, 0), owner_ids)
        second = of_station(by_group(rounds, index + 1), lane % stations)
        partner_mask = jnp.where(of_round, second, partner_mask)
    own_mask = of_station(by_group(rounds, 0), lane % pairs // stations)
    pair_weight = own_mask * partner_mask
    mine = owner_ids == me.astype(jnp.float32)
    from_pair, to_pair = iota((listed, listed), 0), iota((listed, listed), 1)
    before = (from_pair < to_pair) & (from_pair // pairs == to_pair // pairs)
    rank = dot(mine.astype(jnp.bfloat16), before.astype(jnp.bfloat16))
    marked = jnp.where(mine, rank, -1.0).astype(jnp.bfloat16)
    of_group = (iota((rows, groups), 0) // slots) % groups == iota((rows, groups), 1)
    of_group = of_group.astype(jnp.bfloat16)
    row_id, lane_id = iota((rows, listed), 0), iota((rows, listed), 1)
    chosen = (dot(of_group, marked) == (row_id % slots).astype(jnp.float32)) & (
        row_id // (groups * slots) == lane_id // pairs
    )
    weighed = jnp.where(chosen, dot(of_group, pair_weight.astype(jnp.bfloat16)), 0.0)
    chosen = chosen.astype(jnp.bfloat16)
    pair_id = iota((listed, LANES), 0) % pairs
    first = dot(chosen, (pair_id // stations).astype(jnp.bfloat16))
    second = dot(chosen, (pair_id % stations).astype(jnp.bfloat16))
    weight = dot(weighed.astype(jnp.bfloat16), jnp.ones((listed, LANES), jnp.bfloat16))
    return first.astype(jnp.int32), second.astype(jnp.int32), weight


def stack_kernel(sizes, bands_ref, places_ref, me_ref, twist_ref, *refs):
    groups, stations, rounds, slots, band_bins = sizes
    block_refs, refs = refs[:groups], refs[groups:]
    ch_ref, cl_ref, sh_ref, sl_ref, out_ref, first, second, weight, even, odd = refs[:10]
    held, turned, real_high, real_low, imag_high, imag_low = refs[10:]
    step = pl.program_id(0)
    shards = pl.num_programs(0)
    chunks = band_bins // LANES
    depth = 2 * chunks * stations

    @pl.when(step == 0)
    def _():
        extras = [ref[ref.shape[0] - SUBLANES :, :] for ref in block_refs]
        places = [places_ref[position] for position in range(groups)]
        first[...], second[...], weight[...] = pick_slots(
            extras, places, me_ref[0], stations, rounds, slots
        )
        even[...] = jnp.zeros_like(even)
        odd[...] = jnp.zeros_like(odd)

    for position, ref in enumerate(block_refs):
        group = places_ref[position]
        for q in range(chunks):
            lanes = slice(q * LANES, (q + 1) * LANES)
            turn_cos, turn_sin = twist_ref[0, 0:1, lanes], twist_ref[0, 1:2, lanes]
            start = pl.multiple_of(step * depth, depth)
            real = ref[pl.ds(start + q * stations, stations), :]
            imag = ref[pl.ds(start + (chunks + q) * stations, stations), :]
            held[group, q] = real
            held[group, chunks + q] = imag
            turned[group, q] = real * turn_cos + imag * turn_sin
            turned[group, chunks + q] = imag * turn_cos - real * turn_sin

    octets = [
        (group, (group + groups - 1 - index) % groups)
        for index in range(rounds)
        for group in range(groups)
        for _ in range(slots // SUBLANES)
    ]
    for q in range(chunks):
        lanes = slice(q * LANES, (q + 1) * LANES)
        for unit in range(len(octets) // 2):
            reals, imags = [], []
            for octet in (2 * unit, 2 * unit + 1):
                group, partner = octets[octet]
                rows = slice(octet * SUBLANES, (octet + 1) * SUBLANES)
                index_a, index_b = first[rows, :], second[rows, :]
                a_real = jnp.take_along_axis(held[group, q], index_a, axis=0)
                a_imag = jnp.take_along_axis(held[group, chunks + q], index_a, axis=0)
                b_real = jnp.take_along_axis(turned[partner, q], index_b, axis=0)
                b_imag = jnp.take_along_axis(turned[partner, chunks + q], index_b, axis=0)
                reals.append(a_real * b_real + a_imag * b_imag)
                imags.append(a_imag * b_real - a_real * b_imag)
            rows = slice(2 * unit * SUBLANES, 2 * (unit + 1) * SUBLANES)
            high, low = split_bf16(jnp.concatenate(reals, axis=0), 2)
            real_high[rows, lanes] = high
            real_low[rows, lanes] = low
            high, low = split_bf16(jnp.concatenate(imags, axis=0), 2)
            imag_high[rows, lanes] = high
            imag_low[rows, lanes] = low

    def product(high, low, table_high, table_low):
        return dot(high[...], table_high[...]) + (
            dot(high[...], table_low[...]) + dot(low[...], table_high[...])
        )

    even[...] += product(real_high, real_low, ch_ref, cl_ref)
    odd[...] += product(imag_high, imag_low, sh_ref, sl_ref)

    @pl.when(step == shards - 1)
    def _():
        half = even.shape[1]
        row_weight = weight[:, 0:1]
        total = (even[...] + odd[...]) * row_weight
        mirror = (iota((half, half), 0) + iota((half, half), 1) == half - 1).astype(jnp.bfloat16)
        pieces = [dot(piece, mirror) for piece in split_bf16(total, 3)]
        below = pieces[0] + (pieces[1] + pieces[2])
        above = (even[...] - odd[...]) * row_weight
        out_ref[...] = jnp.concatenate([below, above], axis=1)


def swapped(block, axis, mask):
    route = [(i ^ mask, i) for i in range(lax.axis_size(axis))]
    return lax.ppermute(block, axis, route)


def shifted(block, axis, distance):
    size = lax.axis_size(axis)
    return lax.ppermute(block, axis, [((i - distance) % size, i) for i in range(size)])


def of_all(block, axis):
    size = lax.axis_size(axis)
    me = lax.axis_index(axis)
    blocks = [block] + [shifted(block, axis, distance) for distance in range(1, size)]
    places = jnp.stack([(me - distance) % size for distance in range(size)])
    return blocks, places.astype(jnp.int32)


def by_halves(block, axis, join):
    size = lax.axis_size(axis)
    if size & (size - 1):
        return of_all(block, axis)
    me = lax.axis_index(axis)
    blocks, masks = [block], [0]
    bit = size // 2
    while bit:
        blocks += [swapped(held, axis, bit) for held in blocks]
        masks += [mask ^ bit for mask in masks]
        bit //= 2
        if join:
            blocks = [jnp.concatenate(blocks, axis=0)]
    places = jnp.stack([me ^ mask for mask in masks])
    return blocks, places.astype(jnp.int32)


def per_device(spectra, station_mask, owners):
    stations, _, band_bins = spectra.shape
    groups = lax.axis_size("grp")
    shards = lax.axis_size("freq")
    rounds = owners.shape[1]
    pairs = stations * stations
    bin_total = band_bins * shards
    capacity = (2 * pairs + groups - 1) // groups
    slots = padded(capacity, SUBLANES)
    lag_band = LAGS // shards
    half_band = lag_band // 2
    chunks = band_bins // LANES
    rows = rounds * groups * slots

    tiles = spectra.reshape(stations, 2, chunks, LANES).transpose(1, 2, 0, 3)
    tiles = tiles.reshape(2 * chunks * stations, LANES)
    bands, band_places = by_halves(tiles, "freq", True)
    listed = [jnp.pad(owners[0, index, :, 0], (index * pairs, LANES - (index + 1) * pairs)) for index in range(rounds)]
    listed.append(jnp.pad(station_mask, (0, LANES - stations)))
    listed = jnp.stack(listed).astype(jnp.float32)
    listed = jnp.pad(listed, ((0, SUBLANES - listed.shape[0]), (0, 0)))
    blocks, group_places = by_halves(jnp.concatenate(bands + [listed], axis=0), "grp", False)

    me = lax.axis_index("grp").astype(jnp.int32)
    centre = lag_band * (2 * lax.axis_index("freq") + 1) - 1 - LAGS
    turns = jnp.mod(jnp.arange(bin_total, dtype=jnp.int32) * centre, 4 * bin_total)
    angles = turns.astype(jnp.float32) * (math.pi / (2 * bin_total))
    norm = 1.0 / math.sqrt(bin_total)
    twist = jnp.stack([jnp.cos(angles) * norm, jnp.sin(angles) * norm])
    twist = twist.reshape(2, shards, band_bins).transpose(1, 0, 2)
    tables = [jnp.asarray(table) for table in dft_tables(bin_total, half_band)]

    whole = pl.BlockSpec(memory_space=pltpu.VMEM)
    spectrum = pltpu.VMEM((groups, 2 * chunks, stations, LANES), jnp.float32)
    cross = pltpu.VMEM((rows, band_bins), jnp.bfloat16)
    out = pl.pallas_call(
        functools.partial(stack_kernel, (groups, stations, rounds, slots, band_bins)),
        grid_spec=pltpu.PrefetchScalarGridSpec(
            num_scalar_prefetch=3,
            grid=(shards,),
            in_specs=[pl.BlockSpec((1, 2, band_bins), lambda f, places, *_: (places[f], 0, 0))]
            + [whole] * len(blocks)
            + [pl.BlockSpec((band_bins, half_band), lambda f, places, *_: (places[f], 0))] * 4,
            out_specs=pl.BlockSpec((rows, lag_band), lambda f, *_: (0, 0)),
            scratch_shapes=[
                pltpu.VMEM((rows, LANES), jnp.int32),
                pltpu.VMEM((rows, LANES), jnp.int32),
                pltpu.VMEM((rows, LANES), jnp.float32),
                pltpu.VMEM((rows, half_band), jnp.float32),
                pltpu.VMEM((rows, half_band), jnp.float32),
                spectrum,
                spectrum,
                cross,
                cross,
                cross,
                cross,
            ],
        ),
        out_shape=jax.ShapeDtypeStruct((rows, lag_band), jnp.float32),
        compiler_params=pltpu.CompilerParams(
            dimension_semantics=("arbitrary",), vmem_limit_bytes=20 * 1024 * 1024
        ),
        name="owned_stacks",
    )(band_places, group_places, me.reshape(1), twist, *blocks, *tables)
    out = out.reshape(1, rounds, groups, slots, lag_band)
    return out[:, :, :, :capacity]


def solution(mesh):
    placed = (P("grp", None, "freq"), P("grp"), P("grp", None, None, None))
    return jax.shard_map(
        per_device,
        mesh=mesh,
        in_specs=placed,
        out_specs=P("grp", None, None, None, "freq"),
        check_vma=False,
    )
```

time: 64.7 us -> 40.9 us (0.63)
  waiting for transfers between devices: 33.6 us -> 12.2 us
  local copies, waits for them, and re-layouts: 3.47 us -> 8.68 us
  other arithmetic: 4.06 us -> 0.63 us
  Pallas kernels: 12.4 us -> 9.69 us
  starting transfers between devices: 10.5 us -> 9.29 us
    ppermute x10 -> x0, waiting for transfers between devices: 29.2 us -> none  [shifted(): lax.ppermute(block, axis, [((i - distance) % size, i) for i in range(size)])]
    ppermute x10 -> x0, starting transfers between devices: 9.5 us -> none  [shifted(): lax.ppermute(block, axis, [((i - distance) % size, i) for i in range(size)])]
    ppermute x3 -> x6, starting transfers between devices: 1.05 us -> 9.29 us  [swapped(): return lax.ppermute(block, axis, route)]
    ppermute x3 -> x6, waiting for transfers between devices: 4.45 us -> 12.2 us  [swapped(): return lax.ppermute(block, axis, route)]
    unnamed x16 -> x12, local copies, waits for them, and re-layouts: 1.26 us -> 6.39 us
    pallas_call x1, Pallas kernels: 12.4 us -> 9.69 us  [per_device(): pl.pallas_call(functools.partial(stack_kernel, (groups, stations, rounds,...]
    unnamed x1 -> x0, other arithmetic: 1.34 us -> none
    mul x1 -> x0, other arithmetic: 0.83 us -> none  [per_device(): masked = spectra * station_mask.astype(jnp.float32)[:, None, None]]
  transfers between devices with their start and end apart: 13 -> 6, of which waited for: 8 -> 5; matrix products, arithmetic and copies ran while one was open for 8% -> 5% of each run, Pallas kernels for 0% -> 0%
where the time goes in v3:
time: 40.9 us; the launch traced here: 40.6 us
  waiting for transfers between devices  12.2 us (30%)
  Pallas kernels  9.69 us (24%)
  starting transfers between devices  9.29 us (23%)
  local copies, waits for them, and re-layouts  8.68 us (21%)
  other arithmetic  0.63 us (2%)
    ppermute x6, waiting for transfers between devices, swapped(): return lax.ppermute(block, axis, route)  12.2 us
    pallas_call x1, Pallas kernels, per_device(): pl.pallas_call(functools.partial(stack_kernel, (groups, stations, rounds,...  9.69 us
    ppermute x6, starting transfers between devices, swapped(): return lax.ppermute(block, axis, route)  9.29 us
    unnamed x12, local copies, waits for them, and re-layouts  6.39 us
  transfers between devices with their start and end apart: 6, of which 5 were waited for; matrix products, arithmetic and copies ran while one was open for 5% of the time, Pallas kernels for 0%

profile of v3, /device:TPU:0, one launch (start us, length us, event | category | flops | bytes accessed | tf_op | source)
XLA Modules:
  0.0 40.6 jit_solution(1703033619678980539)
XLA Ops:
  0.0 0.8 %reshape.83 = f32[8,2,4,128]{3,2,1,0:T(4,128)S(1)} reshape(f32[8,2,512]{2,1,0:T(2,128)} %param.7) | data formatting | bytes 65536 | tf_op jit(solution)/shard_map/reshape | solution.py:229
  0.8 4.1 %collective-permute-start = (f32[64,128]{1,0:T(8,128)S(1)}, f32[64,128]{1,0:T(8,128)S(1)}, u32[]{:S(2)}, u32[]{:S(2)}) collective-permute-start(f32[64,128]{1,0:T(8,128)S(1)} %bitcast.28), channel_id=1, source_target_pairs={{4,0},{5,1},{6,2},{7,3},{0,4},{1,5},{2,6},{3,7},{12,8},{13,9},{14,... | collective-permute-start | bytes 98312 | tf_op jit(solution)/shard_map/ppermute | solution.py:182
  4.9 0.7 %slice_bitcast_fusion.1 = (s32[64]{0:T(128)S(1)}, s32[64]{0:T(128)S(1)}) fusion(s32[1,2,64,1]{2,3,1,0:T(1,128)} %param.9), kind=kLoop, calls=%fused_computation.22 | loop fusion | bytes 1024 | tf_op jit(solution)/shard_map/squeeze | solution.py:232
  5.6 0.1 pad_bitcast_fusion.1
  5.7 0.7 %pad_bitcast_fusion = s32[1,128]{1,0:T(1,128)S(1)} fusion(s32[8]{0:T(128)} %param.8), kind=kLoop, calls=%fused_computation.18 | loop fusion | bytes 544 | tf_op jit(solution)/shard_map/stack | solution.py:234
  6.3 0.8 %collective-permute-done = f32[64,128]{1,0:T(8,128)S(1)} collective-permute-done((f32[64,128]{1,0:T(8,128)S(1)}, f32[64,128]{1,0:T(8,128)S(1)}, u32[]{:S(2)}, u32[]{:S(2)}) %collective-permute-start) | collective-permute-done | bytes 32800 | tf_op jit(solution)/shard_map/ppermute | solution.py:182
  7.2 1.6 %collective-permute-start.1 = (f32[128,128]{1,0:T(8,128)S(1)}, f32[128,128]{1,0:T(8,128)S(1)}, u32[]{:S(2)}, u32[]{:S(2)}) collective-permute-start(f32[128,128]{1,0:T(8,128)S(1)} %pad_maximum_fusion.1), channel_id=1, source_target_pairs={{2,0},{3,1},{0,2},{1,3},{6,4},{7,5},{4,6},{5,7},{10,8},{11,9},{8,1... | collective-permute-start | bytes 196616 | tf_op jit(solution)/shard_map/ppermute | solution.py:182
  8.7 2.7 %collective-permute-done.1 = f32[128,128]{1,0:T(8,128)S(1)} collective-permute-done((f32[128,128]{1,0:T(8,128)S(1)}, f32[128,128]{1,0:T(8,128)S(1)}, u32[]{:S(2)}, u32[]{:S(2)}) %collective-permute-start.1) | collective-permute-done | bytes 65568 | tf_op jit(solution)/shard_map/ppermute | solution.py:182
  11.4 1.8 %collective-permute-start.2 = (f32[256,128]{1,0:T(8,128)S(1)}, f32[256,128]{1,0:T(8,128)S(1)}, u32[]{:S(2)}, u32[]{:S(2)}) collective-permute-start(f32[256,128]{1,0:T(8,128)S(1)} %pad_maximum_fusion), channel_id=1, source_target_pairs={{1,0},{0,1},{3,2},{2,3},{5,4},{4,5},{7,6},{6,7},{9,8},{8,9},{11,10... | collective-permute-start | bytes 393224 | tf_op jit(solution)/shard_map/ppermute | solution.py:182
  13.2 3.2 %collective-permute-done.2 = f32[256,128]{1,0:T(8,128)S(1)} collective-permute-done((f32[256,128]{1,0:T(8,128)S(1)}, f32[256,128]{1,0:T(8,128)S(1)}, u32[]{:S(2)}, u32[]{:S(2)}) %collective-permute-start.2) | collective-permute-done | bytes 131104 | tf_op jit(solution)/shard_map/ppermute | solution.py:182
  16.5 1.8 %collective-permute-start.3 = (f32[520,128]{1,0:T(8,128)S(1)}, f32[520,128]{1,0:T(8,128)S(1)}, u32[]{:S(2)}, u32[]{:S(2)}) collective-permute-start(f32[520,128]{1,0:T(8,128)S(1)} %constant_dynamic-update-slice_fusion.refs_0_), channel_id=1, source_target_pairs={{16,0},{24,8},{0,16},{8,24},{17,1},{25,9},{1,17},{9,25},{18,2},{26... | collective-permute-start | bytes 798728 | tf_op jit(solution)/shard_map/ppermute | solution.py:182
  18.3 0.1 collective-permute-start.4
  18.4 4.6 %collective-permute-done.3.refs_1_ = f32[520,128]{1,0:T(8,128)S(1)} collective-permute-done((f32[520,128]{1,0:T(8,128)S(1)}, f32[520,128]{1,0:T(8,128)S(1)}, u32[]{:S(2)}, u32[]{:S(2)}) %collective-permute-start.3) | collective-permute-done | bytes 266272 | tf_op jit(solution)/shard_map/ppermute | solution.py:182
  23.0 0.0 collective-permute-start.5
  23.0 0.5 %cosine_multiply_fusion = (f32[1,8,512]{2,0,1:T(1,128)S(1)}, f32[1,8,512]{2,0,1:T(1,128)S(1)}) fusion(f32[1,8,512]{2,1,0:T(8,128)S(1)} %fusion.1), kind=kLoop, calls=%fused_computation.10 | loop fusion | flops 12288 | bytes 49152 | tf_op jit(solution)/shard_map/mul | solution.py:243
  23.5 0.1 stack.67.bands_ref
  23.6 0.1 pad_add_fusion.places_ref
  23.7 0.0 collective-permute-done.4.refs_2_
  23.7 0.8 %collective-permute-done.5.refs_3_ = f32[520,128]{1,0:T(8,128)S(1)} collective-permute-done((f32[520,128]{1,0:T(8,128)S(1)}, f32[520,128]{1,0:T(8,128)S(1)}, u32[]{:S(2)}, u32[]{:S(2)}) %collective-permute-start.5) | collective-permute-done | bytes 266272 | tf_op jit(solution)/shard_map/ppermute | solution.py:182
  24.5 0.0 copy-start
  24.5 1.6 %copy-done = bf16[4096,256]{1,0:T(8,128)(2,1)S(1)} copy-done((bf16[4096,256]{1,0:T(8,128)(2,1)S(1)}, bf16[4096,256]{1,0:T(8,128)(2,1)}, u32[]{:S(2)}) %copy-start) | copy-done | bytes 2097176
  26.1 0.0 copy-start.1
  26.1 1.6 %copy-done.1 = bf16[4096,256]{1,0:T(8,128)(2,1)S(1)} copy-done((bf16[4096,256]{1,0:T(8,128)(2,1)S(1)}, bf16[4096,256]{1,0:T(8,128)(2,1)}, u32[]{:S(2)}) %copy-start.1) | copy-done | bytes 2097176
  27.7 0.0 copy-start.2
  27.7 1.6 %copy-done.2 = bf16[4096,256]{1,0:T(8,128)(2,1)S(1)} copy-done((bf16[4096,256]{1,0:T(8,128)(2,1)S(1)}, bf16[4096,256]{1,0:T(8,128)(2,1)}, u32[]{:S(2)}) %copy-start.2) | copy-done | bytes 2097176
  29.3 0.0 copy-start.3
  29.3 1.6 %copy-done.3 = bf16[4096,256]{1,0:T(8,128)(2,1)S(1)} copy-done((bf16[4096,256]{1,0:T(8,128)(2,1)S(1)}, bf16[4096,256]{1,0:T(8,128)(2,1)}, u32[]{:S(2)}) %copy-start.3) | copy-done | bytes 2097176
  30.9 9.7 %owned_stacks.1 = f32[256,512]{1,0:T(8,128)} custom-call(s32[8]{0:T(128)S(1)} %stack.67.bands_ref, s32[4]{0:T(128)S(1)} %pad_add_fusion.places_ref, s32[1]{0:T(128)} %bitcast.8.me_ref, f32[8,2,512]{2,1,0:T(2,128)S(1)} %maximum_bitcast_fusion.twist_ref, f32[520,128]{1,0:T(8,128)S(1)} %constant_dynamic-update-slice_fusion.refs_0_, ...), custom_call_target="tpu_custom_call" | custom-call | tf_op jit(solution)/shard_map/owned_stacks/pallas_call | solution.py:250
  (11 shorter events, 0.1 us)
Async XLA Ops:
  0.8 6.3 %collective-permute-start = (f32[64,128]{1,0:T(8,128)S(1)}, f32[64,128]{1,0:T(8,128)S(1)}, u32[]{:S(2)}, u32[]{:S(2)}) collective-permute-start(f32[64,128]{1,0:T(8,128)S(1)} %bitcast.28), channel_id=1, source_target_pairs={{4,0},{5,1},{6,2},{7,3},{0,4},{1,5},{2,6},{3,7},{12,8},{13,9},{14,... | collective-permute-start | bytes 98312 | tf_op jit(solution)/shard_map/ppermute | solution.py:182
  7.2 4.3 %collective-permute-start.1 = (f32[128,128]{1,0:T(8,128)S(1)}, f32[128,128]{1,0:T(8,128)S(1)}, u32[]{:S(2)}, u32[]{:S(2)}) collective-permute-start(f32[128,128]{1,0:T(8,128)S(1)} %pad_maximum_fusion.1), channel_id=1, source_target_pairs={{2,0},{3,1},{0,2},{1,3},{6,4},{7,5},{4,6},{5,7},{10,8},{11,9},{8,1... | collective-permute-start | bytes 196616 | tf_op jit(solution)/shard_map/ppermute | solution.py:182
  11.4 5.0 %collective-permute-start.2 = (f32[256,128]{1,0:T(8,128)S(1)}, f32[256,128]{1,0:T(8,128)S(1)}, u32[]{:S(2)}, u32[]{:S(2)}) collective-permute-start(f32[256,128]{1,0:T(8,128)S(1)} %pad_maximum_fusion), channel_id=1, source_target_pairs={{1,0},{0,1},{3,2},{2,3},{5,4},{4,5},{7,6},{6,7},{9,8},{8,9},{11,10... | collective-permute-start | bytes 393224 | tf_op jit(solution)/shard_map/ppermute | solution.py:182
  16.5 6.5 %collective-permute-start.3 = (f32[520,128]{1,0:T(8,128)S(1)}, f32[520,128]{1,0:T(8,128)S(1)}, u32[]{:S(2)}, u32[]{:S(2)}) collective-permute-start(f32[520,128]{1,0:T(8,128)S(1)} %constant_dynamic-update-slice_fusion.refs_0_), channel_id=1, source_target_pairs={{16,0},{24,8},{0,16},{8,24},{17,1},{25,9},{1,17},{9,25},{18,2},{26... | collective-permute-start | bytes 798728 | tf_op jit(solution)/shard_map/ppermute | solution.py:182
  18.3 5.4 %collective-permute-start.4 = (f32[520,128]{1,0:T(8,128)S(1)}, f32[520,128]{1,0:T(8,128)S(1)}, u32[]{:S(2)}, u32[]{:S(2)}) collective-permute-start(f32[520,128]{1,0:T(8,128)S(1)} %constant_dynamic-update-slice_fusion.refs_0_), channel_id=1, source_target_pairs={{8,0},{0,8},{24,16},{16,24},{9,1},{1,9},{25,17},{17,25},{10,2},{2,... | collective-permute-start | bytes 798728 | tf_op jit(solution)/shard_map/ppermute | solution.py:182
  23.0 1.5 %collective-permute-start.5 = (f32[520,128]{1,0:T(8,128)S(1)}, f32[520,128]{1,0:T(8,128)S(1)}, u32[]{:S(2)}, u32[]{:S(2)}) collective-permute-start(f32[520,128]{1,0:T(8,128)S(1)} %collective-permute-done.3.refs_1_), channel_id=1, source_target_pairs={{8,0},{0,8},{24,16},{16,24},{9,1},{1,9},{25,17},{17,25},{10,2},{2,... | collective-permute-start | bytes 798728 | tf_op jit(solution)/shard_map/ppermute | solution.py:182
  24.5 1.6 %copy-start = (bf16[4096,256]{1,0:T(8,128)(2,1)S(1)}, bf16[4096,256]{1,0:T(8,128)(2,1)}, u32[]{:S(2)}) copy-start(bf16[4096,256]{1,0:T(8,128)(2,1)} %constant.64.clone.refs_7_) | copy-start | bytes 6291460
  26.1 1.6 %copy-start.1 = (bf16[4096,256]{1,0:T(8,128)(2,1)S(1)}, bf16[4096,256]{1,0:T(8,128)(2,1)}, u32[]{:S(2)}) copy-start(bf16[4096,256]{1,0:T(8,128)(2,1)} %constant.63.clone.refs_6_) | copy-start | bytes 6291460
  27.7 1.6 %copy-start.2 = (bf16[4096,256]{1,0:T(8,128)(2,1)S(1)}, bf16[4096,256]{1,0:T(8,128)(2,1)}, u32[]{:S(2)}) copy-start(bf16[4096,256]{1,0:T(8,128)(2,1)} %constant.62.clone.refs_5_) | copy-start | bytes 6291460
  29.3 1.6 %copy-start.3 = (bf16[4096,256]{1,0:T(8,128)(2,1)S(1)}, bf16[4096,256]{1,0:T(8,128)(2,1)}, u32[]{:S(2)}) copy-start(bf16[4096,256]{1,0:T(8,128)(2,1)} %constant.61.clone.refs_4_) | copy-start | bytes 6291460

commit v4 on v3

v4 whole, which is shorter than its diff:
```python
import functools
import math

import jax
import jax.numpy as jnp
import numpy as np
from jax import lax
from jax.experimental import pallas as pl
from jax.experimental.pallas import tpu as pltpu
from jax.sharding import PartitionSpec as P

LAGS = 4096
LANES = 128
SUBLANES = 8


def split_bf16(values, parts):
    pieces = []
    for _ in range(parts - 1):
        piece = values.astype(jnp.bfloat16)
        pieces.append(piece)
        values = values - piece.astype(jnp.float32)
    pieces.append(values.astype(jnp.bfloat16))
    return pieces


def base_tables(bin_total, half_band, fine):
    odd = 2 * np.arange(half_band) + 1
    tables = []
    for bins in (np.arange(0, bin_total, fine)[:, None, None], np.arange(fine)[:, None]):
        angles = (bins * odd % (4 * bin_total)) * (math.pi / (2 * bin_total))
        tables += [np.cos(angles).astype(np.float32), np.sin(angles).astype(np.float32)]
    return tables


def iota(shape, axis):
    return lax.broadcasted_iota(jnp.int32, shape, axis)


def dot(left, right):
    return jnp.dot(left, right, preferred_element_type=jnp.float32)


def padded(count, multiple):
    return -(-count // multiple) * multiple


def pick_slots(extras, places, me, stations, rounds, slots):
    groups = len(extras)
    pairs = stations * stations
    listed = rounds * pairs
    rows = rounds * groups * slots
    place = iota((groups, groups), 1)
    held_by = jnp.zeros((groups, groups), jnp.int32)
    for position in range(groups):
        held_by = jnp.where(place == position, places[position], held_by)
    lane = iota((1, listed), 1)

    def by_group(row, shift):
        wanted = (iota((groups, groups), 0) + groups - shift) % groups
        held = jnp.concatenate([extra[row : row + 1, :] for extra in extras], axis=0)
        return dot((held_by == wanted).astype(jnp.bfloat16), held.astype(jnp.bfloat16))

    def of_station(values, number):
        spread = iota((LANES, listed), 0) == number
        return dot(values.astype(jnp.bfloat16), spread.astype(jnp.bfloat16))

    owner_ids = jnp.zeros((groups, listed), jnp.float32)
    partner_mask = jnp.zeros((groups, listed), jnp.float32)
    for index in range(rounds):
        of_round = lane // pairs == index
        owner_ids = jnp.where(of_round, by_group(index, 0), owner_ids)
        second = of_station(by_group(rounds, index + 1), lane % stations)
        partner_mask = jnp.where(of_round, second, partner_mask)
    own_mask = of_station(by_group(rounds, 0), lane % pairs // stations)
    pair_weight = own_mask * partner_mask
    mine = owner_ids == me.astype(jnp.float32)
    from_pair, to_pair = iota((listed, listed), 0), iota((listed, listed), 1)
    before = (from_pair < to_pair) & (from_pair // pairs == to_pair // pairs)
    rank = dot(mine.astype(jnp.bfloat16), before.astype(jnp.bfloat16))
    marked = jnp.where(mine, rank, -1.0).astype(jnp.bfloat16)
    of_group = (iota((rows, groups), 0) // slots) % groups == iota((rows, groups), 1)
    of_group = of_group.astype(jnp.bfloat16)
    row_id, lane_id = iota((rows, listed), 0), iota((rows, listed), 1)
    chosen = (dot(of_group, marked) == (row_id % slots).astype(jnp.float32)) & (
        row_id // (groups * slots) == lane_id // pairs
    )
    weighed = jnp.where(chosen, dot(of_group, pair_weight.astype(jnp.bfloat16)), 0.0)
    chosen = chosen.astype(jnp.bfloat16)
    pair_id = iota((listed, LANES), 0) % pairs
    first = dot(chosen, (pair_id // stations).astype(jnp.bfloat16))
    second = dot(chosen, (pair_id % stations).astype(jnp.bfloat16))
    weight = dot(weighed.astype(jnp.bfloat16), jnp.ones((listed, LANES), jnp.bfloat16))
    return first.astype(jnp.int32), second.astype(jnp.int32), weight


def table_kernel(me_ref, far_cos, far_sin, near_cos, near_sin, *refs):
    cos_high, cos_low, sin_high, sin_low, turn_cos, turn_sin = refs
    fine = near_cos.shape[0]
    shards, _, band_bins = turn_cos.shape
    bin_total = shards * band_bins

    @pl.loop(0, far_cos.shape[0])
    def _(index):
        rows = pl.ds(pl.multiple_of(index * fine, fine), fine)
        cos, sin = far_cos[index], far_sin[index]
        cos_high[rows, :], cos_low[rows, :] = split_bf16(
            cos * near_cos[...] - sin * near_sin[...], 2
        )
        sin_high[rows, :], sin_low[rows, :] = split_bf16(
            sin * near_cos[...] + cos * near_sin[...], 2
        )

    lag_band = 2 * near_cos.shape[1]
    centre = lag_band * (2 * me_ref[1] + 1) - 1 - LAGS
    bins = iota((shards, band_bins), 0) * band_bins + iota((shards, band_bins), 1)
    turns = (bins * centre) & (4 * bin_total - 1)
    angles = turns.astype(jnp.float32) * (math.pi / (2 * bin_total))
    norm = 1.0 / math.sqrt(bin_total)
    cos, sin = jnp.cos(angles) * norm, jnp.sin(angles) * norm
    for shard in range(shards):
        turn_cos[shard] = cos[shard : shard + 1, :]
        turn_sin[shard] = sin[shard : shard + 1, :]


def add_bands(sizes, bands_ref, places, turn_refs, table_refs, block_refs, picks, sums, scratch):
    groups, stations, rounds, slots, band_bins, band_count = sizes
    turn_cos_ref, turn_sin_ref = turn_refs
    cos_high, cos_low, sin_high, sin_low = table_refs
    first, second = picks
    even, odd = sums
    held, turned, real_high, real_low, imag_high, imag_low = scratch
    chunks = band_bins // LANES
    depth = 2 * chunks * stations
    octets = [
        (group, (group + groups - 1 - index) % groups)
        for index in range(rounds)
        for group in range(groups)
        for _ in range(slots // SUBLANES)
    ]

    @pl.loop(0, band_count)
    def _(step):
        band = bands_ref[step]
        for position, ref in enumerate(block_refs):
            group = places[position]
            for q in range(chunks):
                lanes = slice(q * LANES, (q + 1) * LANES)
                turn_cos = turn_cos_ref[band, :, lanes]
                turn_sin = turn_sin_ref[band, :, lanes]
                start = pl.multiple_of(step * depth, depth)
                real = ref[pl.ds(start + q * stations, stations), :]
                imag = ref[pl.ds(start + (chunks + q) * stations, stations), :]
                held[group, q] = real
                held[group, chunks + q] = imag
                turned[group, q] = real * turn_cos + imag * turn_sin
                turned[group, chunks + q] = imag * turn_cos - real * turn_sin

        for q in range(chunks):
            lanes = slice(q * LANES, (q + 1) * LANES)
            for unit in range(len(octets) // 2):
                reals, imags = [], []
                for octet in (2 * unit, 2 * unit + 1):
                    group, partner = octets[octet]
                    rows = slice(octet * SUBLANES, (octet + 1) * SUBLANES)
                    index_a, index_b = first[rows, :], second[rows, :]
                    a_real = jnp.take_along_axis(held[group, q], index_a, axis=0)
                    a_imag = jnp.take_along_axis(held[group, chunks + q], index_a, axis=0)
                    b_real = jnp.take_along_axis(turned[partner, q], index_b, axis=0)
                    b_imag = jnp.take_along_axis(turned[partner, chunks + q], index_b, axis=0)
                    reals.append(a_real * b_real + a_imag * b_imag)
                    imags.append(a_imag * b_real - a_real * b_imag)
                rows = slice(2 * unit * SUBLANES, 2 * (unit + 1) * SUBLANES)
                high, low = split_bf16(jnp.concatenate(reals, axis=0), 2)
                real_high[rows, lanes] = high
                real_low[rows, lanes] = low
                high, low = split_bf16(jnp.concatenate(imags, axis=0), 2)
                imag_high[rows, lanes] = high
                imag_low[rows, lanes] = low

        rows = pl.ds(pl.multiple_of(band * band_bins, band_bins), band_bins)

        def product(high, low, table_high, table_low):
            return dot(high[...], table_high[rows, :]) + (
                dot(high[...], table_low[rows, :]) + dot(low[...], table_high[rows, :])
            )

        even[...] += product(real_high, real_low, cos_high, cos_low)
        odd[...] += product(imag_high, imag_low, sin_high, sin_low)


def first_kernel(sizes, moves, bands_ref, me_ref, *refs):
    groups, stations, rounds, slots = sizes[:4]
    turn_refs, table_refs, refs = refs[:2], refs[2:6], refs[6:]
    block_refs, refs = refs[:groups], refs[groups:]
    (first, second, weight, even, odd), scratch = refs[:5], refs[5:]
    places = [moved(me_ref[0], move, groups) for move in moves]
    extras = [ref[ref.shape[0] - SUBLANES :, :] for ref in block_refs]
    first[...], second[...], weight[...] = pick_slots(
        extras, places, me_ref[0], stations, rounds, slots
    )
    even[...] = jnp.zeros_like(even)
    odd[...] = jnp.zeros_like(odd)
    add_bands(
        sizes, bands_ref, places, turn_refs, table_refs, block_refs,
        (first, second), (even, odd), scratch,
    )


def last_kernel(sizes, moves, bands_ref, me_ref, *refs):
    groups = sizes[0]
    turn_refs, table_refs, refs = refs[:2], refs[2:6], refs[6:]
    block_refs, refs = refs[:groups], refs[groups:]
    (first, second, weight, even_in, odd_in, out_ref, even, odd), scratch = refs[:8], refs[8:]
    even[...] = even_in[...]
    odd[...] = odd_in[...]
    places = [moved(me_ref[0], move, groups) for move in moves]
    add_bands(
        sizes, bands_ref, places, turn_refs, table_refs, block_refs,
        (first, second), (even, odd), scratch,
    )
    half = even.shape[1]
    row_weight = weight[:, 0:1]
    total = (even[...] + odd[...]) * row_weight
    mirror = (iota((half, half), 0) + iota((half, half), 1) == half - 1).astype(jnp.bfloat16)
    pieces = [dot(piece, mirror) for piece in split_bf16(total, 3)]
    below = pieces[0] + (pieces[1] + pieces[2])
    above = (even[...] - odd[...]) * row_weight
    out_ref[...] = jnp.concatenate([below, above], axis=1)


def moved(me, move, size):
    return me ^ move if size & (size - 1) == 0 else lax.rem(me + size - move, size)


def fetched(block, axis, move):
    size = lax.axis_size(axis)
    return lax.ppermute(block, axis, [(moved_index(i, move, size), i) for i in range(size)])


def moved_index(i, move, size):
    return i ^ move if size & (size - 1) == 0 else (i - move) % size


def gathered(block, axis, bits):
    size = lax.axis_size(axis)
    if size & (size - 1):
        moves = list(range(size))
        return [block] + [fetched(block, axis, move) for move in moves[1:]], moves
    blocks, moves = [block], [0]
    for bit in bits:
        blocks += [fetched(held, axis, bit) for held in blocks]
        moves += [move ^ bit for move in moves]
    return blocks, moves


def exchange(tiles, extras):
    groups, shards = lax.axis_size("grp"), lax.axis_size("freq")
    half = shards // 2
    own, band_moves = tiles, [0]
    bit = half
    while bit > 1:
        own = jnp.concatenate([own, fetched(own, "freq", bit)], axis=0)
        band_moves += [move ^ bit for move in band_moves]
        bit //= 2
    with_extras = jnp.concatenate([own, extras], axis=0)
    beside = fetched(own, "freq", 1)
    if groups != 4:
        near, group_moves = gathered(with_extras, "grp", [])
        far, _ = gathered(beside, "grp", [])
        return near, far, band_moves, group_moves
    rows = own.shape[0]
    across = fetched(with_extras, "grp", 2)
    near = [with_extras, across, fetched(with_extras, "grp", 1), fetched(across, "grp", 1)]
    upper = fetched(beside[: rows // 2], "grp", 2)
    lower = fetched(across[rows // 2 : rows], "freq", 1)
    diagonal = jnp.concatenate([upper, lower], axis=0)
    far = [beside, diagonal, fetched(beside, "grp", 1), fetched(diagonal, "grp", 1)]
    return near, far, band_moves, [0, 2, 1, 3]


def per_device(spectra, station_mask, owners):
    stations, _, band_bins = spectra.shape
    groups = lax.axis_size("grp")
    shards = lax.axis_size("freq")
    rounds = owners.shape[1]
    pairs = stations * stations
    bin_total = band_bins * shards
    capacity = (2 * pairs + groups - 1) // groups
    slots = padded(capacity, SUBLANES)
    lag_band = LAGS // shards
    half_band = lag_band // 2
    chunks = band_bins // LANES
    rows = rounds * groups * slots

    tiles = spectra.reshape(stations, 2, chunks, LANES).transpose(1, 2, 0, 3)
    tiles = tiles.reshape(2 * chunks * stations, LANES)
    listed = [
        jnp.pad(owners[0, index, :, 0], (index * pairs, LANES - (index + 1) * pairs))
        for index in range(rounds)
    ]
    listed.append(jnp.pad(station_mask, (0, LANES - stations)))
    listed = jnp.stack(listed).astype(jnp.float32)
    extras = jnp.pad(listed, ((0, SUBLANES - listed.shape[0]), (0, 0)))
    near, far, band_moves, group_moves = exchange(tiles, extras)

    me = jnp.stack([lax.axis_index("grp"), lax.axis_index("freq")]).astype(jnp.int32)
    near_bands = me[1] ^ jnp.asarray(band_moves, jnp.int32)
    far_bands = near_bands ^ 1

    scalar = pl.BlockSpec(memory_space=pltpu.SMEM)
    vector = pl.BlockSpec(memory_space=pltpu.VMEM)

    def in_vmem(shape, kind):
        return pltpu.VMEM(shape, kind)

    def call(kernel, name, scalars, arrays, out_shape, scratch, cost):
        arrays = [pltpu.with_memory_space_constraint(array, pltpu.VMEM) for array in arrays]
        return pl.pallas_call(
            kernel,
            out_shape=out_shape,
            in_specs=[scalar] * len(scalars) + [vector] * len(arrays),
            out_specs=[vector] * len(out_shape),
            scratch_shapes=scratch,
            compiler_params=pltpu.CompilerParams(vmem_limit_bytes=16 * 1024 * 1024),
            cost_estimate=cost,
            name=name,
        )(*scalars, *arrays)

    table = in_vmem((bin_total, half_band), jnp.bfloat16)
    turn = in_vmem((shards, 1, band_bins), jnp.float32)
    tables = call(
        table_kernel,
        "tables",
        [me],
        [jnp.asarray(base) for base in base_tables(bin_total, half_band, 64)],
        [table] * 4 + [turn] * 2,
        [],
        pl.CostEstimate(flops=0, bytes_accessed=8 * bin_total * half_band, transcendentals=0),
    )
    turns, tables = tables[4:], tables[:4]

    sizes = (groups, stations, rounds, slots, band_bins, len(band_moves))
    spectrum = pltpu.VMEM((groups, 2 * chunks, stations, LANES), jnp.float32)
    cross = pltpu.VMEM((rows, band_bins), jnp.bfloat16)
    scratch = [spectrum] * 2 + [cross] * 4
    flops = 6 * rows * bin_total * lag_band // 2
    cost = pl.CostEstimate(flops=flops, bytes_accessed=8 * 1024 * 1024, transcendentals=0)
    picks = [in_vmem((rows, LANES), kind) for kind in (jnp.int32, jnp.int32, jnp.float32)]
    total = in_vmem((rows, half_band), jnp.float32)
    held = call(
        functools.partial(first_kernel, sizes, group_moves),
        "near_bands",
        [near_bands, me],
        [*turns, *tables, *near],
        picks + [total] * 2,
        scratch,
        cost,
    )
    (out,) = call(
        functools.partial(last_kernel, sizes, group_moves),
        "far_bands",
        [far_bands, me],
        [*turns, *tables, *far, *held],
        [in_vmem((rows, lag_band), jnp.float32)],
        [pltpu.VMEM((rows, half_band), jnp.float32)] * 2 + scratch,
        cost,
    )
    out = out.reshape(1, rounds, groups, slots, lag_band)
    return out[:, :, :, :capacity]


def solution(mesh):
    placed = (P("grp", None, "freq"), P("grp"), P("grp", None, None, None))
    return jax.shard_map(
        per_device,
        mesh=mesh,
        in_specs=placed,
        out_specs=P("grp", None, None, None, "freq"),
        check_vma=False,
    )
```

time: 40.9 us -> 40.6 us (level)
  waiting for transfers between devices: 12.2 us -> 8.87 us
  Pallas kernels: 9.69 us -> 12.4 us
  starting transfers between devices: 9.29 us -> 11.7 us
  local copies, waits for them, and re-layouts: 8.68 us -> 6.38 us
    ppermute x6 -> x10, waiting for transfers between devices: 12.2 us -> 8.87 us  [fetched(): lax.ppermute(block, axis, [(moved_index(i, move, size), i) for i in range...]
    pallas_call x1 -> x3, Pallas kernels: 9.69 us -> 12.4 us  [call(): pl.pallas_call(kernel, out_shape=out_shape, in_specs=[scalar] * len(scala...]
    ppermute x6 -> x10, starting transfers between devices: 9.29 us -> 11.7 us  [fetched(): lax.ppermute(block, axis, [(moved_index(i, move, size), i) for i in range...]
    unnamed x12 -> x10, local copies, waits for them, and re-layouts: 6.39 us -> 4.16 us
    xor x0 -> x1, other arithmetic: none -> 0.66 us  [per_device(): near_bands = me[1] ^ jnp.asarray(band_moves, jnp.int32)]
    mul x1 -> x0, other arithmetic: 0.48 us -> none  [per_device(): twist = jnp.stack([jnp.cos(angles) * norm, jnp.sin(angles) * norm])]
  transfers between devices with their start and end apart: 6 -> 10, of which waited for: 5 -> 4; matrix products, arithmetic and copies ran while one was open for 5% -> 5% of each run, Pallas kernels for 0% -> 19%
where the time goes in v4:
time: 40.6 us; the launch traced here: 40.2 us
  Pallas kernels  12.4 us (31%)
  starting transfers between devices  11.7 us (29%)
  waiting for transfers between devices  8.87 us (22%)
  local copies, waits for them, and re-layouts  6.38 us (16%)
  other arithmetic  0.77 us (2%)
    pallas_call x3, Pallas kernels, call(): pl.pallas_call(kernel, out_shape=out_shape, in_specs=[scalar] * len(scala...  12.4 us
    ppermute x10, starting transfers between devices, fetched(): lax.ppermute(block, axis, [(moved_index(i, move, size), i) for i in range...  11.7 us
    ppermute x10, waiting for transfers between devices, fetched(): lax.ppermute(block, axis, [(moved_index(i, move, size), i) for i in range...  8.87 us
    unnamed x10, local copies, waits for them, and re-layouts  4.16 us
  transfers between devices with their start and end apart: 10, of which 4 were waited for; matrix products, arithmetic and copies ran while one was open for 5% of the time, Pallas kernels for 19%

profile of v4, /device:TPU:0, one launch (start us, length us, event | category | flops | bytes accessed | tf_op | source)
XLA Modules:
  0.0 40.2 jit_solution(16250898320884541501)
XLA Ops:
  0.0 0.8 %reshape.9 = f32[8,2,4,128]{3,2,1,0:T(4,128)S(1)} reshape(f32[8,2,512]{2,1,0:T(2,128)} %param.8) | data formatting | bytes 65536 | tf_op jit(solution)/shard_map/reshape | solution.py:296
  0.8 4.1 %collective-permute-start = (f32[64,128]{1,0:T(8,128)S(1)}, f32[64,128]{1,0:T(8,128)S(1)}, u32[]{:S(2)}, u32[]{:S(2)}) collective-permute-start(f32[64,128]{1,0:T(8,128)S(1)} %bitcast.17), channel_id=1, source_target_pairs={{4,0},{5,1},{6,2},{7,3},{0,4},{1,5},{2,6},{3,7},{12,8},{13,9},{14,... | collective-permute-start | bytes 98312 | tf_op jit(solution)/shard_map/ppermute | solution.py:238
  4.9 0.7 %slice_bitcast_fusion.1 = (s32[64]{0:T(128)S(1)}, s32[64]{0:T(128)S(1)}) fusion(s32[1,2,64,1]{2,3,1,0:T(1,128)} %param.10), kind=kLoop, calls=%fused_computation.12 | loop fusion | bytes 1024 | tf_op jit(solution)/shard_map/squeeze | solution.py:299
  5.6 0.1 pad_bitcast_fusion.1
  5.7 0.7 %pad_bitcast_fusion = s32[1,128]{1,0:T(1,128)S(1)} fusion(s32[8]{0:T(128)} %param.9), kind=kLoop, calls=%fused_computation.8 | loop fusion | bytes 544 | tf_op jit(solution)/shard_map/stack | solution.py:303
  6.3 0.8 %collective-permute-done = f32[64,128]{1,0:T(8,128)S(1)} collective-permute-done((f32[64,128]{1,0:T(8,128)S(1)}, f32[64,128]{1,0:T(8,128)S(1)}, u32[]{:S(2)}, u32[]{:S(2)}) %collective-permute-start) | collective-permute-done | bytes 32800 | tf_op jit(solution)/shard_map/ppermute | solution.py:238
  7.2 1.6 %collective-permute-start.1 = (f32[128,128]{1,0:T(8,128)S(1)}, f32[128,128]{1,0:T(8,128)S(1)}, u32[]{:S(2)}, u32[]{:S(2)}) collective-permute-start(f32[128,128]{1,0:T(8,128)S(1)} %pad_maximum_fusion.1), channel_id=1, source_target_pairs={{2,0},{3,1},{0,2},{1,3},{6,4},{7,5},{4,6},{5,7},{10,8},{11,9},{8,1... | collective-permute-start | bytes 196616 | tf_op jit(solution)/shard_map/ppermute | solution.py:238
  8.7 2.7 %collective-permute-done.1 = f32[128,128]{1,0:T(8,128)S(1)} collective-permute-done((f32[128,128]{1,0:T(8,128)S(1)}, f32[128,128]{1,0:T(8,128)S(1)}, u32[]{:S(2)}, u32[]{:S(2)}) %collective-permute-start.1) | collective-permute-done | bytes 65568 | tf_op jit(solution)/shard_map/ppermute | solution.py:238
  11.4 1.8 %collective-permute-start.4 = (f32[264,128]{1,0:T(8,128)S(1)}, f32[264,128]{1,0:T(8,128)S(1)}, u32[]{:S(2)}, u32[]{:S(2)}) collective-permute-start(f32[264,128]{1,0:T(8,128)S(1)} %select_maximum_fusion.refs_6_), channel_id=1, source_target_pairs={{16,0},{24,8},{0,16},{8,24},{17,1},{25,9},{1,17},{9,25},{18,2},{26... | collective-permute-start | bytes 405512 | tf_op jit(solution)/shard_map/ppermute | solution.py:238
  13.2 1.6 %collective-permute-start.2 = (f32[256,128]{1,0:T(8,128)S(1)}, f32[256,128]{1,0:T(8,128)S(1)}, u32[]{:S(2)}, u32[]{:S(2)}) collective-permute-start(f32[256,128]{1,0:T(8,128)S(1)} %pad_maximum_fusion), channel_id=1, source_target_pairs={{1,0},{0,1},{3,2},{2,3},{5,4},{4,5},{7,6},{6,7},{9,8},{8,9},{11,10... | collective-permute-start | bytes 393224 | tf_op jit(solution)/shard_map/ppermute | solution.py:238
  14.8 0.7 %broadcast_xor_fusion.1 = (s32[4]{0:T(128)S(1)}, s32[4]{0:T(128)S(1)}) fusion(s32[4]{0:T(128)} %constant.24.clone, s32[]{:T(128)} %axis_index.22), kind=kLoop, calls=%fused_computation.14 | loop fusion | flops 8 | bytes 52 | tf_op jit(solution)/shard_map/xor | solution.py:308
  15.5 2.8 %collective-permute-done.2.refs_6_ = f32[256,128]{1,0:T(8,128)S(1)} collective-permute-done((f32[256,128]{1,0:T(8,128)S(1)}, f32[256,128]{1,0:T(8,128)S(1)}, u32[]{:S(2)}, u32[]{:S(2)}) %collective-permute-start.2) | collective-permute-done | bytes 131104 | tf_op jit(solution)/shard_map/ppermute | solution.py:238
  18.3 0.3 collective-permute-start.3
  18.6 0.1 pad_add_fusion.me_ref
  18.7 0.0 copy-start
  18.7 0.8 %copy-done = f32[64,1,256]{2,1,0:T(1,128)S(1)} copy-done((f32[64,1,256]{2,1,0:T(1,128)S(1)}, f32[64,1,256]{2,1,0:T(1,128)}, u32[]{:S(2)}) %copy-start) | copy-done | bytes 65560
  19.5 0.0 copy-start.1
  19.5 0.8 %copy-done.1 = f32[64,1,256]{2,1,0:T(1,128)S(1)} copy-done((f32[64,1,256]{2,1,0:T(1,128)S(1)}, f32[64,1,256]{2,1,0:T(1,128)}, u32[]{:S(2)}) %copy-start.1) | copy-done | bytes 65560
  20.3 0.0 copy-start.2
  20.3 0.8 %copy-done.2 = f32[64,256]{1,0:T(8,128)S(1)} copy-done((f32[64,256]{1,0:T(8,128)S(1)}, f32[64,256]{1,0:T(8,128)}, u32[]{:S(2)}) %copy-start.2) | copy-done | bytes 65560
  21.2 0.0 copy-start.3
  21.2 0.8 %copy-done.3 = f32[64,256]{1,0:T(8,128)S(1)} copy-done((f32[64,256]{1,0:T(8,128)S(1)}, f32[64,256]{1,0:T(8,128)}, u32[]{:S(2)}) %copy-start.3) | copy-done | bytes 65560
  22.0 2.8 %tables.1 = (bf16[4096,256]{1,0:T(8,128)(2,1)S(1)}, bf16[4096,256]{1,0:T(8,128)(2,1)S(1)}, bf16[4096,256]{1,0:T(8,128)(2,1)S(1)}, bf16[4096,256]{1,0:T(8,128)(2,...) custom-call(s32[2]{0:T(128)S(1)} %pad_add_fusion.me_ref, f32[64,1,256]{2,1,0:T(1,128)S(1)} %copy-done, ...), custom_call_target="tpu_custom_call" | custom-call | bytes 8388608 | tf_op jit(solution)/shard_map/tables/pallas_call | solution.py:319
  24.8 0.1 collective-permute-start.8
  24.9 0.5 %collective-permute-start.6 = (f32[256,128]{1,0:T(8,128)S(1)}, f32[256,128]{1,0:T(8,128)S(1)}, u32[]{:S(2)}, u32[]{:S(2)}) collective-permute-start(f32[256,128]{1,0:T(8,128)S(1)} %collective-permute-done.2.refs_6_), channel_id=1, source_target_pairs={{8,0},{0,8},{24,16},{16,24},{9,1},{1,9},{25,17},{17,25},{10,2},{2,... | collective-permute-start | bytes 393224 | tf_op jit(solution)/shard_map/ppermute | solution.py:238
  25.4 0.0 collective-permute-done.4.refs_7_
  25.4 1.8 %collective-permute-start.5 = (f32[128,128]{1,0:T(8,128)S(1)}, f32[128,128]{1,0:T(8,128)S(1)}, u32[]{:S(2)}, u32[]{:S(2)}) collective-permute-start(f32[128,128]{1,0:T(8,128)S(1)} %slice.17), channel_id=1, source_target_pairs={{1,0},{0,1},{3,2},{2,3},{5,4},{4,5},{7,6},{6,7},{9,8},{8,9},{11,10... | collective-permute-start | bytes 196616 | tf_op jit(solution)/shard_map/ppermute | solution.py:238
  27.2 0.0 collective-permute-start.9
  27.2 0.0 collective-permute-done.3
  27.2 2.5 %collective-permute-done.5 = f32[128,128]{1,0:T(8,128)S(1)} collective-permute-done((f32[128,128]{1,0:T(8,128)S(1)}, f32[128,128]{1,0:T(8,128)S(1)}, u32[]{:S(2)}, u32[]{:S(2)}) %collective-permute-start.5) | collective-permute-done | bytes 65568 | tf_op jit(solution)/shard_map/ppermute | solution.py:238
  29.7 0.0 collective-permute-start.7
  29.7 0.0 collective-permute-done.8.refs_8_
  29.7 0.0 collective-permute-done.9.refs_9_
  29.8 5.0 %near_bands.1 = (s32[256,128]{1,0:T(8,128)S(1)}, s32[256,128]{1,0:T(8,128)S(1)}, f32[256,128]{1,0:T(8,128)S(1)}, f32[256,256]{1,0:T(8,128)S(1)}, f32[256,256]{1,0:T(8,128)S(1)}) custom-call(s32[4]{0:T(128)S(1)} %get-tuple-element.29.bands_ref, s32[2]{0:T(128)S(1)} %pad_add_fusion.me_ref, f32[8,1,512]{2,1,0:T(1,128)S(1)} %get-tuple-element.16.refs_0_, ...), custom_call_target="tpu_custom_call" | custom-call | flops 1610612736 | bytes 8388608 | tf_op jit(solution)/shard_map/near_bands/pallas_call | solution.py:319
  34.7 0.0 collective-permute-done.6.refs_8_
  34.7 0.0 collective-permute-done.7.refs_9_
  34.7 4.7 %far_bands.1 = f32[256,512]{1,0:T(8,128)S(1)} custom-call(s32[4]{0:T(128)S(1)} %get-tuple-element.30.bands_ref, s32[2]{0:T(128)S(1)} %pad_add_fusion.me_ref, f32[8,1,512]{2,1,0:T(1,128)S(1)} %get-tuple-element.16.refs_0_, f32[8,1,512]{2,1,0:T(1,128)S(1)} %get-tuple-element.17.refs_1_, bf16[4096,256]{1,0:T(8,128)(2,1)S(1)} %get-tuple-element.18.refs_2_, ...), custom_call_target="tpu_custom_call" | custom-call | flops 1610612736 | bytes 8388608 | tf_op jit(solution)/shard_map/far_bands/pallas_call | solution.py:319
  39.4 0.8 %copy.11 = f32[1,2,4,32,512]{4,3,2,1,0:T(8,128)} copy(f32[1,2,4,32,512]{4,3,2,1,0:T(8,128)S(1)} %bitcast.16) | data formatting | bytes 1048576
  (9 shorter events, 0.1 us)
Async XLA Ops:
  0.8 6.3 %collective-permute-start = (f32[64,128]{1,0:T(8,128)S(1)}, f32[64,128]{1,0:T(8,128)S(1)}, u32[]{:S(2)}, u32[]{:S(2)}) collective-permute-start(f32[64,128]{1,0:T(8,128)S(1)} %bitcast.17), channel_id=1, source_target_pairs={{4,0},{5,1},{6,2},{7,3},{0,4},{1,5},{2,6},{3,7},{12,8},{13,9},{14,... | collective-permute-start | bytes 98312 | tf_op jit(solution)/shard_map/ppermute | solution.py:238
  7.2 4.3 %collective-permute-start.1 = (f32[128,128]{1,0:T(8,128)S(1)}, f32[128,128]{1,0:T(8,128)S(1)}, u32[]{:S(2)}, u32[]{:S(2)}) collective-permute-start(f32[128,128]{1,0:T(8,128)S(1)} %pad_maximum_fusion.1), channel_id=1, source_target_pairs={{2,0},{3,1},{0,2},{1,3},{6,4},{7,5},{4,6},{5,7},{10,8},{11,9},{8,1... | collective-permute-start | bytes 196616 | tf_op jit(solution)/shard_map/ppermute | solution.py:238
  11.4 13.9 %collective-permute-start.4 = (f32[264,128]{1,0:T(8,128)S(1)}, f32[264,128]{1,0:T(8,128)S(1)}, u32[]{:S(2)}, u32[]{:S(2)}) collective-permute-start(f32[264,128]{1,0:T(8,128)S(1)} %select_maximum_fusion.refs_6_), channel_id=1, source_target_pairs={{16,0},{24,8},{0,16},{8,24},{17,1},{25,9},{1,17},{9,25},{18,2},{26... | collective-permute-start | bytes 405512 | tf_op jit(solution)/shard_map/ppermute | solution.py:238
  13.2 5.0 %collective-permute-start.2 = (f32[256,128]{1,0:T(8,128)S(1)}, f32[256,128]{1,0:T(8,128)S(1)}, u32[]{:S(2)}, u32[]{:S(2)}) collective-permute-start(f32[256,128]{1,0:T(8,128)S(1)} %pad_maximum_fusion), channel_id=1, source_target_pairs={{1,0},{0,1},{3,2},{2,3},{5,4},{4,5},{7,6},{6,7},{9,8},{8,9},{11,10... | collective-permute-start | bytes 393224 | tf_op jit(solution)/shard_map/ppermute | solution.py:238
  18.3 8.9 %collective-permute-start.3 = (f32[128,128]{1,0:T(8,128)S(1)}, f32[128,128]{1,0:T(8,128)S(1)}, u32[]{:S(2)}, u32[]{:S(2)}) collective-permute-start(f32[128,128]{1,0:T(8,128)S(1)} %slice.16), channel_id=1, source_target_pairs={{16,0},{24,8},{0,16},{8,24},{17,1},{25,9},{1,17},{9,25},{18,2},{26... | collective-permute-start | bytes 196616 | tf_op jit(solution)/shard_map/ppermute | solution.py:238
  18.7 0.8 %copy-start = (f32[64,1,256]{2,1,0:T(1,128)S(1)}, f32[64,1,256]{2,1,0:T(1,128)}, u32[]{:S(2)}) copy-start(f32[64,1,256]{2,1,0:T(1,128)} %constant.25.clone.far_cos) | copy-start | bytes 196612
  19.5 0.8 %copy-start.1 = (f32[64,1,256]{2,1,0:T(1,128)S(1)}, f32[64,1,256]{2,1,0:T(1,128)}, u32[]{:S(2)}) copy-start(f32[64,1,256]{2,1,0:T(1,128)} %constant.26.clone.far_sin) | copy-start | bytes 196612
  20.3 0.8 %copy-start.2 = (f32[64,256]{1,0:T(8,128)S(1)}, f32[64,256]{1,0:T(8,128)}, u32[]{:S(2)}) copy-start(f32[64,256]{1,0:T(8,128)} %constant.27.clone.near_cos) | copy-start | bytes 196612
  21.2 0.8 %copy-start.3 = (f32[64,256]{1,0:T(8,128)S(1)}, f32[64,256]{1,0:T(8,128)}, u32[]{:S(2)}) copy-start(f32[64,256]{1,0:T(8,128)} %constant.28.clone.near_sin) | copy-start | bytes 196612
  24.8 4.9 %collective-permute-start.8 = (f32[264,128]{1,0:T(8,128)S(1)}, f32[264,128]{1,0:T(8,128)S(1)}, u32[]{:S(2)}, u32[]{:S(2)}) collective-permute-start(f32[264,128]{1,0:T(8,128)S(1)} %select_maximum_fusion.refs_6_), channel_id=1, source_target_pairs={{8,0},{0,8},{24,16},{16,24},{9,1},{1,9},{25,17},{17,25},{10,2},{2,... | collective-permute-start | bytes 405512 | tf_op jit(solution)/shard_map/ppermute | solution.py:238
  24.9 9.8 %collective-permute-start.6 = (f32[256,128]{1,0:T(8,128)S(1)}, f32[256,128]{1,0:T(8,128)S(1)}, u32[]{:S(2)}, u32[]{:S(2)}) collective-permute-start(f32[256,128]{1,0:T(8,128)S(1)} %collective-permute-done.2.refs_6_), channel_id=1, source_target_pairs={{8,0},{0,8},{24,16},{16,24},{9,1},{1,9},{25,17},{17,25},{10,2},{2,... | collective-permute-start | bytes 393224 | tf_op jit(solution)/shard_map/ppermute | solution.py:238
  25.4 4.3 %collective-permute-start.5 = (f32[128,128]{1,0:T(8,128)S(1)}, f32[128,128]{1,0:T(8,128)S(1)}, u32[]{:S(2)}, u32[]{:S(2)}) collective-permute-start(f32[128,128]{1,0:T(8,128)S(1)} %slice.17), channel_id=1, source_target_pairs={{1,0},{0,1},{3,2},{2,3},{5,4},{4,5},{7,6},{6,7},{9,8},{8,9},{11,10... | collective-permute-start | bytes 196616 | tf_op jit(solution)/shard_map/ppermute | solution.py:238
  27.2 2.6 %collective-permute-start.9 = (f32[264,128]{1,0:T(8,128)S(1)}, f32[264,128]{1,0:T(8,128)S(1)}, u32[]{:S(2)}, u32[]{:S(2)}) collective-permute-start(f32[264,128]{1,0:T(8,128)S(1)} %collective-permute-done.4.refs_7_), channel_id=1, source_target_pairs={{8,0},{0,8},{24,16},{16,24},{9,1},{1,9},{25,17},{17,25},{10,2},{2,... | collective-permute-start | bytes 405512 | tf_op jit(solution)/shard_map/ppermute | solution.py:238
  29.7 5.0 %collective-permute-start.7 = (f32[256,128]{1,0:T(8,128)S(1)}, f32[256,128]{1,0:T(8,128)S(1)}, u32[]{:S(2)}, u32[]{:S(2)}) collective-permute-start(f32[256,128]{1,0:T(8,128)S(1)} %constant_dynamic-update-slice_fusion.refs_7_), channel_id=1, source_target_pairs={{8,0},{0,8},{24,16},{16,24},{9,1},{1,9},{25,17},{17,25},{10,2},{2,... | collective-permute-start | bytes 393224 | tf_op jit(solution)/shard_map/ppermute | solution.py:238

commit v5 on v4

v5 whole, which is shorter than its diff:
```python
import functools
import math

import jax
import jax.numpy as jnp
from jax import lax
from jax.experimental import pallas as pl
from jax.experimental.pallas import tpu as pltpu
from jax.sharding import PartitionSpec as P

LAGS = 4096
LANES = 128
SUBLANES = 8


def split_bf16(values, parts):
    pieces = []
    for _ in range(parts - 1):
        piece = values.astype(jnp.bfloat16)
        pieces.append(piece)
        values = values - piece.astype(jnp.float32)
    pieces.append(values.astype(jnp.bfloat16))
    return pieces


def iota(shape, axis):
    return lax.broadcasted_iota(jnp.int32, shape, axis)


def dot(left, right):
    return jnp.dot(left, right, preferred_element_type=jnp.float32)


def padded(count, multiple):
    return -(-count // multiple) * multiple


def pick_slots(extras, places, me, stations, rounds, slots):
    groups = len(extras)
    pairs = stations * stations
    listed = rounds * pairs
    rows = rounds * groups * slots
    place = iota((groups, groups), 1)
    held_by = jnp.zeros((groups, groups), jnp.int32)
    for position in range(groups):
        held_by = jnp.where(place == position, places[position], held_by)
    lane = iota((1, listed), 1)

    def by_group(row, shift):
        wanted = (iota((groups, groups), 0) + groups - shift) % groups
        held = jnp.concatenate([extra[row : row + 1, :] for extra in extras], axis=0)
        return dot((held_by == wanted).astype(jnp.bfloat16), held.astype(jnp.bfloat16))

    def of_station(values, number):
        spread = iota((LANES, listed), 0) == number
        return dot(values.astype(jnp.bfloat16), spread.astype(jnp.bfloat16))

    owner_ids = jnp.zeros((groups, listed), jnp.float32)
    partner_mask = jnp.zeros((groups, listed), jnp.float32)
    for index in range(rounds):
        of_round = lane // pairs == index
        owner_ids = jnp.where(of_round, by_group(index, 0), owner_ids)
        second = of_station(by_group(rounds, index + 1), lane % stations)
        partner_mask = jnp.where(of_round, second, partner_mask)
    own_mask = of_station(by_group(rounds, 0), lane % pairs // stations)
    pair_weight = own_mask * partner_mask
    mine = owner_ids == me.astype(jnp.float32)
    from_pair, to_pair = iota((listed, listed), 0), iota((listed, listed), 1)
    before = (from_pair < to_pair) & (from_pair // pairs == to_pair // pairs)
    rank = dot(mine.astype(jnp.bfloat16), before.astype(jnp.bfloat16))
    marked = jnp.where(mine, rank, -1.0).astype(jnp.bfloat16)
    of_group = (iota((rows, groups), 0) // slots) % groups == iota((rows, groups), 1)
    of_group = of_group.astype(jnp.bfloat16)
    row_id, lane_id = iota((rows, listed), 0), iota((rows, listed), 1)
    chosen = (dot(of_group, marked) == (row_id % slots).astype(jnp.float32)) & (
        row_id // (groups * slots) == lane_id // pairs
    )
    weighed = jnp.where(chosen, dot(of_group, pair_weight.astype(jnp.bfloat16)), 0.0)
    weight = dot(weighed.astype(jnp.bfloat16), jnp.ones((listed, LANES), jnp.bfloat16))
    is_first = iota((SUBLANES, listed), 0) == 0
    pair_id = iota((SUBLANES, listed), 1) % pairs
    number = jnp.where(is_first, pair_id // stations, pair_id % stations).astype(jnp.bfloat16)
    picked = lax.dot_general(
        number, chosen.astype(jnp.bfloat16), (((1,), (1,)), ((), ())),
        preferred_element_type=jnp.float32,
    )
    slot_id = iota((SUBLANES, rows), 1)
    group = (slot_id // slots) % groups
    partner = (group + groups - 1 - slot_id // (groups * slots)) % groups
    group = jnp.where(iota((SUBLANES, rows), 0) == 0, group, partner)
    return picked.astype(jnp.int32) + group * stations, weight


def table_kernel(me_ref, owners_ref, mask_ref, *refs):
    cos_high, cos_low, sin_high, sin_low, turn_cos, turn_sin, extras = refs[:7]
    near_cos, near_sin, far_cos, far_sin = refs[7:]
    bin_total, half_band = cos_high.shape
    shards, chunks, _ = turn_cos.shape
    fine = near_cos.shape[0]
    coarse = fine * SUBLANES

    extras[...] = jnp.zeros_like(extras)
    rounds, pairs = owners_ref.shape[1], owners_ref.shape[3]
    for index in range(rounds):
        lanes = slice(index * pairs, (index + 1) * pairs)
        extras[index : index + 1, lanes] = owners_ref[0, index].astype(jnp.float32)
    extras[rounds : rounds + 1, : mask_ref.shape[1]] = mask_ref[...].astype(jnp.float32)

    def circle(turns):
        angles = (turns & (4 * bin_total - 1)).astype(jnp.float32) * (math.pi / (2 * bin_total))
        return jnp.cos(angles), jnp.sin(angles)

    def eight(count, step):
        return circle(iota((count, half_band), 0) * step * (2 * iota((count, half_band), 1) + 1))

    def added(cos, sin, other_cos, other_sin):
        return cos * other_cos - sin * other_sin, sin * other_cos + cos * other_sin

    low_cos, low_sin = eight(SUBLANES, 1)
    high_cos, high_sin = eight(fine // SUBLANES, SUBLANES)
    for index in range(fine // SUBLANES):
        rows, one = slice(index * SUBLANES, (index + 1) * SUBLANES), slice(index, index + 1)
        near_cos[rows, :], near_sin[rows, :] = added(
            high_cos[one], high_sin[one], low_cos, low_sin
        )
    mid_cos, mid_sin = eight(SUBLANES, fine)
    top_cos, top_sin = eight(bin_total // coarse, coarse)
    for index in range(bin_total // coarse):
        far_cos[index] = top_cos[index : index + 1]
        far_sin[index] = top_sin[index : index + 1]

    @pl.loop(0, bin_total // coarse)
    def _(index):
        cos, sin = added(far_cos[index], far_sin[index], mid_cos, mid_sin)
        for part in range(SUBLANES):
            rows = pl.ds(pl.multiple_of(index * coarse, coarse) + part * fine, fine)
            one = slice(part, part + 1)
            cosines, sines = added(cos[one], sin[one], near_cos[...], near_sin[...])
            cos_high[rows, :], cos_low[rows, :] = split_bf16(cosines, 2)
            sin_high[rows, :], sin_low[rows, :] = split_bf16(sines, 2)

    centre = 2 * half_band * (2 * me_ref[1] + 1) - 1 - LAGS
    bins = iota((shards * chunks, LANES), 0) * LANES + iota((shards * chunks, LANES), 1)
    norm = 1.0 / math.sqrt(bin_total)
    cos, sin = circle(bins * centre)
    for shard in range(shards):
        rows = slice(shard * chunks, (shard + 1) * chunks)
        turn_cos[shard] = cos[rows] * norm
        turn_sin[shard] = sin[rows] * norm


def add_bands(sizes, bands_ref, places, turn_refs, table_refs, block_refs, pick, sums, scratch):
    groups, stations, rounds, slots, band_bins, band_count = sizes
    cos_high, cos_low, sin_high, sin_low = table_refs
    even, odd = sums
    chunks = band_bins // LANES
    depth = 2 * chunks * stations
    rows = rounds * groups * slots
    per_tile = SUBLANES // chunks
    tiles = band_count // per_tile
    width = min(chunks, 2)
    parts = SUBLANES // width
    sets = [scratch[8 * tile : 8 * (tile + 1)] for tile in range(2)]

    def prepare(tile):
        held_real, held_imag, turned_real, turned_imag, cos, sin = sets[tile % 2][:6]
        for index in range(per_tile):
            step = tile * per_tile + index
            lines = slice(index * chunks, (index + 1) * chunks)
            cos[lines, :] = turn_refs[0][bands_ref[step]]
            sin[lines, :] = turn_refs[1][bands_ref[step]]
            for position, ref in enumerate(block_refs):
                for station in range(stations):
                    place = places[position] * stations + station
                    start = step * depth + station * 2 * chunks
                    held_real[place, lines, :] = ref[start : start + chunks, :]
                    held_imag[place, lines, :] = ref[start + chunks : start + 2 * chunks, :]
        for place in range(groups * stations):
            real, imag = held_real[place], held_imag[place]
            turned_real[place] = real * cos[...] + imag * sin[...]
            turned_imag[place] = imag * cos[...] - real * sin[...]

    def multiply(tile, part):
        held_real, held_imag, turned_real, turned_imag, _, _, cross_real, cross_imag = sets[tile % 2]
        for slot in range(part * rows // parts, (part + 1) * rows // parts):
            first, second = pick[0, slot], pick[1, slot]
            a_real, a_imag = held_real[first], held_imag[first]
            b_real, b_imag = turned_real[second], turned_imag[second]
            lines = slice(slot * SUBLANES, (slot + 1) * SUBLANES)
            cross_real[lines, :] = a_real * b_real + a_imag * b_imag
            cross_imag[lines, :] = a_imag * b_real - a_real * b_imag

    def transform(tile, part):
        line = part * width
        band = bands_ref[tile * per_tile + line // chunks]
        start = pl.multiple_of(band * band_bins + line % chunks * LANES, LANES)
        bins = pl.ds(start, width * LANES)

        def product(ref, table_high, table_low):
            cross = jnp.concatenate(
                [ref[pl.ds(line + index, rows, stride=SUBLANES), :] for index in range(width)],
                axis=1,
            )
            high, low = split_bf16(cross, 2)
            table = table_high[bins, :]
            return dot(
                jnp.concatenate([high, high, low], axis=1),
                jnp.concatenate([table, table_low[bins, :], table], axis=0),
            )

        cross_real, cross_imag = sets[tile % 2][6:]
        even[...] += product(cross_real, cos_high, cos_low)
        odd[...] += product(cross_imag, sin_high, sin_low)

    prepare(0)
    for part in range(parts):
        multiply(0, part)
    for tile in range(tiles):
        if tile + 1 < tiles:
            prepare(tile + 1)
        for part in range(parts):
            if tile + 1 < tiles:
                multiply(tile + 1, part)
            transform(tile, part)


def near_kernel(sizes, moves, bands_ref, me_ref, *refs):
    groups, stations, rounds, slots = sizes[:4]
    turn_refs, table_refs, refs = refs[:2], refs[2:6], refs[6:]
    block_refs, refs = refs[:groups], refs[groups:]
    (pick_out, weight, even, odd, pick, sem), scratch = refs[:6], refs[6:]
    places = [moved(me_ref[0], move, groups) for move in moves]
    extras = [ref[ref.shape[0] - SUBLANES :, :] for ref in block_refs]
    pick_out[...], weight[...] = pick_slots(extras, places, me_ref[0], stations, rounds, slots)
    copy = pltpu.make_async_copy(pick_out, pick, sem)
    copy.start()
    even[...] = jnp.zeros_like(even)
    odd[...] = jnp.zeros_like(odd)
    copy.wait()
    add_bands(
        sizes, bands_ref, places, turn_refs, table_refs, block_refs, pick, (even, odd), scratch
    )


def far_kernel(sizes, moves, bands_ref, me_ref, *refs):
    groups = sizes[0]
    turn_refs, table_refs, refs = refs[:2], refs[2:6], refs[6:]
    block_refs, refs = refs[:groups], refs[groups:]
    pick_in, weight, even_in, odd_in, out_ref, pick, sem, even, odd, result, out_sem = refs[:11]
    copy = pltpu.make_async_copy(pick_in, pick, sem)
    copy.start()
    even[...] = even_in[...]
    odd[...] = odd_in[...]
    places = [moved(me_ref[0], move, groups) for move in moves]
    copy.wait()
    add_bands(
        sizes, bands_ref, places, turn_refs, table_refs, block_refs, pick, (even, odd), refs[11:]
    )
    half = even.shape[1]
    row_weight = weight[:, 0:1]
    result[:, half:] = (even[...] - odd[...]) * row_weight
    total = (even[...] + odd[...]) * row_weight
    mirror = (iota((half, half), 0) + iota((half, half), 1) == half - 1).astype(jnp.bfloat16)
    pieces = [dot(piece, mirror) for piece in split_bf16(total, 3)]
    result[:, :half] = pieces[0] + (pieces[1] + pieces[2])
    copy = pltpu.make_async_copy(result, out_ref, out_sem)
    copy.start()
    copy.wait()


def moved(me, move, size):
    return me ^ move if size & (size - 1) == 0 else lax.rem(me + size - move, size)


def moved_index(me, move, size):
    return me ^ move if size & (size - 1) == 0 else (me - move) % size


def fetched(block, group_move, band_move):
    groups, shards = lax.axis_size("grp"), lax.axis_size("freq")
    route = [
        (
            moved_index(group, group_move, groups) * shards + moved_index(band, band_move, shards),
            group * shards + band,
        )
        for group in range(groups)
        for band in range(shards)
    ]
    return lax.ppermute(block, ("grp", "freq"), route)


def per_device(spectra, station_mask, owners):
    stations, _, band_bins = spectra.shape
    groups = lax.axis_size("grp")
    shards = lax.axis_size("freq")
    rounds = owners.shape[1]
    pairs = stations * stations
    bin_total = band_bins * shards
    capacity = (2 * pairs + groups - 1) // groups
    slots = padded(capacity, SUBLANES)
    lag_band = LAGS // shards
    half_band = lag_band // 2
    chunks = band_bins // LANES
    rows = rounds * groups * slots

    scalar = pl.BlockSpec(memory_space=pltpu.SMEM)
    vector = pl.BlockSpec(memory_space=pltpu.VMEM)

    def call(kernel, name, scalars, arrays, out_shape, scratch, cost):
        arrays = [pltpu.with_memory_space_constraint(array, pltpu.VMEM) for array in arrays]
        in_hbm = isinstance(out_shape, jax.ShapeDtypeStruct)
        return pl.pallas_call(
            kernel,
            out_shape=out_shape,
            in_specs=[scalar] * len(scalars) + [vector] * len(arrays),
            out_specs=pl.BlockSpec(memory_space=pl.ANY) if in_hbm else [vector] * len(out_shape),
            scratch_shapes=scratch,
            compiler_params=pltpu.CompilerParams(vmem_limit_bytes=24 * 1024 * 1024),
            cost_estimate=cost,
            name=name,
        )(*scalars, *arrays)

    tiles = spectra.reshape(2 * chunks * stations, LANES)
    moves = range(2, shards, 2)
    column = [tiles] + [fetched(tiles, 0, move) for move in moves]
    me = jnp.stack([lax.axis_index("grp"), lax.axis_index("freq")]).astype(jnp.int32)
    table = pltpu.VMEM((bin_total, half_band), jnp.bfloat16)
    turn = pltpu.VMEM((shards, chunks, LANES), jnp.float32)
    base = pltpu.VMEM((64, half_band), jnp.float32)
    far_base = pltpu.VMEM((bin_total // (64 * SUBLANES), 1, half_band), jnp.float32)
    *tables, turn_cos, turn_sin, extras = call(
        table_kernel,
        "tables",
        [me],
        [owners.transpose(0, 1, 3, 2), station_mask.reshape(1, stations)],
        [table] * 4 + [turn] * 2 + [pltpu.VMEM((SUBLANES, LANES), jnp.float32)],
        [base] * 2 + [far_base] * 2,
        pl.CostEstimate(flops=0, bytes_accessed=8 * bin_total * half_band, transcendentals=0),
    )
    column = jnp.concatenate(column + [extras], axis=0)
    near = [column] + [fetched(column, move, 0) for move in range(1, groups)]
    far = [fetched(column, move, 1) for move in range(groups)]

    near_bands = me[1] ^ jnp.arange(0, shards, 2, dtype=jnp.int32)
    far_bands = near_bands ^ 1
    sizes = (groups, stations, rounds, slots, band_bins, shards // 2)
    spectrum = pltpu.VMEM((groups * stations, SUBLANES, LANES), jnp.float32)
    turn_tile = pltpu.VMEM((SUBLANES, LANES), jnp.float32)
    cross = pltpu.VMEM((rows * SUBLANES, LANES), jnp.float32)
    scratch = ([spectrum] * 4 + [turn_tile] * 2 + [cross] * 2) * 2
    flops = 6 * rows * bin_total * lag_band // 2
    cost = pl.CostEstimate(flops=flops, bytes_accessed=8 * 1024 * 1024, transcendentals=0)
    total = pltpu.VMEM((rows, half_band), jnp.float32)
    pick_in_smem = [pltpu.SMEM((SUBLANES, rows), jnp.int32), pltpu.SemaphoreType.DMA]
    held = call(
        functools.partial(near_kernel, sizes, range(groups)),
        "near_bands",
        [near_bands, me],
        [turn_cos, turn_sin, *tables, *near],
        [pltpu.VMEM((SUBLANES, rows), jnp.int32), pltpu.VMEM((rows, LANES), jnp.float32)]
        + [total] * 2,
        pick_in_smem + scratch,
        cost,
    )
    out = call(
        functools.partial(far_kernel, sizes, range(groups)),
        "far_bands",
        [far_bands, me],
        [turn_cos, turn_sin, *tables, *far, *held],
        jax.ShapeDtypeStruct((rows, lag_band), jnp.float32),
        pick_in_smem
        + [total] * 2
        + [pltpu.VMEM((rows, lag_band), jnp.float32), pltpu.SemaphoreType.DMA]
        + scratch,
        cost,
    )
    out = out.reshape(1, rounds, groups, slots, lag_band)
    return out[:, :, :, :capacity]


def solution(mesh):
    placed = (P("grp", None, "freq"), P("grp"), P("grp", None, None, None))
    return jax.shard_map(
        per_device,
        mesh=mesh,
        in_specs=placed,
        out_specs=P("grp", None, None, None, "freq"),
        check_vma=False,
    )
```

time: 40.6 us -> 35.3 us (0.87)
  local copies, waits for them, and re-layouts: 6.38 us -> 2.14 us
  waiting for transfers between devices: 8.87 us -> 4.75 us
  Pallas kernels: 12.4 us -> 15.1 us
  starting transfers between devices: 11.7 us -> 13 us
  other arithmetic: 0.77 us -> 0.08 us
    ppermute x10, waiting for transfers between devices: 8.87 us -> 4.75 us  [fetched(): return lax.ppermute(block, ('grp', 'freq'), route)]
    unnamed x10 -> x8, local copies, waits for them, and re-layouts: 4.16 us -> 1.35 us
    pallas_call x3, Pallas kernels: 12.4 us -> 15.1 us  [call(): pl.pallas_call(kernel, out_shape=out_shape, in_specs=[scalar] * len(scala...]
    ppermute x10, starting transfers between devices: 11.7 us -> 13 us  [fetched(): return lax.ppermute(block, ('grp', 'freq'), route)]
    another operation x2 -> x0, local copies, waits for them, and re-layouts: 0.73 us -> none  [per_device(): listed = jnp.stack(listed).astype(jnp.float32)]
    squeeze x1 -> x0, local copies, waits for them, and re-layouts: 0.67 us -> none  [per_device(): owners[0, index, :, 0]]
    xor x1 -> x2, other arithmetic: 0.66 us -> 0.01 us  [the longest x1 0.01 us: per_device(): far_bands = near_bands ^ 1]
  transfers between devices with their start and end apart: 10 -> 10, of which waited for: 4 -> 4; matrix products, arithmetic and copies ran while one was open for 5% -> 0% of each run, Pallas kernels for 19% -> 23%
where the time goes in v5:
time: 35.3 us; the launch traced here: 35.1 us
  Pallas kernels  15.1 us (43%)
  starting transfers between devices  13 us (37%)
  waiting for transfers between devices  4.75 us (13%)
  local copies, waits for them, and re-layouts  2.14 us (6%)
    pallas_call x3, Pallas kernels, call(): pl.pallas_call(kernel, out_shape=out_shape, in_specs=[scalar] * len(scala...  15.1 us
    ppermute x10, starting transfers between devices, fetched(): return lax.ppermute(block, ('grp', 'freq'), route)  13 us
    ppermute x10, waiting for transfers between devices, fetched(): return lax.ppermute(block, ('grp', 'freq'), route)  4.75 us
    unnamed x8, local copies, waits for them, and re-layouts  1.35 us
    reshape x1, local copies, waits for them, and re-layouts, per_device(): tiles = spectra.reshape(2 * chunks * stations, LANES)  0.78 us
  transfers between devices with their start and end apart: 10, of which 4 were waited for; matrix products, arithmetic and copies ran while one was open for 0% of the time, Pallas kernels for 23%

profile of v5, /device:TPU:0, one launch (start us, length us, event | category | flops | bytes accessed | tf_op | source)
XLA Modules:
  0.0 35.1 jit_solution(8485737849700108217)
XLA Ops:
  0.0 0.8 %reshape.10 = f32[64,128]{1,0:T(8,128)S(1)} reshape(f32[8,2,512]{2,1,0:T(2,128)} %param.3) | data formatting | bytes 65536 | tf_op jit(solution)/shard_map/reshape | solution.py:323
  0.8 3.1 %collective-permute-start = (f32[64,128]{1,0:T(8,128)S(1)}, f32[64,128]{1,0:T(8,128)S(1)}, u32[]{:S(2)}, u32[]{:S(2)}) collective-permute-start(f32[64,128]{1,0:T(8,128)S(1)} %reshape.10), channel_id=1, source_target_pairs={{2,0},{3,1},{0,2},{1,3},{6,4},{7,5},{4,6},{5,7},{10,8},{11,9},{8,1... | collective-permute-start | bytes 98312 | tf_op jit(solution)/shard_map/ppermute | solution.py:289
  3.9 2.6 %collective-permute-start.1 = (f32[64,128]{1,0:T(8,128)S(1)}, f32[64,128]{1,0:T(8,128)S(1)}, u32[]{:S(2)}, u32[]{:S(2)}) collective-permute-start(f32[64,128]{1,0:T(8,128)S(1)} %reshape.10), channel_id=1, source_target_pairs={{4,0},{5,1},{6,2},{7,3},{0,4},{1,5},{2,6},{3,7},{12,8},{13,9},{14,... | collective-permute-start | bytes 98312 | tf_op jit(solution)/shard_map/ppermute | solution.py:289
  6.5 0.0 collective-permute-start.2
  6.5 0.1 pad_add_fusion.me_ref
  6.5 0.0 copy-start
  6.6 0.7 %copy-done = s32[1,2,64,1]{2,3,1,0:T(1,128)S(1)} copy-done((s32[1,2,64,1]{2,3,1,0:T(1,128)S(1)}, s32[1,2,64,1]{2,3,1,0:T(1,128)}, u32[]{:S(2)}) %copy-start) | copy-done | bytes 536
  7.2 0.0 copy-start.1
  7.2 0.7 %copy-done.1 = s32[8]{0:T(128)S(1)} copy-done((s32[8]{0:T(128)S(1)}, s32[8]{0:T(128)}, u32[]{:S(2)}) %copy-start.1) | copy-done | bytes 56
  7.9 3.0 %tables.1 = (bf16[4096,256]{1,0:T(8,128)(2,1)S(1)}, bf16[4096,256]{1,0:T(8,128)(2,1)S(1)}, bf16[4096,256]{1,0:T(8,128)(2,1)S(1)}, bf16[4096,256]{1,0:T(8,128)(2,...) custom-call(s32[2]{0:T(128)S(1)} %pad_add_fusion.me_ref, ...), custom_call_target="tpu_custom_call" | custom-call | bytes 8388608 | tf_op jit(solution)/shard_map/tables/pallas_call | solution.py:312
  10.9 0.0 collective-permute-done
  10.9 0.0 collective-permute-done.1
  10.9 1.2 %collective-permute-done.2 = f32[64,128]{1,0:T(8,128)S(1)} collective-permute-done((f32[64,128]{1,0:T(8,128)S(1)}, f32[64,128]{1,0:T(8,128)S(1)}, u32[]{:S(2)}, u32[]{:S(2)}) %collective-permute-start.2) | collective-permute-done | bytes 32800 | tf_op jit(solution)/shard_map/ppermute | solution.py:289
  12.2 0.0 collective-permute-start.7
  12.2 1.6 %collective-permute-start.8 = (f32[264,128]{1,0:T(8,128)S(1)}, f32[264,128]{1,0:T(8,128)S(1)}, u32[]{:S(2)}, u32[]{:S(2)}) collective-permute-start(f32[264,128]{1,0:T(8,128)S(1)} %constant_dynamic-update-slice_fusion.refs_6_), channel_id=1, source_target_pairs={{16,0},{17,1},{18,2},{19,3},{20,4},{21,5},{22,6},{23,7},{24,8},{25... | collective-permute-start | bytes 405512 | tf_op jit(solution)/shard_map/ppermute | solution.py:289
  13.8 0.3 collective-permute-start.9
  14.1 1.6 %collective-permute-start.3 = (f32[264,128]{1,0:T(8,128)S(1)}, f32[264,128]{1,0:T(8,128)S(1)}, u32[]{:S(2)}, u32[]{:S(2)}) collective-permute-start(f32[264,128]{1,0:T(8,128)S(1)} %constant_dynamic-update-slice_fusion.refs_6_), channel_id=1, source_target_pairs={{1,0},{0,1},{3,2},{2,3},{5,4},{4,5},{7,6},{6,7},{9,8},{8,9},{11,10... | collective-permute-start | bytes 405512 | tf_op jit(solution)/shard_map/ppermute | solution.py:289
  15.6 0.2 collective-permute-start.4
  15.8 0.0 collective-permute-done.7.refs_7_
  15.8 2.4 %collective-permute-start.5 = (f32[264,128]{1,0:T(8,128)S(1)}, f32[264,128]{1,0:T(8,128)S(1)}, u32[]{:S(2)}, u32[]{:S(2)}) collective-permute-start(f32[264,128]{1,0:T(8,128)S(1)} %constant_dynamic-update-slice_fusion.refs_6_), channel_id=1, source_target_pairs={{17,0},{16,1},{19,2},{18,3},{21,4},{20,5},{23,6},{22,7},{25,8},{24... | collective-permute-start | bytes 405512 | tf_op jit(solution)/shard_map/ppermute | solution.py:289
  18.3 0.4 %collective-permute-done.8.refs_8_ = f32[264,128]{1,0:T(8,128)S(1)} collective-permute-done((f32[264,128]{1,0:T(8,128)S(1)}, f32[264,128]{1,0:T(8,128)S(1)}, u32[]{:S(2)}, u32[]{:S(2)}) %collective-permute-start.8) | collective-permute-done | bytes 135200 | tf_op jit(solution)/shard_map/ppermute | solution.py:289
  18.7 1.2 %collective-permute-start.6 = (f32[264,128]{1,0:T(8,128)S(1)}, f32[264,128]{1,0:T(8,128)S(1)}, u32[]{:S(2)}, u32[]{:S(2)}) collective-permute-start(f32[264,128]{1,0:T(8,128)S(1)} %constant_dynamic-update-slice_fusion.refs_6_), channel_id=1, source_target_pairs={{25,0},{24,1},{27,2},{26,3},{29,4},{28,5},{31,6},{30,7},{17,8},{16... | collective-permute-start | bytes 405512 | tf_op jit(solution)/shard_map/ppermute | solution.py:289
  19.9 0.7 %collective-permute-done.9.refs_9_ = f32[264,128]{1,0:T(8,128)S(1)} collective-permute-done((f32[264,128]{1,0:T(8,128)S(1)}, f32[264,128]{1,0:T(8,128)S(1)}, u32[]{:S(2)}, u32[]{:S(2)}) %collective-permute-start.9) | collective-permute-done | bytes 135200 | tf_op jit(solution)/shard_map/ppermute | solution.py:289
  20.6 5.1 %near_bands.1 = (s32[8,256]{1,0:T(8,128)S(1)}, f32[256,128]{1,0:T(8,128)S(1)}, f32[256,256]{1,0:T(8,128)S(1)}, f32[256,256]{1,0:T(8,128)S(1)}) custom-call(s32[4]{0:T(128)S(1)} %multiply_xor_fusion.bands_ref, s32[2]{0:T(128)S(1)} %pad_add_fusion.me_ref, f32[8,4,128]{2,1,0:T(4,128)S(1)} %get-tuple-element.16.refs_0_, ...), custom_call_target="tpu_custom_call" | custom-call | flops 1610612736 | bytes 8388608 | tf_op jit(solution)/shard_map/near_bands/pallas_call | solution.py:312
  25.7 0.0 collective-permute-done.3.refs_6_
  25.7 2.4 %collective-permute-done.4.refs_7_ = f32[264,128]{1,0:T(8,128)S(1)} collective-permute-done((f32[264,128]{1,0:T(8,128)S(1)}, f32[264,128]{1,0:T(8,128)S(1)}, u32[]{:S(2)}, u32[]{:S(2)}) %collective-permute-start.4) | collective-permute-done | bytes 135200 | tf_op jit(solution)/shard_map/ppermute | solution.py:289
  28.1 0.0 collective-permute-done.5.refs_8_
  28.1 0.0 collective-permute-done.6.refs_9_
  28.1 7.0 %far_bands.1 = f32[256,512]{1,0:T(8,128)} custom-call(s32[4]{0:T(128)S(1)} %broadcast_xor_fusion.bands_ref, s32[2]{0:T(128)S(1)} %pad_add_fusion.me_ref, f32[8,4,128]{2,1,0:T(4,128)S(1)} %get-tuple-element.16.refs_0_, f32[8,4,128]{2,1,0:T(4,128)S(1)} %get-tuple-element.17.refs_1_, bf16[4096,256]{1,0:T(8,128)(2,1)S(1)} %get-tuple-element.18.refs_2_, ...), custom_call_target="tpu_custom_call" | custom-call | flops 1610612736 | bytes 8388608 | tf_op jit(solution)/shard_map/far_bands/pallas_call | solution.py:312
  (7 shorter events, 0.0 us)
Async XLA Ops:
  0.8 10.1 %collective-permute-start = (f32[64,128]{1,0:T(8,128)S(1)}, f32[64,128]{1,0:T(8,128)S(1)}, u32[]{:S(2)}, u32[]{:S(2)}) collective-permute-start(f32[64,128]{1,0:T(8,128)S(1)} %reshape.10), channel_id=1, source_target_pairs={{2,0},{3,1},{0,2},{1,3},{6,4},{7,5},{4,6},{5,7},{10,8},{11,9},{8,1... | collective-permute-start | bytes 98312 | tf_op jit(solution)/shard_map/ppermute | solution.py:289
  3.9 7.0 %collective-permute-start.1 = (f32[64,128]{1,0:T(8,128)S(1)}, f32[64,128]{1,0:T(8,128)S(1)}, u32[]{:S(2)}, u32[]{:S(2)}) collective-permute-start(f32[64,128]{1,0:T(8,128)S(1)} %reshape.10), channel_id=1, source_target_pairs={{4,0},{5,1},{6,2},{7,3},{0,4},{1,5},{2,6},{3,7},{12,8},{13,9},{14,... | collective-permute-start | bytes 98312 | tf_op jit(solution)/shard_map/ppermute | solution.py:289
  6.5 5.7 %collective-permute-start.2 = (f32[64,128]{1,0:T(8,128)S(1)}, f32[64,128]{1,0:T(8,128)S(1)}, u32[]{:S(2)}, u32[]{:S(2)}) collective-permute-start(f32[64,128]{1,0:T(8,128)S(1)} %reshape.10), channel_id=1, source_target_pairs={{6,0},{7,1},{4,2},{5,3},{2,4},{3,5},{0,6},{1,7},{14,8},{15,9},{12,... | collective-permute-start | bytes 98312 | tf_op jit(solution)/shard_map/ppermute | solution.py:289
  6.5 0.7 %copy-start = (s32[1,2,64,1]{2,3,1,0:T(1,128)S(1)}, s32[1,2,64,1]{2,3,1,0:T(1,128)}, u32[]{:S(2)}) copy-start(s32[1,2,64,1]{2,3,1,0:T(1,128)} %param.5) | copy-start | bytes 1540
  7.2 0.7 %copy-start.1 = (s32[8]{0:T(128)S(1)}, s32[8]{0:T(128)}, u32[]{:S(2)}) copy-start(s32[8]{0:T(128)} %param.4) | copy-start | bytes 100
  12.2 3.6 %collective-permute-start.7 = (f32[264,128]{1,0:T(8,128)S(1)}, f32[264,128]{1,0:T(8,128)S(1)}, u32[]{:S(2)}, u32[]{:S(2)}) collective-permute-start(f32[264,128]{1,0:T(8,128)S(1)} %constant_dynamic-update-slice_fusion.refs_6_), channel_id=1, source_target_pairs={{8,0},{9,1},{10,2},{11,3},{12,4},{13,5},{14,6},{15,7},{0,8},{1,9},... | collective-permute-start | bytes 405512 | tf_op jit(solution)/shard_map/ppermute | solution.py:289
  12.2 6.5 %collective-permute-start.8 = (f32[264,128]{1,0:T(8,128)S(1)}, f32[264,128]{1,0:T(8,128)S(1)}, u32[]{:S(2)}, u32[]{:S(2)}) collective-permute-start(f32[264,128]{1,0:T(8,128)S(1)} %constant_dynamic-update-slice_fusion.refs_6_), channel_id=1, source_target_pairs={{16,0},{17,1},{18,2},{19,3},{20,4},{21,5},{22,6},{23,7},{24,8},{25... | collective-permute-start | bytes 405512 | tf_op jit(solution)/shard_map/ppermute | solution.py:289
  13.8 6.9 %collective-permute-start.9 = (f32[264,128]{1,0:T(8,128)S(1)}, f32[264,128]{1,0:T(8,128)S(1)}, u32[]{:S(2)}, u32[]{:S(2)}) collective-permute-start(f32[264,128]{1,0:T(8,128)S(1)} %constant_dynamic-update-slice_fusion.refs_6_), channel_id=1, source_target_pairs={{24,0},{25,1},{26,2},{27,3},{28,4},{29,5},{30,6},{31,7},{16,8},{17... | collective-permute-start | bytes 405512 | tf_op jit(solution)/shard_map/ppermute | solution.py:289
  14.1 11.6 %collective-permute-start.3 = (f32[264,128]{1,0:T(8,128)S(1)}, f32[264,128]{1,0:T(8,128)S(1)}, u32[]{:S(2)}, u32[]{:S(2)}) collective-permute-start(f32[264,128]{1,0:T(8,128)S(1)} %constant_dynamic-update-slice_fusion.refs_6_), channel_id=1, source_target_pairs={{1,0},{0,1},{3,2},{2,3},{5,4},{4,5},{7,6},{6,7},{9,8},{8,9},{11,10... | collective-permute-start | bytes 405512 | tf_op jit(solution)/shard_map/ppermute | solution.py:289
  15.6 12.4 %collective-permute-start.4 = (f32[264,128]{1,0:T(8,128)S(1)}, f32[264,128]{1,0:T(8,128)S(1)}, u32[]{:S(2)}, u32[]{:S(2)}) collective-permute-start(f32[264,128]{1,0:T(8,128)S(1)} %constant_dynamic-update-slice_fusion.refs_6_), channel_id=1, source_target_pairs={{9,0},{8,1},{11,2},{10,3},{13,4},{12,5},{15,6},{14,7},{1,8},{0,9},... | collective-permute-start | bytes 405512 | tf_op jit(solution)/shard_map/ppermute | solution.py:289
  15.8 12.3 %collective-permute-start.5 = (f32[264,128]{1,0:T(8,128)S(1)}, f32[264,128]{1,0:T(8,128)S(1)}, u32[]{:S(2)}, u32[]{:S(2)}) collective-permute-start(f32[264,128]{1,0:T(8,128)S(1)} %constant_dynamic-update-slice_fusion.refs_6_), channel_id=1, source_target_pairs={{17,0},{16,1},{19,2},{18,3},{21,4},{20,5},{23,6},{22,7},{25,8},{24... | collective-permute-start | bytes 405512 | tf_op jit(solution)/shard_map/ppermute | solution.py:289
  18.7 9.4 %collective-permute-start.6 = (f32[264,128]{1,0:T(8,128)S(1)}, f32[264,128]{1,0:T(8,128)S(1)}, u32[]{:S(2)}, u32[]{:S(2)}) collective-permute-start(f32[264,128]{1,0:T(8,128)S(1)} %constant_dynamic-update-slice_fusion.refs_6_), channel_id=1, source_target_pairs={{25,0},{24,1},{27,2},{26,3},{29,4},{28,5},{31,6},{30,7},{17,8},{16... | collective-permute-start | bytes 405512 | tf_op jit(solution)/shard_map/ppermute | solution.py:289

commit v6 on v5

--- a/solution.py
+++ b/solution.py
@@ -91,20 +91,19 @@
     return picked.astype(jnp.int32) + group * stations, weight
 
 
-def table_kernel(me_ref, owners_ref, mask_ref, *refs):
-    cos_high, cos_low, sin_high, sin_low, turn_cos, turn_sin, extras = refs[:7]
-    near_cos, near_sin, far_cos, far_sin = refs[7:]
-    bin_total, half_band = cos_high.shape
+def table_kernel(me_ref, owners_hbm, mask_hbm, *refs):
+    cos_table, sin_table, turn_cos, turn_sin, extras = refs[:5]
+    near_cos, near_sin, far_cos, far_sin, owners_ref, mask_ref, sems = refs[5:]
+    bin_total, half_band = cos_table.shape[0], cos_table.shape[1] // 2
+    copies = [
+        pltpu.make_async_copy(owners_hbm, owners_ref, sems.at[0]),
+        pltpu.make_async_copy(mask_hbm, mask_ref, sems.at[1]),
+    ]
+    for copy in copies:
+        copy.start()
     shards, chunks, _ = turn_cos.shape
     fine = near_cos.shape[0]
     coarse = fine * SUBLANES
-
-    extras[...] = jnp.zeros_like(extras)
-    rounds, pairs = owners_ref.shape[1], owners_ref.shape[3]
-    for index in range(rounds):
-        lanes = slice(index * pairs, (index + 1) * pairs)
-        extras[index : index + 1, lanes] = owners_ref[0, index].astype(jnp.float32)
-    extras[rounds : rounds + 1, : mask_ref.shape[1]] = mask_ref[...].astype(jnp.float32)
 
     def circle(turns):
         angles = (turns & (4 * bin_total - 1)).astype(jnp.float32) * (math.pi / (2 * bin_total))
@@ -136,8 +135,8 @@
             rows = pl.ds(pl.multiple_of(index * coarse, coarse) + part * fine, fine)
             one = slice(part, part + 1)
             cosines, sines = added(cos[one], sin[one], near_cos[...], near_sin[...])
-            cos_high[rows, :], cos_low[rows, :] = split_bf16(cosines, 2)
-            sin_high[rows, :], sin_low[rows, :] = split_bf16(sines, 2)
+            for table, values in ((cos_table, cosines), (sin_table, sines)):
+                table[rows, :half_band], table[rows, half_band:] = split_bf16(values, 2)
 
     centre = 2 * half_band * (2 * me_ref[1] + 1) - 1 - LAGS
     bins = iota((shards * chunks, LANES), 0) * LANES + iota((shards * chunks, LANES), 1)
@@ -148,31 +147,36 @@
         turn_cos[shard] = cos[rows] * norm
         turn_sin[shard] = sin[rows] * norm
 
-
-def add_bands(sizes, bands_ref, places, turn_refs, table_refs, block_refs, pick, sums, scratch):
-    groups, stations, rounds, slots, band_bins, band_count = sizes
-    cos_high, cos_low, sin_high, sin_low = table_refs
-    even, odd = sums
+    for copy in copies:
+        copy.wait()
+    extras[...] = jnp.zeros_like(extras)
+    rounds, pairs = owners_ref.shape[1], owners_ref.shape[3]
+    for index in range(rounds):
+        lanes = slice(index * pairs, (index + 1) * pairs)
+        extras[index : index + 1, lanes] = owners_ref[0, index].astype(jnp.float32)
+    extras[rounds : rounds + 1, : mask_ref.shape[1]] = mask_ref[...].astype(jnp.float32)
+
+
+def add_bands(sizes, tiles, bands_ref, places, turn_refs, table_refs, blocks, pick, sums, scratch):
+    groups, stations, rounds, slots, band_bins = sizes
     chunks = band_bins // LANES
     depth = 2 * chunks * stations
     rows = rounds * groups * slots
     per_tile = SUBLANES // chunks
-    tiles = band_count // per_tile
-    width = min(chunks, 2)
-    parts = SUBLANES // width
-    sets = [scratch[8 * tile : 8 * (tile + 1)] for tile in range(2)]
-
-    def prepare(tile):
-        held_real, held_imag, turned_real, turned_imag, cos, sin = sets[tile % 2][:6]
-        for index in range(per_tile):
-            step = tile * per_tile + index
-            lines = slice(index * chunks, (index + 1) * chunks)
+    half = sums[0].shape[1]
+    sets = [scratch[8 * index : 8 * (index + 1)] for index in range(len(tiles))]
+
+    def prepare(index):
+        held_real, held_imag, turned_real, turned_imag, cos, sin = sets[index][:6]
+        for part in range(per_tile):
+            step = tiles[index] * per_tile + part
+            lines = slice(part * chunks, (part + 1) * chunks)
             cos[lines, :] = turn_refs[0][bands_ref[step]]
             sin[lines, :] = turn_refs[1][bands_ref[step]]
-            for position, ref in enumerate(block_refs):
+            for position, (ref, offset) in enumerate(blocks):
                 for station in range(stations):
                     place = places[position] * stations + station
-                    start = step * depth + station * 2 * chunks
+                    start = offset + step * depth + station * 2 * chunks
                     held_real[place, lines, :] = ref[start : start + chunks, :]
                     held_imag[place, lines, :] = ref[start + chunks : start + 2 * chunks, :]
         for place in range(groups * stations):
@@ -180,9 +184,9 @@
             turned_real[place] = real * cos[...] + imag * sin[...]
             turned_imag[place] = imag * cos[...] - real * sin[...]
 
-    def multiply(tile, part):
-        held_real, held_imag, turned_real, turned_imag, _, _, cross_real, cross_imag = sets[tile % 2]
-        for slot in range(part * rows // parts, (part + 1) * rows // parts):
+    def multiply(index, part):
+        held_real, held_imag, turned_real, turned_imag, _, _, cross_real, cross_imag = sets[index]
+        for slot in range(part * rows // per_tile, (part + 1) * rows // per_tile):
             first, second = pick[0, slot], pick[1, slot]
             a_real, a_imag = held_real[first], held_imag[first]
             b_real, b_imag = turned_real[second], turned_imag[second]
@@ -190,47 +194,46 @@
             cross_real[lines, :] = a_real * b_real + a_imag * b_imag
             cross_imag[lines, :] = a_imag * b_real - a_real * b_imag
 
-    def transform(tile, part):
-        line = part * width
-        band = bands_ref[tile * per_tile + line // chunks]
-        start = pl.multiple_of(band * band_bins + line % chunks * LANES, LANES)
-        bins = pl.ds(start, width * LANES)
-
-        def product(ref, table_high, table_low):
+    def transform(index, part):
+        band = bands_ref[tiles[index] * per_tile + part]
+        bins = pl.ds(pl.multiple_of(band * band_bins, band_bins), band_bins)
+        for cross_ref, table_ref, total in zip(sets[index][6:], table_refs, sums):
             cross = jnp.concatenate(
-                [ref[pl.ds(line + index, rows, stride=SUBLANES), :] for index in range(width)],
+                [
+                    cross_ref[pl.ds(part * chunks + chunk, rows, stride=SUBLANES), :]
+                    for chunk in range(chunks)
+                ],
                 axis=1,
             )
             high, low = split_bf16(cross, 2)
-            table = table_high[bins, :]
-            return dot(
-                jnp.concatenate([high, high, low], axis=1),
-                jnp.concatenate([table, table_low[bins, :], table], axis=0),
-            )
-
-        cross_real, cross_imag = sets[tile % 2][6:]
-        even[...] += product(cross_real, cos_high, cos_low)
-        odd[...] += product(cross_imag, sin_high, sin_low)
+            by_high = dot(high, table_ref[bins, :])
+            by_low = dot(low, table_ref[bins, :half])
+            total[...] += by_high[:, :half] + (by_high[:, half:] + by_low)
 
     prepare(0)
-    for part in range(parts):
+    for part in range(per_tile):
         multiply(0, part)
-    for tile in range(tiles):
-        if tile + 1 < tiles:
-            prepare(tile + 1)
-        for part in range(parts):
-            if tile + 1 < tiles:
-                multiply(tile + 1, part)
-            transform(tile, part)
-
-
-def near_kernel(sizes, moves, bands_ref, me_ref, *refs):
+    for index in range(len(tiles)):
+        if index + 1 < len(tiles):
+            prepare(index + 1)
+        for part in range(per_tile):
+            if index + 1 < len(tiles):
+                multiply(index + 1, part)
+            transform(index, part)
+
+
+def placed_blocks(array_refs, layout, me, groups):
+    blocks = [(array_refs[index], offset) for index, offset, _ in layout]
+    return blocks, [moved(me, move, groups) for _, _, move in layout]
+
+
+def near_kernel(sizes, layout, array_count, depth, bands_ref, me_ref, *refs):
     groups, stations, rounds, slots = sizes[:4]
-    turn_refs, table_refs, refs = refs[:2], refs[2:6], refs[6:]
-    block_refs, refs = refs[:groups], refs[groups:]
+    turn_refs, table_refs, refs = refs[:2], refs[2:4], refs[4:]
+    array_refs, refs = refs[:array_count], refs[array_count:]
     (pick_out, weight, even, odd, pick, sem), scratch = refs[:6], refs[6:]
-    places = [moved(me_ref[0], move, groups) for move in moves]
-    extras = [ref[ref.shape[0] - SUBLANES :, :] for ref in block_refs]
+    blocks, places = placed_blocks(array_refs, layout, me_ref[0], groups)
+    extras = [ref[offset + depth : offset + depth + SUBLANES, :] for ref, offset in blocks]
     pick_out[...], weight[...] = pick_slots(extras, places, me_ref[0], stations, rounds, slots)
     copy = pltpu.make_async_copy(pick_out, pick, sem)
     copy.start()
@@ -238,34 +241,60 @@
     odd[...] = jnp.zeros_like(odd)
     copy.wait()
     add_bands(
-        sizes, bands_ref, places, turn_refs, table_refs, block_refs, pick, (even, odd), scratch
-    )
-
-
-def far_kernel(sizes, moves, bands_ref, me_ref, *refs):
-    groups = sizes[0]
-    turn_refs, table_refs, refs = refs[:2], refs[2:6], refs[6:]
-    block_refs, refs = refs[:groups], refs[groups:]
-    pick_in, weight, even_in, odd_in, out_ref, pick, sem, even, odd, result, out_sem = refs[:11]
+        sizes, [0], bands_ref, places, turn_refs, table_refs, blocks, pick, (even, odd), scratch
+    )
+
+
+def next_kernel(sizes, layout, array_count, tiles, bands_ref, me_ref, *refs):
+    turn_refs, table_refs, refs = refs[:2], refs[2:4], refs[4:]
+    array_refs, refs = refs[:array_count], refs[array_count:]
+    (pick_in, even_in, odd_in, even, odd, pick, sem), scratch = refs[:7], refs[7:]
     copy = pltpu.make_async_copy(pick_in, pick, sem)
     copy.start()
     even[...] = even_in[...]
     odd[...] = odd_in[...]
-    places = [moved(me_ref[0], move, groups) for move in moves]
+    blocks, places = placed_blocks(array_refs, layout, me_ref[0], sizes[0])
     copy.wait()
     add_bands(
-        sizes, bands_ref, places, turn_refs, table_refs, block_refs, pick, (even, odd), refs[11:]
+        sizes, tiles, bands_ref, places, turn_refs, table_refs, blocks, pick, (even, odd), scratch
+    )
+
+
+def last_kernel(sizes, layout, array_count, tiles, bands_ref, me_ref, *refs):
+    turn_refs, table_refs, refs = refs[:2], refs[2:4], refs[4:]
+    array_refs, refs = refs[:array_count], refs[array_count:]
+    pick_in, even_in, odd_in, weight, out_ref, pick, sem, even, odd, above, below, sems = refs[:12]
+    copy = pltpu.make_async_copy(pick_in, pick, sem)
+    copy.start()
+    even[...] = even_in[...]
+    odd[...] = odd_in[...]
+    blocks, places = placed_blocks(array_refs, layout, me_ref[0], sizes[0])
+    copy.wait()
+    add_bands(
+        sizes, tiles, bands_ref, places, turn_refs, table_refs, blocks, pick, (even, odd), refs[12:]
     )
     half = even.shape[1]
     row_weight = weight[:, 0:1]
-    result[:, half:] = (even[...] - odd[...]) * row_weight
-    total = (even[...] + odd[...]) * row_weight
     mirror = (iota((half, half), 0) + iota((half, half), 1) == half - 1).astype(jnp.bfloat16)
-    pieces = [dot(piece, mirror) for piece in split_bf16(total, 3)]
-    result[:, :half] = pieces[0] + (pieces[1] + pieces[2])
-    copy = pltpu.make_async_copy(result, out_ref, out_sem)
-    copy.start()
-    copy.wait()
+
+    def mirrored():
+        pieces = [dot(piece, mirror) for piece in split_bf16((even[...] + odd[...]) * row_weight, 3)]
+        return pieces[0] + (pieces[1] + pieces[2])
+
+    if half % LANES:
+        above[:, half:] = (even[...] - odd[...]) * row_weight
+        above[:, :half] = mirrored()
+        copies = [pltpu.make_async_copy(above, out_ref, sems.at[0])]
+        copies[0].start()
+    else:
+        above[...] = (even[...] - odd[...]) * row_weight
+        copies = [pltpu.make_async_copy(above, out_ref.at[:, half:], sems.at[0])]
+        copies[0].start()
+        below[...] = mirrored()
+        copies.append(pltpu.make_async_copy(below, out_ref.at[:, :half], sems.at[1]))
+        copies[1].start()
+    for copy in copies:
+        copy.wait()
 
 
 def moved(me, move, size):
@@ -287,6 +316,29 @@
         for band in range(shards)
     ]
     return lax.ppermute(block, ("grp", "freq"), route)
+
+
+def exchange(column):
+    groups = lax.axis_size("grp")
+    rows = column.shape[0]
+    if groups != 4:
+        near = [column] + [fetched(column, move, 0) for move in range(1, groups)]
+        far = [fetched(column, move, 1) for move in range(groups)]
+        return near, far, [(move, 0, move) for move in range(groups)]
+    across = fetched(column, 2, 0)
+    beside = fetched(column, 0, 1)
+    across, beside = lax.optimization_barrier((across, beside))
+    near = jnp.concatenate([column, across], axis=0)
+    near = [near, fetched(near, 1, 0)]
+    far = [beside, fetched(beside, 2, 0)]
+    return near, far, [(0, 0, 0), (0, rows, 2), (1, 0, 1), (1, rows, 3)]
+
+
+def across_cores(far):
+    if lax.axis_size("grp") != 4:
+        return far
+    far = jnp.concatenate(far, axis=0)
+    return [far, fetched(far, 1, 0)]
 
 
 def per_device(spectra, station_mask, owners):
@@ -305,26 +357,26 @@
 
     scalar = pl.BlockSpec(memory_space=pltpu.SMEM)
     vector = pl.BlockSpec(memory_space=pltpu.VMEM)
-
-    def call(kernel, name, scalars, arrays, out_shape, scratch, cost):
+    anywhere = pl.BlockSpec(memory_space=pl.ANY)
+
+    def call(kernel, name, scalars, arrays, out_shape, scratch, cost, others=()):
         arrays = [pltpu.with_memory_space_constraint(array, pltpu.VMEM) for array in arrays]
         in_hbm = isinstance(out_shape, jax.ShapeDtypeStruct)
         return pl.pallas_call(
             kernel,
             out_shape=out_shape,
-            in_specs=[scalar] * len(scalars) + [vector] * len(arrays),
-            out_specs=pl.BlockSpec(memory_space=pl.ANY) if in_hbm else [vector] * len(out_shape),
+            in_specs=[scalar] * len(scalars) + [anywhere] * len(others) + [vector] * len(arrays),
+            out_specs=anywhere if in_hbm else [vector] * len(out_shape),
             scratch_shapes=scratch,
             compiler_params=pltpu.CompilerParams(vmem_limit_bytes=24 * 1024 * 1024),
             cost_estimate=cost,
             name=name,
-        )(*scalars, *arrays)
+        )(*scalars, *others, *arrays)
 
     tiles = spectra.reshape(2 * chunks * stations, LANES)
-    moves = range(2, shards, 2)
-    column = [tiles] + [fetched(tiles, 0, move) for move in moves]
+    column = [tiles] + [fetched(tiles, 0, move) for move in range(2, shards, 2)]
     me = jnp.stack([lax.axis_index("grp"), lax.axis_index("freq")]).astype(jnp.int32)
-    table = pltpu.VMEM((bin_total, half_band), jnp.bfloat16)
+    table = pltpu.VMEM((bin_total, lag_band), jnp.bfloat16)
     turn = pltpu.VMEM((shards, chunks, LANES), jnp.float32)
     base = pltpu.VMEM((64, half_band), jnp.float32)
     far_base = pltpu.VMEM((bin_total // (64 * SUBLANES), 1, half_band), jnp.float32)
@@ -332,47 +384,73 @@
         table_kernel,
         "tables",
         [me],
+        [],
+        [table] * 2 + [turn] * 2 + [pltpu.VMEM((SUBLANES, LANES), jnp.float32)],
+        [base] * 2
+        + [far_base] * 2
+        + [
+            pltpu.VMEM((1, rounds, 1, pairs), jnp.int32),
+            pltpu.VMEM((1, stations), jnp.int32),
+            pltpu.SemaphoreType.DMA((2,)),
+        ],
+        pl.CostEstimate(flops=0, bytes_accessed=8 * bin_total * half_band, transcendentals=0),
         [owners.transpose(0, 1, 3, 2), station_mask.reshape(1, stations)],
-        [table] * 4 + [turn] * 2 + [pltpu.VMEM((SUBLANES, LANES), jnp.float32)],
-        [base] * 2 + [far_base] * 2,
-        pl.CostEstimate(flops=0, bytes_accessed=8 * bin_total * half_band, transcendentals=0),
     )
     column = jnp.concatenate(column + [extras], axis=0)
-    near = [column] + [fetched(column, move, 0) for move in range(1, groups)]
-    far = [fetched(column, move, 1) for move in range(groups)]
+    near, far, layout = exchange(column)
 
     near_bands = me[1] ^ jnp.arange(0, shards, 2, dtype=jnp.int32)
     far_bands = near_bands ^ 1
-    sizes = (groups, stations, rounds, slots, band_bins, shards // 2)
+    sizes = (groups, stations, rounds, slots, band_bins)
+    depth = column.shape[0] - SUBLANES
     spectrum = pltpu.VMEM((groups * stations, SUBLANES, LANES), jnp.float32)
     turn_tile = pltpu.VMEM((SUBLANES, LANES), jnp.float32)
     cross = pltpu.VMEM((rows * SUBLANES, LANES), jnp.float32)
-    scratch = ([spectrum] * 4 + [turn_tile] * 2 + [cross] * 2) * 2
-    flops = 6 * rows * bin_total * lag_band // 2
-    cost = pl.CostEstimate(flops=flops, bytes_accessed=8 * 1024 * 1024, transcendentals=0)
+    one_set = [spectrum] * 4 + [turn_tile] * 2 + [cross] * 2
+    tile_count = shards // 2 * chunks // SUBLANES
+
+    def cost(tiles):
+        flops = 6 * rows * bin_total * lag_band * tiles // (2 * tile_count)
+        return pl.CostEstimate(flops=flops, bytes_accessed=4 * 1024 * 1024, transcendentals=0)
+
     total = pltpu.VMEM((rows, half_band), jnp.float32)
+    half_result = total if half_band % LANES == 0 else pltpu.VMEM((rows, lag_band), jnp.float32)
     pick_in_smem = [pltpu.SMEM((SUBLANES, rows), jnp.int32), pltpu.SemaphoreType.DMA]
-    held = call(
-        functools.partial(near_kernel, sizes, range(groups)),
-        "near_bands",
+    shared = [turn_cos, turn_sin, *tables]
+    pick, weight, even, odd = call(
+        functools.partial(near_kernel, sizes, layout, len(near), depth),
+        "near_first",
         [near_bands, me],
-        [turn_cos, turn_sin, *tables, *near],
+        [*shared, *near],
         [pltpu.VMEM((SUBLANES, rows), jnp.int32), pltpu.VMEM((rows, LANES), jnp.float32)]
         + [total] * 2,
-        pick_in_smem + scratch,
-        cost,
+        pick_in_smem + one_set,
+        cost(1),
+    )
+    *far, even = lax.optimization_barrier((*far, even))
+    far = across_cores(far)
+    later = list(range(1, tile_count))
+    even, odd = call(
+        functools.partial(next_kernel, sizes, layout, len(near), later),
+        "near_next",
+        [near_bands, me],
+        [*shared, *near, pick, even, odd],
+        [total] * 2,
+        pick_in_smem + one_set * len(later),
+        cost(len(later)),
     )
     out = call(
-        functools.partial(far_kernel, sizes, range(groups)),
+        functools.partial(last_kernel, sizes, layout, len(far), list(range(tile_count))),
         "far_bands",
         [far_bands, me],
-        [turn_cos, turn_sin, *tables, *far, *held],
+        [*shared, *far, pick, even, odd, weight],
         jax.ShapeDtypeStruct((rows, lag_band), jnp.float32),
         pick_in_smem
         + [total] * 2
-        + [pltpu.VMEM((rows, lag_band), jnp.float32), pltpu.SemaphoreType.DMA]
-        + scratch,
-        cost,
+        + [half_result] * 2
+        + [pltpu.SemaphoreType.DMA((2,))]
+        + one_set * tile_count,
+        cost(tile_count),
     )
     out = out.reshape(1, rounds, groups, slots, lag_band)
     return out[:, :, :, :capacity]

time: 35.3 us -> 34.2 us (0.969)
  starting transfers between devices: 13 us -> 10.7 us
  Pallas kernels: 15.1 us -> 16.5 us
    ppermute x10 -> x8, starting transfers between devices: 13 us -> 10.7 us  [fetched(): return lax.ppermute(block, ('grp', 'freq'), route)]
    pallas_call x3 -> x4, Pallas kernels: 15.1 us -> 16.5 us  [call(): pl.pallas_call(kernel, out_shape=out_shape, in_specs=[scalar] * len(scala...]
    ppermute x10 -> x8, waiting for transfers between devices: 4.75 us -> 4.46 us  [fetched(): return lax.ppermute(block, ('grp', 'freq'), route)]
    unnamed x8 -> x10, local copies, waits for them, and re-layouts: 1.35 us -> 1.38 us
  transfers between devices with their start and end apart: 10 -> 8, of which waited for: 4 -> 3; matrix products, arithmetic and copies ran while one was open for 0% -> 0% of each run, Pallas kernels for 23% -> 28%
where the time goes in v6:
time: 34.2 us; the launch traced here: 34 us
  Pallas kernels  16.5 us (48%)
  starting transfers between devices  10.7 us (31%)
  waiting for transfers between devices  4.46 us (13%)
  local copies, waits for them, and re-layouts  2.18 us (6%)
    pallas_call x4, Pallas kernels, call(): pl.pallas_call(kernel, out_shape=out_shape, in_specs=[scalar] * len(scala...  16.5 us
    ppermute x8, starting transfers between devices, fetched(): return lax.ppermute(block, ('grp', 'freq'), route)  10.7 us
    ppermute x8, waiting for transfers between devices, fetched(): return lax.ppermute(block, ('grp', 'freq'), route)  4.46 us
    unnamed x10, local copies, waits for them, and re-layouts  1.38 us
    reshape x1, local copies, waits for them, and re-layouts, per_device(): tiles = spectra.reshape(2 * chunks * stations, LANES)  0.78 us
  transfers between devices with their start and end apart: 8, of which 3 were waited for; matrix products, arithmetic and copies ran while one was open for 0% of the time, Pallas kernels for 28%

profile of v6, /device:TPU:0, one launch (start us, length us, event | category | flops | bytes accessed | tf_op | source)
XLA Modules:
  0.0 34.0 jit_solution(63031781069514205)
XLA Ops:
  0.0 0.8 %reshape.10 = f32[64,128]{1,0:T(8,128)S(1)} reshape(f32[8,2,512]{2,1,0:T(2,128)} %param.3) | data formatting | bytes 65536 | tf_op jit(solution)/shard_map/reshape | solution.py:376
  0.8 5.1 %collective-permute-start.2 = (f32[64,128]{1,0:T(8,128)S(1)}, f32[64,128]{1,0:T(8,128)S(1)}, u32[]{:S(2)}, u32[]{:S(2)}) collective-permute-start(f32[64,128]{1,0:T(8,128)S(1)} %reshape.10), channel_id=1, source_target_pairs={{6,0},{7,1},{4,2},{5,3},{2,4},{3,5},{0,6},{1,7},{14,8},{15,9},{12,... | collective-permute-start | bytes 98312 | tf_op jit(solution)/shard_map/ppermute | solution.py:318
  5.9 0.0 collective-permute-start.1
  5.9 0.6 %collective-permute-start = (f32[64,128]{1,0:T(8,128)S(1)}, f32[64,128]{1,0:T(8,128)S(1)}, u32[]{:S(2)}, u32[]{:S(2)}) collective-permute-start(f32[64,128]{1,0:T(8,128)S(1)} %reshape.10), channel_id=1, source_target_pairs={{2,0},{3,1},{0,2},{1,3},{6,4},{7,5},{4,6},{5,7},{10,8},{11,9},{8,1... | collective-permute-start | bytes 98312 | tf_op jit(solution)/shard_map/ppermute | solution.py:318
  6.6 0.1 pad_add_fusion.me_ref
  6.6 0.0 copy-start
  6.6 0.7 %copy-done = s32[1,2,64,1]{2,3,1,0:T(1,128)S(1)} copy-done((s32[1,2,64,1]{2,3,1,0:T(1,128)S(1)}, s32[1,2,64,1]{2,3,1,0:T(1,128)}, u32[]{:S(2)}) %copy-start) | copy-done | bytes 536
  7.3 0.0 copy-start.1
  7.3 0.7 %copy-done.1 = s32[8]{0:T(128)S(1)} copy-done((s32[8]{0:T(128)S(1)}, s32[8]{0:T(128)}, u32[]{:S(2)}) %copy-start.1) | copy-done | bytes 56
  8.0 3.2 %tables.1 = (bf16[4096,512]{1,0:T(8,128)(2,1)S(1)}, bf16[4096,512]{1,0:T(8,128)(2,1)S(1)}, f32[8,4,128]{2,1,0:T(4,128)S(1)}, f32[8,4,128]{2,1,0:T(4,128)S(1)}, f32[8,128]{1,0:T(8,128)S(1)}) custom-call(s32[2]{0:T(128)S(1)} %pad_add_fusion.me_ref, s32[1,2,1,64]{3,2,1,0:T(1,128)S(1)} %bitcast.7, s32[1,8]{1,0:T(1,128)S(1)} %bitcast.8), custom_call_target="tpu_custom_call" | custom-call | bytes 8388608 | tf_op jit(solution)/shard_map/tables/pallas_call | solution.py:365
  11.2 0.0 collective-permute-done
  11.2 0.0 collective-permute-done.1
  11.2 0.0 collective-permute-done.2
  11.3 1.7 %collective-permute-start.4 = (f32[264,128]{1,0:T(8,128)S(1)}, f32[264,128]{1,0:T(8,128)S(1)}, u32[]{:S(2)}, u32[]{:S(2)}) collective-permute-start(f32[264,128]{1,0:T(8,128)S(1)} %get-tuple-element.46), channel_id=1, source_target_pairs={{1,0},{0,1},{3,2},{2,3},{5,4},{4,5},{7,6},{6,7},{9,8},{8,9},{11,10... | collective-permute-start | bytes 405512 | tf_op jit(solution)/shard_map/ppermute | solution.py:318
  13.0 1.5 %collective-permute-start.3 = (f32[264,128]{1,0:T(8,128)S(1)}, f32[264,128]{1,0:T(8,128)S(1)}, u32[]{:S(2)}, u32[]{:S(2)}) collective-permute-start(f32[264,128]{1,0:T(8,128)S(1)} %get-tuple-element.46), channel_id=1, source_target_pairs={{16,0},{17,1},{18,2},{19,3},{20,4},{21,5},{22,6},{23,7},{24,8},{25... | collective-permute-start | bytes 405512 | tf_op jit(solution)/shard_map/ppermute | solution.py:318
  14.5 1.9 %collective-permute-done.4 = f32[264,128]{1,0:T(8,128)S(1)} collective-permute-done((f32[264,128]{1,0:T(8,128)S(1)}, f32[264,128]{1,0:T(8,128)S(1)}, u32[]{:S(2)}, u32[]{:S(2)}) %collective-permute-start.4) | collective-permute-done | bytes 135200 | tf_op jit(solution)/shard_map/ppermute | solution.py:318
  16.4 1.7 %collective-permute-done.3 = f32[264,128]{1,0:T(8,128)S(1)} collective-permute-done((f32[264,128]{1,0:T(8,128)S(1)}, f32[264,128]{1,0:T(8,128)S(1)}, u32[]{:S(2)}, u32[]{:S(2)}) %collective-permute-start.3) | collective-permute-done | bytes 135200 | tf_op jit(solution)/shard_map/ppermute | solution.py:318
  18.0 0.1 collective-permute-start.6
  18.1 1.6 %collective-permute-start.5 = (f32[264,128]{1,0:T(8,128)S(1)}, f32[264,128]{1,0:T(8,128)S(1)}, u32[]{:S(2)}, u32[]{:S(2)}) collective-permute-start(f32[264,128]{1,0:T(8,128)S(1)} %collective-permute-done.4), channel_id=1, source_target_pairs={{16,0},{17,1},{18,2},{19,3},{20,4},{21,5},{22,6},{23,7},{24,8},{25... | collective-permute-start | bytes 405512 | tf_op jit(solution)/shard_map/ppermute | solution.py:318
  19.7 0.0 collective-permute-done.6.refs_5_
  19.7 3.5 %near_first.1 = (s32[8,256]{1,0:T(8,128)S(1)}, f32[256,128]{1,0:T(8,128)S(1)}, f32[256,256]{1,0:T(8,128)S(1)}, f32[256,256]{1,0:T(8,128)S(1)}) custom-call(s32[4]{0:T(128)S(1)} %multiply_xor_fusion.bands_ref, s32[2]{0:T(128)S(1)} %pad_add_fusion.me_ref, f32[8,4,128]{2,1,0:T(4,128)S(1)} %get-tuple-element.21.refs_0_, ...), custom_call_target="tpu_custom_call" | custom-call | flops 805306368 | bytes 4194304 | tf_op jit(solution)/shard_map/near_first/pallas_call | solution.py:365
  23.2 0.9 %collective-permute-done.5 = f32[264,128]{1,0:T(8,128)S(1)} collective-permute-done((f32[264,128]{1,0:T(8,128)S(1)}, f32[264,128]{1,0:T(8,128)S(1)}, u32[]{:S(2)}, u32[]{:S(2)}) %collective-permute-start.5) | collective-permute-done | bytes 135200 | tf_op jit(solution)/shard_map/ppermute | solution.py:318
  24.1 0.1 collective-permute-start.7
  24.2 3.0 %near_next.1 = (f32[256,256]{1,0:T(8,128)S(1)}, f32[256,256]{1,0:T(8,128)S(1)}) custom-call(s32[4]{0:T(128)S(1)} %multiply_xor_fusion.bands_ref, s32[2]{0:T(128)S(1)} %pad_add_fusion.me_ref, f32[8,4,128]{2,1,0:T(4,128)S(1)} %get-tuple-element.21.refs_0_, f32[8,4,128]{2,1,0:T(4,128)S(1)} %get-tuple-element.22.refs_1_, ...), custom_call_target="tpu_custom_call" | custom-call | flops 805306368 | bytes 4194304 | tf_op jit(solution)/shard_map/near_next/pallas_call | solution.py:365
  27.2 0.0 collective-permute-done.7.refs_5_
  27.2 6.8 %far_bands.1 = f32[256,512]{1,0:T(8,128)} custom-call(s32[4]{0:T(128)S(1)} %broadcast_xor_fusion.bands_ref, s32[2]{0:T(128)S(1)} %pad_add_fusion.me_ref, f32[8,4,128]{2,1,0:T(4,128)S(1)} %get-tuple-element.21.refs_0_, f32[8,4,128]{2,1,0:T(4,128)S(1)} %get-tuple-element.22.refs_1_, bf16[4096,512]{1,0:T(8,128)(2,1)S(1)} %get-tuple-element.23.refs_2_, ...), custom_call_target="tpu_custom_call" | custom-call | flops 1610612736 | bytes 4194304 | tf_op jit(solution)/shard_map/far_bands/pallas_call | solution.py:365
  (10 shorter events, 0.1 us)
Async XLA Ops:
  0.8 10.5 %collective-permute-start.2 = (f32[64,128]{1,0:T(8,128)S(1)}, f32[64,128]{1,0:T(8,128)S(1)}, u32[]{:S(2)}, u32[]{:S(2)}) collective-permute-start(f32[64,128]{1,0:T(8,128)S(1)} %reshape.10), channel_id=1, source_target_pairs={{6,0},{7,1},{4,2},{5,3},{2,4},{3,5},{0,6},{1,7},{14,8},{15,9},{12,... | collective-permute-start | bytes 98312 | tf_op jit(solution)/shard_map/ppermute | solution.py:318
  5.9 5.3 %collective-permute-start.1 = (f32[64,128]{1,0:T(8,128)S(1)}, f32[64,128]{1,0:T(8,128)S(1)}, u32[]{:S(2)}, u32[]{:S(2)}) collective-permute-start(f32[64,128]{1,0:T(8,128)S(1)} %reshape.10), channel_id=1, source_target_pairs={{4,0},{5,1},{6,2},{7,3},{0,4},{1,5},{2,6},{3,7},{12,8},{13,9},{14,... | collective-permute-start | bytes 98312 | tf_op jit(solution)/shard_map/ppermute | solution.py:318
  5.9 5.3 %collective-permute-start = (f32[64,128]{1,0:T(8,128)S(1)}, f32[64,128]{1,0:T(8,128)S(1)}, u32[]{:S(2)}, u32[]{:S(2)}) collective-permute-start(f32[64,128]{1,0:T(8,128)S(1)} %reshape.10), channel_id=1, source_target_pairs={{2,0},{3,1},{0,2},{1,3},{6,4},{7,5},{4,6},{5,7},{10,8},{11,9},{8,1... | collective-permute-start | bytes 98312 | tf_op jit(solution)/shard_map/ppermute | solution.py:318
  6.6 0.7 %copy-start = (s32[1,2,64,1]{2,3,1,0:T(1,128)S(1)}, s32[1,2,64,1]{2,3,1,0:T(1,128)}, u32[]{:S(2)}) copy-start(s32[1,2,64,1]{2,3,1,0:T(1,128)} %param.5) | copy-start | bytes 1540
  7.3 0.7 %copy-start.1 = (s32[8]{0:T(128)S(1)}, s32[8]{0:T(128)}, u32[]{:S(2)}) copy-start(s32[8]{0:T(128)} %param.4) | copy-start | bytes 100
  11.3 5.1 %collective-permute-start.4 = (f32[264,128]{1,0:T(8,128)S(1)}, f32[264,128]{1,0:T(8,128)S(1)}, u32[]{:S(2)}, u32[]{:S(2)}) collective-permute-start(f32[264,128]{1,0:T(8,128)S(1)} %get-tuple-element.46), channel_id=1, source_target_pairs={{1,0},{0,1},{3,2},{2,3},{5,4},{4,5},{7,6},{6,7},{9,8},{8,9},{11,10... | collective-permute-start | bytes 405512 | tf_op jit(solution)/shard_map/ppermute | solution.py:318
  13.0 5.0 %collective-permute-start.3 = (f32[264,128]{1,0:T(8,128)S(1)}, f32[264,128]{1,0:T(8,128)S(1)}, u32[]{:S(2)}, u32[]{:S(2)}) collective-permute-start(f32[264,128]{1,0:T(8,128)S(1)} %get-tuple-element.46), channel_id=1, source_target_pairs={{16,0},{17,1},{18,2},{19,3},{20,4},{21,5},{22,6},{23,7},{24,8},{25... | collective-permute-start | bytes 405512 | tf_op jit(solution)/shard_map/ppermute | solution.py:318
  18.0 1.6 %collective-permute-start.6 = (f32[528,128]{1,0:T(8,128)S(1)}, f32[528,128]{1,0:T(8,128)S(1)}, u32[]{:S(2)}, u32[]{:S(2)}) collective-permute-start(f32[528,128]{1,0:T(8,128)S(1)} %constant_dynamic-update-slice_fusion.5.refs_4_), channel_id=1, source_target_pairs={{8,0},{9,1},{10,2},{11,3},{12,4},{13,5},{14,6},{15,7},{0,8},{1,9},... | collective-permute-start | bytes 811016 | tf_op jit(solution)/shard_map/ppermute | solution.py:318
  18.1 6.0 %collective-permute-start.5 = (f32[264,128]{1,0:T(8,128)S(1)}, f32[264,128]{1,0:T(8,128)S(1)}, u32[]{:S(2)}, u32[]{:S(2)}) collective-permute-start(f32[264,128]{1,0:T(8,128)S(1)} %collective-permute-done.4), channel_id=1, source_target_pairs={{16,0},{17,1},{18,2},{19,3},{20,4},{21,5},{22,6},{23,7},{24,8},{25... | collective-permute-start | bytes 405512 | tf_op jit(solution)/shard_map/ppermute | solution.py:318
  24.1 3.1 %collective-permute-start.7 = (f32[528,128]{1,0:T(8,128)S(1)}, f32[528,128]{1,0:T(8,128)S(1)}, u32[]{:S(2)}, u32[]{:S(2)}) collective-permute-start(f32[528,128]{1,0:T(8,128)S(1)} %constant_dynamic-update-slice_fusion.11.refs_4_), channel_id=1, source_target_pairs={{8,0},{9,1},{10,2},{11,3},{12,4},{13,5},{14,6},{15,7},{0,8},{1,9},... | collective-permute-start | bytes 811016 | tf_op jit(solution)/shard_map/ppermute | solution.py:318

commit v7 on v6

v7 whole, which is shorter than its diff:
```python
import functools
import math

import jax
import jax.numpy as jnp
from jax import lax
from jax.experimental import pallas as pl
from jax.experimental.pallas import tpu as pltpu
from jax.sharding import PartitionSpec as P

LAGS = 4096
LANES = 128
SUBLANES = 8


def split_bf16(values, parts):
    pieces = []
    for _ in range(parts - 1):
        piece = values.astype(jnp.bfloat16)
        pieces.append(piece)
        values = values - piece.astype(jnp.float32)
    pieces.append(values.astype(jnp.bfloat16))
    return pieces


def iota(shape, axis):
    return lax.broadcasted_iota(jnp.int32, shape, axis)


def dot(left, right):
    return jnp.dot(left, right, preferred_element_type=jnp.float32)


def padded(count, multiple):
    return -(-count // multiple) * multiple


def pick_slots(extras, places, me, stations, rounds, slots):
    groups = len(extras)
    pairs = stations * stations
    listed = rounds * pairs
    rows = rounds * groups * slots
    place = iota((groups, groups), 1)
    held_by = jnp.zeros((groups, groups), jnp.int32)
    for position in range(groups):
        held_by = jnp.where(place == position, places[position], held_by)
    lane = iota((1, listed), 1)

    def by_group(row, shift):
        wanted = (iota((groups, groups), 0) + groups - shift) % groups
        held = jnp.concatenate([extra[row : row + 1, :] for extra in extras], axis=0)
        return dot((held_by == wanted).astype(jnp.bfloat16), held.astype(jnp.bfloat16))

    def of_station(values, number):
        spread = iota((LANES, listed), 0) == number
        return dot(values.astype(jnp.bfloat16), spread.astype(jnp.bfloat16))

    owner_ids = jnp.zeros((groups, listed), jnp.float32)
    partner_mask = jnp.zeros((groups, listed), jnp.float32)
    for index in range(rounds):
        of_round = lane // pairs == index
        owner_ids = jnp.where(of_round, by_group(index, 0), owner_ids)
        second = of_station(by_group(rounds, index + 1), lane % stations)
        partner_mask = jnp.where(of_round, second, partner_mask)
    own_mask = of_station(by_group(rounds, 0), lane % pairs // stations)
    pair_weight = own_mask * partner_mask
    mine = owner_ids == me.astype(jnp.float32)
    from_pair, to_pair = iota((listed, listed), 0), iota((listed, listed), 1)
    before = (from_pair < to_pair) & (from_pair // pairs == to_pair // pairs)
    rank = dot(mine.astype(jnp.bfloat16), before.astype(jnp.bfloat16))
    marked = jnp.where(mine, rank, -1.0).astype(jnp.bfloat16)
    of_group = (iota((rows, groups), 0) // slots) % groups == iota((rows, groups), 1)
    of_group = of_group.astype(jnp.bfloat16)
    row_id, lane_id = iota((rows, listed), 0), iota((rows, listed), 1)
    chosen = (dot(of_group, marked) == (row_id % slots).astype(jnp.float32)) & (
        row_id // (groups * slots) == lane_id // pairs
    )
    weighed = jnp.where(chosen, dot(of_group, pair_weight.astype(jnp.bfloat16)), 0.0)
    weight = dot(weighed.astype(jnp.bfloat16), jnp.ones((listed, LANES), jnp.bfloat16))
    chosen = chosen.astype(jnp.bfloat16)
    pair_id = iota((listed, LANES), 0) % pairs
    first = dot(chosen, (pair_id // stations).astype(jnp.bfloat16))
    second = dot(chosen, (pair_id % stations).astype(jnp.bfloat16))
    return first.astype(jnp.int32), second.astype(jnp.int32), weight


def make_tables(bands_ref, place, table_refs, turn_refs, base_refs, bin_total):
    near_cos, near_sin = base_refs
    fine, half_band = near_cos.shape
    steps, chunks, _ = turn_refs[0].shape
    band_bins = chunks * LANES

    def circle(turns):
        angles = (turns & (4 * bin_total - 1)).astype(jnp.float32) * (math.pi / (2 * bin_total))
        return jnp.cos(angles), jnp.sin(angles)

    def every(count, start, step):
        bins = start + iota((count, half_band), 0) * step
        return circle(bins * (2 * iota((count, half_band), 1) + 1))

    def added(cos, sin, other_cos, other_sin):
        return cos * other_cos - sin * other_sin, sin * other_cos + cos * other_sin

    low_cos, low_sin = every(SUBLANES, 0, 1)
    high_cos, high_sin = every(fine // SUBLANES, 0, SUBLANES)
    for index in range(fine // SUBLANES):
        rows, one = slice(index * SUBLANES, (index + 1) * SUBLANES), slice(index, index + 1)
        near_cos[rows, :], near_sin[rows, :] = added(
            high_cos[one], high_sin[one], low_cos, low_sin
        )

    centre = 2 * half_band * (2 * place + 1) - 1 - LAGS
    norm = 1.0 / math.sqrt(bin_total)
    for step in range(steps):
        start = bands_ref[step] * band_bins
        cos, sin = every(band_bins // fine, start, fine)
        for part in range(band_bins // fine):
            one = slice(part, part + 1)
            values = added(cos[one], sin[one], near_cos[...], near_sin[...])
            rows = slice(step * band_bins + part * fine, step * band_bins + (part + 1) * fine)
            for table, value in zip(table_refs, values):
                table[rows, :half_band], table[rows, half_band:] = split_bf16(value, 2)
        bins = start + iota((chunks, LANES), 0) * LANES + iota((chunks, LANES), 1)
        for turn, value in zip(turn_refs, circle(bins * centre)):
            turn[step] = value * norm


def near_tables(bin_total, bands_ref, me_ref, owners_hbm, mask_hbm, *refs):
    table_refs, turn_refs, extras = refs[:2], refs[2:4], refs[4]
    base_refs, (owners_ref, mask_ref, sems) = refs[5:7], refs[7:]
    copies = [
        pltpu.make_async_copy(owners_hbm, owners_ref, sems.at[0]),
        pltpu.make_async_copy(mask_hbm, mask_ref, sems.at[1]),
    ]
    for copy in copies:
        copy.start()
    make_tables(bands_ref, me_ref[1], table_refs, turn_refs, base_refs, bin_total)
    for copy in copies:
        copy.wait()
    extras[...] = jnp.zeros_like(extras)
    rounds, pairs = owners_ref.shape[1], owners_ref.shape[3]
    for index in range(rounds):
        lanes = slice(index * pairs, (index + 1) * pairs)
        extras[index : index + 1, lanes] = owners_ref[0, index].astype(jnp.float32)
    extras[rounds : rounds + 1, : mask_ref.shape[1]] = mask_ref[...].astype(jnp.float32)


def far_tables(bin_total, bands_ref, me_ref, *refs):
    make_tables(bands_ref, me_ref[1], refs[:2], refs[2:4], refs[4:], bin_total)


def add_bands(sizes, steps, places, turn_refs, table_refs, blocks, picks, sums, scratch):
    groups, stations, rounds, slots, band_bins = sizes
    chunks = band_bins // LANES
    depth = 2 * chunks * stations
    half = sums[0].shape[1]
    first, second = picks
    sets = [scratch[6 * index : 6 * (index + 1)] for index in range(2)]
    octets = [
        (group, (group + groups - 1 - index) % groups)
        for index in range(rounds)
        for group in range(groups)
        for _ in range(slots // SUBLANES)
    ]
    units = len(octets) // 2

    def prepare(index):
        step, (held, turned) = steps[index], sets[index % 2][:2]
        for position, (ref, offset) in enumerate(blocks):
            group = places[position]
            for q in range(chunks):
                turn_cos, turn_sin = [turn[step, q : q + 1, :] for turn in turn_refs]
                start = offset + step * depth + q * stations
                real = ref[start : start + stations, :]
                start += chunks * stations
                imag = ref[start : start + stations, :]
                held[group, q] = real
                held[group, chunks + q] = imag
                turned[group, q] = real * turn_cos + imag * turn_sin
                turned[group, chunks + q] = imag * turn_cos - real * turn_sin

    def multiply(index, part, parts):
        held, turned, *cross = sets[index % 2]
        for unit in range(part * units // parts, (part + 1) * units // parts):
            rows = slice(2 * unit * SUBLANES, 2 * (unit + 1) * SUBLANES)
            for q in range(chunks):
                lanes = slice(q * LANES, (q + 1) * LANES)
                reals, imags = [], []
                for octet in (2 * unit, 2 * unit + 1):
                    group, partner = octets[octet]
                    lines = slice(octet * SUBLANES, (octet + 1) * SUBLANES)
                    index_a, index_b = first[lines, :], second[lines, :]
                    a_real = jnp.take_along_axis(held[group, q], index_a, axis=0)
                    a_imag = jnp.take_along_axis(held[group, chunks + q], index_a, axis=0)
                    b_real = jnp.take_along_axis(turned[partner, q], index_b, axis=0)
                    b_imag = jnp.take_along_axis(turned[partner, chunks + q], index_b, axis=0)
                    reals.append(a_real * b_real + a_imag * b_imag)
                    imags.append(a_imag * b_real - a_real * b_imag)
                for place, values in ((0, reals), (2, imags)):
                    high, low = split_bf16(jnp.concatenate(values, axis=0), 2)
                    cross[place][rows, lanes] = high
                    cross[place + 1][rows, lanes] = low

    def transform(index, which):
        step, (high, low) = steps[index], sets[index % 2][2 + 2 * which : 4 + 2 * which]
        bins = slice(step * band_bins, (step + 1) * band_bins)
        table, total = table_refs[which], sums[which]
        by_high = dot(high[...], table[bins, :])
        by_low = dot(low[...], table[bins, :half])
        total[...] += by_high[:, :half] + (by_high[:, half:] + by_low)

    prepare(0)
    multiply(0, 0, 1)
    for index in range(len(steps)):
        more = index + 1 < len(steps)
        if more:
            prepare(index + 1)
        for which in range(2):
            if more:
                multiply(index + 1, which, 2)
            transform(index, which)


def placed_blocks(array_refs, layout, me, groups):
    blocks = [(array_refs[index], offset) for index, offset, _ in layout]
    return blocks, [moved(me, move, groups) for _, _, move in layout]


def near_kernel(sizes, layout, array_count, depth, steps, me_ref, *refs):
    groups, stations, rounds, slots = sizes[:4]
    turn_refs, table_refs, refs = refs[:2], refs[2:4], refs[4:]
    array_refs, refs = refs[:array_count], refs[array_count:]
    (first, second, weight, even, odd), scratch = refs[:5], refs[5:]
    blocks, places = placed_blocks(array_refs, layout, me_ref[0], groups)
    extras = [ref[offset + depth : offset + depth + SUBLANES, :] for ref, offset in blocks]
    first[...], second[...], weight[...] = pick_slots(
        extras, places, me_ref[0], stations, rounds, slots
    )
    even[...] = jnp.zeros_like(even)
    odd[...] = jnp.zeros_like(odd)
    add_bands(
        sizes, steps, places, turn_refs, table_refs, blocks, (first, second), (even, odd), scratch
    )


def next_kernel(sizes, layout, array_count, steps, me_ref, *refs):
    turn_refs, table_refs, refs = refs[:2], refs[2:4], refs[4:]
    array_refs, refs = refs[:array_count], refs[array_count:]
    (first, second, even_in, odd_in, even, odd), scratch = refs[:6], refs[6:]
    even[...] = even_in[...]
    odd[...] = odd_in[...]
    blocks, places = placed_blocks(array_refs, layout, me_ref[0], sizes[0])
    add_bands(
        sizes, steps, places, turn_refs, table_refs, blocks, (first, second), (even, odd), scratch
    )


def last_kernel(sizes, layout, array_count, steps, me_ref, *refs):
    turn_refs, table_refs, refs = refs[:2], refs[2:4], refs[4:]
    array_refs, refs = refs[:array_count], refs[array_count:]
    first, second, even_in, odd_in, weight, out_ref, even, odd, above, below, sems = refs[:11]
    even[...] = even_in[...]
    odd[...] = odd_in[...]
    blocks, places = placed_blocks(array_refs, layout, me_ref[0], sizes[0])
    add_bands(
        sizes, steps, places, turn_refs, table_refs, blocks, (first, second), (even, odd), refs[11:]
    )
    half = even.shape[1]
    row_weight = weight[:, 0:1]
    mirror = (iota((half, half), 0) + iota((half, half), 1) == half - 1).astype(jnp.bfloat16)

    def mirrored():
        pieces = [dot(piece, mirror) for piece in split_bf16((even[...] + odd[...]) * row_weight, 3)]
        return pieces[0] + (pieces[1] + pieces[2])

    if half % LANES:
        above[:, half:] = (even[...] - odd[...]) * row_weight
        above[:, :half] = mirrored()
        copies = [pltpu.make_async_copy(above, out_ref, sems.at[0])]
        copies[0].start()
    else:
        above[...] = (even[...] - odd[...]) * row_weight
        copies = [pltpu.make_async_copy(above, out_ref.at[:, half:], sems.at[0])]
        copies[0].start()
        below[...] = mirrored()
        copies.append(pltpu.make_async_copy(below, out_ref.at[:, :half], sems.at[1]))
        copies[1].start()
    for copy in copies:
        copy.wait()


def moved(me, move, size):
    return me ^ move if size & (size - 1) == 0 else lax.rem(me + size - move, size)


def moved_index(me, move, size):
    return me ^ move if size & (size - 1) == 0 else (me - move) % size


def fetched(block, group_move, band_move):
    groups, shards = lax.axis_size("grp"), lax.axis_size("freq")
    route = [
        (
            moved_index(group, group_move, groups) * shards + moved_index(band, band_move, shards),
            group * shards + band,
        )
        for group in range(groups)
        for band in range(shards)
    ]
    return lax.ppermute(block, ("grp", "freq"), route)


def exchange(column, ready):
    groups = lax.axis_size("grp")
    rows = column.shape[0]
    if groups != 4:
        near = [column] + [fetched(column, move, 0) for move in range(1, groups)]
        far = [fetched(column, move, 1) for move in range(groups)]
        return near, far, [(move, 0, move) for move in range(groups)], ready
    across = fetched(column, 2, 0)
    beside = fetched(column, 0, 1)
    across, beside, *ready = lax.optimization_barrier((across, beside, *ready))
    near = jnp.concatenate([column, across], axis=0)
    near = [near, fetched(near, 1, 0)]
    far = [beside, fetched(beside, 2, 0)]
    return near, far, [(0, 0, 0), (0, rows, 2), (1, 0, 1), (1, rows, 3)], ready


def across_cores(far):
    if lax.axis_size("grp") != 4:
        return far
    far = jnp.concatenate(far, axis=0)
    return [far, fetched(far, 1, 0)]


def per_device(spectra, station_mask, owners):
    stations, _, band_bins = spectra.shape
    groups = lax.axis_size("grp")
    shards = lax.axis_size("freq")
    rounds = owners.shape[1]
    pairs = stations * stations
    bin_total = band_bins * shards
    capacity = (2 * pairs + groups - 1) // groups
    slots = padded(capacity, SUBLANES)
    lag_band = LAGS // shards
    half_band = lag_band // 2
    chunks = band_bins // LANES
    rows = rounds * groups * slots

    scalar = pl.BlockSpec(memory_space=pltpu.SMEM)
    vector = pl.BlockSpec(memory_space=pltpu.VMEM)
    in_hbm = pl.BlockSpec(memory_space=pltpu.HBM)

    def call(kernel, name, scalars, arrays, out_shape, scratch, cost, others=()):
        arrays = [pltpu.with_memory_space_constraint(array, pltpu.VMEM) for array in arrays]
        others = [pltpu.with_memory_space_constraint(array, pltpu.HBM) for array in others]
        to_hbm = isinstance(out_shape, jax.ShapeDtypeStruct)
        return pl.pallas_call(
            kernel,
            out_shape=out_shape,
            in_specs=[scalar] * len(scalars) + [in_hbm] * len(others) + [vector] * len(arrays),
            out_specs=in_hbm if to_hbm else [vector] * len(out_shape),
            scratch_shapes=scratch,
            compiler_params=pltpu.CompilerParams(vmem_limit_bytes=24 * 1024 * 1024),
            cost_estimate=cost,
            name=name,
        )(*scalars, *others, *arrays)

    steps = shards // 2
    me = jnp.stack([lax.axis_index("grp"), lax.axis_index("freq")]).astype(jnp.int32)
    near_bands = me[1] ^ jnp.arange(0, shards, 2, dtype=jnp.int32)
    tiles = spectra.reshape(stations, 2, chunks, LANES).transpose(1, 2, 0, 3)
    tiles = tiles.reshape(2 * chunks * stations, LANES)
    column = [tiles] + [fetched(tiles, 0, move) for move in range(2, shards, 2)]

    table = pltpu.VMEM((steps * band_bins, lag_band), jnp.bfloat16)
    turn = pltpu.VMEM((steps, chunks, LANES), jnp.float32)
    base = pltpu.VMEM((64, half_band), jnp.float32)
    table_cost = pl.CostEstimate(
        flops=0, bytes_accessed=4 * bin_total * half_band, transcendentals=0
    )
    *near_table, extras = call(
        functools.partial(near_tables, bin_total),
        "near_tables",
        [near_bands, me],
        [],
        [table] * 2 + [turn] * 2 + [pltpu.VMEM((SUBLANES, LANES), jnp.float32)],
        [base] * 2
        + [
            pltpu.VMEM((1, rounds, 1, pairs), jnp.int32),
            pltpu.VMEM((1, stations), jnp.int32),
            pltpu.SemaphoreType.DMA((2,)),
        ],
        table_cost,
        [owners.transpose(0, 1, 3, 2), station_mask.reshape(1, stations)],
    )
    column = jnp.concatenate(column + [extras], axis=0)
    column, far_bands = lax.optimization_barrier((column, near_bands ^ 1))
    far_table = call(
        functools.partial(far_tables, bin_total),
        "far_tables",
        [far_bands, me],
        [],
        [table] * 2 + [turn] * 2,
        [base] * 2,
        table_cost,
    )
    near, far, layout, far_table = exchange(column, far_table)

    sizes = (groups, stations, rounds, slots, band_bins)
    depth = column.shape[0] - SUBLANES
    spectrum = pltpu.VMEM((groups, 2 * chunks, stations, LANES), jnp.float32)
    cross = pltpu.VMEM((rows, band_bins), jnp.bfloat16)
    scratch = ([spectrum] * 2 + [cross] * 4) * 2

    def cost(count):
        flops = 6 * rows * band_bins * lag_band * count
        return pl.CostEstimate(flops=flops, bytes_accessed=2 * 1024 * 1024, transcendentals=0)

    total = pltpu.VMEM((rows, half_band), jnp.float32)
    half_result = total if half_band % LANES == 0 else pltpu.VMEM((rows, lag_band), jnp.float32)
    index = pltpu.VMEM((rows, LANES), jnp.int32)
    table_at = [2, 3, 0, 1]
    first, second, weight, even, odd = call(
        functools.partial(near_kernel, sizes, layout, len(near), depth, range(steps // 2)),
        "near_first",
        [me],
        [near_table[place] for place in table_at] + near,
        [index] * 2 + [pltpu.VMEM((rows, LANES), jnp.float32)] + [total] * 2,
        scratch,
        cost(steps // 2),
    )
    *far, even = lax.optimization_barrier((*far, even))
    far = across_cores(far)
    even, odd = call(
        functools.partial(next_kernel, sizes, layout, len(near), range(steps // 2, steps)),
        "near_next",
        [me],
        [near_table[place] for place in table_at] + near + [first, second, even, odd],
        [total] * 2,
        scratch,
        cost(steps - steps // 2),
    )
    out = call(
        functools.partial(last_kernel, sizes, layout, len(far), range(steps)),
        "far_bands",
        [me],
        [far_table[place] for place in table_at] + far + [first, second, even, odd, weight],
        jax.ShapeDtypeStruct((rows, lag_band), jnp.float32),
        [total] * 2 + [half_result] * 2 + [pltpu.SemaphoreType.DMA((2,))] + scratch,
        cost(steps),
    )
    out = out.reshape(1, rounds, groups, slots, lag_band)
    return out[:, :, :, :capacity]


def solution(mesh):
    placed = (P("grp", None, "freq"), P("grp"), P("grp", None, None, None))
    return jax.shard_map(
        per_device,
        mesh=mesh,
        in_specs=placed,
        out_specs=P("grp", None, None, None, "freq"),
        check_vma=False,
    )
```

time: 34.2 us -> 31 us (0.906)
  Pallas kernels: 16.5 us -> 13.6 us
  local copies, waits for them, and re-layouts: 2.18 us -> 0.86 us
  waiting for transfers between devices: 4.46 us -> 5.54 us
    pallas_call x4 -> x5, Pallas kernels: 16.5 us -> 13.6 us  [call(): pl.pallas_call(kernel, out_shape=out_shape, in_specs=[scalar] * len(scala...]
    unnamed x10 -> x6, local copies, waits for them, and re-layouts: 1.38 us -> 0.04 us
    ppermute x8, waiting for transfers between devices: 4.46 us -> 5.54 us  [fetched(): return lax.ppermute(block, ('grp', 'freq'), route)]
    reshape x1 -> x2, local copies, waits for them, and re-layouts: 0.78 us -> 0.8 us  [per_device(): tiles = spectra.reshape(stations, 2, chunks, LANES).transpose(1, 2, 0, 3)]
  transfers between devices with their start and end apart: 8 -> 8, of which waited for: 3 -> 5; matrix products, arithmetic and copies ran while one was open for 0% -> 0% of each run, Pallas kernels for 28% -> 28%
where the time goes in v7:
time: 31 us; the launch traced here: 30.7 us
  Pallas kernels  13.6 us (44%)
  starting transfers between devices  10.5 us (34%)
  waiting for transfers between devices  5.54 us (18%)
  local copies, waits for them, and re-layouts  0.86 us (3%)
    pallas_call x5, Pallas kernels, call(): pl.pallas_call(kernel, out_shape=out_shape, in_specs=[scalar] * len(scala...  13.6 us
    ppermute x8, starting transfers between devices, fetched(): return lax.ppermute(block, ('grp', 'freq'), route)  10.5 us
    ppermute x8, waiting for transfers between devices, fetched(): return lax.ppermute(block, ('grp', 'freq'), route)  5.54 us
    reshape x2, local copies, waits for them, and re-layouts, per_device(): tiles = spectra.reshape(stations, 2, chunks, LANES).transpose(1, 2, 0, 3)  0.8 us
  transfers between devices with their start and end apart: 8, of which 5 were waited for; matrix products, arithmetic and copies ran while one was open for 0% of the time, Pallas kernels for 28%

profile of v7, /device:TPU:0, one launch (start us, length us, event | category | flops | bytes accessed | tf_op | source)
XLA Modules:
  0.0 30.7 jit_solution(16077423109341196317)
XLA Ops:
  0.0 0.8 %reshape.12 = f32[8,2,4,128]{3,2,1,0:T(4,128)S(1)} reshape(f32[8,2,512]{2,1,0:T(2,128)} %param.3) | data formatting | bytes 65536 | tf_op jit(solution)/shard_map/reshape | solution.py:372
  0.8 5.1 %collective-permute-start.2 = (f32[64,128]{1,0:T(8,128)S(1)}, f32[64,128]{1,0:T(8,128)S(1)}, u32[]{:S(2)}, u32[]{:S(2)}) collective-permute-start(f32[64,128]{1,0:T(8,128)S(1)} %bitcast.10), channel_id=1, source_target_pairs={{6,0},{7,1},{4,2},{5,3},{2,4},{3,5},{0,6},{1,7},{14,8},{15,9},{12,... | collective-permute-start | bytes 98312 | tf_op jit(solution)/shard_map/ppermute | solution.py:310
  5.9 0.0 collective-permute-start.1
  5.9 0.6 %collective-permute-start = (f32[64,128]{1,0:T(8,128)S(1)}, f32[64,128]{1,0:T(8,128)S(1)}, u32[]{:S(2)}, u32[]{:S(2)}) collective-permute-start(f32[64,128]{1,0:T(8,128)S(1)} %bitcast.12), channel_id=1, source_target_pairs={{2,0},{3,1},{0,2},{1,3},{6,4},{7,5},{4,6},{5,7},{10,8},{11,9},{8,1... | collective-permute-start | bytes 98312 | tf_op jit(solution)/shard_map/ppermute | solution.py:310
  6.6 0.1 pad_add_fusion.me_ref
  6.7 1.9 %near_tables.1 = (bf16[2048,512]{1,0:T(8,128)(2,1)S(1)}, bf16[2048,512]{1,0:T(8,128)(2,1)S(1)}, f32[4,4,128]{2,1,0:T(4,128)S(1)}, f32[4,4,128]{2,1,0:T(4,128)S(1)}, f32[8,128]{1,0:T(8,128)S(1)}) custom-call(s32[4]{0:T(128)S(1)} %multiply_xor_fusion.bands_ref, s32[2]{0:T(128)S(1)} %pad_add_fusion.me_ref, s32[1,2,1,64]{3,2,1,0:T(1,128)} %bitcast.14, ...), custom_call_target="tpu_custom_call" | custom-call | bytes 4194304 | tf_op jit(solution)/shard_map/near_tables/pallas_call | solution.py:358
  8.5 1.3 %collective-permute-done = f32[64,128]{1,0:T(8,128)S(1)} collective-permute-done((f32[64,128]{1,0:T(8,128)S(1)}, f32[64,128]{1,0:T(8,128)S(1)}, u32[]{:S(2)}, u32[]{:S(2)}) %collective-permute-start) | collective-permute-done | bytes 32800 | tf_op jit(solution)/shard_map/ppermute | solution.py:310
  9.8 0.9 %collective-permute-done.1 = f32[64,128]{1,0:T(8,128)S(1)} collective-permute-done((f32[64,128]{1,0:T(8,128)S(1)}, f32[64,128]{1,0:T(8,128)S(1)}, u32[]{:S(2)}, u32[]{:S(2)}) %collective-permute-start.1) | collective-permute-done | bytes 32800 | tf_op jit(solution)/shard_map/ppermute | solution.py:310
  10.7 0.0 collective-permute-done.2
  10.8 1.6 %collective-permute-start.4 = (f32[264,128]{1,0:T(8,128)S(1)}, f32[264,128]{1,0:T(8,128)S(1)}, u32[]{:S(2)}, u32[]{:S(2)}) collective-permute-start(f32[264,128]{1,0:T(8,128)S(1)} %constant_dynamic-update-slice_fusion), channel_id=1, source_target_pairs={{1,0},{0,1},{3,2},{2,3},{5,4},{4,5},{7,6},{6,7},{9,8},{8,9},{11,10... | collective-permute-start | bytes 405512 | tf_op jit(solution)/shard_map/ppermute | solution.py:310
  12.4 1.5 %collective-permute-start.3 = (f32[264,128]{1,0:T(8,128)S(1)}, f32[264,128]{1,0:T(8,128)S(1)}, u32[]{:S(2)}, u32[]{:S(2)}) collective-permute-start(f32[264,128]{1,0:T(8,128)S(1)} %constant_dynamic-update-slice_fusion), channel_id=1, source_target_pairs={{16,0},{17,1},{18,2},{19,3},{20,4},{21,5},{22,6},{23,7},{24,8},{25... | collective-permute-start | bytes 405512 | tf_op jit(solution)/shard_map/ppermute | solution.py:310
  13.8 1.8 %far_tables.1 = (bf16[2048,512]{1,0:T(8,128)(2,1)S(1)}, bf16[2048,512]{1,0:T(8,128)(2,1)S(1)}, f32[4,4,128]{2,1,0:T(4,128)S(1)}, f32[4,4,128]{2,1,0:T(4,128)S(1)}) custom-call(s32[4]{0:T(128)S(1)} %broadcast_xor_fusion.bands_ref, s32[2]{0:T(128)S(1)} %pad_add_fusion.me_ref), custom_call_target="tpu_custom_call" | custom-call | bytes 4194304 | tf_op jit(solution)/shard_map/far_tables/pallas_call | solution.py:358
  15.6 0.2 collective-permute-done.4
  15.8 1.5 %collective-permute-done.3 = f32[264,128]{1,0:T(8,128)S(1)} collective-permute-done((f32[264,128]{1,0:T(8,128)S(1)}, f32[264,128]{1,0:T(8,128)S(1)}, u32[]{:S(2)}, u32[]{:S(2)}) %collective-permute-start.3) | collective-permute-done | bytes 135200 | tf_op jit(solution)/shard_map/ppermute | solution.py:310
  17.4 0.1 collective-permute-start.6
  17.5 1.6 %collective-permute-start.5 = (f32[264,128]{1,0:T(8,128)S(1)}, f32[264,128]{1,0:T(8,128)S(1)}, u32[]{:S(2)}, u32[]{:S(2)}) collective-permute-start(f32[264,128]{1,0:T(8,128)S(1)} %collective-permute-done.4), channel_id=1, source_target_pairs={{16,0},{17,1},{18,2},{19,3},{20,4},{21,5},{22,6},{23,7},{24,8},{25... | collective-permute-start | bytes 405512 | tf_op jit(solution)/shard_map/ppermute | solution.py:310
  19.0 0.0 collective-permute-done.6.refs_5_
  19.0 2.8 %near_first.1 = (s32[256,128]{1,0:T(8,128)S(1)}, s32[256,128]{1,0:T(8,128)S(1)}, f32[256,128]{1,0:T(8,128)S(1)}, f32[256,256]{1,0:T(8,128)S(1)}, f32[256,256]{1,0:T(8,128)S(1)}) custom-call(s32[2]{0:T(128)S(1)} %pad_add_fusion.me_ref, f32[4,4,128]{2,1,0:T(4,128)S(1)} %get-tuple-element.44.refs_0_, f32[4,4,128]{2,1,0:T(4,128)S(1)} %get-tuple-element.45.refs_1_, ...), custom_call_target="tpu_custom_call" | custom-call | flops 805306368 | bytes 2097152 | tf_op jit(solution)/shard_map/near_first/pallas_call | solution.py:358
  21.9 1.6 %collective-permute-done.5 = f32[264,128]{1,0:T(8,128)S(1)} collective-permute-done((f32[264,128]{1,0:T(8,128)S(1)}, f32[264,128]{1,0:T(8,128)S(1)}, u32[]{:S(2)}, u32[]{:S(2)}) %collective-permute-start.5) | collective-permute-done | bytes 135200 | tf_op jit(solution)/shard_map/ppermute | solution.py:310
  23.5 0.1 collective-permute-start.7
  23.6 2.0 %near_next.1 = (f32[256,256]{1,0:T(8,128)S(1)}, f32[256,256]{1,0:T(8,128)S(1)}) custom-call(s32[2]{0:T(128)S(1)} %pad_add_fusion.me_ref, f32[4,4,128]{2,1,0:T(4,128)S(1)} %get-tuple-element.44.refs_0_, f32[4,4,128]{2,1,0:T(4,128)S(1)} %get-tuple-element.45.refs_1_, bf16[2048,512]{1,0:T(8,128)(2,1)S(1)} %get-tuple-element.46.refs_2_, ...), custom_call_target="tpu_custom_call" | custom-call | flops 805306368 | bytes 2097152 | tf_op jit(solution)/shard_map/near_next/pallas_call | solution.py:358
  25.6 0.0 collective-permute-done.7.refs_5_
  25.6 5.1 %far_bands.1 = f32[256,512]{1,0:T(8,128)} custom-call(s32[2]{0:T(128)S(1)} %pad_add_fusion.me_ref, f32[4,4,128]{2,1,0:T(4,128)S(1)} %get-tuple-element.39.refs_0_, f32[4,4,128]{2,1,0:T(4,128)S(1)} %get-tuple-element.40.refs_1_, bf16[2048,512]{1,0:T(8,128)(2,1)S(1)} %get-tuple-element.41.refs_2_, bf16[2048,512]{1,0:T(8,128)(2,1)S(1)} %get-tuple-element.42.refs_3_, ...), custom_call_target="tpu_custom_call" | custom-call | flops 1610612736 | bytes 2097152 | tf_op jit(solution)/shard_map/far_bands/pallas_call | solution.py:358
  (12 shorter events, 0.1 us)
Async XLA Ops:
  0.8 9.9 %collective-permute-start.2 = (f32[64,128]{1,0:T(8,128)S(1)}, f32[64,128]{1,0:T(8,128)S(1)}, u32[]{:S(2)}, u32[]{:S(2)}) collective-permute-start(f32[64,128]{1,0:T(8,128)S(1)} %bitcast.10), channel_id=1, source_target_pairs={{6,0},{7,1},{4,2},{5,3},{2,4},{3,5},{0,6},{1,7},{14,8},{15,9},{12,... | collective-permute-start | bytes 98312 | tf_op jit(solution)/shard_map/ppermute | solution.py:310
  5.9 4.8 %collective-permute-start.1 = (f32[64,128]{1,0:T(8,128)S(1)}, f32[64,128]{1,0:T(8,128)S(1)}, u32[]{:S(2)}, u32[]{:S(2)}) collective-permute-start(f32[64,128]{1,0:T(8,128)S(1)} %bitcast.11), channel_id=1, source_target_pairs={{4,0},{5,1},{6,2},{7,3},{0,4},{1,5},{2,6},{3,7},{12,8},{13,9},{14,... | collective-permute-start | bytes 98312 | tf_op jit(solution)/shard_map/ppermute | solution.py:310
  5.9 3.9 %collective-permute-start = (f32[64,128]{1,0:T(8,128)S(1)}, f32[64,128]{1,0:T(8,128)S(1)}, u32[]{:S(2)}, u32[]{:S(2)}) collective-permute-start(f32[64,128]{1,0:T(8,128)S(1)} %bitcast.12), channel_id=1, source_target_pairs={{2,0},{3,1},{0,2},{1,3},{6,4},{7,5},{4,6},{5,7},{10,8},{11,9},{8,1... | collective-permute-start | bytes 98312 | tf_op jit(solution)/shard_map/ppermute | solution.py:310
  10.8 5.1 %collective-permute-start.4 = (f32[264,128]{1,0:T(8,128)S(1)}, f32[264,128]{1,0:T(8,128)S(1)}, u32[]{:S(2)}, u32[]{:S(2)}) collective-permute-start(f32[264,128]{1,0:T(8,128)S(1)} %constant_dynamic-update-slice_fusion), channel_id=1, source_target_pairs={{1,0},{0,1},{3,2},{2,3},{5,4},{4,5},{7,6},{6,7},{9,8},{8,9},{11,10... | collective-permute-start | bytes 405512 | tf_op jit(solution)/shard_map/ppermute | solution.py:310
  12.4 5.0 %collective-permute-start.3 = (f32[264,128]{1,0:T(8,128)S(1)}, f32[264,128]{1,0:T(8,128)S(1)}, u32[]{:S(2)}, u32[]{:S(2)}) collective-permute-start(f32[264,128]{1,0:T(8,128)S(1)} %constant_dynamic-update-slice_fusion), channel_id=1, source_target_pairs={{16,0},{17,1},{18,2},{19,3},{20,4},{21,5},{22,6},{23,7},{24,8},{25... | collective-permute-start | bytes 405512 | tf_op jit(solution)/shard_map/ppermute | solution.py:310
  17.4 1.6 %collective-permute-start.6 = (f32[528,128]{1,0:T(8,128)S(1)}, f32[528,128]{1,0:T(8,128)S(1)}, u32[]{:S(2)}, u32[]{:S(2)}) collective-permute-start(f32[528,128]{1,0:T(8,128)S(1)} %constant_dynamic-update-slice_fusion.5.refs_4_), channel_id=1, source_target_pairs={{8,0},{9,1},{10,2},{11,3},{12,4},{13,5},{14,6},{15,7},{0,8},{1,9},... | collective-permute-start | bytes 811016 | tf_op jit(solution)/shard_map/ppermute | solution.py:310
  17.5 6.0 %collective-permute-start.5 = (f32[264,128]{1,0:T(8,128)S(1)}, f32[264,128]{1,0:T(8,128)S(1)}, u32[]{:S(2)}, u32[]{:S(2)}) collective-permute-start(f32[264,128]{1,0:T(8,128)S(1)} %collective-permute-done.4), channel_id=1, source_target_pairs={{16,0},{17,1},{18,2},{19,3},{20,4},{21,5},{22,6},{23,7},{24,8},{25... | collective-permute-start | bytes 405512 | tf_op jit(solution)/shard_map/ppermute | solution.py:310
  23.5 2.1 %collective-permute-start.7 = (f32[528,128]{1,0:T(8,128)S(1)}, f32[528,128]{1,0:T(8,128)S(1)}, u32[]{:S(2)}, u32[]{:S(2)}) collective-permute-start(f32[528,128]{1,0:T(8,128)S(1)} %constant_dynamic-update-slice_fusion.7.refs_4_), channel_id=1, source_target_pairs={{8,0},{9,1},{10,2},{11,3},{12,4},{13,5},{14,6},{15,7},{0,8},{1,9},... | collective-permute-start | bytes 811016 | tf_op jit(solution)/shard_map/ppermute | solution.py:310

commit v8 on v7

--- a/solution.py
+++ b/solution.py
@@ -165,12 +165,12 @@
     units = len(octets) // 2
 
     def prepare(index):
-        step, (held, turned) = steps[index], sets[index % 2][:2]
+        (step, place_step), (held, turned) = steps[index], sets[index % 2][:2]
         for position, (ref, offset) in enumerate(blocks):
             group = places[position]
             for q in range(chunks):
                 turn_cos, turn_sin = [turn[step, q : q + 1, :] for turn in turn_refs]
-                start = offset + step * depth + q * stations
+                start = offset + place_step * depth + q * stations
                 real = ref[start : start + stations, :]
                 start += chunks * stations
                 imag = ref[start : start + stations, :]
@@ -202,7 +202,7 @@
                     cross[place + 1][rows, lanes] = low
 
     def transform(index, which):
-        step, (high, low) = steps[index], sets[index % 2][2 + 2 * which : 4 + 2 * which]
+        step, (high, low) = steps[index][0], sets[index % 2][2 + 2 * which : 4 + 2 * which]
         bins = slice(step * band_bins, (step + 1) * band_bins)
         table, total = table_refs[which], sums[which]
         by_high = dot(high[...], table[bins, :])
@@ -310,27 +310,34 @@
     return lax.ppermute(block, ("grp", "freq"), route)
 
 
-def exchange(column, ready):
+def exchange(column, depth, parts, ready):
     groups = lax.axis_size("grp")
-    rows = column.shape[0]
     if groups != 4:
         near = [column] + [fetched(column, move, 0) for move in range(1, groups)]
-        far = [fetched(column, move, 1) for move in range(groups)]
-        return near, far, [(move, 0, move) for move in range(groups)], ready
-    across = fetched(column, 2, 0)
-    beside = fetched(column, 0, 1)
-    across, beside, *ready = lax.optimization_barrier((across, beside, *ready))
+        layout = [(move, 0, move) for move in range(groups)]
+        fars = [
+            [fetched(column[first * depth : last * depth], move, 1) for move in range(groups)]
+            for first, last in parts
+        ]
+        return near, layout, fars, ready
+    across, *ready = lax.optimization_barrier((fetched(column, 2, 0), *ready))
     near = jnp.concatenate([column, across], axis=0)
     near = [near, fetched(near, 1, 0)]
-    far = [beside, fetched(beside, 2, 0)]
-    return near, far, [(0, 0, 0), (0, rows, 2), (1, 0, 1), (1, rows, 3)], ready
+    fars = []
+    for first, last in parts:
+        rows = slice(first * depth, last * depth)
+        fars.append([fetched(jnp.concatenate([column[rows], across[rows]], axis=0), 0, 1)])
+    return near, two_columns(column.shape[0]), fars, ready
+
+
+def two_columns(rows):
+    return [(0, 0, 0), (0, rows, 2), (1, 0, 1), (1, rows, 3)]
 
 
 def across_cores(far):
     if lax.axis_size("grp") != 4:
-        return far
-    far = jnp.concatenate(far, axis=0)
-    return [far, fetched(far, 1, 0)]
+        return far, [(move, 0, move) for move in range(len(far))]
+    return [far[0], fetched(far[0], 1, 0)], two_columns(far[0].shape[0] // 2)
 
 
 def per_device(spectra, station_mask, owners):
@@ -405,10 +412,11 @@
         [base] * 2,
         table_cost,
     )
-    near, far, layout, far_table = exchange(column, far_table)
+    depth = 2 * chunks * stations
+    parts = [(0, steps // 2), (steps // 2, steps)]
+    near, layout, fars, far_table = exchange(column, depth, parts, far_table)
 
     sizes = (groups, stations, rounds, slots, band_bins)
-    depth = column.shape[0] - SUBLANES
     spectrum = pltpu.VMEM((groups, 2 * chunks, stations, LANES), jnp.float32)
     cross = pltpu.VMEM((rows, band_bins), jnp.bfloat16)
     scratch = ([spectrum] * 2 + [cross] * 4) * 2
@@ -420,35 +428,48 @@
     total = pltpu.VMEM((rows, half_band), jnp.float32)
     half_result = total if half_band % LANES == 0 else pltpu.VMEM((rows, lag_band), jnp.float32)
     index = pltpu.VMEM((rows, LANES), jnp.int32)
-    table_at = [2, 3, 0, 1]
+    near_table = [near_table[place] for place in (2, 3, 0, 1)]
+    far_table = [far_table[place] for place in (2, 3, 0, 1)]
+
+    def more(name, layout, arrays, tables, first_step, last_step, place_step, sums):
+        some = [(step, step - place_step) for step in range(first_step, last_step)]
+        return call(
+            functools.partial(next_kernel, sizes, layout, len(arrays), some),
+            name,
+            [me],
+            [*tables, *arrays, first, second, *sums],
+            [total] * 2,
+            scratch,
+            cost(len(some)),
+        )
+
+    split = steps - steps // 4
     first, second, weight, even, odd = call(
-        functools.partial(near_kernel, sizes, layout, len(near), depth, range(steps // 2)),
+        functools.partial(
+            near_kernel, sizes, layout, len(near), steps * depth, [(i, i) for i in range(split)]
+        ),
         "near_first",
         [me],
-        [near_table[place] for place in table_at] + near,
+        near_table + near,
         [index] * 2 + [pltpu.VMEM((rows, LANES), jnp.float32)] + [total] * 2,
         scratch,
-        cost(steps // 2),
-    )
-    *far, even = lax.optimization_barrier((*far, even))
-    far = across_cores(far)
-    even, odd = call(
-        functools.partial(next_kernel, sizes, layout, len(near), range(steps // 2, steps)),
-        "near_next",
+        cost(split),
+    )
+    *far, even = lax.optimization_barrier((*fars[0], even))
+    far, far_layout = across_cores(far)
+    even, odd = more("near_next", layout, near, near_table, split, steps, 0, (even, odd))
+    *last, even = lax.optimization_barrier((*fars[1], even))
+    last, _ = across_cores(last)
+    even, odd = more("far_first", far_layout, far, far_table, *parts[0], 0, (even, odd))
+    some = [(step, step - parts[1][0]) for step in range(*parts[1])]
+    out = call(
+        functools.partial(last_kernel, sizes, far_layout, len(last), some),
+        "far_next",
         [me],
-        [near_table[place] for place in table_at] + near + [first, second, even, odd],
-        [total] * 2,
-        scratch,
-        cost(steps - steps // 2),
-    )
-    out = call(
-        functools.partial(last_kernel, sizes, layout, len(far), range(steps)),
-        "far_bands",
-        [me],
-        [far_table[place] for place in table_at] + far + [first, second, even, odd, weight],
+        [*far_table, *last, first, second, even, odd, weight],
         jax.ShapeDtypeStruct((rows, lag_band), jnp.float32),
         [total] * 2 + [half_result] * 2 + [pltpu.SemaphoreType.DMA((2,))] + scratch,
-        cost(steps),
+        cost(len(some)),
     )
     out = out.reshape(1, rounds, groups, slots, lag_band)
     return out[:, :, :, :capacity]

time: 31 us -> 30.3 us (0.977)
  starting transfers between devices: 10.5 us -> 9.55 us
    ppermute x8 -> x9, starting transfers between devices: 10.5 us -> 9.55 us  [fetched(): return lax.ppermute(block, ('grp', 'freq'), route)]
    pallas_call x5 -> x6, Pallas kernels: 13.6 us -> 13.9 us  [call(): pl.pallas_call(kernel, out_shape=out_shape, in_specs=[scalar] * len(scala...]
    ppermute x8 -> x9, waiting for transfers between devices: 5.54 us -> 5.5 us  [fetched(): return lax.ppermute(block, ('grp', 'freq'), route)]
  transfers between devices with their start and end apart: 8 -> 9, of which waited for: 5 -> 5; matrix products, arithmetic and copies ran while one was open for 0% -> 0% of each run, Pallas kernels for 28% -> 36%
where the time goes in v8:
time: 30.3 us; the launch traced here: 30 us
  Pallas kernels  13.9 us (46%)
  starting transfers between devices  9.55 us (32%)
  waiting for transfers between devices  5.5 us (18%)
  local copies, waits for them, and re-layouts  0.86 us (3%)
    pallas_call x6, Pallas kernels, call(): pl.pallas_call(kernel, out_shape=out_shape, in_specs=[scalar] * len(scala...  13.9 us
    ppermute x9, starting transfers between devices, fetched(): return lax.ppermute(block, ('grp', 'freq'), route)  9.55 us
    ppermute x9, waiting for transfers between devices, fetched(): return lax.ppermute(block, ('grp', 'freq'), route)  5.5 us
    reshape x2, local copies, waits for them, and re-layouts, per_device(): tiles = spectra.reshape(stations, 2, chunks, LANES).transpose(1, 2, 0, 3)  0.8 us
  transfers between devices with their start and end apart: 9, of which 5 were waited for; matrix products, arithmetic and copies ran while one was open for 0% of the time, Pallas kernels for 36%

profile of v8, /device:TPU:0, one launch (start us, length us, event | category | flops | bytes accessed | tf_op | source)
XLA Modules:
  0.0 30.0 jit_solution(14986518938969680769)
XLA Ops:
  0.0 0.8 %reshape.12 = f32[8,2,4,128]{3,2,1,0:T(4,128)S(1)} reshape(f32[8,2,512]{2,1,0:T(2,128)} %param.3) | data formatting | bytes 65536 | tf_op jit(solution)/shard_map/reshape | solution.py:379
  0.8 5.1 %collective-permute-start.2 = (f32[64,128]{1,0:T(8,128)S(1)}, f32[64,128]{1,0:T(8,128)S(1)}, u32[]{:S(2)}, u32[]{:S(2)}) collective-permute-start(f32[64,128]{1,0:T(8,128)S(1)} %bitcast.10), channel_id=1, source_target_pairs={{6,0},{7,1},{4,2},{5,3},{2,4},{3,5},{0,6},{1,7},{14,8},{15,9},{12,... | collective-permute-start | bytes 98312 | tf_op jit(solution)/shard_map/ppermute | solution.py:310
  5.9 0.0 collective-permute-start.1
  5.9 0.6 %collective-permute-start = (f32[64,128]{1,0:T(8,128)S(1)}, f32[64,128]{1,0:T(8,128)S(1)}, u32[]{:S(2)}, u32[]{:S(2)}) collective-permute-start(f32[64,128]{1,0:T(8,128)S(1)} %bitcast.12), channel_id=1, source_target_pairs={{2,0},{3,1},{0,2},{1,3},{6,4},{7,5},{4,6},{5,7},{10,8},{11,9},{8,1... | collective-permute-start | bytes 98312 | tf_op jit(solution)/shard_map/ppermute | solution.py:310
  6.6 0.1 pad_add_fusion.me_ref
  6.7 1.9 %near_tables.1 = (bf16[2048,512]{1,0:T(8,128)(2,1)S(1)}, bf16[2048,512]{1,0:T(8,128)(2,1)S(1)}, f32[4,4,128]{2,1,0:T(4,128)S(1)}, f32[4,4,128]{2,1,0:T(4,128)S(1)}, f32[8,128]{1,0:T(8,128)S(1)}) custom-call(s32[4]{0:T(128)S(1)} %multiply_xor_fusion.bands_ref, s32[2]{0:T(128)S(1)} %pad_add_fusion.me_ref, s32[1,2,1,64]{3,2,1,0:T(1,128)} %bitcast.14, ...), custom_call_target="tpu_custom_call" | custom-call | bytes 4194304 | tf_op jit(solution)/shard_map/near_tables/pallas_call | solution.py:365
  8.5 1.3 %collective-permute-done = f32[64,128]{1,0:T(8,128)S(1)} collective-permute-done((f32[64,128]{1,0:T(8,128)S(1)}, f32[64,128]{1,0:T(8,128)S(1)}, u32[]{:S(2)}, u32[]{:S(2)}) %collective-permute-start) | collective-permute-done | bytes 32800 | tf_op jit(solution)/shard_map/ppermute | solution.py:310
  9.8 0.9 %collective-permute-done.1 = f32[64,128]{1,0:T(8,128)S(1)} collective-permute-done((f32[64,128]{1,0:T(8,128)S(1)}, f32[64,128]{1,0:T(8,128)S(1)}, u32[]{:S(2)}, u32[]{:S(2)}) %collective-permute-start.1) | collective-permute-done | bytes 32800 | tf_op jit(solution)/shard_map/ppermute | solution.py:310
  10.7 0.0 collective-permute-done.2
  10.8 1.6 %collective-permute-start.3 = (f32[264,128]{1,0:T(8,128)S(1)}, f32[264,128]{1,0:T(8,128)S(1)}, u32[]{:S(2)}, u32[]{:S(2)}) collective-permute-start(f32[264,128]{1,0:T(8,128)S(1)} %constant_dynamic-update-slice_fusion), channel_id=1, source_target_pairs={{16,0},{17,1},{18,2},{19,3},{20,4},{21,5},{22,6},{23,7},{24,8},{25... | collective-permute-start | bytes 405512 | tf_op jit(solution)/shard_map/ppermute | solution.py:310
  12.3 1.8 %far_tables.1 = (bf16[2048,512]{1,0:T(8,128)(2,1)S(1)}, bf16[2048,512]{1,0:T(8,128)(2,1)S(1)}, f32[4,4,128]{2,1,0:T(4,128)S(1)}, f32[4,4,128]{2,1,0:T(4,128)S(1)}) custom-call(s32[4]{0:T(128)S(1)} %broadcast_xor_fusion.bands_ref, s32[2]{0:T(128)S(1)} %pad_add_fusion.me_ref), custom_call_target="tpu_custom_call" | custom-call | bytes 4194304 | tf_op jit(solution)/shard_map/far_tables/pallas_call | solution.py:365
  14.1 1.7 %collective-permute-done.3 = f32[264,128]{1,0:T(8,128)S(1)} collective-permute-done((f32[264,128]{1,0:T(8,128)S(1)}, f32[264,128]{1,0:T(8,128)S(1)}, u32[]{:S(2)}, u32[]{:S(2)}) %collective-permute-start.3) | collective-permute-done | bytes 135200 | tf_op jit(solution)/shard_map/ppermute | solution.py:310
  15.9 0.1 collective-permute-start.5
  16.0 1.6 %collective-permute-start.6 = (f32[256,128]{1,0:T(8,128)S(1)}, f32[256,128]{1,0:T(8,128)S(1)}, u32[]{:S(2)}, u32[]{:S(2)}) collective-permute-start(f32[256,128]{1,0:T(8,128)S(1)} %pad_maximum_fusion.1), channel_id=1, source_target_pairs={{1,0},{0,1},{3,2},{2,3},{5,4},{4,5},{7,6},{6,7},{9,8},{8,9},{11,10... | collective-permute-start | bytes 393224 | tf_op jit(solution)/shard_map/ppermute | solution.py:310
  17.6 0.6 %collective-permute-start.4 = (f32[256,128]{1,0:T(8,128)S(1)}, f32[256,128]{1,0:T(8,128)S(1)}, u32[]{:S(2)}, u32[]{:S(2)}) collective-permute-start(f32[256,128]{1,0:T(8,128)S(1)} %pad_maximum_fusion), channel_id=1, source_target_pairs={{1,0},{0,1},{3,2},{2,3},{5,4},{4,5},{7,6},{6,7},{9,8},{8,9},{11,10... | collective-permute-start | bytes 393224 | tf_op jit(solution)/shard_map/ppermute | solution.py:310
  18.1 0.0 collective-permute-done.5.refs_5_
  18.1 3.6 %near_first.1 = (s32[256,128]{1,0:T(8,128)S(1)}, s32[256,128]{1,0:T(8,128)S(1)}, f32[256,128]{1,0:T(8,128)S(1)}, f32[256,256]{1,0:T(8,128)S(1)}, f32[256,256]{1,0:T(8,128)S(1)}) custom-call(s32[2]{0:T(128)S(1)} %pad_add_fusion.me_ref, f32[4,4,128]{2,1,0:T(4,128)S(1)} %get-tuple-element.46.refs_0_, f32[4,4,128]{2,1,0:T(4,128)S(1)} %get-tuple-element.47.refs_1_, ...), custom_call_target="tpu_custom_call" | custom-call | flops 1207959552 | bytes 2097152 | tf_op jit(solution)/shard_map/near_first/pallas_call | solution.py:365
  21.8 0.6 %collective-permute-done.6.refs_4_ = f32[256,128]{1,0:T(8,128)S(1)} collective-permute-done((f32[256,128]{1,0:T(8,128)S(1)}, f32[256,128]{1,0:T(8,128)S(1)}, u32[]{:S(2)}, u32[]{:S(2)}) %collective-permute-start.6) | collective-permute-done | bytes 131104 | tf_op jit(solution)/shard_map/ppermute | solution.py:310
  22.3 0.0 collective-permute-start.8
  22.3 1.4 %near_next.1 = (f32[256,256]{1,0:T(8,128)S(1)}, f32[256,256]{1,0:T(8,128)S(1)}) custom-call(s32[2]{0:T(128)S(1)} %pad_add_fusion.me_ref, f32[4,4,128]{2,1,0:T(4,128)S(1)} %get-tuple-element.46.refs_0_, f32[4,4,128]{2,1,0:T(4,128)S(1)} %get-tuple-element.47.refs_1_, bf16[2048,512]{1,0:T(8,128)(2,1)S(1)} %get-tuple-element.48.refs_2_, ...), custom_call_target="tpu_custom_call" | custom-call | flops 402653184 | bytes 2097152 | tf_op jit(solution)/shard_map/near_next/pallas_call | solution.py:365
  23.7 1.0 %collective-permute-done.4.refs_4_ = f32[256,128]{1,0:T(8,128)S(1)} collective-permute-done((f32[256,128]{1,0:T(8,128)S(1)}, f32[256,128]{1,0:T(8,128)S(1)}, u32[]{:S(2)}, u32[]{:S(2)}) %collective-permute-start.4) | collective-permute-done | bytes 131104 | tf_op jit(solution)/shard_map/ppermute | solution.py:310
  24.7 0.0 collective-permute-start.7
  24.7 0.0 collective-permute-done.8.refs_5_
  24.7 2.0 %far_first.1 = (f32[256,256]{1,0:T(8,128)S(1)}, f32[256,256]{1,0:T(8,128)S(1)}) custom-call(s32[2]{0:T(128)S(1)} %pad_add_fusion.me_ref, f32[4,4,128]{2,1,0:T(4,128)S(1)} %get-tuple-element.41.refs_0_, f32[4,4,128]{2,1,0:T(4,128)S(1)} %get-tuple-element.42.refs_1_, bf16[2048,512]{1,0:T(8,128)(2,1)S(1)} %get-tuple-element.43.refs_2_, ...), custom_call_target="tpu_custom_call" | custom-call | flops 805306368 | bytes 2097152 | tf_op jit(solution)/shard_map/far_first/pallas_call | solution.py:365
  26.8 0.0 collective-permute-done.7.refs_5_
  26.8 3.2 %far_next.1 = f32[256,512]{1,0:T(8,128)} custom-call(s32[2]{0:T(128)S(1)} %pad_add_fusion.me_ref, f32[4,4,128]{2,1,0:T(4,128)S(1)} %get-tuple-element.41.refs_0_, f32[4,4,128]{2,1,0:T(4,128)S(1)} %get-tuple-element.42.refs_1_, bf16[2048,512]{1,0:T(8,128)(2,1)S(1)} %get-tuple-element.43.refs_2_, bf16[2048,512]{1,0:T(8,128)(2,1)S(1)} %get-tuple-element.44.refs_3_, ...), custom_call_target="tpu_custom_call" | custom-call | flops 805306368 | bytes 2097152 | tf_op jit(solution)/shard_map/far_next/pallas_call | solution.py:365
  (14 shorter events, 0.1 us)
Async XLA Ops:
  0.8 9.9 %collective-permute-start.2 = (f32[64,128]{1,0:T(8,128)S(1)}, f32[64,128]{1,0:T(8,128)S(1)}, u32[]{:S(2)}, u32[]{:S(2)}) collective-permute-start(f32[64,128]{1,0:T(8,128)S(1)} %bitcast.10), channel_id=1, source_target_pairs={{6,0},{7,1},{4,2},{5,3},{2,4},{3,5},{0,6},{1,7},{14,8},{15,9},{12,... | collective-permute-start | bytes 98312 | tf_op jit(solution)/shard_map/ppermute | solution.py:310
  5.9 4.8 %collective-permute-start.1 = (f32[64,128]{1,0:T(8,128)S(1)}, f32[64,128]{1,0:T(8,128)S(1)}, u32[]{:S(2)}, u32[]{:S(2)}) collective-permute-start(f32[64,128]{1,0:T(8,128)S(1)} %bitcast.11), channel_id=1, source_target_pairs={{4,0},{5,1},{6,2},{7,3},{0,4},{1,5},{2,6},{3,7},{12,8},{13,9},{14,... | collective-permute-start | bytes 98312 | tf_op jit(solution)/shard_map/ppermute | solution.py:310
  5.9 3.9 %collective-permute-start = (f32[64,128]{1,0:T(8,128)S(1)}, f32[64,128]{1,0:T(8,128)S(1)}, u32[]{:S(2)}, u32[]{:S(2)}) collective-permute-start(f32[64,128]{1,0:T(8,128)S(1)} %bitcast.12), channel_id=1, source_target_pairs={{2,0},{3,1},{0,2},{1,3},{6,4},{7,5},{4,6},{5,7},{10,8},{11,9},{8,1... | collective-permute-start | bytes 98312 | tf_op jit(solution)/shard_map/ppermute | solution.py:310
  10.8 5.1 %collective-permute-start.3 = (f32[264,128]{1,0:T(8,128)S(1)}, f32[264,128]{1,0:T(8,128)S(1)}, u32[]{:S(2)}, u32[]{:S(2)}) collective-permute-start(f32[264,128]{1,0:T(8,128)S(1)} %constant_dynamic-update-slice_fusion), channel_id=1, source_target_pairs={{16,0},{17,1},{18,2},{19,3},{20,4},{21,5},{22,6},{23,7},{24,8},{25... | collective-permute-start | bytes 405512 | tf_op jit(solution)/shard_map/ppermute | solution.py:310
  15.9 2.3 %collective-permute-start.5 = (f32[528,128]{1,0:T(8,128)S(1)}, f32[528,128]{1,0:T(8,128)S(1)}, u32[]{:S(2)}, u32[]{:S(2)}) collective-permute-start(f32[528,128]{1,0:T(8,128)S(1)} %constant_dynamic-update-slice_fusion.5.refs_4_), channel_id=1, source_target_pairs={{8,0},{9,1},{10,2},{11,3},{12,4},{13,5},{14,6},{15,7},{0,8},{1,9},... | collective-permute-start | bytes 811016 | tf_op jit(solution)/shard_map/ppermute | solution.py:310
  16.0 6.4 %collective-permute-start.6 = (f32[256,128]{1,0:T(8,128)S(1)}, f32[256,128]{1,0:T(8,128)S(1)}, u32[]{:S(2)}, u32[]{:S(2)}) collective-permute-start(f32[256,128]{1,0:T(8,128)S(1)} %pad_maximum_fusion.1), channel_id=1, source_target_pairs={{1,0},{0,1},{3,2},{2,3},{5,4},{4,5},{7,6},{6,7},{9,8},{8,9},{11,10... | collective-permute-start | bytes 393224 | tf_op jit(solution)/shard_map/ppermute | solution.py:310
  17.6 7.2 %collective-permute-start.4 = (f32[256,128]{1,0:T(8,128)S(1)}, f32[256,128]{1,0:T(8,128)S(1)}, u32[]{:S(2)}, u32[]{:S(2)}) collective-permute-start(f32[256,128]{1,0:T(8,128)S(1)} %pad_maximum_fusion), channel_id=1, source_target_pairs={{1,0},{0,1},{3,2},{2,3},{5,4},{4,5},{7,6},{6,7},{9,8},{8,9},{11,10... | collective-permute-start | bytes 393224 | tf_op jit(solution)/shard_map/ppermute | solution.py:310
  22.3 2.4 %collective-permute-start.8 = (f32[256,128]{1,0:T(8,128)S(1)}, f32[256,128]{1,0:T(8,128)S(1)}, u32[]{:S(2)}, u32[]{:S(2)}) collective-permute-start(f32[256,128]{1,0:T(8,128)S(1)} %collective-permute-done.6.refs_4_), channel_id=1, source_target_pairs={{8,0},{9,1},{10,2},{11,3},{12,4},{13,5},{14,6},{15,7},{0,8},{1,9},... | collective-permute-start | bytes 393224 | tf_op jit(solution)/shard_map/ppermute | solution.py:310
  24.7 2.1 %collective-permute-start.7 = (f32[256,128]{1,0:T(8,128)S(1)}, f32[256,128]{1,0:T(8,128)S(1)}, u32[]{:S(2)}, u32[]{:S(2)}) collective-permute-start(f32[256,128]{1,0:T(8,128)S(1)} %collective-permute-done.4.refs_4_), channel_id=1, source_target_pairs={{8,0},{9,1},{10,2},{11,3},{12,4},{13,5},{14,6},{15,7},{0,8},{1,9},... | collective-permute-start | bytes 393224 | tf_op jit(solution)/shard_map/ppermute | solution.py:310

commit v9 on v8

--- a/solution.py
+++ b/solution.py
@@ -11,6 +11,7 @@
 LAGS = 4096
 LANES = 128
 SUBLANES = 8
+PARTS = 4
 
 
 def split_bf16(values, parts):
@@ -156,13 +157,9 @@
     half = sums[0].shape[1]
     first, second = picks
     sets = [scratch[6 * index : 6 * (index + 1)] for index in range(2)]
-    octets = [
-        (group, (group + groups - 1 - index) % groups)
-        for index in range(rounds)
-        for group in range(groups)
-        for _ in range(slots // SUBLANES)
-    ]
-    units = len(octets) // 2
+    part_groups = [range(part * groups // PARTS, (part + 1) * groups // PARTS) for part in range(PARTS)]
+    bins_at_once = max(band_bins // 2, LANES)
+    pieces = [(which, start) for which in range(2) for start in range(0, band_bins, bins_at_once)]
 
     def prepare(index):
         (step, place_step), (held, turned) = steps[index], sets[index % 2][:2]
@@ -179,46 +176,55 @@
                 turned[group, q] = real * turn_cos + imag * turn_sin
                 turned[group, chunks + q] = imag * turn_cos - real * turn_sin
 
-    def multiply(index, part, parts):
+    def multiply(index, part):
         held, turned, *cross = sets[index % 2]
-        for unit in range(part * units // parts, (part + 1) * units // parts):
-            rows = slice(2 * unit * SUBLANES, 2 * (unit + 1) * SUBLANES)
+        for group in part_groups[part]:
+            sources = []
+            for number in range(rounds):
+                start = (number * groups + group) * slots
+                lines = [slice(start + o, start + o + SUBLANES) for o in range(0, slots, SUBLANES)]
+                partner = (group + groups - 1 - number) % groups
+                sources.append((start, partner, [(first[line, :], second[line, :]) for line in lines]))
             for q in range(chunks):
                 lanes = slice(q * LANES, (q + 1) * LANES)
-                reals, imags = [], []
-                for octet in (2 * unit, 2 * unit + 1):
-                    group, partner = octets[octet]
-                    lines = slice(octet * SUBLANES, (octet + 1) * SUBLANES)
-                    index_a, index_b = first[lines, :], second[lines, :]
-                    a_real = jnp.take_along_axis(held[group, q], index_a, axis=0)
-                    a_imag = jnp.take_along_axis(held[group, chunks + q], index_a, axis=0)
-                    b_real = jnp.take_along_axis(turned[partner, q], index_b, axis=0)
-                    b_imag = jnp.take_along_axis(turned[partner, chunks + q], index_b, axis=0)
-                    reals.append(a_real * b_real + a_imag * b_imag)
-                    imags.append(a_imag * b_real - a_real * b_imag)
-                for place, values in ((0, reals), (2, imags)):
-                    high, low = split_bf16(jnp.concatenate(values, axis=0), 2)
-                    cross[place][rows, lanes] = high
-                    cross[place + 1][rows, lanes] = low
-
-    def transform(index, which):
+                own_real, own_imag = held[group, q], held[group, chunks + q]
+                for start, partner, indices in sources:
+                    real, imag = turned[partner, q], turned[partner, chunks + q]
+                    reals, imags = [], []
+                    for index_a, index_b in indices:
+                        a_real = jnp.take_along_axis(own_real, index_a, axis=0)
+                        a_imag = jnp.take_along_axis(own_imag, index_a, axis=0)
+                        b_real = jnp.take_along_axis(real, index_b, axis=0)
+                        b_imag = jnp.take_along_axis(imag, index_b, axis=0)
+                        reals.append(a_real * b_real + a_imag * b_imag)
+                        imags.append(a_imag * b_real - a_real * b_imag)
+                    rows = slice(start, start + slots)
+                    for place, values in ((0, reals), (2, imags)):
+                        high, low = split_bf16(jnp.concatenate(values, axis=0), 2)
+                        cross[place][rows, lanes] = high
+                        cross[place + 1][rows, lanes] = low
+
+    def transform(index, which, start):
         step, (high, low) = steps[index][0], sets[index % 2][2 + 2 * which : 4 + 2 * which]
-        bins = slice(step * band_bins, (step + 1) * band_bins)
+        lanes = slice(start, start + bins_at_once)
+        bins = slice(step * band_bins + start, step * band_bins + start + bins_at_once)
         table, total = table_refs[which], sums[which]
-        by_high = dot(high[...], table[bins, :])
-        by_low = dot(low[...], table[bins, :half])
+        by_high = dot(high[:, lanes], table[bins, :])
+        by_low = dot(low[:, lanes], table[bins, :half])
         total[...] += by_high[:, :half] + (by_high[:, half:] + by_low)
 
     prepare(0)
-    multiply(0, 0, 1)
+    for part in range(PARTS):
+        multiply(0, part)
     for index in range(len(steps)):
         more = index + 1 < len(steps)
         if more:
             prepare(index + 1)
-        for which in range(2):
+        for part in range(PARTS):
             if more:
-                multiply(index + 1, which, 2)
-            transform(index, which)
+                multiply(index + 1, part)
+            if part < len(pieces):
+                transform(index, *pieces[part])
 
 
 def placed_blocks(array_refs, layout, me, groups):
@@ -348,7 +354,7 @@
     pairs = stations * stations
     bin_total = band_bins * shards
     capacity = (2 * pairs + groups - 1) // groups
-    slots = padded(capacity, SUBLANES)
+    slots = padded(capacity, 2 * SUBLANES)
     lag_band = LAGS // shards
     half_band = lag_band // 2
     chunks = band_bins // LANES

time: 30.3 us -> 30 us (0.990)
  Pallas kernels: 13.9 us -> 13.3 us
  waiting for transfers between devices: 5.5 us -> 5.86 us
    pallas_call x6, Pallas kernels: 13.9 us -> 13.3 us  [call(): pl.pallas_call(kernel, out_shape=out_shape, in_specs=[scalar] * len(scala...]
    ppermute x9, waiting for transfers between devices: 5.5 us -> 5.86 us  [fetched(): return lax.ppermute(block, ('grp', 'freq'), route)]
  transfers between devices with their start and end apart: 9 -> 9, of which waited for: 5 -> 5; matrix products, arithmetic and copies ran while one was open for 0% -> 1% of each run, Pallas kernels for 36% -> 34%
where the time goes in v9:
time: 30 us; the launch traced here: 29.8 us
  Pallas kernels  13.3 us (44%)
  starting transfers between devices  9.55 us (32%)
  waiting for transfers between devices  5.86 us (20%)
  local copies, waits for them, and re-layouts  0.86 us (3%)
    pallas_call x6, Pallas kernels, call(): pl.pallas_call(kernel, out_shape=out_shape, in_specs=[scalar] * len(scala...  13.3 us
    ppermute x9, starting transfers between devices, fetched(): return lax.ppermute(block, ('grp', 'freq'), route)  9.55 us
    ppermute x9, waiting for transfers between devices, fetched(): return lax.ppermute(block, ('grp', 'freq'), route)  5.86 us
    reshape x2, local copies, waits for them, and re-layouts, per_device(): tiles = spectra.reshape(stations, 2, chunks, LANES).transpose(1, 2, 0, 3)  0.8 us
  transfers between devices with their start and end apart: 9, of which 5 were waited for; matrix products, arithmetic and copies ran while one was open for 1% of the time, Pallas kernels for 34%

profile of v9, /device:TPU:0, one launch (start us, length us, event | category | flops | bytes accessed | tf_op | source)
XLA Modules:
  0.0 29.8 jit_solution(2006565040599729904)
XLA Ops:
  0.0 0.8 %reshape.12 = f32[8,2,4,128]{3,2,1,0:T(4,128)S(1)} reshape(f32[8,2,512]{2,1,0:T(2,128)} %param.3) | data formatting | bytes 65536 | tf_op jit(solution)/shard_map/reshape | solution.py:385
  0.8 5.1 %collective-permute-start.2 = (f32[64,128]{1,0:T(8,128)S(1)}, f32[64,128]{1,0:T(8,128)S(1)}, u32[]{:S(2)}, u32[]{:S(2)}) collective-permute-start(f32[64,128]{1,0:T(8,128)S(1)} %bitcast.10), channel_id=1, source_target_pairs={{6,0},{7,1},{4,2},{5,3},{2,4},{3,5},{0,6},{1,7},{14,8},{15,9},{12,... | collective-permute-start | bytes 98312 | tf_op jit(solution)/shard_map/ppermute | solution.py:316
  5.9 0.0 collective-permute-start.1
  5.9 0.6 %collective-permute-start = (f32[64,128]{1,0:T(8,128)S(1)}, f32[64,128]{1,0:T(8,128)S(1)}, u32[]{:S(2)}, u32[]{:S(2)}) collective-permute-start(f32[64,128]{1,0:T(8,128)S(1)} %bitcast.12), channel_id=1, source_target_pairs={{2,0},{3,1},{0,2},{1,3},{6,4},{7,5},{4,6},{5,7},{10,8},{11,9},{8,1... | collective-permute-start | bytes 98312 | tf_op jit(solution)/shard_map/ppermute | solution.py:316
  6.6 0.1 pad_add_fusion.me_ref
  6.7 1.9 %near_tables.1 = (bf16[2048,512]{1,0:T(8,128)(2,1)S(1)}, bf16[2048,512]{1,0:T(8,128)(2,1)S(1)}, f32[4,4,128]{2,1,0:T(4,128)S(1)}, f32[4,4,128]{2,1,0:T(4,128)S(1)}, f32[8,128]{1,0:T(8,128)S(1)}) custom-call(s32[4]{0:T(128)S(1)} %multiply_xor_fusion.bands_ref, s32[2]{0:T(128)S(1)} %pad_add_fusion.me_ref, s32[1,2,1,64]{3,2,1,0:T(1,128)} %bitcast.14, ...), custom_call_target="tpu_custom_call" | custom-call | bytes 4194304 | tf_op jit(solution)/shard_map/near_tables/pallas_call | solution.py:371
  8.5 1.3 %collective-permute-done = f32[64,128]{1,0:T(8,128)S(1)} collective-permute-done((f32[64,128]{1,0:T(8,128)S(1)}, f32[64,128]{1,0:T(8,128)S(1)}, u32[]{:S(2)}, u32[]{:S(2)}) %collective-permute-start) | collective-permute-done | bytes 32800 | tf_op jit(solution)/shard_map/ppermute | solution.py:316
  9.8 0.9 %collective-permute-done.1 = f32[64,128]{1,0:T(8,128)S(1)} collective-permute-done((f32[64,128]{1,0:T(8,128)S(1)}, f32[64,128]{1,0:T(8,128)S(1)}, u32[]{:S(2)}, u32[]{:S(2)}) %collective-permute-start.1) | collective-permute-done | bytes 32800 | tf_op jit(solution)/shard_map/ppermute | solution.py:316
  10.7 0.0 collective-permute-done.2
  10.8 1.6 %collective-permute-start.3 = (f32[264,128]{1,0:T(8,128)S(1)}, f32[264,128]{1,0:T(8,128)S(1)}, u32[]{:S(2)}, u32[]{:S(2)}) collective-permute-start(f32[264,128]{1,0:T(8,128)S(1)} %constant_dynamic-update-slice_fusion), channel_id=1, source_target_pairs={{16,0},{17,1},{18,2},{19,3},{20,4},{21,5},{22,6},{23,7},{24,8},{25... | collective-permute-start | bytes 405512 | tf_op jit(solution)/shard_map/ppermute | solution.py:316
  12.3 1.8 %far_tables.1 = (bf16[2048,512]{1,0:T(8,128)(2,1)S(1)}, bf16[2048,512]{1,0:T(8,128)(2,1)S(1)}, f32[4,4,128]{2,1,0:T(4,128)S(1)}, f32[4,4,128]{2,1,0:T(4,128)S(1)}) custom-call(s32[4]{0:T(128)S(1)} %broadcast_xor_fusion.bands_ref, s32[2]{0:T(128)S(1)} %pad_add_fusion.me_ref), custom_call_target="tpu_custom_call" | custom-call | bytes 4194304 | tf_op jit(solution)/shard_map/far_tables/pallas_call | solution.py:371
  14.1 1.7 %collective-permute-done.3 = f32[264,128]{1,0:T(8,128)S(1)} collective-permute-done((f32[264,128]{1,0:T(8,128)S(1)}, f32[264,128]{1,0:T(8,128)S(1)}, u32[]{:S(2)}, u32[]{:S(2)}) %collective-permute-start.3) | collective-permute-done | bytes 135200 | tf_op jit(solution)/shard_map/ppermute | solution.py:316
  15.9 0.1 collective-permute-start.5
  16.0 1.6 %collective-permute-start.6 = (f32[256,128]{1,0:T(8,128)S(1)}, f32[256,128]{1,0:T(8,128)S(1)}, u32[]{:S(2)}, u32[]{:S(2)}) collective-permute-start(f32[256,128]{1,0:T(8,128)S(1)} %pad_maximum_fusion.1), channel_id=1, source_target_pairs={{1,0},{0,1},{3,2},{2,3},{5,4},{4,5},{7,6},{6,7},{9,8},{8,9},{11,10... | collective-permute-start | bytes 393224 | tf_op jit(solution)/shard_map/ppermute | solution.py:316
  17.6 0.6 %collective-permute-start.4 = (f32[256,128]{1,0:T(8,128)S(1)}, f32[256,128]{1,0:T(8,128)S(1)}, u32[]{:S(2)}, u32[]{:S(2)}) collective-permute-start(f32[256,128]{1,0:T(8,128)S(1)} %pad_maximum_fusion), channel_id=1, source_target_pairs={{1,0},{0,1},{3,2},{2,3},{5,4},{4,5},{7,6},{6,7},{9,8},{8,9},{11,10... | collective-permute-start | bytes 393224 | tf_op jit(solution)/shard_map/ppermute | solution.py:316
  18.1 0.0 collective-permute-done.5.refs_5_
  18.1 3.3 %near_first.1 = (s32[256,128]{1,0:T(8,128)S(1)}, s32[256,128]{1,0:T(8,128)S(1)}, f32[256,128]{1,0:T(8,128)S(1)}, f32[256,256]{1,0:T(8,128)S(1)}, f32[256,256]{1,0:T(8,128)S(1)}) custom-call(s32[2]{0:T(128)S(1)} %pad_add_fusion.me_ref, f32[4,4,128]{2,1,0:T(4,128)S(1)} %get-tuple-element.46.refs_0_, f32[4,4,128]{2,1,0:T(4,128)S(1)} %get-tuple-element.47.refs_1_, ...), custom_call_target="tpu_custom_call" | custom-call | flops 1207959552 | bytes 2097152 | tf_op jit(solution)/shard_map/near_first/pallas_call | solution.py:371
  21.5 0.8 %collective-permute-done.6.refs_4_ = f32[256,128]{1,0:T(8,128)S(1)} collective-permute-done((f32[256,128]{1,0:T(8,128)S(1)}, f32[256,128]{1,0:T(8,128)S(1)}, u32[]{:S(2)}, u32[]{:S(2)}) %collective-permute-start.6) | collective-permute-done | bytes 131104 | tf_op jit(solution)/shard_map/ppermute | solution.py:316
  22.3 0.0 collective-permute-start.8
  22.3 1.3 %near_next.1 = (f32[256,256]{1,0:T(8,128)S(1)}, f32[256,256]{1,0:T(8,128)S(1)}) custom-call(s32[2]{0:T(128)S(1)} %pad_add_fusion.me_ref, f32[4,4,128]{2,1,0:T(4,128)S(1)} %get-tuple-element.46.refs_0_, f32[4,4,128]{2,1,0:T(4,128)S(1)} %get-tuple-element.47.refs_1_, bf16[2048,512]{1,0:T(8,128)(2,1)S(1)} %get-tuple-element.48.refs_2_, ...), custom_call_target="tpu_custom_call" | custom-call | flops 402653184 | bytes 2097152 | tf_op jit(solution)/shard_map/near_next/pallas_call | solution.py:371
  23.6 1.1 %collective-permute-done.4.refs_4_ = f32[256,128]{1,0:T(8,128)S(1)} collective-permute-done((f32[256,128]{1,0:T(8,128)S(1)}, f32[256,128]{1,0:T(8,128)S(1)}, u32[]{:S(2)}, u32[]{:S(2)}) %collective-permute-start.4) | collective-permute-done | bytes 131104 | tf_op jit(solution)/shard_map/ppermute | solution.py:316
  24.7 0.0 collective-permute-start.7
  24.7 0.0 collective-permute-done.8.refs_5_
  24.7 1.8 %far_first.1 = (f32[256,256]{1,0:T(8,128)S(1)}, f32[256,256]{1,0:T(8,128)S(1)}) custom-call(s32[2]{0:T(128)S(1)} %pad_add_fusion.me_ref, f32[4,4,128]{2,1,0:T(4,128)S(1)} %get-tuple-element.41.refs_0_, f32[4,4,128]{2,1,0:T(4,128)S(1)} %get-tuple-element.42.refs_1_, bf16[2048,512]{1,0:T(8,128)(2,1)S(1)} %get-tuple-element.43.refs_2_, ...), custom_call_target="tpu_custom_call" | custom-call | flops 805306368 | bytes 2097152 | tf_op jit(solution)/shard_map/far_first/pallas_call | solution.py:371
  26.6 0.0 collective-permute-done.7.refs_5_
  26.6 3.1 %far_next.1 = f32[256,512]{1,0:T(8,128)} custom-call(s32[2]{0:T(128)S(1)} %pad_add_fusion.me_ref, f32[4,4,128]{2,1,0:T(4,128)S(1)} %get-tuple-element.41.refs_0_, f32[4,4,128]{2,1,0:T(4,128)S(1)} %get-tuple-element.42.refs_1_, bf16[2048,512]{1,0:T(8,128)(2,1)S(1)} %get-tuple-element.43.refs_2_, bf16[2048,512]{1,0:T(8,128)(2,1)S(1)} %get-tuple-element.44.refs_3_, ...), custom_call_target="tpu_custom_call" | custom-call | flops 805306368 | bytes 2097152 | tf_op jit(solution)/shard_map/far_next/pallas_call | solution.py:371
  (14 shorter events, 0.1 us)
Async XLA Ops:
  0.8 9.9 %collective-permute-start.2 = (f32[64,128]{1,0:T(8,128)S(1)}, f32[64,128]{1,0:T(8,128)S(1)}, u32[]{:S(2)}, u32[]{:S(2)}) collective-permute-start(f32[64,128]{1,0:T(8,128)S(1)} %bitcast.10), channel_id=1, source_target_pairs={{6,0},{7,1},{4,2},{5,3},{2,4},{3,5},{0,6},{1,7},{14,8},{15,9},{12,... | collective-permute-start | bytes 98312 | tf_op jit(solution)/shard_map/ppermute | solution.py:316
  5.9 4.8 %collective-permute-start.1 = (f32[64,128]{1,0:T(8,128)S(1)}, f32[64,128]{1,0:T(8,128)S(1)}, u32[]{:S(2)}, u32[]{:S(2)}) collective-permute-start(f32[64,128]{1,0:T(8,128)S(1)} %bitcast.11), channel_id=1, source_target_pairs={{4,0},{5,1},{6,2},{7,3},{0,4},{1,5},{2,6},{3,7},{12,8},{13,9},{14,... | collective-permute-start | bytes 98312 | tf_op jit(solution)/shard_map/ppermute | solution.py:316
  5.9 3.9 %collective-permute-start = (f32[64,128]{1,0:T(8,128)S(1)}, f32[64,128]{1,0:T(8,128)S(1)}, u32[]{:S(2)}, u32[]{:S(2)}) collective-permute-start(f32[64,128]{1,0:T(8,128)S(1)} %bitcast.12), channel_id=1, source_target_pairs={{2,0},{3,1},{0,2},{1,3},{6,4},{7,5},{4,6},{5,7},{10,8},{11,9},{8,1... | collective-permute-start | bytes 98312 | tf_op jit(solution)/shard_map/ppermute | solution.py:316
  10.8 5.1 %collective-permute-start.3 = (f32[264,128]{1,0:T(8,128)S(1)}, f32[264,128]{1,0:T(8,128)S(1)}, u32[]{:S(2)}, u32[]{:S(2)}) collective-permute-start(f32[264,128]{1,0:T(8,128)S(1)} %constant_dynamic-update-slice_fusion), channel_id=1, source_target_pairs={{16,0},{17,1},{18,2},{19,3},{20,4},{21,5},{22,6},{23,7},{24,8},{25... | collective-permute-start | bytes 405512 | tf_op jit(solution)/shard_map/ppermute | solution.py:316
  15.9 2.3 %collective-permute-start.5 = (f32[528,128]{1,0:T(8,128)S(1)}, f32[528,128]{1,0:T(8,128)S(1)}, u32[]{:S(2)}, u32[]{:S(2)}) collective-permute-start(f32[528,128]{1,0:T(8,128)S(1)} %constant_dynamic-update-slice_fusion.5.refs_4_), channel_id=1, source_target_pairs={{8,0},{9,1},{10,2},{11,3},{12,4},{13,5},{14,6},{15,7},{0,8},{1,9},... | collective-permute-start | bytes 811016 | tf_op jit(solution)/shard_map/ppermute | solution.py:316
  16.0 6.4 %collective-permute-start.6 = (f32[256,128]{1,0:T(8,128)S(1)}, f32[256,128]{1,0:T(8,128)S(1)}, u32[]{:S(2)}, u32[]{:S(2)}) collective-permute-start(f32[256,128]{1,0:T(8,128)S(1)} %pad_maximum_fusion.1), channel_id=1, source_target_pairs={{1,0},{0,1},{3,2},{2,3},{5,4},{4,5},{7,6},{6,7},{9,8},{8,9},{11,10... | collective-permute-start | bytes 393224 | tf_op jit(solution)/shard_map/ppermute | solution.py:316
  17.6 7.2 %collective-permute-start.4 = (f32[256,128]{1,0:T(8,128)S(1)}, f32[256,128]{1,0:T(8,128)S(1)}, u32[]{:S(2)}, u32[]{:S(2)}) collective-permute-start(f32[256,128]{1,0:T(8,128)S(1)} %pad_maximum_fusion), channel_id=1, source_target_pairs={{1,0},{0,1},{3,2},{2,3},{5,4},{4,5},{7,6},{6,7},{9,8},{8,9},{11,10... | collective-permute-start | bytes 393224 | tf_op jit(solution)/shard_map/ppermute | solution.py:316
  22.3 2.4 %collective-permute-start.8 = (f32[256,128]{1,0:T(8,128)S(1)}, f32[256,128]{1,0:T(8,128)S(1)}, u32[]{:S(2)}, u32[]{:S(2)}) collective-permute-start(f32[256,128]{1,0:T(8,128)S(1)} %collective-permute-done.6.refs_4_), channel_id=1, source_target_pairs={{8,0},{9,1},{10,2},{11,3},{12,4},{13,5},{14,6},{15,7},{0,8},{1,9},... | collective-permute-start | bytes 393224 | tf_op jit(solution)/shard_map/ppermute | solution.py:316
  24.7 1.9 %collective-permute-start.7 = (f32[256,128]{1,0:T(8,128)S(1)}, f32[256,128]{1,0:T(8,128)S(1)}, u32[]{:S(2)}, u32[]{:S(2)}) collective-permute-start(f32[256,128]{1,0:T(8,128)S(1)} %collective-permute-done.4.refs_4_), channel_id=1, source_target_pairs={{8,0},{9,1},{10,2},{11,3},{12,4},{13,5},{14,6},{15,7},{0,8},{1,9},... | collective-permute-start | bytes 393224 | tf_op jit(solution)/shard_map/ppermute | solution.py:316

commit v10 on v9

--- a/solution.py
+++ b/solution.py
@@ -316,24 +316,18 @@
     return lax.ppermute(block, ("grp", "freq"), route)
 
 
-def exchange(column, depth, parts, ready):
+def exchange(column, ready):
     groups = lax.axis_size("grp")
     if groups != 4:
         near = [column] + [fetched(column, move, 0) for move in range(1, groups)]
         layout = [(move, 0, move) for move in range(groups)]
-        fars = [
-            [fetched(column[first * depth : last * depth], move, 1) for move in range(groups)]
-            for first, last in parts
-        ]
-        return near, layout, fars, ready
-    across, *ready = lax.optimization_barrier((fetched(column, 2, 0), *ready))
+        far = [fetched(column, move, 1) for move in range(groups)]
+        return near, layout, far, ready
+    across, beside = fetched(column, 2, 0), fetched(column, 0, 1)
+    across, beside, *ready = lax.optimization_barrier((across, beside, *ready))
     near = jnp.concatenate([column, across], axis=0)
     near = [near, fetched(near, 1, 0)]
-    fars = []
-    for first, last in parts:
-        rows = slice(first * depth, last * depth)
-        fars.append([fetched(jnp.concatenate([column[rows], across[rows]], axis=0), 0, 1)])
-    return near, two_columns(column.shape[0]), fars, ready
+    return near, two_columns(column.shape[0]), [beside, fetched(across, 0, 1)], ready
 
 
 def two_columns(rows):
@@ -342,8 +336,9 @@
 
 def across_cores(far):
     if lax.axis_size("grp") != 4:
-        return far, [(move, 0, move) for move in range(len(far))]
-    return [far[0], fetched(far[0], 1, 0)], two_columns(far[0].shape[0] // 2)
+        return far
+    far = jnp.concatenate(far, axis=0)
+    return [far, fetched(far, 1, 0)]
 
 
 def per_device(spectra, station_mask, owners):
@@ -419,8 +414,7 @@
         table_cost,
     )
     depth = 2 * chunks * stations
-    parts = [(0, steps // 2), (steps // 2, steps)]
-    near, layout, fars, far_table = exchange(column, depth, parts, far_table)
+    near, layout, far, far_table = exchange(column, far_table)
 
     sizes = (groups, stations, rounds, slots, band_bins)
     spectrum = pltpu.VMEM((groups, 2 * chunks, stations, LANES), jnp.float32)
@@ -436,18 +430,6 @@
     index = pltpu.VMEM((rows, LANES), jnp.int32)
     near_table = [near_table[place] for place in (2, 3, 0, 1)]
     far_table = [far_table[place] for place in (2, 3, 0, 1)]
-
-    def more(name, layout, arrays, tables, first_step, last_step, place_step, sums):
-        some = [(step, step - place_step) for step in range(first_step, last_step)]
-        return call(
-            functools.partial(next_kernel, sizes, layout, len(arrays), some),
-            name,
-            [me],
-            [*tables, *arrays, first, second, *sums],
-            [total] * 2,
-            scratch,
-            cost(len(some)),
-        )
 
     split = steps - steps // 4
     first, second, weight, even, odd = call(
@@ -461,21 +443,27 @@
         scratch,
         cost(split),
     )
-    *far, even = lax.optimization_barrier((*fars[0], even))
-    far, far_layout = across_cores(far)
-    even, odd = more("near_next", layout, near, near_table, split, steps, 0, (even, odd))
-    *last, even = lax.optimization_barrier((*fars[1], even))
-    last, _ = across_cores(last)
-    even, odd = more("far_first", far_layout, far, far_table, *parts[0], 0, (even, odd))
-    some = [(step, step - parts[1][0]) for step in range(*parts[1])]
+    *far, even = lax.optimization_barrier((*far, even))
+    far = across_cores(far)
+    even, odd = call(
+        functools.partial(
+            next_kernel, sizes, layout, len(near), [(i, i) for i in range(split, steps)]
+        ),
+        "near_next",
+        [me],
+        [*near_table, *near, first, second, even, odd],
+        [total] * 2,
+        scratch,
+        cost(steps - split),
+    )
     out = call(
-        functools.partial(last_kernel, sizes, far_layout, len(last), some),
-        "far_next",
+        functools.partial(last_kernel, sizes, layout, len(far), [(i, i) for i in range(steps)]),
+        "far_bands",
         [me],
-        [*far_table, *last, first, second, even, odd, weight],
+        [*far_table, *far, first, second, even, odd, weight],
         jax.ShapeDtypeStruct((rows, lag_band), jnp.float32),
         [total] * 2 + [half_result] * 2 + [pltpu.SemaphoreType.DMA((2,))] + scratch,
-        cost(len(some)),
+        cost(steps),
     )
     out = out.reshape(1, rounds, groups, slots, lag_band)
     return out[:, :, :, :capacity]

time: 30 us -> 30.4 us (1.013)
  waiting for transfers between devices: 5.86 us -> 6.23 us
    ppermute x9 -> x8, waiting for transfers between devices: 5.86 us -> 6.23 us  [fetched(): return lax.ppermute(block, ('grp', 'freq'), route)]
    pallas_call x6 -> x5, Pallas kernels: 13.3 us -> 13.4 us  [call(): pl.pallas_call(kernel, out_shape=out_shape, in_specs=[scalar] * len(scala...]
    ppermute x9 -> x8, starting transfers between devices: 9.55 us -> 9.55 us  [fetched(): return lax.ppermute(block, ('grp', 'freq'), route)]
  transfers between devices with their start and end apart: 9 -> 8, of which waited for: 5 -> 7; matrix products, arithmetic and copies ran while one was open for 1% -> 0% of each run, Pallas kernels for 34% -> 27%
where the time goes in v10:
time: 30.4 us; the launch traced here: 30.2 us
  Pallas kernels  13.4 us (44%)
  starting transfers between devices  9.55 us (31%)
  waiting for transfers between devices  6.23 us (20%)
  local copies, waits for them, and re-layouts  0.86 us (3%)
    pallas_call x5, Pallas kernels, call(): pl.pallas_call(kernel, out_shape=out_shape, in_specs=[scalar] * len(scala...  13.4 us
    ppermute x8, starting transfers between devices, fetched(): return lax.ppermute(block, ('grp', 'freq'), route)  9.55 us
    ppermute x8, waiting for transfers between devices, fetched(): return lax.ppermute(block, ('grp', 'freq'), route)  6.23 us
    reshape x2, local copies, waits for them, and re-layouts, per_device(): tiles = spectra.reshape(stations, 2, chunks, LANES).transpose(1, 2, 0, 3)  0.8 us
  transfers between devices with their start and end apart: 8, of which 7 were waited for; matrix products, arithmetic and copies ran while one was open for 0% of the time, Pallas kernels for 27%

profile of v10, /device:TPU:0, one launch (start us, length us, event | category | flops | bytes accessed | tf_op | source)
XLA Modules:
  0.0 30.2 jit_solution(855121328499747429)
XLA Ops:
  0.0 0.8 %reshape.12 = f32[8,2,4,128]{3,2,1,0:T(4,128)S(1)} reshape(f32[8,2,512]{2,1,0:T(2,128)} %param.3) | data formatting | bytes 65536 | tf_op jit(solution)/shard_map/reshape | solution.py:380
  0.8 5.1 %collective-permute-start.2 = (f32[64,128]{1,0:T(8,128)S(1)}, f32[64,128]{1,0:T(8,128)S(1)}, u32[]{:S(2)}, u32[]{:S(2)}) collective-permute-start(f32[64,128]{1,0:T(8,128)S(1)} %bitcast.10), channel_id=1, source_target_pairs={{6,0},{7,1},{4,2},{5,3},{2,4},{3,5},{0,6},{1,7},{14,8},{15,9},{12,... | collective-permute-start | bytes 98312 | tf_op jit(solution)/shard_map/ppermute | solution.py:316
  5.9 0.0 collective-permute-start.1
  5.9 0.6 %collective-permute-start = (f32[64,128]{1,0:T(8,128)S(1)}, f32[64,128]{1,0:T(8,128)S(1)}, u32[]{:S(2)}, u32[]{:S(2)}) collective-permute-start(f32[64,128]{1,0:T(8,128)S(1)} %bitcast.12), channel_id=1, source_target_pairs={{2,0},{3,1},{0,2},{1,3},{6,4},{7,5},{4,6},{5,7},{10,8},{11,9},{8,1... | collective-permute-start | bytes 98312 | tf_op jit(solution)/shard_map/ppermute | solution.py:316
  6.6 0.1 pad_add_fusion.me_ref
  6.7 1.9 %near_tables.1 = (bf16[2048,512]{1,0:T(8,128)(2,1)S(1)}, bf16[2048,512]{1,0:T(8,128)(2,1)S(1)}, f32[4,4,128]{2,1,0:T(4,128)S(1)}, f32[4,4,128]{2,1,0:T(4,128)S(1)}, f32[8,128]{1,0:T(8,128)S(1)}) custom-call(s32[4]{0:T(128)S(1)} %multiply_xor_fusion.bands_ref, s32[2]{0:T(128)S(1)} %pad_add_fusion.me_ref, s32[1,2,1,64]{3,2,1,0:T(1,128)} %bitcast.14, ...), custom_call_target="tpu_custom_call" | custom-call | bytes 4194304 | tf_op jit(solution)/shard_map/near_tables/pallas_call | solution.py:366
  8.5 1.3 %collective-permute-done = f32[64,128]{1,0:T(8,128)S(1)} collective-permute-done((f32[64,128]{1,0:T(8,128)S(1)}, f32[64,128]{1,0:T(8,128)S(1)}, u32[]{:S(2)}, u32[]{:S(2)}) %collective-permute-start) | collective-permute-done | bytes 32800 | tf_op jit(solution)/shard_map/ppermute | solution.py:316
  9.8 0.9 %collective-permute-done.1 = f32[64,128]{1,0:T(8,128)S(1)} collective-permute-done((f32[64,128]{1,0:T(8,128)S(1)}, f32[64,128]{1,0:T(8,128)S(1)}, u32[]{:S(2)}, u32[]{:S(2)}) %collective-permute-start.1) | collective-permute-done | bytes 32800 | tf_op jit(solution)/shard_map/ppermute | solution.py:316
  10.7 0.0 collective-permute-done.2
  10.8 1.6 %collective-permute-start.4 = (f32[264,128]{1,0:T(8,128)S(1)}, f32[264,128]{1,0:T(8,128)S(1)}, u32[]{:S(2)}, u32[]{:S(2)}) collective-permute-start(f32[264,128]{1,0:T(8,128)S(1)} %constant_dynamic-update-slice_fusion), channel_id=1, source_target_pairs={{1,0},{0,1},{3,2},{2,3},{5,4},{4,5},{7,6},{6,7},{9,8},{8,9},{11,10... | collective-permute-start | bytes 405512 | tf_op jit(solution)/shard_map/ppermute | solution.py:316
  12.4 1.5 %collective-permute-start.3 = (f32[264,128]{1,0:T(8,128)S(1)}, f32[264,128]{1,0:T(8,128)S(1)}, u32[]{:S(2)}, u32[]{:S(2)}) collective-permute-start(f32[264,128]{1,0:T(8,128)S(1)} %constant_dynamic-update-slice_fusion), channel_id=1, source_target_pairs={{16,0},{17,1},{18,2},{19,3},{20,4},{21,5},{22,6},{23,7},{24,8},{25... | collective-permute-start | bytes 405512 | tf_op jit(solution)/shard_map/ppermute | solution.py:316
  13.8 1.8 %far_tables.1 = (bf16[2048,512]{1,0:T(8,128)(2,1)S(1)}, bf16[2048,512]{1,0:T(8,128)(2,1)S(1)}, f32[4,4,128]{2,1,0:T(4,128)S(1)}, f32[4,4,128]{2,1,0:T(4,128)S(1)}) custom-call(s32[4]{0:T(128)S(1)} %broadcast_xor_fusion.bands_ref, s32[2]{0:T(128)S(1)} %pad_add_fusion.me_ref), custom_call_target="tpu_custom_call" | custom-call | bytes 4194304 | tf_op jit(solution)/shard_map/far_tables/pallas_call | solution.py:366
  15.6 0.2 collective-permute-done.4
  15.8 1.5 %collective-permute-done.3 = f32[264,128]{1,0:T(8,128)S(1)} collective-permute-done((f32[264,128]{1,0:T(8,128)S(1)}, f32[264,128]{1,0:T(8,128)S(1)}, u32[]{:S(2)}, u32[]{:S(2)}) %collective-permute-start.3) | collective-permute-done | bytes 135200 | tf_op jit(solution)/shard_map/ppermute | solution.py:316
  17.4 0.1 collective-permute-start.6
  17.5 0.6 %collective-permute-start.5 = (f32[264,128]{1,0:T(8,128)S(1)}, f32[264,128]{1,0:T(8,128)S(1)}, u32[]{:S(2)}, u32[]{:S(2)}) collective-permute-start(f32[264,128]{1,0:T(8,128)S(1)} %collective-permute-done.3), channel_id=1, source_target_pairs={{1,0},{0,1},{3,2},{2,3},{5,4},{4,5},{7,6},{6,7},{9,8},{8,9},{11,10... | collective-permute-start | bytes 405512 | tf_op jit(solution)/shard_map/ppermute | solution.py:316
  18.0 1.0 %collective-permute-done.6.refs_5_ = f32[528,128]{1,0:T(8,128)S(1)} collective-permute-done((f32[528,128]{1,0:T(8,128)S(1)}, f32[528,128]{1,0:T(8,128)S(1)}, u32[]{:S(2)}, u32[]{:S(2)}) %collective-permute-start.6) | collective-permute-done | bytes 270368 | tf_op jit(solution)/shard_map/ppermute | solution.py:316
  19.0 3.4 %near_first.1 = (s32[256,128]{1,0:T(8,128)S(1)}, s32[256,128]{1,0:T(8,128)S(1)}, f32[256,128]{1,0:T(8,128)S(1)}, f32[256,256]{1,0:T(8,128)S(1)}, f32[256,256]{1,0:T(8,128)S(1)}) custom-call(s32[2]{0:T(128)S(1)} %pad_add_fusion.me_ref, f32[4,4,128]{2,1,0:T(4,128)S(1)} %get-tuple-element.45.refs_0_, f32[4,4,128]{2,1,0:T(4,128)S(1)} %get-tuple-element.46.refs_1_, ...), custom_call_target="tpu_custom_call" | custom-call | flops 1207959552 | bytes 2097152 | tf_op jit(solution)/shard_map/near_first/pallas_call | solution.py:366
  22.3 1.1 %collective-permute-done.5 = f32[264,128]{1,0:T(8,128)S(1)} collective-permute-done((f32[264,128]{1,0:T(8,128)S(1)}, f32[264,128]{1,0:T(8,128)S(1)}, u32[]{:S(2)}, u32[]{:S(2)}) %collective-permute-start.5) | collective-permute-done | bytes 135200 | tf_op jit(solution)/shard_map/ppermute | solution.py:316
  23.5 0.1 collective-permute-start.7
  23.6 1.3 %near_next.1 = (f32[256,256]{1,0:T(8,128)S(1)}, f32[256,256]{1,0:T(8,128)S(1)}) custom-call(s32[2]{0:T(128)S(1)} %pad_add_fusion.me_ref, f32[4,4,128]{2,1,0:T(4,128)S(1)} %get-tuple-element.45.refs_0_, f32[4,4,128]{2,1,0:T(4,128)S(1)} %get-tuple-element.46.refs_1_, bf16[2048,512]{1,0:T(8,128)(2,1)S(1)} %get-tuple-element.47.refs_2_, ...), custom_call_target="tpu_custom_call" | custom-call | flops 402653184 | bytes 2097152 | tf_op jit(solution)/shard_map/near_next/pallas_call | solution.py:366
  24.9 0.2 collective-permute-done.7.refs_5_
  25.1 5.1 %far_bands.1 = f32[256,512]{1,0:T(8,128)} custom-call(s32[2]{0:T(128)S(1)} %pad_add_fusion.me_ref, f32[4,4,128]{2,1,0:T(4,128)S(1)} %get-tuple-element.39.refs_0_, f32[4,4,128]{2,1,0:T(4,128)S(1)} %get-tuple-element.40.refs_1_, bf16[2048,512]{1,0:T(8,128)(2,1)S(1)} %get-tuple-element.41.refs_2_, bf16[2048,512]{1,0:T(8,128)(2,1)S(1)} %get-tuple-element.42.refs_3_, ...), custom_call_target="tpu_custom_call" | custom-call | flops 1610612736 | bytes 2097152 | tf_op jit(solution)/shard_map/far_bands/pallas_call | solution.py:366
  (12 shorter events, 0.1 us)
Async XLA Ops:
  0.8 9.9 %collective-permute-start.2 = (f32[64,128]{1,0:T(8,128)S(1)}, f32[64,128]{1,0:T(8,128)S(1)}, u32[]{:S(2)}, u32[]{:S(2)}) collective-permute-start(f32[64,128]{1,0:T(8,128)S(1)} %bitcast.10), channel_id=1, source_target_pairs={{6,0},{7,1},{4,2},{5,3},{2,4},{3,5},{0,6},{1,7},{14,8},{15,9},{12,... | collective-permute-start | bytes 98312 | tf_op jit(solution)/shard_map/ppermute | solution.py:316
  5.9 4.8 %collective-permute-start.1 = (f32[64,128]{1,0:T(8,128)S(1)}, f32[64,128]{1,0:T(8,128)S(1)}, u32[]{:S(2)}, u32[]{:S(2)}) collective-permute-start(f32[64,128]{1,0:T(8,128)S(1)} %bitcast.11), channel_id=1, source_target_pairs={{4,0},{5,1},{6,2},{7,3},{0,4},{1,5},{2,6},{3,7},{12,8},{13,9},{14,... | collective-permute-start | bytes 98312 | tf_op jit(solution)/shard_map/ppermute | solution.py:316
  5.9 3.9 %collective-permute-start = (f32[64,128]{1,0:T(8,128)S(1)}, f32[64,128]{1,0:T(8,128)S(1)}, u32[]{:S(2)}, u32[]{:S(2)}) collective-permute-start(f32[64,128]{1,0:T(8,128)S(1)} %bitcast.12), channel_id=1, source_target_pairs={{2,0},{3,1},{0,2},{1,3},{6,4},{7,5},{4,6},{5,7},{10,8},{11,9},{8,1... | collective-permute-start | bytes 98312 | tf_op jit(solution)/shard_map/ppermute | solution.py:316
  10.8 5.1 %collective-permute-start.4 = (f32[264,128]{1,0:T(8,128)S(1)}, f32[264,128]{1,0:T(8,128)S(1)}, u32[]{:S(2)}, u32[]{:S(2)}) collective-permute-start(f32[264,128]{1,0:T(8,128)S(1)} %constant_dynamic-update-slice_fusion), channel_id=1, source_target_pairs={{1,0},{0,1},{3,2},{2,3},{5,4},{4,5},{7,6},{6,7},{9,8},{8,9},{11,10... | collective-permute-start | bytes 405512 | tf_op jit(solution)/shard_map/ppermute | solution.py:316
  12.4 5.0 %collective-permute-start.3 = (f32[264,128]{1,0:T(8,128)S(1)}, f32[264,128]{1,0:T(8,128)S(1)}, u32[]{:S(2)}, u32[]{:S(2)}) collective-permute-start(f32[264,128]{1,0:T(8,128)S(1)} %constant_dynamic-update-slice_fusion), channel_id=1, source_target_pairs={{16,0},{17,1},{18,2},{19,3},{20,4},{21,5},{22,6},{23,7},{24,8},{25... | collective-permute-start | bytes 405512 | tf_op jit(solution)/shard_map/ppermute | solution.py:316
  17.4 1.6 %collective-permute-start.6 = (f32[528,128]{1,0:T(8,128)S(1)}, f32[528,128]{1,0:T(8,128)S(1)}, u32[]{:S(2)}, u32[]{:S(2)}) collective-permute-start(f32[528,128]{1,0:T(8,128)S(1)} %constant_dynamic-update-slice_fusion.5.refs_4_), channel_id=1, source_target_pairs={{8,0},{9,1},{10,2},{11,3},{12,4},{13,5},{14,6},{15,7},{0,8},{1,9},... | collective-permute-start | bytes 811016 | tf_op jit(solution)/shard_map/ppermute | solution.py:316
  17.5 6.0 %collective-permute-start.5 = (f32[264,128]{1,0:T(8,128)S(1)}, f32[264,128]{1,0:T(8,128)S(1)}, u32[]{:S(2)}, u32[]{:S(2)}) collective-permute-start(f32[264,128]{1,0:T(8,128)S(1)} %collective-permute-done.3), channel_id=1, source_target_pairs={{1,0},{0,1},{3,2},{2,3},{5,4},{4,5},{7,6},{6,7},{9,8},{8,9},{11,10... | collective-permute-start | bytes 405512 | tf_op jit(solution)/shard_map/ppermute | solution.py:316
  23.5 1.6 %collective-permute-start.7 = (f32[528,128]{1,0:T(8,128)S(1)}, f32[528,128]{1,0:T(8,128)S(1)}, u32[]{:S(2)}, u32[]{:S(2)}) collective-permute-start(f32[528,128]{1,0:T(8,128)S(1)} %constant_dynamic-update-slice_fusion.7.refs_4_), channel_id=1, source_target_pairs={{8,0},{9,1},{10,2},{11,3},{12,4},{13,5},{14,6},{15,7},{0,8},{1,9},... | collective-permute-start | bytes 811016 | tf_op jit(solution)/shard_map/ppermute | solution.py:316

commit v11 on v9

--- a/solution.py
+++ b/solution.py
@@ -162,12 +162,12 @@
     pieces = [(which, start) for which in range(2) for start in range(0, band_bins, bins_at_once)]
 
     def prepare(index):
-        (step, place_step), (held, turned) = steps[index], sets[index % 2][:2]
+        step, (held, turned) = steps[index], sets[index % 2][:2]
         for position, (ref, offset) in enumerate(blocks):
             group = places[position]
             for q in range(chunks):
                 turn_cos, turn_sin = [turn[step, q : q + 1, :] for turn in turn_refs]
-                start = offset + place_step * depth + q * stations
+                start = offset + step * depth + q * stations
                 real = ref[start : start + stations, :]
                 start += chunks * stations
                 imag = ref[start : start + stations, :]
@@ -205,7 +205,7 @@
                         cross[place + 1][rows, lanes] = low
 
     def transform(index, which, start):
-        step, (high, low) = steps[index][0], sets[index % 2][2 + 2 * which : 4 + 2 * which]
+        step, (high, low) = steps[index], sets[index % 2][2 + 2 * which : 4 + 2 * which]
         lanes = slice(start, start + bins_at_once)
         bins = slice(step * band_bins + start, step * band_bins + start + bins_at_once)
         table, total = table_refs[which], sums[which]
@@ -232,33 +232,26 @@
     return blocks, [moved(me, move, groups) for _, _, move in layout]
 
 
-def near_kernel(sizes, layout, array_count, depth, steps, me_ref, *refs):
-    groups, stations, rounds, slots = sizes[:4]
+def pick_kernel(sizes, layout, array_count, me_ref, *refs):
+    groups, stations, rounds, slots, _ = sizes
+    blocks, places = placed_blocks(refs[:array_count], layout, me_ref[0], groups)
+    extras = [ref[offset : offset + SUBLANES, :] for ref, offset in blocks]
+    first, second, weight = refs[array_count:]
+    first[...], second[...], weight[...] = pick_slots(
+        extras, places, me_ref[0], stations, rounds, slots
+    )
+
+
+def band_kernel(sizes, layout, array_count, steps, is_start, me_ref, *refs):
     turn_refs, table_refs, refs = refs[:2], refs[2:4], refs[4:]
     array_refs, refs = refs[:array_count], refs[array_count:]
-    (first, second, weight, even, odd), scratch = refs[:5], refs[5:]
-    blocks, places = placed_blocks(array_refs, layout, me_ref[0], groups)
-    extras = [ref[offset + depth : offset + depth + SUBLANES, :] for ref, offset in blocks]
-    first[...], second[...], weight[...] = pick_slots(
-        extras, places, me_ref[0], stations, rounds, slots
-    )
-    even[...] = jnp.zeros_like(even)
-    odd[...] = jnp.zeros_like(odd)
-    add_bands(
-        sizes, steps, places, turn_refs, table_refs, blocks, (first, second), (even, odd), scratch
-    )
-
-
-def next_kernel(sizes, layout, array_count, steps, me_ref, *refs):
-    turn_refs, table_refs, refs = refs[:2], refs[2:4], refs[4:]
-    array_refs, refs = refs[:array_count], refs[array_count:]
-    (first, second, even_in, odd_in, even, odd), scratch = refs[:6], refs[6:]
-    even[...] = even_in[...]
-    odd[...] = odd_in[...]
+    picks, refs = refs[:2], refs[2:]
+    sums_in, refs = ((), refs) if is_start else (refs[:2], refs[2:])
+    sums, scratch = refs[:2], refs[2:]
+    for place, total in enumerate(sums):
+        total[...] = jnp.zeros_like(total) if is_start else sums_in[place][...]
     blocks, places = placed_blocks(array_refs, layout, me_ref[0], sizes[0])
-    add_bands(
-        sizes, steps, places, turn_refs, table_refs, blocks, (first, second), (even, odd), scratch
-    )
+    add_bands(sizes, steps, places, turn_refs, table_refs, blocks, picks, sums, scratch)
 
 
 def last_kernel(sizes, layout, array_count, steps, me_ref, *refs):
@@ -316,34 +309,19 @@
     return lax.ppermute(block, ("grp", "freq"), route)
 
 
-def exchange(column, depth, parts, ready):
+def across_x(block):
+    return [block, fetched(block, 2, 0)] if lax.axis_size("grp") == 4 else [block]
+
+
+def across_cores(blocks):
     groups = lax.axis_size("grp")
     if groups != 4:
-        near = [column] + [fetched(column, move, 0) for move in range(1, groups)]
-        layout = [(move, 0, move) for move in range(groups)]
-        fars = [
-            [fetched(column[first * depth : last * depth], move, 1) for move in range(groups)]
-            for first, last in parts
-        ]
-        return near, layout, fars, ready
-    across, *ready = lax.optimization_barrier((fetched(column, 2, 0), *ready))
-    near = jnp.concatenate([column, across], axis=0)
-    near = [near, fetched(near, 1, 0)]
-    fars = []
-    for first, last in parts:
-        rows = slice(first * depth, last * depth)
-        fars.append([fetched(jnp.concatenate([column[rows], across[rows]], axis=0), 0, 1)])
-    return near, two_columns(column.shape[0]), fars, ready
-
-
-def two_columns(rows):
-    return [(0, 0, 0), (0, rows, 2), (1, 0, 1), (1, rows, 3)]
-
-
-def across_cores(far):
-    if lax.axis_size("grp") != 4:
-        return far, [(move, 0, move) for move in range(len(far))]
-    return [far[0], fetched(far[0], 1, 0)], two_columns(far[0].shape[0] // 2)
+        arrays = blocks + [fetched(blocks[0], move, 0) for move in range(1, groups)]
+        return arrays, [(move, 0, move) for move in range(groups)]
+    rows = blocks[0].shape[0]
+    both = blocks[0] if len(blocks) == 1 else jnp.concatenate(blocks, axis=0)
+    layout = [(core, part * rows, 2 * part + core) for core in range(2) for part in range(len(blocks))]
+    return [both, fetched(both, 1, 0)], layout
 
 
 def per_device(spectra, station_mask, owners):
@@ -407,8 +385,9 @@
         table_cost,
         [owners.transpose(0, 1, 3, 2), station_mask.reshape(1, stations)],
     )
-    column = jnp.concatenate(column + [extras], axis=0)
-    column, far_bands = lax.optimization_barrier((column, near_bands ^ 1))
+    ahead = across_x(extras)
+    column = jnp.concatenate(column, axis=0)
+    column, far_bands, *ahead = lax.optimization_barrier((column, near_bands ^ 1, *ahead))
     far_table = call(
         functools.partial(far_tables, bin_total),
         "far_tables",
@@ -418,11 +397,29 @@
         [base] * 2,
         table_cost,
     )
-    depth = 2 * chunks * stations
-    parts = [(0, steps // 2), (steps // 2, steps)]
-    near, layout, fars, far_table = exchange(column, depth, parts, far_table)
-
     sizes = (groups, stations, rounds, slots, band_bins)
+    index = pltpu.VMEM((rows, LANES), jnp.int32)
+    ahead, layout = across_cores(ahead)
+    picks = call(
+        functools.partial(pick_kernel, sizes, layout, len(ahead)),
+        "picks",
+        [me],
+        ahead,
+        [index] * 2 + [pltpu.VMEM((rows, LANES), jnp.float32)],
+        [],
+        table_cost,
+    )
+    across, beside = across_x(column), fetched(column, 0, 1)
+    across, beside, far_table, picks = lax.optimization_barrier((across, beside, far_table, picks))
+    near, layout = across_cores(across)
+    split, middle = steps - steps // 4, steps // 2
+    depth = column.shape[0] // steps
+    fars, layout_near = [], layout
+    beside, _ = across_cores([beside])
+    for start, stop in ((0, middle), (middle, steps)):
+        rows_of = slice(start * depth, stop * depth)
+        fars.append([fetched(source[rows_of], 0, 1) for source in across[1:]])
+
     spectrum = pltpu.VMEM((groups, 2 * chunks, stations, LANES), jnp.float32)
     cross = pltpu.VMEM((rows, band_bins), jnp.bfloat16)
     scratch = ([spectrum] * 2 + [cross] * 4) * 2
@@ -433,49 +430,44 @@
 
     total = pltpu.VMEM((rows, half_band), jnp.float32)
     half_result = total if half_band % LANES == 0 else pltpu.VMEM((rows, lag_band), jnp.float32)
-    index = pltpu.VMEM((rows, LANES), jnp.int32)
     near_table = [near_table[place] for place in (2, 3, 0, 1)]
     far_table = [far_table[place] for place in (2, 3, 0, 1)]
 
-    def more(name, layout, arrays, tables, first_step, last_step, place_step, sums):
-        some = [(step, step - place_step) for step in range(first_step, last_step)]
+    def add(name, layout, arrays, tables, some, sums):
         return call(
-            functools.partial(next_kernel, sizes, layout, len(arrays), some),
+            functools.partial(band_kernel, sizes, layout, len(arrays), some, not sums),
             name,
             [me],
-            [*tables, *arrays, first, second, *sums],
+            [*tables, *arrays, *picks[:2], *sums],
             [total] * 2,
             scratch,
             cost(len(some)),
         )
 
-    split = steps - steps // 4
-    first, second, weight, even, odd = call(
-        functools.partial(
-            near_kernel, sizes, layout, len(near), steps * depth, [(i, i) for i in range(split)]
-        ),
-        "near_first",
-        [me],
-        near_table + near,
-        [index] * 2 + [pltpu.VMEM((rows, LANES), jnp.float32)] + [total] * 2,
-        scratch,
-        cost(split),
-    )
-    *far, even = lax.optimization_barrier((*fars[0], even))
-    far, far_layout = across_cores(far)
-    even, odd = more("near_next", layout, near, near_table, split, steps, 0, (even, odd))
-    *last, even = lax.optimization_barrier((*fars[1], even))
-    last, _ = across_cores(last)
-    even, odd = more("far_first", far_layout, far, far_table, *parts[0], 0, (even, odd))
-    some = [(step, step - parts[1][0]) for step in range(*parts[1])]
+    def far_blocks(diagonal, start):
+        arrays = list(beside)
+        layout = [(move, 0, move) for move in range(len(arrays))]
+        for block in diagonal:
+            layout += [(len(arrays) + core, -start * depth, 2 + core) for core in range(2)]
+            arrays += across_cores([block])[0]
+        return layout, arrays
+
+    every = list(range(steps))
+    even, odd = add("near_first", layout_near, near, near_table, every[:split], ())
+    *diagonal, even = lax.optimization_barrier((*fars[0], even))
+    layout, far = far_blocks(diagonal, 0)
+    even, odd = add("near_next", layout_near, near, near_table, every[split:], (even, odd))
+    *diagonal, even = lax.optimization_barrier((*fars[1], even))
+    layout_last, last = far_blocks(diagonal, middle)
+    even, odd = add("far_first", layout, far, far_table, every[:middle], (even, odd))
     out = call(
-        functools.partial(last_kernel, sizes, far_layout, len(last), some),
+        functools.partial(last_kernel, sizes, layout_last, len(last), every[middle:]),
         "far_next",
         [me],
-        [*far_table, *last, first, second, even, odd, weight],
+        [*far_table, *last, *picks[:2], even, odd, picks[2]],
         jax.ShapeDtypeStruct((rows, lag_band), jnp.float32),
         [total] * 2 + [half_result] * 2 + [pltpu.SemaphoreType.DMA((2,))] + scratch,
-        cost(len(some)),
+        cost(steps - middle),
     )
     out = out.reshape(1, rounds, groups, slots, lag_band)
     return out[:, :, :, :capacity]

time: 30 us -> 31.2 us (1.040)
  starting transfers between devices: 9.55 us -> 13.5 us
  waiting for transfers between devices: 5.86 us -> 2.4 us
  Pallas kernels: 13.3 us -> 14 us
    ppermute x9 -> x13, starting transfers between devices: 9.55 us -> 13.5 us  [fetched(): return lax.ppermute(block, ('grp', 'freq'), route)]
    ppermute x9 -> x13, waiting for transfers between devices: 5.86 us -> 2.4 us  [fetched(): return lax.ppermute(block, ('grp', 'freq'), route)]
    pallas_call x6 -> x7, Pallas kernels: 13.3 us -> 14 us  [call(): pl.pallas_call(kernel, out_shape=out_shape, in_specs=[scalar] * len(scala...]
  transfers between devices with their start and end apart: 9 -> 13, of which waited for: 5 -> 2; matrix products, arithmetic and copies ran while one was open for 1% -> 0% of each run, Pallas kernels for 34% -> 35%
where the time goes in v11:
time: 31.2 us; the launch traced here: 31 us
  Pallas kernels  14 us (45%)
  starting transfers between devices  13.5 us (43%)
  waiting for transfers between devices  2.4 us (8%)
  local copies, waits for them, and re-layouts  0.83 us (3%)
    pallas_call x7, Pallas kernels, call(): pl.pallas_call(kernel, out_shape=out_shape, in_specs=[scalar] * len(scala...  14 us
    ppermute x13, starting transfers between devices, fetched(): return lax.ppermute(block, ('grp', 'freq'), route)  13.5 us
    ppermute x13, waiting for transfers between devices, fetched(): return lax.ppermute(block, ('grp', 'freq'), route)  2.4 us
    reshape x2, local copies, waits for them, and re-layouts, per_device(): tiles = spectra.reshape(stations, 2, chunks, LANES).transpose(1, 2, 0, 3)  0.8 us
  transfers between devices with their start and end apart: 13, of which 2 were waited for; matrix products, arithmetic and copies ran while one was open for 0% of the time, Pallas kernels for 35%

profile of v11, /device:TPU:0, one launch (start us, length us, event | category | flops | bytes accessed | tf_op | source)
XLA Modules:
  0.0 31.0 jit_solution(12931487167694170192)
XLA Ops:
  0.0 0.8 %reshape.12 = f32[8,2,4,128]{3,2,1,0:T(4,128)S(1)} reshape(f32[8,2,512]{2,1,0:T(2,128)} %param.3) | data formatting | bytes 65536 | tf_op jit(solution)/shard_map/reshape | solution.py:363
  0.8 3.1 %collective-permute-start = (f32[64,128]{1,0:T(8,128)S(1)}, f32[64,128]{1,0:T(8,128)S(1)}, u32[]{:S(2)}, u32[]{:S(2)}) collective-permute-start(f32[64,128]{1,0:T(8,128)S(1)} %bitcast.10), channel_id=1, source_target_pairs={{2,0},{3,1},{0,2},{1,3},{6,4},{7,5},{4,6},{5,7},{10,8},{11,9},{8,1... | collective-permute-start | bytes 98312 | tf_op jit(solution)/shard_map/ppermute | solution.py:309
  3.9 2.6 %collective-permute-start.1 = (f32[64,128]{1,0:T(8,128)S(1)}, f32[64,128]{1,0:T(8,128)S(1)}, u32[]{:S(2)}, u32[]{:S(2)}) collective-permute-start(f32[64,128]{1,0:T(8,128)S(1)} %bitcast.11), channel_id=1, source_target_pairs={{4,0},{5,1},{6,2},{7,3},{0,4},{1,5},{2,6},{3,7},{12,8},{13,9},{14,... | collective-permute-start | bytes 98312 | tf_op jit(solution)/shard_map/ppermute | solution.py:309
  6.5 0.0 collective-permute-start.2
  6.5 0.1 pad_add_fusion.me_ref
  6.6 1.9 %near_tables.1 = (bf16[2048,512]{1,0:T(8,128)(2,1)S(1)}, bf16[2048,512]{1,0:T(8,128)(2,1)S(1)}, f32[4,4,128]{2,1,0:T(4,128)S(1)}, f32[4,4,128]{2,1,0:T(4,128)S(1)}, f32[8,128]{1,0:T(8,128)S(1)}) custom-call(s32[4]{0:T(128)S(1)} %multiply_xor_fusion.bands_ref, s32[2]{0:T(128)S(1)} %pad_add_fusion.me_ref, s32[1,2,1,64]{3,2,1,0:T(1,128)} %bitcast.14, ...), custom_call_target="tpu_custom_call" | custom-call | bytes 4194304 | tf_op jit(solution)/shard_map/near_tables/pallas_call | solution.py:349
  8.4 1.8 %collective-permute-start.3 = (f32[8,128]{1,0:T(8,128)S(1)}, f32[8,128]{1,0:T(8,128)S(1)}, u32[]{:S(2)}, u32[]{:S(2)}) collective-permute-start(f32[8,128]{1,0:T(8,128)S(1)} %get-tuple-element.48), channel_id=1, source_target_pairs={{16,0},{17,1},{18,2},{19,3},{20,4},{21,5},{22,6},{23,7},{24,8},{25... | collective-permute-start | bytes 12296 | tf_op jit(solution)/shard_map/ppermute | solution.py:309
  10.2 0.0 collective-permute-done
  10.2 0.0 collective-permute-done.1
  10.2 2.0 %collective-permute-done.2 = f32[64,128]{1,0:T(8,128)S(1)} collective-permute-done((f32[64,128]{1,0:T(8,128)S(1)}, f32[64,128]{1,0:T(8,128)S(1)}, u32[]{:S(2)}, u32[]{:S(2)}) %collective-permute-start.2) | collective-permute-done | bytes 32800 | tf_op jit(solution)/shard_map/ppermute | solution.py:309
  12.2 0.0 collective-permute-done.3
  12.2 1.6 %collective-permute-start.4 = (f32[256,128]{1,0:T(8,128)S(1)}, f32[256,128]{1,0:T(8,128)S(1)}, u32[]{:S(2)}, u32[]{:S(2)}) collective-permute-start(f32[256,128]{1,0:T(8,128)S(1)} %pad_maximum_fusion), channel_id=1, source_target_pairs={{16,0},{17,1},{18,2},{19,3},{20,4},{21,5},{22,6},{23,7},{24,8},{25... | collective-permute-start | bytes 393224 | tf_op jit(solution)/shard_map/ppermute | solution.py:309
  13.8 1.5 %collective-permute-start.5 = (f32[256,128]{1,0:T(8,128)S(1)}, f32[256,128]{1,0:T(8,128)S(1)}, u32[]{:S(2)}, u32[]{:S(2)}) collective-permute-start(f32[256,128]{1,0:T(8,128)S(1)} %pad_maximum_fusion), channel_id=1, source_target_pairs={{1,0},{0,1},{3,2},{2,3},{5,4},{4,5},{7,6},{6,7},{9,8},{8,9},{11,10... | collective-permute-start | bytes 393224 | tf_op jit(solution)/shard_map/ppermute | solution.py:309
  15.4 0.0 collective-permute-start.6
  15.4 1.8 %far_tables.1 = (bf16[2048,512]{1,0:T(8,128)(2,1)S(1)}, bf16[2048,512]{1,0:T(8,128)(2,1)S(1)}, f32[4,4,128]{2,1,0:T(4,128)S(1)}, f32[4,4,128]{2,1,0:T(4,128)S(1)}) custom-call(s32[4]{0:T(128)S(1)} %broadcast_xor_fusion.bands_ref, s32[2]{0:T(128)S(1)} %pad_add_fusion.me_ref), custom_call_target="tpu_custom_call" | custom-call | bytes 4194304 | tf_op jit(solution)/shard_map/far_tables/pallas_call | solution.py:349
  17.1 0.0 collective-permute-done.6.refs_1_
  17.1 1.2 %picks.1 = (s32[256,128]{1,0:T(8,128)S(1)}, s32[256,128]{1,0:T(8,128)S(1)}, f32[256,128]{1,0:T(8,128)S(1)}) custom-call(s32[2]{0:T(128)S(1)} %pad_add_fusion.me_ref, f32[16,128]{1,0:T(8,128)S(1)} %constant_dynamic-update-slice_fusion.refs_0_, f32[16,128]{1,0:T(8,128)S(1)} %collective-permute-done.6.refs_1_), custom_call_target="tpu_custom_call" | custom-call | bytes 4194304 | tf_op jit(solution)/shard_map/picks/pallas_call | solution.py:349
  18.4 0.0 collective-permute-done.4
  18.4 0.4 %collective-permute-done.5.refs_4_ = f32[256,128]{1,0:T(8,128)S(1)} collective-permute-done((f32[256,128]{1,0:T(8,128)S(1)}, f32[256,128]{1,0:T(8,128)S(1)}, u32[]{:S(2)}, u32[]{:S(2)}) %collective-permute-start.5) | collective-permute-done | bytes 131104 | tf_op jit(solution)/shard_map/ppermute | solution.py:309
  18.8 0.2 collective-permute-start.9
  19.0 1.5 %collective-permute-start.10 = (f32[128,128]{1,0:T(8,128)S(1)}, f32[128,128]{1,0:T(8,128)S(1)}, u32[]{:S(2)}, u32[]{:S(2)}) collective-permute-start(f32[128,128]{1,0:T(8,128)S(1)} %get-tuple-element.77), channel_id=1, source_target_pairs={{1,0},{0,1},{3,2},{2,3},{5,4},{4,5},{7,6},{6,7},{9,8},{8,9},{11,10... | collective-permute-start | bytes 196616 | tf_op jit(solution)/shard_map/ppermute | solution.py:309
  20.5 0.6 %collective-permute-start.8 = (f32[128,128]{1,0:T(8,128)S(1)}, f32[128,128]{1,0:T(8,128)S(1)}, u32[]{:S(2)}, u32[]{:S(2)}) collective-permute-start(f32[128,128]{1,0:T(8,128)S(1)} %get-tuple-element.78), channel_id=1, source_target_pairs={{1,0},{0,1},{3,2},{2,3},{5,4},{4,5},{7,6},{6,7},{9,8},{8,9},{11,10... | collective-permute-start | bytes 196616 | tf_op jit(solution)/shard_map/ppermute | solution.py:309
  21.1 0.0 collective-permute-start.7
  21.2 0.0 collective-permute-done.9.refs_5_
  21.2 2.8 %near_first.1 = (f32[256,256]{1,0:T(8,128)S(1)}, f32[256,256]{1,0:T(8,128)S(1)}) custom-call(s32[2]{0:T(128)S(1)} %pad_add_fusion.me_ref, f32[4,4,128]{2,1,0:T(4,128)S(1)} %get-tuple-element.59.refs_0_, f32[4,4,128]{2,1,0:T(4,128)S(1)} %get-tuple-element.60.refs_1_, bf16[2048,512]{1,0:T(8,128)(2,1)S(1)} %get-tuple-element.61.refs_2_, ...), custom_call_target="tpu_custom_call" | custom-call | flops 1207959552 | bytes 2097152 | tf_op jit(solution)/shard_map/near_first/pallas_call | solution.py:349
  24.0 0.0 collective-permute-done.10.refs_6_
  24.0 0.6 %collective-permute-start.12 = (f32[128,128]{1,0:T(8,128)S(1)}, f32[128,128]{1,0:T(8,128)S(1)}, u32[]{:S(2)}, u32[]{:S(2)}) collective-permute-start(f32[128,128]{1,0:T(8,128)S(1)} %collective-permute-done.10.refs_6_), channel_id=1, source_target_pairs={{8,0},{9,1},{10,2},{11,3},{12,4},{13,5},{14,6},{15,7},{0,8},{1,9},... | collective-permute-start | bytes 196616 | tf_op jit(solution)/shard_map/ppermute | solution.py:309
  24.6 1.3 %near_next.1 = (f32[256,256]{1,0:T(8,128)S(1)}, f32[256,256]{1,0:T(8,128)S(1)}) custom-call(s32[2]{0:T(128)S(1)} %pad_add_fusion.me_ref, f32[4,4,128]{2,1,0:T(4,128)S(1)} %get-tuple-element.59.refs_0_, f32[4,4,128]{2,1,0:T(4,128)S(1)} %get-tuple-element.60.refs_1_, bf16[2048,512]{1,0:T(8,128)(2,1)S(1)} %get-tuple-element.61.refs_2_, ...), custom_call_target="tpu_custom_call" | custom-call | flops 402653184 | bytes 2097152 | tf_op jit(solution)/shard_map/near_next/pallas_call | solution.py:349
  25.9 0.0 collective-permute-done.8.refs_6_
  25.9 0.1 collective-permute-start.11
  25.9 0.0 collective-permute-done.7.refs_5_
  26.0 0.0 collective-permute-done.12.refs_7_
  26.0 1.8 %far_first.1 = (f32[256,256]{1,0:T(8,128)S(1)}, f32[256,256]{1,0:T(8,128)S(1)}) custom-call(s32[2]{0:T(128)S(1)} %pad_add_fusion.me_ref, f32[4,4,128]{2,1,0:T(4,128)S(1)} %get-tuple-element.53.refs_0_, f32[4,4,128]{2,1,0:T(4,128)S(1)} %get-tuple-element.54.refs_1_, bf16[2048,512]{1,0:T(8,128)(2,1)S(1)} %get-tuple-element.55.refs_2_, ...), custom_call_target="tpu_custom_call" | custom-call | flops 805306368 | bytes 2097152 | tf_op jit(solution)/shard_map/far_first/pallas_call | solution.py:349
  27.8 0.0 collective-permute-done.11.refs_7_
  27.8 3.1 %far_next.1 = f32[256,512]{1,0:T(8,128)} custom-call(s32[2]{0:T(128)S(1)} %pad_add_fusion.me_ref, f32[4,4,128]{2,1,0:T(4,128)S(1)} %get-tuple-element.53.refs_0_, f32[4,4,128]{2,1,0:T(4,128)S(1)} %get-tuple-element.54.refs_1_, bf16[2048,512]{1,0:T(8,128)(2,1)S(1)} %get-tuple-element.55.refs_2_, bf16[2048,512]{1,0:T(8,128)(2,1)S(1)} %get-tuple-element.56.refs_3_, ...), custom_call_target="tpu_custom_call" | custom-call | flops 805306368 | bytes 2097152 | tf_op jit(solution)/shard_map/far_next/pallas_call | solution.py:349
  (9 shorter events, 0.1 us)
Async XLA Ops:
  0.8 9.4 %collective-permute-start = (f32[64,128]{1,0:T(8,128)S(1)}, f32[64,128]{1,0:T(8,128)S(1)}, u32[]{:S(2)}, u32[]{:S(2)}) collective-permute-start(f32[64,128]{1,0:T(8,128)S(1)} %bitcast.10), channel_id=1, source_target_pairs={{2,0},{3,1},{0,2},{1,3},{6,4},{7,5},{4,6},{5,7},{10,8},{11,9},{8,1... | collective-permute-start | bytes 98312 | tf_op jit(solution)/shard_map/ppermute | solution.py:309
  3.9 6.3 %collective-permute-start.1 = (f32[64,128]{1,0:T(8,128)S(1)}, f32[64,128]{1,0:T(8,128)S(1)}, u32[]{:S(2)}, u32[]{:S(2)}) collective-permute-start(f32[64,128]{1,0:T(8,128)S(1)} %bitcast.11), channel_id=1, source_target_pairs={{4,0},{5,1},{6,2},{7,3},{0,4},{1,5},{2,6},{3,7},{12,8},{13,9},{14,... | collective-permute-start | bytes 98312 | tf_op jit(solution)/shard_map/ppermute | solution.py:309
  6.5 5.7 %collective-permute-start.2 = (f32[64,128]{1,0:T(8,128)S(1)}, f32[64,128]{1,0:T(8,128)S(1)}, u32[]{:S(2)}, u32[]{:S(2)}) collective-permute-start(f32[64,128]{1,0:T(8,128)S(1)} %bitcast.12), channel_id=1, source_target_pairs={{6,0},{7,1},{4,2},{5,3},{2,4},{3,5},{0,6},{1,7},{14,8},{15,9},{12,... | collective-permute-start | bytes 98312 | tf_op jit(solution)/shard_map/ppermute | solution.py:309
  8.4 3.8 %collective-permute-start.3 = (f32[8,128]{1,0:T(8,128)S(1)}, f32[8,128]{1,0:T(8,128)S(1)}, u32[]{:S(2)}, u32[]{:S(2)}) collective-permute-start(f32[8,128]{1,0:T(8,128)S(1)} %get-tuple-element.48), channel_id=1, source_target_pairs={{16,0},{17,1},{18,2},{19,3},{20,4},{21,5},{22,6},{23,7},{24,8},{25... | collective-permute-start | bytes 12296 | tf_op jit(solution)/shard_map/ppermute | solution.py:309
  12.2 6.2 %collective-permute-start.4 = (f32[256,128]{1,0:T(8,128)S(1)}, f32[256,128]{1,0:T(8,128)S(1)}, u32[]{:S(2)}, u32[]{:S(2)}) collective-permute-start(f32[256,128]{1,0:T(8,128)S(1)} %pad_maximum_fusion), channel_id=1, source_target_pairs={{16,0},{17,1},{18,2},{19,3},{20,4},{21,5},{22,6},{23,7},{24,8},{25... | collective-permute-start | bytes 393224 | tf_op jit(solution)/shard_map/ppermute | solution.py:309
  13.8 5.0 %collective-permute-start.5 = (f32[256,128]{1,0:T(8,128)S(1)}, f32[256,128]{1,0:T(8,128)S(1)}, u32[]{:S(2)}, u32[]{:S(2)}) collective-permute-start(f32[256,128]{1,0:T(8,128)S(1)} %pad_maximum_fusion), channel_id=1, source_target_pairs={{1,0},{0,1},{3,2},{2,3},{5,4},{4,5},{7,6},{6,7},{9,8},{8,9},{11,10... | collective-permute-start | bytes 393224 | tf_op jit(solution)/shard_map/ppermute | solution.py:309
  15.4 1.8 %collective-permute-start.6 = (f32[16,128]{1,0:T(8,128)S(1)}, f32[16,128]{1,0:T(8,128)S(1)}, u32[]{:S(2)}, u32[]{:S(2)}) collective-permute-start(f32[16,128]{1,0:T(8,128)S(1)} %constant_dynamic-update-slice_fusion.refs_0_), channel_id=1, source_target_pairs={{8,0},{9,1},{10,2},{11,3},{12,4},{13,5},{14,6},{15,7},{0,8},{1,9},... | collective-permute-start | bytes 24584 | tf_op jit(solution)/shard_map/ppermute | solution.py:309
  18.8 2.3 %collective-permute-start.9 = (f32[512,128]{1,0:T(8,128)S(1)}, f32[512,128]{1,0:T(8,128)S(1)}, u32[]{:S(2)}, u32[]{:S(2)}) collective-permute-start(f32[512,128]{1,0:T(8,128)S(1)} %constant_dynamic-update-slice_fusion.2.refs_4_), channel_id=1, source_target_pairs={{8,0},{9,1},{10,2},{11,3},{12,4},{13,5},{14,6},{15,7},{0,8},{1,9},... | collective-permute-start | bytes 786440 | tf_op jit(solution)/shard_map/ppermute | solution.py:309
  19.0 5.0 %collective-permute-start.10 = (f32[128,128]{1,0:T(8,128)S(1)}, f32[128,128]{1,0:T(8,128)S(1)}, u32[]{:S(2)}, u32[]{:S(2)}) collective-permute-start(f32[128,128]{1,0:T(8,128)S(1)} %get-tuple-element.77), channel_id=1, source_target_pairs={{1,0},{0,1},{3,2},{2,3},{5,4},{4,5},{7,6},{6,7},{9,8},{8,9},{11,10... | collective-permute-start | bytes 196616 | tf_op jit(solution)/shard_map/ppermute | solution.py:309
  20.5 5.3 %collective-permute-start.8 = (f32[128,128]{1,0:T(8,128)S(1)}, f32[128,128]{1,0:T(8,128)S(1)}, u32[]{:S(2)}, u32[]{:S(2)}) collective-permute-start(f32[128,128]{1,0:T(8,128)S(1)} %get-tuple-element.78), channel_id=1, source_target_pairs={{1,0},{0,1},{3,2},{2,3},{5,4},{4,5},{7,6},{6,7},{9,8},{8,9},{11,10... | collective-permute-start | bytes 196616 | tf_op jit(solution)/shard_map/ppermute | solution.py:309
  21.1 4.8 %collective-permute-start.7 = (f32[256,128]{1,0:T(8,128)S(1)}, f32[256,128]{1,0:T(8,128)S(1)}, u32[]{:S(2)}, u32[]{:S(2)}) collective-permute-start(f32[256,128]{1,0:T(8,128)S(1)} %collective-permute-done.5.refs_4_), channel_id=1, source_target_pairs={{8,0},{9,1},{10,2},{11,3},{12,4},{13,5},{14,6},{15,7},{0,8},{1,9},... | collective-permute-start | bytes 393224 | tf_op jit(solution)/shard_map/ppermute | solution.py:309
  24.0 2.0 %collective-permute-start.12 = (f32[128,128]{1,0:T(8,128)S(1)}, f32[128,128]{1,0:T(8,128)S(1)}, u32[]{:S(2)}, u32[]{:S(2)}) collective-permute-start(f32[128,128]{1,0:T(8,128)S(1)} %collective-permute-done.10.refs_6_), channel_id=1, source_target_pairs={{8,0},{9,1},{10,2},{11,3},{12,4},{13,5},{14,6},{15,7},{0,8},{1,9},... | collective-permute-start | bytes 196616 | tf_op jit(solution)/shard_map/ppermute | solution.py:309
  25.9 1.9 %collective-permute-start.11 = (f32[128,128]{1,0:T(8,128)S(1)}, f32[128,128]{1,0:T(8,128)S(1)}, u32[]{:S(2)}, u32[]{:S(2)}) collective-permute-start(f32[128,128]{1,0:T(8,128)S(1)} %collective-permute-done.8.refs_6_), channel_id=1, source_target_pairs={{8,0},{9,1},{10,2},{11,3},{12,4},{13,5},{14,6},{15,7},{0,8},{1,9},... | collective-permute-start | bytes 196616 | tf_op jit(solution)/shard_map/ppermute | solution.py:309

commit v12 on v10

--- a/solution.py
+++ b/solution.py
@@ -85,7 +85,8 @@
     return first.astype(jnp.int32), second.astype(jnp.int32), weight
 
 
-def make_tables(bands_ref, place, table_refs, turn_refs, base_refs, bin_total):
+def make_tables(parity, table_refs, turn_refs, base_refs, bin_total):
+    place = lax.axis_index("freq").astype(jnp.int32)
     near_cos, near_sin = base_refs
     fine, half_band = near_cos.shape
     steps, chunks, _ = turn_refs[0].shape
@@ -113,7 +114,7 @@
     centre = 2 * half_band * (2 * place + 1) - 1 - LAGS
     norm = 1.0 / math.sqrt(bin_total)
     for step in range(steps):
-        start = bands_ref[step] * band_bins
+        start = (place ^ (2 * step + parity)) * band_bins
         cos, sin = every(band_bins // fine, start, fine)
         for part in range(band_bins // fine):
             one = slice(part, part + 1)
@@ -126,7 +127,7 @@
             turn[step] = value * norm
 
 
-def near_tables(bin_total, bands_ref, me_ref, owners_hbm, mask_hbm, *refs):
+def near_tables(bin_total, owners_hbm, mask_hbm, *refs):
     table_refs, turn_refs, extras = refs[:2], refs[2:4], refs[4]
     base_refs, (owners_ref, mask_ref, sems) = refs[5:7], refs[7:]
     copies = [
@@ -135,7 +136,7 @@
     ]
     for copy in copies:
         copy.start()
-    make_tables(bands_ref, me_ref[1], table_refs, turn_refs, base_refs, bin_total)
+    make_tables(0, table_refs, turn_refs, base_refs, bin_total)
     for copy in copies:
         copy.wait()
     extras[...] = jnp.zeros_like(extras)
@@ -146,8 +147,8 @@
     extras[rounds : rounds + 1, : mask_ref.shape[1]] = mask_ref[...].astype(jnp.float32)
 
 
-def far_tables(bin_total, bands_ref, me_ref, *refs):
-    make_tables(bands_ref, me_ref[1], refs[:2], refs[2:4], refs[4:], bin_total)
+def far_tables(bin_total, _, *refs):
+    make_tables(1, refs[:2], refs[2:4], refs[4:], bin_total)
 
 
 def add_bands(sizes, steps, places, turn_refs, table_refs, blocks, picks, sums, scratch):
@@ -227,20 +228,21 @@
                 transform(index, *pieces[part])
 
 
-def placed_blocks(array_refs, layout, me, groups):
+def placed_blocks(array_refs, layout, groups):
+    me = lax.axis_index("grp").astype(jnp.int32)
     blocks = [(array_refs[index], offset) for index, offset, _ in layout]
     return blocks, [moved(me, move, groups) for _, _, move in layout]
 
 
-def near_kernel(sizes, layout, array_count, depth, steps, me_ref, *refs):
+def near_kernel(sizes, layout, array_count, depth, steps, *refs):
     groups, stations, rounds, slots = sizes[:4]
     turn_refs, table_refs, refs = refs[:2], refs[2:4], refs[4:]
     array_refs, refs = refs[:array_count], refs[array_count:]
     (first, second, weight, even, odd), scratch = refs[:5], refs[5:]
-    blocks, places = placed_blocks(array_refs, layout, me_ref[0], groups)
+    blocks, places = placed_blocks(array_refs, layout, groups)
     extras = [ref[offset + depth : offset + depth + SUBLANES, :] for ref, offset in blocks]
     first[...], second[...], weight[...] = pick_slots(
-        extras, places, me_ref[0], stations, rounds, slots
+        extras, places, lax.axis_index("grp"), stations, rounds, slots
     )
     even[...] = jnp.zeros_like(even)
     odd[...] = jnp.zeros_like(odd)
@@ -249,25 +251,25 @@
     )
 
 
-def next_kernel(sizes, layout, array_count, steps, me_ref, *refs):
+def next_kernel(sizes, layout, array_count, steps, *refs):
     turn_refs, table_refs, refs = refs[:2], refs[2:4], refs[4:]
     array_refs, refs = refs[:array_count], refs[array_count:]
     (first, second, even_in, odd_in, even, odd), scratch = refs[:6], refs[6:]
     even[...] = even_in[...]
     odd[...] = odd_in[...]
-    blocks, places = placed_blocks(array_refs, layout, me_ref[0], sizes[0])
+    blocks, places = placed_blocks(array_refs, layout, sizes[0])
     add_bands(
         sizes, steps, places, turn_refs, table_refs, blocks, (first, second), (even, odd), scratch
     )
 
 
-def last_kernel(sizes, layout, array_count, steps, me_ref, *refs):
+def last_kernel(sizes, layout, array_count, steps, *refs):
     turn_refs, table_refs, refs = refs[:2], refs[2:4], refs[4:]
     array_refs, refs = refs[:array_count], refs[array_count:]
     first, second, even_in, odd_in, weight, out_ref, even, odd, above, below, sems = refs[:11]
     even[...] = even_in[...]
     odd[...] = odd_in[...]
-    blocks, places = placed_blocks(array_refs, layout, me_ref[0], sizes[0])
+    blocks, places = placed_blocks(array_refs, layout, sizes[0])
     add_bands(
         sizes, steps, places, turn_refs, table_refs, blocks, (first, second), (even, odd), refs[11:]
     )
@@ -355,28 +357,25 @@
     chunks = band_bins // LANES
     rows = rounds * groups * slots
 
-    scalar = pl.BlockSpec(memory_space=pltpu.SMEM)
     vector = pl.BlockSpec(memory_space=pltpu.VMEM)
     in_hbm = pl.BlockSpec(memory_space=pltpu.HBM)
 
-    def call(kernel, name, scalars, arrays, out_shape, scratch, cost, others=()):
+    def call(kernel, name, arrays, out_shape, scratch, cost, others=()):
         arrays = [pltpu.with_memory_space_constraint(array, pltpu.VMEM) for array in arrays]
         others = [pltpu.with_memory_space_constraint(array, pltpu.HBM) for array in others]
         to_hbm = isinstance(out_shape, jax.ShapeDtypeStruct)
         return pl.pallas_call(
             kernel,
             out_shape=out_shape,
-            in_specs=[scalar] * len(scalars) + [in_hbm] * len(others) + [vector] * len(arrays),
+            in_specs=[in_hbm] * len(others) + [vector] * len(arrays),
             out_specs=in_hbm if to_hbm else [vector] * len(out_shape),
             scratch_shapes=scratch,
             compiler_params=pltpu.CompilerParams(vmem_limit_bytes=24 * 1024 * 1024),
             cost_estimate=cost,
             name=name,
-        )(*scalars, *others, *arrays)
+        )(*others, *arrays)
 
     steps = shards // 2
-    me = jnp.stack([lax.axis_index("grp"), lax.axis_index("freq")]).astype(jnp.int32)
-    near_bands = me[1] ^ jnp.arange(0, shards, 2, dtype=jnp.int32)
     tiles = spectra.reshape(stations, 2, chunks, LANES).transpose(1, 2, 0, 3)
     tiles = tiles.reshape(2 * chunks * stations, LANES)
     column = [tiles] + [fetched(tiles, 0, move) for move in range(2, shards, 2)]
@@ -390,7 +389,6 @@
     *near_table, extras = call(
         functools.partial(near_tables, bin_total),
         "near_tables",
-        [near_bands, me],
         [],
         [table] * 2 + [turn] * 2 + [pltpu.VMEM((SUBLANES, LANES), jnp.float32)],
         [base] * 2
@@ -403,12 +401,10 @@
         [owners.transpose(0, 1, 3, 2), station_mask.reshape(1, stations)],
     )
     column = jnp.concatenate(column + [extras], axis=0)
-    column, far_bands = lax.optimization_barrier((column, near_bands ^ 1))
     far_table = call(
         functools.partial(far_tables, bin_total),
         "far_tables",
-        [far_bands, me],
-        [],
+        [column],
         [table] * 2 + [turn] * 2,
         [base] * 2,
         table_cost,
@@ -437,7 +433,6 @@
             near_kernel, sizes, layout, len(near), steps * depth, [(i, i) for i in range(split)]
         ),
         "near_first",
-        [me],
         near_table + near,
         [index] * 2 + [pltpu.VMEM((rows, LANES), jnp.float32)] + [total] * 2,
         scratch,
@@ -450,7 +445,6 @@
             next_kernel, sizes, layout, len(near), [(i, i) for i in range(split, steps)]
         ),
         "near_next",
-        [me],
         [*near_table, *near, first, second, even, odd],
         [total] * 2,
         scratch,
@@ -459,7 +453,6 @@
     out = call(
         functools.partial(last_kernel, sizes, layout, len(far), [(i, i) for i in range(steps)]),
         "far_bands",
-        [me],
         [*far_table, *far, first, second, even, odd, weight],
         jax.ShapeDtypeStruct((rows, lag_band), jnp.float32),
         [total] * 2 + [half_result] * 2 + [pltpu.SemaphoreType.DMA((2,))] + scratch,

time: 30.4 us -> 29.8 us (0.980)
  Pallas kernels: 13.4 us -> 10.5 us
  waiting for transfers between devices: 6.23 us -> 8.62 us
    pallas_call x5, Pallas kernels: 13.4 us -> 10.5 us  [call(): pl.pallas_call(kernel, out_shape=out_shape, in_specs=[in_hbm] * len(other...]
    ppermute x8, waiting for transfers between devices: 6.23 us -> 8.62 us  [fetched(): return lax.ppermute(block, ('grp', 'freq'), route)]
  transfers between devices with their start and end apart: 8 -> 8, of which waited for: 7 -> 7; matrix products, arithmetic and copies ran while one was open for 0% -> 0% of each run, Pallas kernels for 27% -> 20%
where the time goes in v12:
time: 29.8 us; the launch traced here: 29.7 us
  Pallas kernels  10.5 us (35%)
  starting transfers between devices  9.55 us (32%)
  waiting for transfers between devices  8.62 us (29%)
  local copies, waits for them, and re-layouts  0.86 us (3%)
    pallas_call x5, Pallas kernels, call(): pl.pallas_call(kernel, out_shape=out_shape, in_specs=[in_hbm] * len(other...  10.5 us
    ppermute x8, starting transfers between devices, fetched(): return lax.ppermute(block, ('grp', 'freq'), route)  9.55 us
    ppermute x8, waiting for transfers between devices, fetched(): return lax.ppermute(block, ('grp', 'freq'), route)  8.62 us
    reshape x2, local copies, waits for them, and re-layouts, per_device(): tiles = spectra.reshape(stations, 2, chunks, LANES).transpose(1, 2, 0, 3)  0.8 us
  transfers between devices with their start and end apart: 8, of which 7 were waited for; matrix products, arithmetic and copies ran while one was open for 0% of the time, Pallas kernels for 20%

profile of v12, /device:TPU:0, one launch (start us, length us, event | category | flops | bytes accessed | tf_op | source)
XLA Modules:
  0.0 29.7 jit_solution(3457384465368630973)
XLA Ops:
  0.0 0.8 %reshape.12 = f32[8,2,4,128]{3,2,1,0:T(4,128)S(1)} reshape(f32[8,2,512]{2,1,0:T(2,128)} %param.3) | data formatting | bytes 65536 | tf_op jit(solution)/shard_map/reshape | solution.py:379
  0.8 5.1 %collective-permute-start.2 = (f32[64,128]{1,0:T(8,128)S(1)}, f32[64,128]{1,0:T(8,128)S(1)}, u32[]{:S(2)}, u32[]{:S(2)}) collective-permute-start(f32[64,128]{1,0:T(8,128)S(1)} %bitcast.8), channel_id=1, source_target_pairs={{6,0},{7,1},{4,2},{5,3},{2,4},{3,5},{0,6},{1,7},{14,8},{15,9},{12,... | collective-permute-start | bytes 98312 | tf_op jit(solution)/shard_map/ppermute | solution.py:318
  5.9 0.0 collective-permute-start.1
  5.9 0.6 %collective-permute-start = (f32[64,128]{1,0:T(8,128)S(1)}, f32[64,128]{1,0:T(8,128)S(1)}, u32[]{:S(2)}, u32[]{:S(2)}) collective-permute-start(f32[64,128]{1,0:T(8,128)S(1)} %bitcast.10), channel_id=1, source_target_pairs={{2,0},{3,1},{0,2},{1,3},{6,4},{7,5},{4,6},{5,7},{10,8},{11,9},{8,1... | collective-permute-start | bytes 98312 | tf_op jit(solution)/shard_map/ppermute | solution.py:318
  6.6 1.3 %near_tables.1 = (bf16[2048,512]{1,0:T(8,128)(2,1)S(1)}, bf16[2048,512]{1,0:T(8,128)(2,1)S(1)}, f32[4,4,128]{2,1,0:T(4,128)S(1)}, f32[4,4,128]{2,1,0:T(4,128)S(1)}, f32[8,128]{1,0:T(8,128)S(1)}) custom-call(s32[1,2,1,64]{3,2,1,0:T(1,128)} %bitcast.12, s32[1,8]{1,0:T(1,128)} %bitcast.13), custom_call_target="tpu_custom_call" | custom-call | bytes 4194304 | tf_op jit(solution)/shard_map/near_tables/pallas_call | solution.py:367
  7.9 1.9 %collective-permute-done = f32[64,128]{1,0:T(8,128)S(1)} collective-permute-done((f32[64,128]{1,0:T(8,128)S(1)}, f32[64,128]{1,0:T(8,128)S(1)}, u32[]{:S(2)}, u32[]{:S(2)}) %collective-permute-start) | collective-permute-done | bytes 32800 | tf_op jit(solution)/shard_map/ppermute | solution.py:318
  9.8 0.9 %collective-permute-done.1 = f32[64,128]{1,0:T(8,128)S(1)} collective-permute-done((f32[64,128]{1,0:T(8,128)S(1)}, f32[64,128]{1,0:T(8,128)S(1)}, u32[]{:S(2)}, u32[]{:S(2)}) %collective-permute-start.1) | collective-permute-done | bytes 32800 | tf_op jit(solution)/shard_map/ppermute | solution.py:318
  10.7 0.0 collective-permute-done.2
  10.8 1.6 %collective-permute-start.4 = (f32[264,128]{1,0:T(8,128)S(1)}, f32[264,128]{1,0:T(8,128)S(1)}, u32[]{:S(2)}, u32[]{:S(2)}) collective-permute-start(f32[264,128]{1,0:T(8,128)S(1)} %get-tuple-element.64._), channel_id=1, source_target_pairs={{1,0},{0,1},{3,2},{2,3},{5,4},{4,5},{7,6},{6,7},{9,8},{8,9},{11,10... | collective-permute-start | bytes 405512 | tf_op jit(solution)/shard_map/ppermute | solution.py:318
  12.4 1.5 %collective-permute-start.3 = (f32[264,128]{1,0:T(8,128)S(1)}, f32[264,128]{1,0:T(8,128)S(1)}, u32[]{:S(2)}, u32[]{:S(2)}) collective-permute-start(f32[264,128]{1,0:T(8,128)S(1)} %get-tuple-element.64._), channel_id=1, source_target_pairs={{16,0},{17,1},{18,2},{19,3},{20,4},{21,5},{22,6},{23,7},{24,8},{25... | collective-permute-start | bytes 405512 | tf_op jit(solution)/shard_map/ppermute | solution.py:318
  13.9 1.2 %far_tables.1 = (bf16[2048,512]{1,0:T(8,128)(2,1)S(1)}, bf16[2048,512]{1,0:T(8,128)(2,1)S(1)}, f32[4,4,128]{2,1,0:T(4,128)S(1)}, f32[4,4,128]{2,1,0:T(4,128)S(1)}) custom-call(f32[264,128]{1,0:T(8,128)S(1)} %get-tuple-element.64._), custom_call_target="tpu_custom_call" | custom-call | bytes 4194304 | tf_op jit(solution)/shard_map/far_tables/pallas_call | solution.py:367
  15.1 0.8 %collective-permute-done.4 = f32[264,128]{1,0:T(8,128)S(1)} collective-permute-done((f32[264,128]{1,0:T(8,128)S(1)}, f32[264,128]{1,0:T(8,128)S(1)}, u32[]{:S(2)}, u32[]{:S(2)}) %collective-permute-start.4) | collective-permute-done | bytes 135200 | tf_op jit(solution)/shard_map/ppermute | solution.py:318
  15.9 1.5 %collective-permute-done.3 = f32[264,128]{1,0:T(8,128)S(1)} collective-permute-done((f32[264,128]{1,0:T(8,128)S(1)}, f32[264,128]{1,0:T(8,128)S(1)}, u32[]{:S(2)}, u32[]{:S(2)}) %collective-permute-start.3) | collective-permute-done | bytes 135200 | tf_op jit(solution)/shard_map/ppermute | solution.py:318
  17.4 0.1 collective-permute-start.6
  17.5 0.6 %collective-permute-start.5 = (f32[264,128]{1,0:T(8,128)S(1)}, f32[264,128]{1,0:T(8,128)S(1)}, u32[]{:S(2)}, u32[]{:S(2)}) collective-permute-start(f32[264,128]{1,0:T(8,128)S(1)} %collective-permute-done.3), channel_id=1, source_target_pairs={{1,0},{0,1},{3,2},{2,3},{5,4},{4,5},{7,6},{6,7},{9,8},{8,9},{11,10... | collective-permute-start | bytes 405512 | tf_op jit(solution)/shard_map/ppermute | solution.py:318
  18.0 1.0 %collective-permute-done.6.refs_5_ = f32[528,128]{1,0:T(8,128)S(1)} collective-permute-done((f32[528,128]{1,0:T(8,128)S(1)}, f32[528,128]{1,0:T(8,128)S(1)}, u32[]{:S(2)}, u32[]{:S(2)}) %collective-permute-start.6) | collective-permute-done | bytes 270368 | tf_op jit(solution)/shard_map/ppermute | solution.py:318
  19.0 2.7 %near_first.1 = (s32[256,128]{1,0:T(8,128)S(1)}, s32[256,128]{1,0:T(8,128)S(1)}, f32[256,128]{1,0:T(8,128)S(1)}, f32[256,256]{1,0:T(8,128)S(1)}, f32[256,256]{1,0:T(8,128)S(1)}) custom-call(f32[4,4,128]{2,1,0:T(4,128)S(1)} %get-tuple-element.41.refs_0_, f32[4,4,128]{2,1,0:T(4,128)S(1)} %get-tuple-element.42.refs_1_, ...), custom_call_target="tpu_custom_call" | custom-call | flops 1207959552 | bytes 2097152 | tf_op jit(solution)/shard_map/near_first/pallas_call | solution.py:367
  21.7 1.7 %collective-permute-done.5 = f32[264,128]{1,0:T(8,128)S(1)} collective-permute-done((f32[264,128]{1,0:T(8,128)S(1)}, f32[264,128]{1,0:T(8,128)S(1)}, u32[]{:S(2)}, u32[]{:S(2)}) %collective-permute-start.5) | collective-permute-done | bytes 135200 | tf_op jit(solution)/shard_map/ppermute | solution.py:318
  23.5 0.1 collective-permute-start.7
  23.6 0.7 %near_next.1 = (f32[256,256]{1,0:T(8,128)S(1)}, f32[256,256]{1,0:T(8,128)S(1)}) custom-call(f32[4,4,128]{2,1,0:T(4,128)S(1)} %get-tuple-element.41.refs_0_, f32[4,4,128]{2,1,0:T(4,128)S(1)} %get-tuple-element.42.refs_1_, bf16[2048,512]{1,0:T(8,128)(2,1)S(1)} %get-tuple-element.43.refs_2_, bf16[2048,512]{1,0:T(8,128)(2,1)S(1)} %get-tuple-element.44.refs_3_, ...), custom_call_target="tpu_custom_call" | custom-call | flops 402653184 | bytes 2097152 | tf_op jit(solution)/shard_map/near_next/pallas_call | solution.py:367
  24.3 0.8 %collective-permute-done.7.refs_5_ = f32[528,128]{1,0:T(8,128)S(1)} collective-permute-done((f32[528,128]{1,0:T(8,128)S(1)}, f32[528,128]{1,0:T(8,128)S(1)}, u32[]{:S(2)}, u32[]{:S(2)}) %collective-permute-start.7) | collective-permute-done | bytes 270368 | tf_op jit(solution)/shard_map/ppermute | solution.py:318
  25.1 4.5 %far_bands.1 = f32[256,512]{1,0:T(8,128)} custom-call(f32[4,4,128]{2,1,0:T(4,128)S(1)} %get-tuple-element.35.refs_0_, f32[4,4,128]{2,1,0:T(4,128)S(1)} %get-tuple-element.36.refs_1_, bf16[2048,512]{1,0:T(8,128)(2,1)S(1)} %get-tuple-element.37.refs_2_, bf16[2048,512]{1,0:T(8,128)(2,1)S(1)} %get-tuple-element.38.refs_3_, ...), custom_call_target="tpu_custom_call" | custom-call | flops 1610612736 | bytes 2097152 | tf_op jit(solution)/shard_map/far_bands/pallas_call | solution.py:367
  (9 shorter events, 0.1 us)
Async XLA Ops:
  0.8 9.9 %collective-permute-start.2 = (f32[64,128]{1,0:T(8,128)S(1)}, f32[64,128]{1,0:T(8,128)S(1)}, u32[]{:S(2)}, u32[]{:S(2)}) collective-permute-start(f32[64,128]{1,0:T(8,128)S(1)} %bitcast.8), channel_id=1, source_target_pairs={{6,0},{7,1},{4,2},{5,3},{2,4},{3,5},{0,6},{1,7},{14,8},{15,9},{12,... | collective-permute-start | bytes 98312 | tf_op jit(solution)/shard_map/ppermute | solution.py:318
  5.9 4.8 %collective-permute-start.1 = (f32[64,128]{1,0:T(8,128)S(1)}, f32[64,128]{1,0:T(8,128)S(1)}, u32[]{:S(2)}, u32[]{:S(2)}) collective-permute-start(f32[64,128]{1,0:T(8,128)S(1)} %bitcast.9), channel_id=1, source_target_pairs={{4,0},{5,1},{6,2},{7,3},{0,4},{1,5},{2,6},{3,7},{12,8},{13,9},{14,... | collective-permute-start | bytes 98312 | tf_op jit(solution)/shard_map/ppermute | solution.py:318
  5.9 3.9 %collective-permute-start = (f32[64,128]{1,0:T(8,128)S(1)}, f32[64,128]{1,0:T(8,128)S(1)}, u32[]{:S(2)}, u32[]{:S(2)}) collective-permute-start(f32[64,128]{1,0:T(8,128)S(1)} %bitcast.10), channel_id=1, source_target_pairs={{2,0},{3,1},{0,2},{1,3},{6,4},{7,5},{4,6},{5,7},{10,8},{11,9},{8,1... | collective-permute-start | bytes 98312 | tf_op jit(solution)/shard_map/ppermute | solution.py:318
  10.8 5.1 %collective-permute-start.4 = (f32[264,128]{1,0:T(8,128)S(1)}, f32[264,128]{1,0:T(8,128)S(1)}, u32[]{:S(2)}, u32[]{:S(2)}) collective-permute-start(f32[264,128]{1,0:T(8,128)S(1)} %get-tuple-element.64._), channel_id=1, source_target_pairs={{1,0},{0,1},{3,2},{2,3},{5,4},{4,5},{7,6},{6,7},{9,8},{8,9},{11,10... | collective-permute-start | bytes 405512 | tf_op jit(solution)/shard_map/ppermute | solution.py:318
  12.4 5.0 %collective-permute-start.3 = (f32[264,128]{1,0:T(8,128)S(1)}, f32[264,128]{1,0:T(8,128)S(1)}, u32[]{:S(2)}, u32[]{:S(2)}) collective-permute-start(f32[264,128]{1,0:T(8,128)S(1)} %get-tuple-element.64._), channel_id=1, source_target_pairs={{16,0},{17,1},{18,2},{19,3},{20,4},{21,5},{22,6},{23,7},{24,8},{25... | collective-permute-start | bytes 405512 | tf_op jit(solution)/shard_map/ppermute | solution.py:318
  17.4 1.6 %collective-permute-start.6 = (f32[528,128]{1,0:T(8,128)S(1)}, f32[528,128]{1,0:T(8,128)S(1)}, u32[]{:S(2)}, u32[]{:S(2)}) collective-permute-start(f32[528,128]{1,0:T(8,128)S(1)} %constant_dynamic-update-slice_fusion.5.refs_4_), channel_id=1, source_target_pairs={{8,0},{9,1},{10,2},{11,3},{12,4},{13,5},{14,6},{15,7},{0,8},{1,9},... | collective-permute-start | bytes 811016 | tf_op jit(solution)/shard_map/ppermute | solution.py:318
  17.5 6.0 %collective-permute-start.5 = (f32[264,128]{1,0:T(8,128)S(1)}, f32[264,128]{1,0:T(8,128)S(1)}, u32[]{:S(2)}, u32[]{:S(2)}) collective-permute-start(f32[264,128]{1,0:T(8,128)S(1)} %collective-permute-done.3), channel_id=1, source_target_pairs={{1,0},{0,1},{3,2},{2,3},{5,4},{4,5},{7,6},{6,7},{9,8},{8,9},{11,10... | collective-permute-start | bytes 405512 | tf_op jit(solution)/shard_map/ppermute | solution.py:318
  23.5 1.6 %collective-permute-start.7 = (f32[528,128]{1,0:T(8,128)S(1)}, f32[528,128]{1,0:T(8,128)S(1)}, u32[]{:S(2)}, u32[]{:S(2)}) collective-permute-start(f32[528,128]{1,0:T(8,128)S(1)} %constant_dynamic-update-slice_fusion.11.refs_4_), channel_id=1, source_target_pairs={{8,0},{9,1},{10,2},{11,3},{12,4},{13,5},{14,6},{15,7},{0,8},{1,9},... | collective-permute-start | bytes 811016 | tf_op jit(solution)/shard_map/ppermute | solution.py:318

commit v13 on v12

--- a/solution.py
+++ b/solution.py
@@ -325,22 +325,21 @@
         layout = [(move, 0, move) for move in range(groups)]
         far = [fetched(column, move, 1) for move in range(groups)]
         return near, layout, far, ready
-    across, beside = fetched(column, 2, 0), fetched(column, 0, 1)
-    across, beside, *ready = lax.optimization_barrier((across, beside, *ready))
-    near = jnp.concatenate([column, across], axis=0)
-    near = [near, fetched(near, 1, 0)]
-    return near, two_columns(column.shape[0]), [beside, fetched(across, 0, 1)], ready
-
-
-def two_columns(rows):
-    return [(0, 0, 0), (0, rows, 2), (1, 0, 1), (1, rows, 3)]
+    across, core = fetched(column, 2, 0), fetched(column, 1, 0)
+    beside = fetched(longer(column), 0, 1)
+    across, core, *ready = lax.optimization_barrier((across, core, *ready))
+    near = [column, core, across, fetched(across, 1, 0)]
+    diagonal = fetched(longer(across), 0, 1)
+    far = [beside, fetched(beside, 1, 0), diagonal]
+    return near, [(place, 0, place) for place in range(4)], far, ready
+
+
+def longer(block):
+    return jnp.concatenate([block, block[-SUBLANES:]], axis=0)
 
 
 def across_cores(far):
-    if lax.axis_size("grp") != 4:
-        return far
-    far = jnp.concatenate(far, axis=0)
-    return [far, fetched(far, 1, 0)]
+    return far + [fetched(far[-1], 1, 0)] if lax.axis_size("grp") == 4 else far
 
 
 def per_device(spectra, station_mask, owners):

time: 29.8 us -> 29.1 us (0.977)
  waiting for transfers between devices: 8.62 us -> 6.76 us
  starting transfers between devices: 9.55 us -> 10.7 us
    ppermute x8 -> x10, waiting for transfers between devices: 8.62 us -> 6.76 us  [fetched(): return lax.ppermute(block, ('grp', 'freq'), route)]
    ppermute x8 -> x10, starting transfers between devices: 9.55 us -> 10.7 us  [fetched(): return lax.ppermute(block, ('grp', 'freq'), route)]
  transfers between devices with their start and end apart: 8 -> 10, of which waited for: 7 -> 5; matrix products, arithmetic and copies ran while one was open for 0% -> 0% of each run, Pallas kernels for 20% -> 21%
where the time goes in v13:
time: 29.1 us; the launch traced here: 28.9 us
  starting transfers between devices  10.7 us (37%)
  Pallas kernels  10.5 us (36%)
  waiting for transfers between devices  6.76 us (23%)
  local copies, waits for them, and re-layouts  0.83 us (3%)
    ppermute x10, starting transfers between devices, fetched(): return lax.ppermute(block, ('grp', 'freq'), route)  10.7 us
    pallas_call x5, Pallas kernels, call(): pl.pallas_call(kernel, out_shape=out_shape, in_specs=[in_hbm] * len(other...  10.5 us
    ppermute x10, waiting for transfers between devices, fetched(): return lax.ppermute(block, ('grp', 'freq'), route)  6.76 us
    reshape x2, local copies, waits for them, and re-layouts, per_device(): tiles = spectra.reshape(stations, 2, chunks, LANES).transpose(1, 2, 0, 3)  0.8 us
  transfers between devices with their start and end apart: 10, of which 5 were waited for; matrix products, arithmetic and copies ran while one was open for 0% of the time, Pallas kernels for 21%

profile of v13, /device:TPU:0, one launch (start us, length us, event | category | flops | bytes accessed | tf_op | source)
XLA Modules:
  0.0 28.9 jit_solution(16930566997128096845)
XLA Ops:
  0.0 0.8 %reshape.12 = f32[8,2,4,128]{3,2,1,0:T(4,128)S(1)} reshape(f32[8,2,512]{2,1,0:T(2,128)} %param.3) | data formatting | bytes 65536 | tf_op jit(solution)/shard_map/reshape | solution.py:378
  0.8 5.1 %collective-permute-start.2 = (f32[64,128]{1,0:T(8,128)S(1)}, f32[64,128]{1,0:T(8,128)S(1)}, u32[]{:S(2)}, u32[]{:S(2)}) collective-permute-start(f32[64,128]{1,0:T(8,128)S(1)} %bitcast.8), channel_id=1, source_target_pairs={{6,0},{7,1},{4,2},{5,3},{2,4},{3,5},{0,6},{1,7},{14,8},{15,9},{12,... | collective-permute-start | bytes 98312 | tf_op jit(solution)/shard_map/ppermute | solution.py:318
  5.9 0.0 collective-permute-start.1
  5.9 0.6 %collective-permute-start = (f32[64,128]{1,0:T(8,128)S(1)}, f32[64,128]{1,0:T(8,128)S(1)}, u32[]{:S(2)}, u32[]{:S(2)}) collective-permute-start(f32[64,128]{1,0:T(8,128)S(1)} %bitcast.10), channel_id=1, source_target_pairs={{2,0},{3,1},{0,2},{1,3},{6,4},{7,5},{4,6},{5,7},{10,8},{11,9},{8,1... | collective-permute-start | bytes 98312 | tf_op jit(solution)/shard_map/ppermute | solution.py:318
  6.6 1.3 %near_tables.1 = (bf16[2048,512]{1,0:T(8,128)(2,1)S(1)}, bf16[2048,512]{1,0:T(8,128)(2,1)S(1)}, f32[4,4,128]{2,1,0:T(4,128)S(1)}, f32[4,4,128]{2,1,0:T(4,128)S(1)}, f32[8,128]{1,0:T(8,128)S(1)}) custom-call(s32[1,2,1,64]{3,2,1,0:T(1,128)} %bitcast.12, s32[1,8]{1,0:T(1,128)} %bitcast.13), custom_call_target="tpu_custom_call" | custom-call | bytes 4194304 | tf_op jit(solution)/shard_map/near_tables/pallas_call | solution.py:366
  7.9 1.9 %collective-permute-done = f32[64,128]{1,0:T(8,128)S(1)} collective-permute-done((f32[64,128]{1,0:T(8,128)S(1)}, f32[64,128]{1,0:T(8,128)S(1)}, u32[]{:S(2)}, u32[]{:S(2)}) %collective-permute-start) | collective-permute-done | bytes 32800 | tf_op jit(solution)/shard_map/ppermute | solution.py:318
  9.8 0.9 %collective-permute-done.1 = f32[64,128]{1,0:T(8,128)S(1)} collective-permute-done((f32[64,128]{1,0:T(8,128)S(1)}, f32[64,128]{1,0:T(8,128)S(1)}, u32[]{:S(2)}, u32[]{:S(2)}) %collective-permute-start.1) | collective-permute-done | bytes 32800 | tf_op jit(solution)/shard_map/ppermute | solution.py:318
  10.7 0.0 collective-permute-done.2
  10.8 0.1 collective-permute-start.4
  10.9 1.6 %collective-permute-start.3 = (f32[264,128]{1,0:T(8,128)S(1)}, f32[264,128]{1,0:T(8,128)S(1)}, u32[]{:S(2)}, u32[]{:S(2)}) collective-permute-start(f32[264,128]{1,0:T(8,128)S(1)} %get-tuple-element.66._.refs_4_), channel_id=1, source_target_pairs={{16,0},{17,1},{18,2},{19,3},{20,4},{21,5},{22,6},{23,7},{24,8},{25... | collective-permute-start | bytes 405512 | tf_op jit(solution)/shard_map/ppermute | solution.py:318
  12.4 1.5 %collective-permute-start.5 = (f32[272,128]{1,0:T(8,128)S(1)}, f32[272,128]{1,0:T(8,128)S(1)}, u32[]{:S(2)}, u32[]{:S(2)}) collective-permute-start(f32[272,128]{1,0:T(8,128)S(1)} %get-tuple-element.65), channel_id=1, source_target_pairs={{1,0},{0,1},{3,2},{2,3},{5,4},{4,5},{7,6},{6,7},{9,8},{8,9},{11,10... | collective-permute-start | bytes 417800 | tf_op jit(solution)/shard_map/ppermute | solution.py:318
  13.9 1.2 %far_tables.1 = (bf16[2048,512]{1,0:T(8,128)(2,1)S(1)}, bf16[2048,512]{1,0:T(8,128)(2,1)S(1)}, f32[4,4,128]{2,1,0:T(4,128)S(1)}, f32[4,4,128]{2,1,0:T(4,128)S(1)}) custom-call(f32[264,128]{1,0:T(8,128)S(1)} %get-tuple-element.66._.refs_4_), custom_call_target="tpu_custom_call" | custom-call | bytes 4194304 | tf_op jit(solution)/shard_map/far_tables/pallas_call | solution.py:366
  15.2 0.0 collective-permute-done.4.refs_5_
  15.2 1.7 %collective-permute-done.3.refs_6_ = f32[264,128]{1,0:T(8,128)S(1)} collective-permute-done((f32[264,128]{1,0:T(8,128)S(1)}, f32[264,128]{1,0:T(8,128)S(1)}, u32[]{:S(2)}, u32[]{:S(2)}) %collective-permute-start.3) | collective-permute-done | bytes 135200 | tf_op jit(solution)/shard_map/ppermute | solution.py:318
  16.9 0.0 collective-permute-start.8
  16.9 1.6 %collective-permute-start.7 = (f32[272,128]{1,0:T(8,128)S(1)}, f32[272,128]{1,0:T(8,128)S(1)}, u32[]{:S(2)}, u32[]{:S(2)}) collective-permute-start(f32[272,128]{1,0:T(8,128)S(1)} %pad_maximum_fusion), channel_id=1, source_target_pairs={{1,0},{0,1},{3,2},{2,3},{5,4},{4,5},{7,6},{6,7},{9,8},{8,9},{11,10... | collective-permute-start | bytes 417800 | tf_op jit(solution)/shard_map/ppermute | solution.py:318
  18.5 0.0 collective-permute-done.5.refs_4_
  18.5 0.2 collective-permute-start.6
  18.7 0.0 collective-permute-done.8.refs_7_
  18.7 2.7 %near_first.1 = (s32[256,128]{1,0:T(8,128)S(1)}, s32[256,128]{1,0:T(8,128)S(1)}, f32[256,128]{1,0:T(8,128)S(1)}, f32[256,256]{1,0:T(8,128)S(1)}, f32[256,256]{1,0:T(8,128)S(1)}) custom-call(f32[4,4,128]{2,1,0:T(4,128)S(1)} %get-tuple-element.41.refs_0_, f32[4,4,128]{2,1,0:T(4,128)S(1)} %get-tuple-element.42.refs_1_, ...), custom_call_target="tpu_custom_call" | custom-call | flops 1207959552 | bytes 2097152 | tf_op jit(solution)/shard_map/near_first/pallas_call | solution.py:366
  21.4 1.6 %collective-permute-done.7.refs_6_ = f32[272,128]{1,0:T(8,128)S(1)} collective-permute-done((f32[272,128]{1,0:T(8,128)S(1)}, f32[272,128]{1,0:T(8,128)S(1)}, u32[]{:S(2)}, u32[]{:S(2)}) %collective-permute-start.7) | collective-permute-done | bytes 139296 | tf_op jit(solution)/shard_map/ppermute | solution.py:318
  23.0 0.0 collective-permute-done.6.refs_5_
  23.0 0.0 collective-permute-start.9
  23.0 0.7 %near_next.1 = (f32[256,256]{1,0:T(8,128)S(1)}, f32[256,256]{1,0:T(8,128)S(1)}) custom-call(f32[4,4,128]{2,1,0:T(4,128)S(1)} %get-tuple-element.41.refs_0_, f32[4,4,128]{2,1,0:T(4,128)S(1)} %get-tuple-element.42.refs_1_, bf16[2048,512]{1,0:T(8,128)(2,1)S(1)} %get-tuple-element.43.refs_2_, bf16[2048,512]{1,0:T(8,128)(2,1)S(1)} %get-tuple-element.44.refs_3_, ...), custom_call_target="tpu_custom_call" | custom-call | flops 402653184 | bytes 2097152 | tf_op jit(solution)/shard_map/near_next/pallas_call | solution.py:366
  23.8 0.6 %collective-permute-done.9.refs_7_ = f32[272,128]{1,0:T(8,128)S(1)} collective-permute-done((f32[272,128]{1,0:T(8,128)S(1)}, f32[272,128]{1,0:T(8,128)S(1)}, u32[]{:S(2)}, u32[]{:S(2)}) %collective-permute-start.9) | collective-permute-done | bytes 139296 | tf_op jit(solution)/shard_map/ppermute | solution.py:318
  24.4 4.5 %far_bands.1 = f32[256,512]{1,0:T(8,128)} custom-call(f32[4,4,128]{2,1,0:T(4,128)S(1)} %get-tuple-element.36.refs_0_, f32[4,4,128]{2,1,0:T(4,128)S(1)} %get-tuple-element.37.refs_1_, bf16[2048,512]{1,0:T(8,128)(2,1)S(1)} %get-tuple-element.38.refs_2_, bf16[2048,512]{1,0:T(8,128)(2,1)S(1)} %get-tuple-element.39.refs_3_, ...), custom_call_target="tpu_custom_call" | custom-call | flops 1610612736 | bytes 2097152 | tf_op jit(solution)/shard_map/far_bands/pallas_call | solution.py:366
  (9 shorter events, 0.1 us)
Async XLA Ops:
  0.8 9.9 %collective-permute-start.2 = (f32[64,128]{1,0:T(8,128)S(1)}, f32[64,128]{1,0:T(8,128)S(1)}, u32[]{:S(2)}, u32[]{:S(2)}) collective-permute-start(f32[64,128]{1,0:T(8,128)S(1)} %bitcast.8), channel_id=1, source_target_pairs={{6,0},{7,1},{4,2},{5,3},{2,4},{3,5},{0,6},{1,7},{14,8},{15,9},{12,... | collective-permute-start | bytes 98312 | tf_op jit(solution)/shard_map/ppermute | solution.py:318
  5.9 4.8 %collective-permute-start.1 = (f32[64,128]{1,0:T(8,128)S(1)}, f32[64,128]{1,0:T(8,128)S(1)}, u32[]{:S(2)}, u32[]{:S(2)}) collective-permute-start(f32[64,128]{1,0:T(8,128)S(1)} %bitcast.9), channel_id=1, source_target_pairs={{4,0},{5,1},{6,2},{7,3},{0,4},{1,5},{2,6},{3,7},{12,8},{13,9},{14,... | collective-permute-start | bytes 98312 | tf_op jit(solution)/shard_map/ppermute | solution.py:318
  5.9 3.9 %collective-permute-start = (f32[64,128]{1,0:T(8,128)S(1)}, f32[64,128]{1,0:T(8,128)S(1)}, u32[]{:S(2)}, u32[]{:S(2)}) collective-permute-start(f32[64,128]{1,0:T(8,128)S(1)} %bitcast.10), channel_id=1, source_target_pairs={{2,0},{3,1},{0,2},{1,3},{6,4},{7,5},{4,6},{5,7},{10,8},{11,9},{8,1... | collective-permute-start | bytes 98312 | tf_op jit(solution)/shard_map/ppermute | solution.py:318
  10.8 4.4 %collective-permute-start.4 = (f32[264,128]{1,0:T(8,128)S(1)}, f32[264,128]{1,0:T(8,128)S(1)}, u32[]{:S(2)}, u32[]{:S(2)}) collective-permute-start(f32[264,128]{1,0:T(8,128)S(1)} %get-tuple-element.66._.refs_4_), channel_id=1, source_target_pairs={{8,0},{9,1},{10,2},{11,3},{12,4},{13,5},{14,6},{15,7},{0,8},{1,9},... | collective-permute-start | bytes 405512 | tf_op jit(solution)/shard_map/ppermute | solution.py:318
  10.9 6.0 %collective-permute-start.3 = (f32[264,128]{1,0:T(8,128)S(1)}, f32[264,128]{1,0:T(8,128)S(1)}, u32[]{:S(2)}, u32[]{:S(2)}) collective-permute-start(f32[264,128]{1,0:T(8,128)S(1)} %get-tuple-element.66._.refs_4_), channel_id=1, source_target_pairs={{16,0},{17,1},{18,2},{19,3},{20,4},{21,5},{22,6},{23,7},{24,8},{25... | collective-permute-start | bytes 405512 | tf_op jit(solution)/shard_map/ppermute | solution.py:318
  12.4 6.1 %collective-permute-start.5 = (f32[272,128]{1,0:T(8,128)S(1)}, f32[272,128]{1,0:T(8,128)S(1)}, u32[]{:S(2)}, u32[]{:S(2)}) collective-permute-start(f32[272,128]{1,0:T(8,128)S(1)} %get-tuple-element.65), channel_id=1, source_target_pairs={{1,0},{0,1},{3,2},{2,3},{5,4},{4,5},{7,6},{6,7},{9,8},{8,9},{11,10... | collective-permute-start | bytes 417800 | tf_op jit(solution)/shard_map/ppermute | solution.py:318
  16.9 1.8 %collective-permute-start.8 = (f32[264,128]{1,0:T(8,128)S(1)}, f32[264,128]{1,0:T(8,128)S(1)}, u32[]{:S(2)}, u32[]{:S(2)}) collective-permute-start(f32[264,128]{1,0:T(8,128)S(1)} %collective-permute-done.3.refs_6_), channel_id=1, source_target_pairs={{8,0},{9,1},{10,2},{11,3},{12,4},{13,5},{14,6},{15,7},{0,8},{1,9},... | collective-permute-start | bytes 405512 | tf_op jit(solution)/shard_map/ppermute | solution.py:318
  16.9 6.1 %collective-permute-start.7 = (f32[272,128]{1,0:T(8,128)S(1)}, f32[272,128]{1,0:T(8,128)S(1)}, u32[]{:S(2)}, u32[]{:S(2)}) collective-permute-start(f32[272,128]{1,0:T(8,128)S(1)} %pad_maximum_fusion), channel_id=1, source_target_pairs={{1,0},{0,1},{3,2},{2,3},{5,4},{4,5},{7,6},{6,7},{9,8},{8,9},{11,10... | collective-permute-start | bytes 417800 | tf_op jit(solution)/shard_map/ppermute | solution.py:318
  18.5 4.6 %collective-permute-start.6 = (f32[272,128]{1,0:T(8,128)S(1)}, f32[272,128]{1,0:T(8,128)S(1)}, u32[]{:S(2)}, u32[]{:S(2)}) collective-permute-start(f32[272,128]{1,0:T(8,128)S(1)} %collective-permute-done.5.refs_4_), channel_id=1, source_target_pairs={{8,0},{9,1},{10,2},{11,3},{12,4},{13,5},{14,6},{15,7},{0,8},{1,9},... | collective-permute-start | bytes 417800 | tf_op jit(solution)/shard_map/ppermute | solution.py:318
  23.0 1.4 %collective-permute-start.9 = (f32[272,128]{1,0:T(8,128)S(1)}, f32[272,128]{1,0:T(8,128)S(1)}, u32[]{:S(2)}, u32[]{:S(2)}) collective-permute-start(f32[272,128]{1,0:T(8,128)S(1)} %collective-permute-done.7.refs_6_), channel_id=1, source_target_pairs={{8,0},{9,1},{10,2},{11,3},{12,4},{13,5},{14,6},{15,7},{0,8},{1,9},... | collective-permute-start | bytes 417800 | tf_op jit(solution)/shard_map/ppermute | solution.py:318

commit v14 on v13

--- a/solution.py
+++ b/solution.py
@@ -127,16 +127,17 @@
             turn[step] = value * norm
 
 
-def near_tables(bin_total, owners_hbm, mask_hbm, *refs):
-    table_refs, turn_refs, extras = refs[:2], refs[2:4], refs[4]
-    base_refs, (owners_ref, mask_ref, sems) = refs[5:7], refs[7:]
+def table_kernel(bin_total, owners_hbm, mask_hbm, *refs):
+    near_refs, far_refs, extras = refs[:4], refs[4:8], refs[8]
+    base_refs, (owners_ref, mask_ref, sems) = refs[9:11], refs[11:]
     copies = [
         pltpu.make_async_copy(owners_hbm, owners_ref, sems.at[0]),
         pltpu.make_async_copy(mask_hbm, mask_ref, sems.at[1]),
     ]
     for copy in copies:
         copy.start()
-    make_tables(0, table_refs, turn_refs, base_refs, bin_total)
+    make_tables(0, near_refs[:2], near_refs[2:], base_refs, bin_total)
+    make_tables(1, far_refs[:2], far_refs[2:], base_refs, bin_total)
     for copy in copies:
         copy.wait()
     extras[...] = jnp.zeros_like(extras)
@@ -145,10 +146,6 @@
         lanes = slice(index * pairs, (index + 1) * pairs)
         extras[index : index + 1, lanes] = owners_ref[0, index].astype(jnp.float32)
     extras[rounds : rounds + 1, : mask_ref.shape[1]] = mask_ref[...].astype(jnp.float32)
-
-
-def far_tables(bin_total, _, *refs):
-    make_tables(1, refs[:2], refs[2:4], refs[4:], bin_total)
 
 
 def add_bands(sizes, steps, places, turn_refs, table_refs, blocks, picks, sums, scratch):
@@ -318,28 +315,32 @@
     return lax.ppermute(block, ("grp", "freq"), route)
 
 
-def exchange(column, ready):
+def exchange(column, parts):
     groups = lax.axis_size("grp")
     if groups != 4:
         near = [column] + [fetched(column, move, 0) for move in range(1, groups)]
         layout = [(move, 0, move) for move in range(groups)]
         far = [fetched(column, move, 1) for move in range(groups)]
-        return near, layout, far, ready
+        return near, layout, far, [[] for _ in parts]
     across, core = fetched(column, 2, 0), fetched(column, 1, 0)
     beside = fetched(longer(column), 0, 1)
-    across, core, *ready = lax.optimization_barrier((across, core, *ready))
+    across, core = lax.optimization_barrier((across, core))
     near = [column, core, across, fetched(across, 1, 0)]
-    diagonal = fetched(longer(across), 0, 1)
-    far = [beside, fetched(beside, 1, 0), diagonal]
-    return near, [(place, 0, place) for place in range(4)], far, ready
+    diagonals = [[fetched(longer(across[start:stop]), 0, 1)] for start, stop in parts]
+    far = [beside, fetched(beside, 1, 0)]
+    return near, [(place, 0, place) for place in range(4)], far, diagonals
 
 
 def longer(block):
     return jnp.concatenate([block, block[-SUBLANES:]], axis=0)
 
 
-def across_cores(far):
-    return far + [fetched(far[-1], 1, 0)] if lax.axis_size("grp") == 4 else far
+def across_cores(far, diagonal, first_row):
+    arrays = far + [block for own in diagonal for block in (own, fetched(own, 1, 0))]
+    layout = [
+        (place, 0 if place < len(far) else -first_row, place) for place in range(len(arrays))
+    ]
+    return arrays, layout
 
 
 def per_device(spectra, station_mask, owners):
@@ -385,11 +386,11 @@
     table_cost = pl.CostEstimate(
         flops=0, bytes_accessed=4 * bin_total * half_band, transcendentals=0
     )
-    *near_table, extras = call(
-        functools.partial(near_tables, bin_total),
-        "near_tables",
+    *band_tables, extras = call(
+        functools.partial(table_kernel, bin_total),
+        "tables",
         [],
-        [table] * 2 + [turn] * 2 + [pltpu.VMEM((SUBLANES, LANES), jnp.float32)],
+        ([table] * 2 + [turn] * 2) * 2 + [pltpu.VMEM((SUBLANES, LANES), jnp.float32)],
         [base] * 2
         + [
             pltpu.VMEM((1, rounds, 1, pairs), jnp.int32),
@@ -400,16 +401,10 @@
         [owners.transpose(0, 1, 3, 2), station_mask.reshape(1, stations)],
     )
     column = jnp.concatenate(column + [extras], axis=0)
-    far_table = call(
-        functools.partial(far_tables, bin_total),
-        "far_tables",
-        [column],
-        [table] * 2 + [turn] * 2,
-        [base] * 2,
-        table_cost,
-    )
     depth = 2 * chunks * stations
-    near, layout, far, far_table = exchange(column, far_table)
+    split, middle = steps - steps // 4, steps // 2
+    parts = [(0, middle * depth), (middle * depth, steps * depth)]
+    near, layout, far, diagonals = exchange(column, parts)
 
     sizes = (groups, stations, rounds, slots, band_bins)
     spectrum = pltpu.VMEM((groups, 2 * chunks, stations, LANES), jnp.float32)
@@ -423,10 +418,9 @@
     total = pltpu.VMEM((rows, half_band), jnp.float32)
     half_result = total if half_band % LANES == 0 else pltpu.VMEM((rows, lag_band), jnp.float32)
     index = pltpu.VMEM((rows, LANES), jnp.int32)
-    near_table = [near_table[place] for place in (2, 3, 0, 1)]
-    far_table = [far_table[place] for place in (2, 3, 0, 1)]
-
-    split = steps - steps // 4
+    near_table = [band_tables[place] for place in (2, 3, 0, 1)]
+    far_table = [band_tables[place] for place in (6, 7, 4, 5)]
+
     first, second, weight, even, odd = call(
         functools.partial(
             near_kernel, sizes, layout, len(near), steps * depth, [(i, i) for i in range(split)]
@@ -437,25 +431,30 @@
         scratch,
         cost(split),
     )
-    *far, even = lax.optimization_barrier((*far, even))
-    far = across_cores(far)
-    even, odd = call(
-        functools.partial(
-            next_kernel, sizes, layout, len(near), [(i, i) for i in range(split, steps)]
-        ),
-        "near_next",
-        [*near_table, *near, first, second, even, odd],
-        [total] * 2,
-        scratch,
-        cost(steps - split),
-    )
+    def add(name, layout, arrays, tables, some, sums):
+        return call(
+            functools.partial(next_kernel, sizes, layout, len(arrays), [(i, i) for i in some]),
+            name,
+            [*tables, *arrays, first, second, *sums],
+            [total] * 2,
+            scratch,
+            cost(len(some)),
+        )
+
+    *diagonal, even = lax.optimization_barrier((*diagonals[0], even))
+    far_first, layout_first = across_cores(far, diagonal, parts[0][0])
+    even, odd = add("near_next", layout, near, near_table, range(split, steps), (even, odd))
+    *diagonal, even = lax.optimization_barrier((*diagonals[1], even))
+    far_next, layout_next = across_cores(far, diagonal, parts[1][0])
+    even, odd = add("far_first", layout_first, far_first, far_table, range(middle), (even, odd))
+    some = [(i, i) for i in range(middle, steps)]
     out = call(
-        functools.partial(last_kernel, sizes, layout, len(far), [(i, i) for i in range(steps)]),
-        "far_bands",
-        [*far_table, *far, first, second, even, odd, weight],
+        functools.partial(last_kernel, sizes, layout_next, len(far_next), some),
+        "far_next",
+        [*far_table, *far_next, first, second, even, odd, weight],
         jax.ShapeDtypeStruct((rows, lag_band), jnp.float32),
         [total] * 2 + [half_result] * 2 + [pltpu.SemaphoreType.DMA((2,))] + scratch,
-        cost(steps),
+        cost(len(some)),
     )
     out = out.reshape(1, rounds, groups, slots, lag_band)
     return out[:, :, :, :capacity]

time: 29.1 us -> 28.1 us (0.966)
  waiting for transfers between devices: 6.76 us -> 5.63 us
  starting transfers between devices: 10.7 us -> 11.6 us
  Pallas kernels: 10.5 us -> 9.75 us
    ppermute x10 -> x12, waiting for transfers between devices: 6.76 us -> 5.63 us  [fetched(): return lax.ppermute(block, ('grp', 'freq'), route)]
    ppermute x10 -> x12, starting transfers between devices: 10.7 us -> 11.6 us  [fetched(): return lax.ppermute(block, ('grp', 'freq'), route)]
    pallas_call x5, Pallas kernels: 10.5 us -> 9.75 us  [call(): pl.pallas_call(kernel, out_shape=out_shape, in_specs=[in_hbm] * len(other...]
  transfers between devices with their start and end apart: 10 -> 12, of which waited for: 5 -> 5; matrix products, arithmetic and copies ran while one was open for 0% -> 0% of each run, Pallas kernels for 21% -> 26%
where the time goes in v14:
time: 28.1 us; the launch traced here: 27.9 us
  starting transfers between devices  11.6 us (41%)
  Pallas kernels  9.75 us (35%)
  waiting for transfers between devices  5.63 us (20%)
  local copies, waits for them, and re-layouts  0.84 us (3%)
    ppermute x12, starting transfers between devices, fetched(): return lax.ppermute(block, ('grp', 'freq'), route)  11.6 us
    pallas_call x5, Pallas kernels, call(): pl.pallas_call(kernel, out_shape=out_shape, in_specs=[in_hbm] * len(other...  9.75 us
    ppermute x12, waiting for transfers between devices, fetched(): return lax.ppermute(block, ('grp', 'freq'), route)  5.63 us
    reshape x2, local copies, waits for them, and re-layouts, per_device(): tiles = spectra.reshape(stations, 2, chunks, LANES).transpose(1, 2, 0, 3)  0.8 us
  transfers between devices with their start and end apart: 12, of which 5 were waited for; matrix products, arithmetic and copies ran while one was open for 0% of the time, Pallas kernels for 26%

profile of v14, /device:TPU:0, one launch (start us, length us, event | category | flops | bytes accessed | tf_op | source)
XLA Modules:
  0.0 27.9 jit_solution(8681078325498558034)
XLA Ops:
  0.0 0.8 %reshape.13 = f32[8,2,4,128]{3,2,1,0:T(4,128)S(1)} reshape(f32[8,2,512]{2,1,0:T(2,128)} %param.3) | data formatting | bytes 65536 | tf_op jit(solution)/shard_map/reshape | solution.py:379
  0.8 3.1 %collective-permute-start = (f32[64,128]{1,0:T(8,128)S(1)}, f32[64,128]{1,0:T(8,128)S(1)}, u32[]{:S(2)}, u32[]{:S(2)}) collective-permute-start(f32[64,128]{1,0:T(8,128)S(1)} %bitcast.8), channel_id=1, source_target_pairs={{2,0},{3,1},{0,2},{1,3},{6,4},{7,5},{4,6},{5,7},{10,8},{11,9},{8,1... | collective-permute-start | bytes 98312 | tf_op jit(solution)/shard_map/ppermute | solution.py:315
  3.9 2.6 %collective-permute-start.1 = (f32[64,128]{1,0:T(8,128)S(1)}, f32[64,128]{1,0:T(8,128)S(1)}, u32[]{:S(2)}, u32[]{:S(2)}) collective-permute-start(f32[64,128]{1,0:T(8,128)S(1)} %bitcast.9), channel_id=1, source_target_pairs={{4,0},{5,1},{6,2},{7,3},{0,4},{1,5},{2,6},{3,7},{12,8},{13,9},{14,... | collective-permute-start | bytes 98312 | tf_op jit(solution)/shard_map/ppermute | solution.py:315
  6.5 0.0 collective-permute-start.2
  6.5 2.5 %tables.1 = (bf16[2048,512]{1,0:T(8,128)(2,1)S(1)}, bf16[2048,512]{1,0:T(8,128)(2,1)S(1)}, f32[4,4,128]{2,1,0:T(4,128)S(1)}, f32[4,4,128]{2,1,0:T(4,128)S(1)}, b...) custom-call(s32[1,2,1,64]{3,2,1,0:T(1,128)} %bitcast.12, ...), custom_call_target="tpu_custom_call" | custom-call | bytes 4194304 | tf_op jit(solution)/shard_map/tables/pallas_call | solution.py:367
  9.0 0.0 collective-permute-done
  9.0 0.3 %collective-permute-done.1 = f32[64,128]{1,0:T(8,128)S(1)} collective-permute-done((f32[64,128]{1,0:T(8,128)S(1)}, f32[64,128]{1,0:T(8,128)S(1)}, u32[]{:S(2)}, u32[]{:S(2)}) %collective-permute-start.1) | collective-permute-done | bytes 32800 | tf_op jit(solution)/shard_map/ppermute | solution.py:315
  9.3 2.9 %collective-permute-done.2 = f32[64,128]{1,0:T(8,128)S(1)} collective-permute-done((f32[64,128]{1,0:T(8,128)S(1)}, f32[64,128]{1,0:T(8,128)S(1)}, u32[]{:S(2)}, u32[]{:S(2)}) %collective-permute-start.2) | collective-permute-done | bytes 32800 | tf_op jit(solution)/shard_map/ppermute | solution.py:315
  12.2 1.6 %collective-permute-start.5 = (f32[264,128]{1,0:T(8,128)S(1)}, f32[264,128]{1,0:T(8,128)S(1)}, u32[]{:S(2)}, u32[]{:S(2)}) collective-permute-start(f32[264,128]{1,0:T(8,128)S(1)} %get-tuple-element.65.refs_4_), channel_id=1, source_target_pairs={{16,0},{17,1},{18,2},{19,3},{20,4},{21,5},{22,6},{23,7},{24,8},{25... | collective-permute-start | bytes 405512 | tf_op jit(solution)/shard_map/ppermute | solution.py:315
  13.8 0.0 collective-permute-start.6
  13.8 1.5 %collective-permute-start.3 = (f32[272,128]{1,0:T(8,128)S(1)}, f32[272,128]{1,0:T(8,128)S(1)}, u32[]{:S(2)}, u32[]{:S(2)}) collective-permute-start(f32[272,128]{1,0:T(8,128)S(1)} %constant_dynamic-update-slice_fusion), channel_id=1, source_target_pairs={{1,0},{0,1},{3,2},{2,3},{5,4},{4,5},{7,6},{6,7},{9,8},{8,9},{11,10... | collective-permute-start | bytes 417800 | tf_op jit(solution)/shard_map/ppermute | solution.py:315
  15.3 2.0 %collective-permute-done.5.refs_6_ = f32[264,128]{1,0:T(8,128)S(1)} collective-permute-done((f32[264,128]{1,0:T(8,128)S(1)}, f32[264,128]{1,0:T(8,128)S(1)}, u32[]{:S(2)}, u32[]{:S(2)}) %collective-permute-start.5) | collective-permute-done | bytes 135200 | tf_op jit(solution)/shard_map/ppermute | solution.py:315
  17.3 0.0 collective-permute-done.6.refs_5_
  17.3 0.1 collective-permute-start.8
  17.4 1.6 %collective-permute-start.9 = (f32[136,128]{1,0:T(8,128)S(1)}, f32[136,128]{1,0:T(8,128)S(1)}, u32[]{:S(2)}, u32[]{:S(2)}) collective-permute-start(f32[136,128]{1,0:T(8,128)S(1)} %pad_maximum_fusion.1), channel_id=1, source_target_pairs={{1,0},{0,1},{3,2},{2,3},{5,4},{4,5},{7,6},{6,7},{9,8},{8,9},{11,10... | collective-permute-start | bytes 208904 | tf_op jit(solution)/shard_map/ppermute | solution.py:315
  19.0 0.5 %collective-permute-start.7 = (f32[136,128]{1,0:T(8,128)S(1)}, f32[136,128]{1,0:T(8,128)S(1)}, u32[]{:S(2)}, u32[]{:S(2)}) collective-permute-start(f32[136,128]{1,0:T(8,128)S(1)} %pad_maximum_fusion), channel_id=1, source_target_pairs={{1,0},{0,1},{3,2},{2,3},{5,4},{4,5},{7,6},{6,7},{9,8},{8,9},{11,10... | collective-permute-start | bytes 208904 | tf_op jit(solution)/shard_map/ppermute | solution.py:315
  19.5 0.3 %collective-permute-done.3.refs_4_ = f32[272,128]{1,0:T(8,128)S(1)} collective-permute-done((f32[272,128]{1,0:T(8,128)S(1)}, f32[272,128]{1,0:T(8,128)S(1)}, u32[]{:S(2)}, u32[]{:S(2)}) %collective-permute-start.3) | collective-permute-done | bytes 139296 | tf_op jit(solution)/shard_map/ppermute | solution.py:315
  19.9 0.0 collective-permute-start.4
  19.9 0.0 collective-permute-done.8.refs_7_
  19.9 2.8 %near_first.1 = (s32[256,128]{1,0:T(8,128)S(1)}, s32[256,128]{1,0:T(8,128)S(1)}, f32[256,128]{1,0:T(8,128)S(1)}, f32[256,256]{1,0:T(8,128)S(1)}, f32[256,256]{1,0:T(8,128)S(1)}) custom-call(f32[4,4,128]{2,1,0:T(4,128)S(1)} %get-tuple-element.35.refs_0_, f32[4,4,128]{2,1,0:T(4,128)S(1)} %get-tuple-element.36.refs_1_, ...), custom_call_target="tpu_custom_call" | custom-call | flops 1207959552 | bytes 2097152 | tf_op jit(solution)/shard_map/near_first/pallas_call | solution.py:367
  22.7 0.0 collective-permute-done.9.refs_6_
  22.7 0.6 %collective-permute-start.11 = (f32[136,128]{1,0:T(8,128)S(1)}, f32[136,128]{1,0:T(8,128)S(1)}, u32[]{:S(2)}, u32[]{:S(2)}) collective-permute-start(f32[136,128]{1,0:T(8,128)S(1)} %collective-permute-done.9.refs_6_), channel_id=1, source_target_pairs={{8,0},{9,1},{10,2},{11,3},{12,4},{13,5},{14,6},{15,7},{0,8},{1,9},... | collective-permute-start | bytes 208904 | tf_op jit(solution)/shard_map/ppermute | solution.py:315
  23.2 0.7 %near_next.1 = (f32[256,256]{1,0:T(8,128)S(1)}, f32[256,256]{1,0:T(8,128)S(1)}) custom-call(f32[4,4,128]{2,1,0:T(4,128)S(1)} %get-tuple-element.35.refs_0_, f32[4,4,128]{2,1,0:T(4,128)S(1)} %get-tuple-element.36.refs_1_, bf16[2048,512]{1,0:T(8,128)(2,1)S(1)} %get-tuple-element.37.refs_2_, bf16[2048,512]{1,0:T(8,128)(2,1)S(1)} %get-tuple-element.38.refs_3_, ...), custom_call_target="tpu_custom_call" | custom-call | flops 402653184 | bytes 2097152 | tf_op jit(solution)/shard_map/near_next/pallas_call | solution.py:367
  24.0 0.0 collective-permute-done.7.refs_6_
  24.0 0.1 collective-permute-start.10
  24.1 0.0 collective-permute-done.4.refs_5_
  24.1 0.1 collective-permute-done.11.refs_7_
  24.1 1.2 %far_first.1 = (f32[256,256]{1,0:T(8,128)S(1)}, f32[256,256]{1,0:T(8,128)S(1)}) custom-call(f32[4,4,128]{2,1,0:T(4,128)S(1)} %get-tuple-element.29.refs_0_, f32[4,4,128]{2,1,0:T(4,128)S(1)} %get-tuple-element.30.refs_1_, bf16[2048,512]{1,0:T(8,128)(2,1)S(1)} %get-tuple-element.31.refs_2_, bf16[2048,512]{1,0:T(8,128)(2,1)S(1)} %get-tuple-element.32.refs_3_, ...), custom_call_target="tpu_custom_call" | custom-call | flops 805306368 | bytes 2097152 | tf_op jit(solution)/shard_map/far_first/pallas_call | solution.py:367
  25.4 0.0 collective-permute-done.10.refs_7_
  25.4 2.5 %far_next.1 = f32[256,512]{1,0:T(8,128)} custom-call(f32[4,4,128]{2,1,0:T(4,128)S(1)} %get-tuple-element.29.refs_0_, f32[4,4,128]{2,1,0:T(4,128)S(1)} %get-tuple-element.30.refs_1_, bf16[2048,512]{1,0:T(8,128)(2,1)S(1)} %get-tuple-element.31.refs_2_, bf16[2048,512]{1,0:T(8,128)(2,1)S(1)} %get-tuple-element.32.refs_3_, ...), custom_call_target="tpu_custom_call" | custom-call | flops 805306368 | bytes 2097152 | tf_op jit(solution)/shard_map/far_next/pallas_call | solution.py:367
  (11 shorter events, 0.1 us)
Async XLA Ops:
  0.8 8.2 %collective-permute-start = (f32[64,128]{1,0:T(8,128)S(1)}, f32[64,128]{1,0:T(8,128)S(1)}, u32[]{:S(2)}, u32[]{:S(2)}) collective-permute-start(f32[64,128]{1,0:T(8,128)S(1)} %bitcast.8), channel_id=1, source_target_pairs={{2,0},{3,1},{0,2},{1,3},{6,4},{7,5},{4,6},{5,7},{10,8},{11,9},{8,1... | collective-permute-start | bytes 98312 | tf_op jit(solution)/shard_map/ppermute | solution.py:315
  3.9 5.4 %collective-permute-start.1 = (f32[64,128]{1,0:T(8,128)S(1)}, f32[64,128]{1,0:T(8,128)S(1)}, u32[]{:S(2)}, u32[]{:S(2)}) collective-permute-start(f32[64,128]{1,0:T(8,128)S(1)} %bitcast.9), channel_id=1, source_target_pairs={{4,0},{5,1},{6,2},{7,3},{0,4},{1,5},{2,6},{3,7},{12,8},{13,9},{14,... | collective-permute-start | bytes 98312 | tf_op jit(solution)/shard_map/ppermute | solution.py:315
  6.5 5.7 %collective-permute-start.2 = (f32[64,128]{1,0:T(8,128)S(1)}, f32[64,128]{1,0:T(8,128)S(1)}, u32[]{:S(2)}, u32[]{:S(2)}) collective-permute-start(f32[64,128]{1,0:T(8,128)S(1)} %bitcast.10), channel_id=1, source_target_pairs={{6,0},{7,1},{4,2},{5,3},{2,4},{3,5},{0,6},{1,7},{14,8},{15,9},{12,... | collective-permute-start | bytes 98312 | tf_op jit(solution)/shard_map/ppermute | solution.py:315
  12.2 5.1 %collective-permute-start.5 = (f32[264,128]{1,0:T(8,128)S(1)}, f32[264,128]{1,0:T(8,128)S(1)}, u32[]{:S(2)}, u32[]{:S(2)}) collective-permute-start(f32[264,128]{1,0:T(8,128)S(1)} %get-tuple-element.65.refs_4_), channel_id=1, source_target_pairs={{16,0},{17,1},{18,2},{19,3},{20,4},{21,5},{22,6},{23,7},{24,8},{25... | collective-permute-start | bytes 405512 | tf_op jit(solution)/shard_map/ppermute | solution.py:315
  13.8 3.5 %collective-permute-start.6 = (f32[264,128]{1,0:T(8,128)S(1)}, f32[264,128]{1,0:T(8,128)S(1)}, u32[]{:S(2)}, u32[]{:S(2)}) collective-permute-start(f32[264,128]{1,0:T(8,128)S(1)} %get-tuple-element.65.refs_4_), channel_id=1, source_target_pairs={{8,0},{9,1},{10,2},{11,3},{12,4},{13,5},{14,6},{15,7},{0,8},{1,9},... | collective-permute-start | bytes 405512 | tf_op jit(solution)/shard_map/ppermute | solution.py:315
  13.8 6.1 %collective-permute-start.3 = (f32[272,128]{1,0:T(8,128)S(1)}, f32[272,128]{1,0:T(8,128)S(1)}, u32[]{:S(2)}, u32[]{:S(2)}) collective-permute-start(f32[272,128]{1,0:T(8,128)S(1)} %constant_dynamic-update-slice_fusion), channel_id=1, source_target_pairs={{1,0},{0,1},{3,2},{2,3},{5,4},{4,5},{7,6},{6,7},{9,8},{8,9},{11,10... | collective-permute-start | bytes 417800 | tf_op jit(solution)/shard_map/ppermute | solution.py:315
  17.3 2.5 %collective-permute-start.8 = (f32[264,128]{1,0:T(8,128)S(1)}, f32[264,128]{1,0:T(8,128)S(1)}, u32[]{:S(2)}, u32[]{:S(2)}) collective-permute-start(f32[264,128]{1,0:T(8,128)S(1)} %collective-permute-done.5.refs_6_), channel_id=1, source_target_pairs={{8,0},{9,1},{10,2},{11,3},{12,4},{13,5},{14,6},{15,7},{0,8},{1,9},... | collective-permute-start | bytes 405512 | tf_op jit(solution)/shard_map/ppermute | solution.py:315
  17.4 5.2 %collective-permute-start.9 = (f32[136,128]{1,0:T(8,128)S(1)}, f32[136,128]{1,0:T(8,128)S(1)}, u32[]{:S(2)}, u32[]{:S(2)}) collective-permute-start(f32[136,128]{1,0:T(8,128)S(1)} %pad_maximum_fusion.1), channel_id=1, source_target_pairs={{1,0},{0,1},{3,2},{2,3},{5,4},{4,5},{7,6},{6,7},{9,8},{8,9},{11,10... | collective-permute-start | bytes 208904 | tf_op jit(solution)/shard_map/ppermute | solution.py:315
  19.0 5.0 %collective-permute-start.7 = (f32[136,128]{1,0:T(8,128)S(1)}, f32[136,128]{1,0:T(8,128)S(1)}, u32[]{:S(2)}, u32[]{:S(2)}) collective-permute-start(f32[136,128]{1,0:T(8,128)S(1)} %pad_maximum_fusion), channel_id=1, source_target_pairs={{1,0},{0,1},{3,2},{2,3},{5,4},{4,5},{7,6},{6,7},{9,8},{8,9},{11,10... | collective-permute-start | bytes 208904 | tf_op jit(solution)/shard_map/ppermute | solution.py:315
  19.9 4.2 %collective-permute-start.4 = (f32[272,128]{1,0:T(8,128)S(1)}, f32[272,128]{1,0:T(8,128)S(1)}, u32[]{:S(2)}, u32[]{:S(2)}) collective-permute-start(f32[272,128]{1,0:T(8,128)S(1)} %collective-permute-done.3.refs_4_), channel_id=1, source_target_pairs={{8,0},{9,1},{10,2},{11,3},{12,4},{13,5},{14,6},{15,7},{0,8},{1,9},... | collective-permute-start | bytes 417800 | tf_op jit(solution)/shard_map/ppermute | solution.py:315
  22.7 1.5 %collective-permute-start.11 = (f32[136,128]{1,0:T(8,128)S(1)}, f32[136,128]{1,0:T(8,128)S(1)}, u32[]{:S(2)}, u32[]{:S(2)}) collective-permute-start(f32[136,128]{1,0:T(8,128)S(1)} %collective-permute-done.9.refs_6_), channel_id=1, source_target_pairs={{8,0},{9,1},{10,2},{11,3},{12,4},{13,5},{14,6},{15,7},{0,8},{1,9},... | collective-permute-start | bytes 208904 | tf_op jit(solution)/shard_map/ppermute | solution.py:315
  24.0 1.4 %collective-permute-start.10 = (f32[136,128]{1,0:T(8,128)S(1)}, f32[136,128]{1,0:T(8,128)S(1)}, u32[]{:S(2)}, u32[]{:S(2)}) collective-permute-start(f32[136,128]{1,0:T(8,128)S(1)} %collective-permute-done.7.refs_6_), channel_id=1, source_target_pairs={{8,0},{9,1},{10,2},{11,3},{12,4},{13,5},{14,6},{15,7},{0,8},{1,9},... | collective-permute-start | bytes 208904 | tf_op jit(solution)/shard_map/ppermute | solution.py:315

commit v15 on v14

--- a/solution.py
+++ b/solution.py
@@ -85,12 +85,17 @@
     return first.astype(jnp.int32), second.astype(jnp.int32), weight
 
 
+def band_moves(shards):
+    return [0] + list(range(shards - 2, 0, -2))
+
+
 def make_tables(parity, table_refs, turn_refs, base_refs, bin_total):
     place = lax.axis_index("freq").astype(jnp.int32)
     near_cos, near_sin = base_refs
     fine, half_band = near_cos.shape
     steps, chunks, _ = turn_refs[0].shape
     band_bins = chunks * LANES
+    moves = band_moves(bin_total // band_bins)
 
     def circle(turns):
         angles = (turns & (4 * bin_total - 1)).astype(jnp.float32) * (math.pi / (2 * bin_total))
@@ -114,7 +119,7 @@
     centre = 2 * half_band * (2 * place + 1) - 1 - LAGS
     norm = 1.0 / math.sqrt(bin_total)
     for step in range(steps):
-        start = (place ^ (2 * step + parity)) * band_bins
+        start = (place ^ (moves[step] + parity)) * band_bins
         cos, sin = every(band_bins // fine, start, fine)
         for part in range(band_bins // fine):
             one = slice(part, part + 1)
@@ -207,9 +212,11 @@
         lanes = slice(start, start + bins_at_once)
         bins = slice(step * band_bins + start, step * band_bins + start + bins_at_once)
         table, total = table_refs[which], sums[which]
-        by_high = dot(high[:, lanes], table[bins, :])
-        by_low = dot(low[:, lanes], table[bins, :half])
-        total[...] += by_high[:, :half] + (by_high[:, half:] + by_low)
+        cross, exact = high[:, lanes], table[bins, :half]
+        total[...] += dot(
+            jnp.concatenate([cross, cross, low[:, lanes]], axis=1),
+            jnp.concatenate([exact, table[bins, half:], exact], axis=0),
+        )
 
     prepare(0)
     for part in range(PARTS):
@@ -263,33 +270,25 @@
 def last_kernel(sizes, layout, array_count, steps, *refs):
     turn_refs, table_refs, refs = refs[:2], refs[2:4], refs[4:]
     array_refs, refs = refs[:array_count], refs[array_count:]
-    first, second, even_in, odd_in, weight, out_ref, even, odd, above, below, sems = refs[:11]
+    first, second, even_in, odd_in, weight, out_ref, even, odd, result, sems = refs[:10]
     even[...] = even_in[...]
     odd[...] = odd_in[...]
     blocks, places = placed_blocks(array_refs, layout, sizes[0])
     add_bands(
-        sizes, steps, places, turn_refs, table_refs, blocks, (first, second), (even, odd), refs[11:]
+        sizes, steps, places, turn_refs, table_refs, blocks, (first, second), (even, odd), refs[10:]
     )
     half = even.shape[1]
-    row_weight = weight[:, 0:1]
     mirror = (iota((half, half), 0) + iota((half, half), 1) == half - 1).astype(jnp.bfloat16)
-
-    def mirrored():
-        pieces = [dot(piece, mirror) for piece in split_bf16((even[...] + odd[...]) * row_weight, 3)]
-        return pieces[0] + (pieces[1] + pieces[2])
-
-    if half % LANES:
-        above[:, half:] = (even[...] - odd[...]) * row_weight
-        above[:, :half] = mirrored()
-        copies = [pltpu.make_async_copy(above, out_ref, sems.at[0])]
-        copies[0].start()
-    else:
-        above[...] = (even[...] - odd[...]) * row_weight
-        copies = [pltpu.make_async_copy(above, out_ref.at[:, half:], sems.at[0])]
-        copies[0].start()
-        below[...] = mirrored()
-        copies.append(pltpu.make_async_copy(below, out_ref.at[:, :half], sems.at[1]))
-        copies[1].start()
+    copies = []
+    block = even.shape[0] // PARTS
+    for part in range(PARTS):
+        lines = slice(part * block, (part + 1) * block)
+        row_weight = weight[lines, 0:1]
+        high, low = split_bf16((even[lines, :] + odd[lines, :]) * row_weight, 2)
+        result[lines, :half] = dot(high, mirror) + dot(low, mirror)
+        result[lines, half:] = (even[lines, :] - odd[lines, :]) * row_weight
+        copies.append(pltpu.make_async_copy(result.at[lines], out_ref.at[lines], sems.at[part]))
+        copies[part].start()
     for copy in copies:
         copy.wait()
 
@@ -378,7 +377,7 @@
     steps = shards // 2
     tiles = spectra.reshape(stations, 2, chunks, LANES).transpose(1, 2, 0, 3)
     tiles = tiles.reshape(2 * chunks * stations, LANES)
-    column = [tiles] + [fetched(tiles, 0, move) for move in range(2, shards, 2)]
+    column = [fetched(tiles, 0, move) if move else tiles for move in band_moves(shards)]
 
     table = pltpu.VMEM((steps * band_bins, lag_band), jnp.bfloat16)
     turn = pltpu.VMEM((steps, chunks, LANES), jnp.float32)
@@ -416,7 +415,6 @@
         return pl.CostEstimate(flops=flops, bytes_accessed=2 * 1024 * 1024, transcendentals=0)
 
     total = pltpu.VMEM((rows, half_band), jnp.float32)
-    half_result = total if half_band % LANES == 0 else pltpu.VMEM((rows, lag_band), jnp.float32)
     index = pltpu.VMEM((rows, LANES), jnp.int32)
     near_table = [band_tables[place] for place in (2, 3, 0, 1)]
     far_table = [band_tables[place] for place in (6, 7, 4, 5)]
@@ -453,7 +451,7 @@
         "far_next",
         [*far_table, *far_next, first, second, even, odd, weight],
         jax.ShapeDtypeStruct((rows, lag_band), jnp.float32),
-        [total] * 2 + [half_result] * 2 + [pltpu.SemaphoreType.DMA((2,))] + scratch,
+        [total] * 2 + [pltpu.VMEM((rows, lag_band), jnp.float32), pltpu.SemaphoreType.DMA((PARTS,))] + scratch,
         cost(len(some)),
     )
     out = out.reshape(1, rounds, groups, slots, lag_band)

time: 28.1 us -> 26.3 us (0.936)
  waiting for transfers between devices: 5.63 us -> 4.11 us
  Pallas kernels: 9.75 us -> 9.41 us
    ppermute x12, waiting for transfers between devices: 5.63 us -> 4.11 us  [fetched(): return lax.ppermute(block, ('grp', 'freq'), route)]
    pallas_call x5, Pallas kernels: 9.75 us -> 9.41 us  [call(): pl.pallas_call(kernel, out_shape=out_shape, in_specs=[in_hbm] * len(other...]
  transfers between devices with their start and end apart: 12 -> 12, of which waited for: 5 -> 4; matrix products, arithmetic and copies ran while one was open for 0% -> 0% of each run, Pallas kernels for 26% -> 28%
where the time goes in v15:
time: 26.3 us; the launch traced here: 26.2 us
  starting transfers between devices  11.7 us (44%)
  Pallas kernels  9.41 us (36%)
  waiting for transfers between devices  4.11 us (16%)
  local copies, waits for them, and re-layouts  0.84 us (3%)
    ppermute x12, starting transfers between devices, fetched(): return lax.ppermute(block, ('grp', 'freq'), route)  11.7 us
    pallas_call x5, Pallas kernels, call(): pl.pallas_call(kernel, out_shape=out_shape, in_specs=[in_hbm] * len(other...  9.41 us
    ppermute x12, waiting for transfers between devices, fetched(): return lax.ppermute(block, ('grp', 'freq'), route)  4.11 us
    reshape x2, local copies, waits for them, and re-layouts, per_device(): tiles = spectra.reshape(stations, 2, chunks, LANES).transpose(1, 2, 0, 3)  0.8 us
  transfers between devices with their start and end apart: 12, of which 4 were waited for; matrix products, arithmetic and copies ran while one was open for 0% of the time, Pallas kernels for 28%

profile of v15, /device:TPU:0, one launch (start us, length us, event | category | flops | bytes accessed | tf_op | source)
XLA Modules:
  0.0 26.2 jit_solution(7470973521240657206)
XLA Ops:
  0.0 0.8 %reshape.13 = f32[8,2,4,128]{3,2,1,0:T(4,128)S(1)} reshape(f32[8,2,512]{2,1,0:T(2,128)} %param.3) | data formatting | bytes 65536 | tf_op jit(solution)/shard_map/reshape | solution.py:378
  0.8 5.1 %collective-permute-start = (f32[64,128]{1,0:T(8,128)S(1)}, f32[64,128]{1,0:T(8,128)S(1)}, u32[]{:S(2)}, u32[]{:S(2)}) collective-permute-start(f32[64,128]{1,0:T(8,128)S(1)} %bitcast.8), channel_id=1, source_target_pairs={{6,0},{7,1},{4,2},{5,3},{2,4},{3,5},{0,6},{1,7},{14,8},{15,9},{12,... | collective-permute-start | bytes 98312 | tf_op jit(solution)/shard_map/ppermute | solution.py:314
  5.9 0.0 collective-permute-start.1
  5.9 0.6 %collective-permute-start.2 = (f32[64,128]{1,0:T(8,128)S(1)}, f32[64,128]{1,0:T(8,128)S(1)}, u32[]{:S(2)}, u32[]{:S(2)}) collective-permute-start(f32[64,128]{1,0:T(8,128)S(1)} %bitcast.10), channel_id=1, source_target_pairs={{2,0},{3,1},{0,2},{1,3},{6,4},{7,5},{4,6},{5,7},{10,8},{11,9},{8,1... | collective-permute-start | bytes 98312 | tf_op jit(solution)/shard_map/ppermute | solution.py:314
  6.6 2.4 %tables.1 = (bf16[2048,512]{1,0:T(8,128)(2,1)S(1)}, bf16[2048,512]{1,0:T(8,128)(2,1)S(1)}, f32[4,4,128]{2,1,0:T(4,128)S(1)}, f32[4,4,128]{2,1,0:T(4,128)S(1)}, b...) custom-call(s32[1,2,1,64]{3,2,1,0:T(1,128)} %bitcast.12, ...), custom_call_target="tpu_custom_call" | custom-call | bytes 4194304 | tf_op jit(solution)/shard_map/tables/pallas_call | solution.py:366
  9.0 0.0 collective-permute-done
  9.1 1.7 %collective-permute-done.1 = f32[64,128]{1,0:T(8,128)S(1)} collective-permute-done((f32[64,128]{1,0:T(8,128)S(1)}, f32[64,128]{1,0:T(8,128)S(1)}, u32[]{:S(2)}, u32[]{:S(2)}) %collective-permute-start.1) | collective-permute-done | bytes 32800 | tf_op jit(solution)/shard_map/ppermute | solution.py:314
  10.7 0.0 collective-permute-done.2
  10.8 1.6 %collective-permute-start.5 = (f32[264,128]{1,0:T(8,128)S(1)}, f32[264,128]{1,0:T(8,128)S(1)}, u32[]{:S(2)}, u32[]{:S(2)}) collective-permute-start(f32[264,128]{1,0:T(8,128)S(1)} %get-tuple-element.65.refs_4_), channel_id=1, source_target_pairs={{16,0},{17,1},{18,2},{19,3},{20,4},{21,5},{22,6},{23,7},{24,8},{25... | collective-permute-start | bytes 405512 | tf_op jit(solution)/shard_map/ppermute | solution.py:314
  12.3 0.0 collective-permute-start.6
  12.3 1.5 %collective-permute-start.3 = (f32[272,128]{1,0:T(8,128)S(1)}, f32[272,128]{1,0:T(8,128)S(1)}, u32[]{:S(2)}, u32[]{:S(2)}) collective-permute-start(f32[272,128]{1,0:T(8,128)S(1)} %constant_dynamic-update-slice_fusion), channel_id=1, source_target_pairs={{1,0},{0,1},{3,2},{2,3},{5,4},{4,5},{7,6},{6,7},{9,8},{8,9},{11,10... | collective-permute-start | bytes 417800 | tf_op jit(solution)/shard_map/ppermute | solution.py:314
  13.9 2.0 %collective-permute-done.5.refs_6_ = f32[264,128]{1,0:T(8,128)S(1)} collective-permute-done((f32[264,128]{1,0:T(8,128)S(1)}, f32[264,128]{1,0:T(8,128)S(1)}, u32[]{:S(2)}, u32[]{:S(2)}) %collective-permute-start.5) | collective-permute-done | bytes 135200 | tf_op jit(solution)/shard_map/ppermute | solution.py:314
  15.9 0.0 collective-permute-done.6.refs_5_
  15.9 0.1 collective-permute-start.8
  16.0 1.6 %collective-permute-start.9 = (f32[136,128]{1,0:T(8,128)S(1)}, f32[136,128]{1,0:T(8,128)S(1)}, u32[]{:S(2)}, u32[]{:S(2)}) collective-permute-start(f32[136,128]{1,0:T(8,128)S(1)} %pad_maximum_fusion.1), channel_id=1, source_target_pairs={{1,0},{0,1},{3,2},{2,3},{5,4},{4,5},{7,6},{6,7},{9,8},{8,9},{11,10... | collective-permute-start | bytes 208904 | tf_op jit(solution)/shard_map/ppermute | solution.py:314
  17.6 0.5 %collective-permute-start.7 = (f32[136,128]{1,0:T(8,128)S(1)}, f32[136,128]{1,0:T(8,128)S(1)}, u32[]{:S(2)}, u32[]{:S(2)}) collective-permute-start(f32[136,128]{1,0:T(8,128)S(1)} %pad_maximum_fusion), channel_id=1, source_target_pairs={{1,0},{0,1},{3,2},{2,3},{5,4},{4,5},{7,6},{6,7},{9,8},{8,9},{11,10... | collective-permute-start | bytes 208904 | tf_op jit(solution)/shard_map/ppermute | solution.py:314
  18.1 0.3 %collective-permute-done.3.refs_4_ = f32[272,128]{1,0:T(8,128)S(1)} collective-permute-done((f32[272,128]{1,0:T(8,128)S(1)}, f32[272,128]{1,0:T(8,128)S(1)}, u32[]{:S(2)}, u32[]{:S(2)}) %collective-permute-start.3) | collective-permute-done | bytes 139296 | tf_op jit(solution)/shard_map/ppermute | solution.py:314
  18.4 0.0 collective-permute-start.4
  18.4 0.0 collective-permute-done.8.refs_7_
  18.4 2.8 %near_first.1 = (s32[256,128]{1,0:T(8,128)S(1)}, s32[256,128]{1,0:T(8,128)S(1)}, f32[256,128]{1,0:T(8,128)S(1)}, f32[256,256]{1,0:T(8,128)S(1)}, f32[256,256]{1,0:T(8,128)S(1)}) custom-call(f32[4,4,128]{2,1,0:T(4,128)S(1)} %get-tuple-element.35.refs_0_, f32[4,4,128]{2,1,0:T(4,128)S(1)} %get-tuple-element.36.refs_1_, ...), custom_call_target="tpu_custom_call" | custom-call | flops 1207959552 | bytes 2097152 | tf_op jit(solution)/shard_map/near_first/pallas_call | solution.py:366
  21.2 0.0 collective-permute-done.9.refs_6_
  21.2 0.6 %collective-permute-start.11 = (f32[136,128]{1,0:T(8,128)S(1)}, f32[136,128]{1,0:T(8,128)S(1)}, u32[]{:S(2)}, u32[]{:S(2)}) collective-permute-start(f32[136,128]{1,0:T(8,128)S(1)} %collective-permute-done.9.refs_6_), channel_id=1, source_target_pairs={{8,0},{9,1},{10,2},{11,3},{12,4},{13,5},{14,6},{15,7},{0,8},{1,9},... | collective-permute-start | bytes 208904 | tf_op jit(solution)/shard_map/ppermute | solution.py:314
  21.8 0.7 %near_next.1 = (f32[256,256]{1,0:T(8,128)S(1)}, f32[256,256]{1,0:T(8,128)S(1)}) custom-call(f32[4,4,128]{2,1,0:T(4,128)S(1)} %get-tuple-element.35.refs_0_, f32[4,4,128]{2,1,0:T(4,128)S(1)} %get-tuple-element.36.refs_1_, bf16[2048,512]{1,0:T(8,128)(2,1)S(1)} %get-tuple-element.37.refs_2_, bf16[2048,512]{1,0:T(8,128)(2,1)S(1)} %get-tuple-element.38.refs_3_, ...), custom_call_target="tpu_custom_call" | custom-call | flops 402653184 | bytes 2097152 | tf_op jit(solution)/shard_map/near_next/pallas_call | solution.py:366
  22.5 0.0 collective-permute-done.7.refs_6_
  22.6 0.1 collective-permute-start.10
  22.6 0.0 collective-permute-done.4.refs_5_
  22.6 0.1 collective-permute-done.11.refs_7_
  22.7 1.3 %far_first.1 = (f32[256,256]{1,0:T(8,128)S(1)}, f32[256,256]{1,0:T(8,128)S(1)}) custom-call(f32[4,4,128]{2,1,0:T(4,128)S(1)} %get-tuple-element.29.refs_0_, f32[4,4,128]{2,1,0:T(4,128)S(1)} %get-tuple-element.30.refs_1_, bf16[2048,512]{1,0:T(8,128)(2,1)S(1)} %get-tuple-element.31.refs_2_, bf16[2048,512]{1,0:T(8,128)(2,1)S(1)} %get-tuple-element.32.refs_3_, ...), custom_call_target="tpu_custom_call" | custom-call | flops 805306368 | bytes 2097152 | tf_op jit(solution)/shard_map/far_first/pallas_call | solution.py:366
  24.0 0.0 collective-permute-done.10.refs_7_
  24.0 2.2 %far_next.1 = f32[256,512]{1,0:T(8,128)} custom-call(f32[4,4,128]{2,1,0:T(4,128)S(1)} %get-tuple-element.29.refs_0_, f32[4,4,128]{2,1,0:T(4,128)S(1)} %get-tuple-element.30.refs_1_, bf16[2048,512]{1,0:T(8,128)(2,1)S(1)} %get-tuple-element.31.refs_2_, bf16[2048,512]{1,0:T(8,128)(2,1)S(1)} %get-tuple-element.32.refs_3_, ...), custom_call_target="tpu_custom_call" | custom-call | flops 805306368 | bytes 2097152 | tf_op jit(solution)/shard_map/far_next/pallas_call | solution.py:366
  (11 shorter events, 0.1 us)
Async XLA Ops:
  0.8 8.2 %collective-permute-start = (f32[64,128]{1,0:T(8,128)S(1)}, f32[64,128]{1,0:T(8,128)S(1)}, u32[]{:S(2)}, u32[]{:S(2)}) collective-permute-start(f32[64,128]{1,0:T(8,128)S(1)} %bitcast.8), channel_id=1, source_target_pairs={{6,0},{7,1},{4,2},{5,3},{2,4},{3,5},{0,6},{1,7},{14,8},{15,9},{12,... | collective-permute-start | bytes 98312 | tf_op jit(solution)/shard_map/ppermute | solution.py:314
  5.9 4.8 %collective-permute-start.1 = (f32[64,128]{1,0:T(8,128)S(1)}, f32[64,128]{1,0:T(8,128)S(1)}, u32[]{:S(2)}, u32[]{:S(2)}) collective-permute-start(f32[64,128]{1,0:T(8,128)S(1)} %bitcast.9), channel_id=1, source_target_pairs={{4,0},{5,1},{6,2},{7,3},{0,4},{1,5},{2,6},{3,7},{12,8},{13,9},{14,... | collective-permute-start | bytes 98312 | tf_op jit(solution)/shard_map/ppermute | solution.py:314
  5.9 4.8 %collective-permute-start.2 = (f32[64,128]{1,0:T(8,128)S(1)}, f32[64,128]{1,0:T(8,128)S(1)}, u32[]{:S(2)}, u32[]{:S(2)}) collective-permute-start(f32[64,128]{1,0:T(8,128)S(1)} %bitcast.10), channel_id=1, source_target_pairs={{2,0},{3,1},{0,2},{1,3},{6,4},{7,5},{4,6},{5,7},{10,8},{11,9},{8,1... | collective-permute-start | bytes 98312 | tf_op jit(solution)/shard_map/ppermute | solution.py:314
  10.8 5.1 %collective-permute-start.5 = (f32[264,128]{1,0:T(8,128)S(1)}, f32[264,128]{1,0:T(8,128)S(1)}, u32[]{:S(2)}, u32[]{:S(2)}) collective-permute-start(f32[264,128]{1,0:T(8,128)S(1)} %get-tuple-element.65.refs_4_), channel_id=1, source_target_pairs={{16,0},{17,1},{18,2},{19,3},{20,4},{21,5},{22,6},{23,7},{24,8},{25... | collective-permute-start | bytes 405512 | tf_op jit(solution)/shard_map/ppermute | solution.py:314
  12.3 3.5 %collective-permute-start.6 = (f32[264,128]{1,0:T(8,128)S(1)}, f32[264,128]{1,0:T(8,128)S(1)}, u32[]{:S(2)}, u32[]{:S(2)}) collective-permute-start(f32[264,128]{1,0:T(8,128)S(1)} %get-tuple-element.65.refs_4_), channel_id=1, source_target_pairs={{8,0},{9,1},{10,2},{11,3},{12,4},{13,5},{14,6},{15,7},{0,8},{1,9},... | collective-permute-start | bytes 405512 | tf_op jit(solution)/shard_map/ppermute | solution.py:314
  12.3 6.1 %collective-permute-start.3 = (f32[272,128]{1,0:T(8,128)S(1)}, f32[272,128]{1,0:T(8,128)S(1)}, u32[]{:S(2)}, u32[]{:S(2)}) collective-permute-start(f32[272,128]{1,0:T(8,128)S(1)} %constant_dynamic-update-slice_fusion), channel_id=1, source_target_pairs={{1,0},{0,1},{3,2},{2,3},{5,4},{4,5},{7,6},{6,7},{9,8},{8,9},{11,10... | collective-permute-start | bytes 417800 | tf_op jit(solution)/shard_map/ppermute | solution.py:314
  15.9 2.5 %collective-permute-start.8 = (f32[264,128]{1,0:T(8,128)S(1)}, f32[264,128]{1,0:T(8,128)S(1)}, u32[]{:S(2)}, u32[]{:S(2)}) collective-permute-start(f32[264,128]{1,0:T(8,128)S(1)} %collective-permute-done.5.refs_6_), channel_id=1, source_target_pairs={{8,0},{9,1},{10,2},{11,3},{12,4},{13,5},{14,6},{15,7},{0,8},{1,9},... | collective-permute-start | bytes 405512 | tf_op jit(solution)/shard_map/ppermute | solution.py:314
  16.0 5.2 %collective-permute-start.9 = (f32[136,128]{1,0:T(8,128)S(1)}, f32[136,128]{1,0:T(8,128)S(1)}, u32[]{:S(2)}, u32[]{:S(2)}) collective-permute-start(f32[136,128]{1,0:T(8,128)S(1)} %pad_maximum_fusion.1), channel_id=1, source_target_pairs={{1,0},{0,1},{3,2},{2,3},{5,4},{4,5},{7,6},{6,7},{9,8},{8,9},{11,10... | collective-permute-start | bytes 208904 | tf_op jit(solution)/shard_map/ppermute | solution.py:314
  17.6 5.0 %collective-permute-start.7 = (f32[136,128]{1,0:T(8,128)S(1)}, f32[136,128]{1,0:T(8,128)S(1)}, u32[]{:S(2)}, u32[]{:S(2)}) collective-permute-start(f32[136,128]{1,0:T(8,128)S(1)} %pad_maximum_fusion), channel_id=1, source_target_pairs={{1,0},{0,1},{3,2},{2,3},{5,4},{4,5},{7,6},{6,7},{9,8},{8,9},{11,10... | collective-permute-start | bytes 208904 | tf_op jit(solution)/shard_map/ppermute | solution.py:314
  18.4 4.2 %collective-permute-start.4 = (f32[272,128]{1,0:T(8,128)S(1)}, f32[272,128]{1,0:T(8,128)S(1)}, u32[]{:S(2)}, u32[]{:S(2)}) collective-permute-start(f32[272,128]{1,0:T(8,128)S(1)} %collective-permute-done.3.refs_4_), channel_id=1, source_target_pairs={{8,0},{9,1},{10,2},{11,3},{12,4},{13,5},{14,6},{15,7},{0,8},{1,9},... | collective-permute-start | bytes 417800 | tf_op jit(solution)/shard_map/ppermute | solution.py:314
  21.2 1.5 %collective-permute-start.11 = (f32[136,128]{1,0:T(8,128)S(1)}, f32[136,128]{1,0:T(8,128)S(1)}, u32[]{:S(2)}, u32[]{:S(2)}) collective-permute-start(f32[136,128]{1,0:T(8,128)S(1)} %collective-permute-done.9.refs_6_), channel_id=1, source_target_pairs={{8,0},{9,1},{10,2},{11,3},{12,4},{13,5},{14,6},{15,7},{0,8},{1,9},... | collective-permute-start | bytes 208904 | tf_op jit(solution)/shard_map/ppermute | solution.py:314
  22.6 1.4 %collective-permute-start.10 = (f32[136,128]{1,0:T(8,128)S(1)}, f32[136,128]{1,0:T(8,128)S(1)}, u32[]{:S(2)}, u32[]{:S(2)}) collective-permute-start(f32[136,128]{1,0:T(8,128)S(1)} %collective-permute-done.7.refs_6_), channel_id=1, source_target_pairs={{8,0},{9,1},{10,2},{11,3},{12,4},{13,5},{14,6},{15,7},{0,8},{1,9},... | collective-permute-start | bytes 208904 | tf_op jit(solution)/shard_map/ppermute | solution.py:314

commit v16 on v15

--- a/solution.py
+++ b/solution.py
@@ -82,7 +82,12 @@
     pair_id = iota((listed, LANES), 0) % pairs
     first = dot(chosen, (pair_id // stations).astype(jnp.bfloat16))
     second = dot(chosen, (pair_id % stations).astype(jnp.bfloat16))
-    return first.astype(jnp.int32), second.astype(jnp.int32), weight
+    columns = 2 * groups * stations
+    row_id, column = iota((rows, columns), 0), iota((rows, columns), 1)
+    partner = ((row_id // slots) % groups + groups - 1 - row_id // (groups * slots)) % groups
+    wanted = partner * stations + second[:, 0:1].astype(jnp.int32)
+    picks_second = (column % (groups * stations) == wanted).astype(jnp.bfloat16)
+    return first.astype(jnp.int32), picks_second, weight
 
 
 def band_moves(shards):
@@ -159,13 +164,13 @@
     depth = 2 * chunks * stations
     half = sums[0].shape[1]
     first, second = picks
-    sets = [scratch[6 * index : 6 * (index + 1)] for index in range(2)]
+    sets = [scratch[7 * index : 7 * (index + 1)] for index in range(2)]
     part_groups = [range(part * groups // PARTS, (part + 1) * groups // PARTS) for part in range(PARTS)]
     bins_at_once = max(band_bins // 2, LANES)
     pieces = [(which, start) for which in range(2) for start in range(0, band_bins, bins_at_once)]
 
     def prepare(index):
-        (step, place_step), (held, turned) = steps[index], sets[index % 2][:2]
+        (step, place_step), (held, turned, second_of) = steps[index], sets[index % 2][:3]
         for position, (ref, offset) in enumerate(blocks):
             group = places[position]
             for q in range(chunks):
@@ -178,27 +183,30 @@
                 held[group, chunks + q] = imag
                 turned[group, q] = real * turn_cos + imag * turn_sin
                 turned[group, chunks + q] = imag * turn_cos - real * turn_sin
+        parts = [
+            jnp.concatenate(split_bf16(turned[:, q].reshape(groups * stations, LANES), 2), axis=0)
+            for q in range(2 * chunks)
+        ]
+        second_of[...] = dot(second[...], jnp.concatenate(parts, axis=1))
 
     def multiply(index, part):
-        held, turned, *cross = sets[index % 2]
+        held, _, second_of, *cross = sets[index % 2]
         for group in part_groups[part]:
             sources = []
             for number in range(rounds):
                 start = (number * groups + group) * slots
                 lines = [slice(start + o, start + o + SUBLANES) for o in range(0, slots, SUBLANES)]
-                partner = (group + groups - 1 - number) % groups
-                sources.append((start, partner, [(first[line, :], second[line, :]) for line in lines]))
+                sources.append((start, [(line, first[line, :]) for line in lines]))
             for q in range(chunks):
                 lanes = slice(q * LANES, (q + 1) * LANES)
+                imag_lanes = slice((chunks + q) * LANES, (chunks + q + 1) * LANES)
                 own_real, own_imag = held[group, q], held[group, chunks + q]
-                for start, partner, indices in sources:
-                    real, imag = turned[partner, q], turned[partner, chunks + q]
+                for start, indices in sources:
                     reals, imags = [], []
-                    for index_a, index_b in indices:
+                    for line, index_a in indices:
                         a_real = jnp.take_along_axis(own_real, index_a, axis=0)
                         a_imag = jnp.take_along_axis(own_imag, index_a, axis=0)
-                        b_real = jnp.take_along_axis(real, index_b, axis=0)
-                        b_imag = jnp.take_along_axis(imag, index_b, axis=0)
+                        b_real, b_imag = second_of[line, lanes], second_of[line, imag_lanes]
                         reals.append(a_real * b_real + a_imag * b_imag)
                         imags.append(a_imag * b_real - a_real * b_imag)
                     rows = slice(start, start + slots)
@@ -208,7 +216,7 @@
                         cross[place + 1][rows, lanes] = low
 
     def transform(index, which, start):
-        step, (high, low) = steps[index][0], sets[index % 2][2 + 2 * which : 4 + 2 * which]
+        step, (high, low) = steps[index][0], sets[index % 2][3 + 2 * which : 5 + 2 * which]
         lanes = slice(start, start + bins_at_once)
         bins = slice(step * band_bins + start, step * band_bins + start + bins_at_once)
         table, total = table_refs[which], sums[which]
@@ -408,14 +416,14 @@
     sizes = (groups, stations, rounds, slots, band_bins)
     spectrum = pltpu.VMEM((groups, 2 * chunks, stations, LANES), jnp.float32)
     cross = pltpu.VMEM((rows, band_bins), jnp.bfloat16)
-    scratch = ([spectrum] * 2 + [cross] * 4) * 2
+    second_of = pltpu.VMEM((rows, 2 * band_bins), jnp.float32)
+    scratch = ([spectrum] * 2 + [second_of] + [cross] * 4) * 2
 
     def cost(count):
         flops = 6 * rows * band_bins * lag_band * count
         return pl.CostEstimate(flops=flops, bytes_accessed=2 * 1024 * 1024, transcendentals=0)
 
     total = pltpu.VMEM((rows, half_band), jnp.float32)
-    index = pltpu.VMEM((rows, LANES), jnp.int32)
     near_table = [band_tables[place] for place in (2, 3, 0, 1)]
     far_table = [band_tables[place] for place in (6, 7, 4, 5)]
 
@@ -425,7 +433,12 @@
         ),
         "near_first",
         near_table + near,
-        [index] * 2 + [pltpu.VMEM((rows, LANES), jnp.float32)] + [total] * 2,
+        [
+            pltpu.VMEM((rows, LANES), jnp.int32),
+            pltpu.VMEM((rows, 2 * groups * stations), jnp.bfloat16),
+            pltpu.VMEM((rows, LANES), jnp.float32),
+        ]
+        + [total] * 2,
         scratch,
         cost(split),
     )

time: 26.3 us -> 28.1 us (1.068)
  Pallas kernels: 9.41 us -> 11.2 us
    pallas_call x5, Pallas kernels: 9.41 us -> 11.2 us  [call(): pl.pallas_call(kernel, out_shape=out_shape, in_specs=[in_hbm] * len(other...]
  transfers between devices with their start and end apart: 12 -> 12, of which waited for: 4 -> 3; matrix products, arithmetic and copies ran while one was open for 0% -> 0% of each run, Pallas kernels for 28% -> 30%
where the time goes in v16:
time: 28.1 us; the launch traced here: 27.9 us
  starting transfers between devices  11.6 us (41%)
  Pallas kernels  11.2 us (40%)
  waiting for transfers between devices  4.05 us (14%)
  local copies, waits for them, and re-layouts  0.84 us (3%)
    ppermute x12, starting transfers between devices, fetched(): return lax.ppermute(block, ('grp', 'freq'), route)  11.6 us
    pallas_call x5, Pallas kernels, call(): pl.pallas_call(kernel, out_shape=out_shape, in_specs=[in_hbm] * len(other...  11.2 us
    ppermute x12, waiting for transfers between devices, fetched(): return lax.ppermute(block, ('grp', 'freq'), route)  4.05 us
    reshape x2, local copies, waits for them, and re-layouts, per_device(): tiles = spectra.reshape(stations, 2, chunks, LANES).transpose(1, 2, 0, 3)  0.8 us
  transfers between devices with their start and end apart: 12, of which 3 were waited for; matrix products, arithmetic and copies ran while one was open for 0% of the time, Pallas kernels for 30%

profile of v16, /device:TPU:0, one launch (start us, length us, event | category | flops | bytes accessed | tf_op | source)
XLA Modules:
  0.0 27.9 jit_solution(17137310724004353455)
XLA Ops:
  0.0 0.8 %reshape.13 = f32[8,2,4,128]{3,2,1,0:T(4,128)S(1)} reshape(f32[8,2,512]{2,1,0:T(2,128)} %param.3) | data formatting | bytes 65536 | tf_op jit(solution)/shard_map/reshape | solution.py:386
  0.8 5.1 %collective-permute-start = (f32[64,128]{1,0:T(8,128)S(1)}, f32[64,128]{1,0:T(8,128)S(1)}, u32[]{:S(2)}, u32[]{:S(2)}) collective-permute-start(f32[64,128]{1,0:T(8,128)S(1)} %bitcast.8), channel_id=1, source_target_pairs={{6,0},{7,1},{4,2},{5,3},{2,4},{3,5},{0,6},{1,7},{14,8},{15,9},{12,... | collective-permute-start | bytes 98312 | tf_op jit(solution)/shard_map/ppermute | solution.py:322
  5.9 0.0 collective-permute-start.1
  5.9 0.6 %collective-permute-start.2 = (f32[64,128]{1,0:T(8,128)S(1)}, f32[64,128]{1,0:T(8,128)S(1)}, u32[]{:S(2)}, u32[]{:S(2)}) collective-permute-start(f32[64,128]{1,0:T(8,128)S(1)} %bitcast.10), channel_id=1, source_target_pairs={{2,0},{3,1},{0,2},{1,3},{6,4},{7,5},{4,6},{5,7},{10,8},{11,9},{8,1... | collective-permute-start | bytes 98312 | tf_op jit(solution)/shard_map/ppermute | solution.py:322
  6.6 2.4 %tables.1 = (bf16[2048,512]{1,0:T(8,128)(2,1)S(1)}, bf16[2048,512]{1,0:T(8,128)(2,1)S(1)}, f32[4,4,128]{2,1,0:T(4,128)S(1)}, f32[4,4,128]{2,1,0:T(4,128)S(1)}, b...) custom-call(s32[1,2,1,64]{3,2,1,0:T(1,128)} %bitcast.12, ...), custom_call_target="tpu_custom_call" | custom-call | bytes 4194304 | tf_op jit(solution)/shard_map/tables/pallas_call | solution.py:374
  9.0 0.0 collective-permute-done
  9.1 1.7 %collective-permute-done.1 = f32[64,128]{1,0:T(8,128)S(1)} collective-permute-done((f32[64,128]{1,0:T(8,128)S(1)}, f32[64,128]{1,0:T(8,128)S(1)}, u32[]{:S(2)}, u32[]{:S(2)}) %collective-permute-start.1) | collective-permute-done | bytes 32800 | tf_op jit(solution)/shard_map/ppermute | solution.py:322
  10.7 0.0 collective-permute-done.2
  10.8 1.6 %collective-permute-start.5 = (f32[264,128]{1,0:T(8,128)S(1)}, f32[264,128]{1,0:T(8,128)S(1)}, u32[]{:S(2)}, u32[]{:S(2)}) collective-permute-start(f32[264,128]{1,0:T(8,128)S(1)} %get-tuple-element.65.refs_4_), channel_id=1, source_target_pairs={{16,0},{17,1},{18,2},{19,3},{20,4},{21,5},{22,6},{23,7},{24,8},{25... | collective-permute-start | bytes 405512 | tf_op jit(solution)/shard_map/ppermute | solution.py:322
  12.3 0.0 collective-permute-start.6
  12.3 1.5 %collective-permute-start.3 = (f32[272,128]{1,0:T(8,128)S(1)}, f32[272,128]{1,0:T(8,128)S(1)}, u32[]{:S(2)}, u32[]{:S(2)}) collective-permute-start(f32[272,128]{1,0:T(8,128)S(1)} %constant_dynamic-update-slice_fusion), channel_id=1, source_target_pairs={{1,0},{0,1},{3,2},{2,3},{5,4},{4,5},{7,6},{6,7},{9,8},{8,9},{11,10... | collective-permute-start | bytes 417800 | tf_op jit(solution)/shard_map/ppermute | solution.py:322
  13.9 2.0 %collective-permute-done.5.refs_6_ = f32[264,128]{1,0:T(8,128)S(1)} collective-permute-done((f32[264,128]{1,0:T(8,128)S(1)}, f32[264,128]{1,0:T(8,128)S(1)}, u32[]{:S(2)}, u32[]{:S(2)}) %collective-permute-start.5) | collective-permute-done | bytes 135200 | tf_op jit(solution)/shard_map/ppermute | solution.py:322
  15.9 0.0 collective-permute-done.6.refs_5_
  15.9 0.1 collective-permute-start.8
  16.0 1.6 %collective-permute-start.9 = (f32[136,128]{1,0:T(8,128)S(1)}, f32[136,128]{1,0:T(8,128)S(1)}, u32[]{:S(2)}, u32[]{:S(2)}) collective-permute-start(f32[136,128]{1,0:T(8,128)S(1)} %pad_maximum_fusion.1), channel_id=1, source_target_pairs={{1,0},{0,1},{3,2},{2,3},{5,4},{4,5},{7,6},{6,7},{9,8},{8,9},{11,10... | collective-permute-start | bytes 208904 | tf_op jit(solution)/shard_map/ppermute | solution.py:322
  17.6 0.5 %collective-permute-start.7 = (f32[136,128]{1,0:T(8,128)S(1)}, f32[136,128]{1,0:T(8,128)S(1)}, u32[]{:S(2)}, u32[]{:S(2)}) collective-permute-start(f32[136,128]{1,0:T(8,128)S(1)} %pad_maximum_fusion), channel_id=1, source_target_pairs={{1,0},{0,1},{3,2},{2,3},{5,4},{4,5},{7,6},{6,7},{9,8},{8,9},{11,10... | collective-permute-start | bytes 208904 | tf_op jit(solution)/shard_map/ppermute | solution.py:322
  18.1 0.3 %collective-permute-done.3.refs_4_ = f32[272,128]{1,0:T(8,128)S(1)} collective-permute-done((f32[272,128]{1,0:T(8,128)S(1)}, f32[272,128]{1,0:T(8,128)S(1)}, u32[]{:S(2)}, u32[]{:S(2)}) %collective-permute-start.3) | collective-permute-done | bytes 139296 | tf_op jit(solution)/shard_map/ppermute | solution.py:322
  18.4 0.0 collective-permute-start.4
  18.4 0.0 collective-permute-done.8.refs_7_
  18.4 3.2 %near_first.1 = (s32[256,128]{1,0:T(8,128)S(1)}, bf16[256,64]{1,0:T(8,128)(2,1)S(1)}, f32[256,128]{1,0:T(8,128)S(1)}, f32[256,256]{1,0:T(8,128)S(1)}, f32[256,256]{1,0:T(8,128)S(1)}) custom-call(f32[4,4,128]{2,1,0:T(4,128)S(1)} %get-tuple-element.35.refs_0_, f32[4,4,128]{2,1,0:T(4,128)S(1)} %get-tuple-element.36.refs_1_, ...), custom_call_target="tpu_custom_call" | custom-call | flops 1207959552 | bytes 2097152 | tf_op jit(solution)/shard_map/near_first/pallas_call | solution.py:374
  21.6 0.0 collective-permute-done.9.refs_6_
  21.6 0.6 %collective-permute-start.11 = (f32[136,128]{1,0:T(8,128)S(1)}, f32[136,128]{1,0:T(8,128)S(1)}, u32[]{:S(2)}, u32[]{:S(2)}) collective-permute-start(f32[136,128]{1,0:T(8,128)S(1)} %collective-permute-done.9.refs_6_), channel_id=1, source_target_pairs={{8,0},{9,1},{10,2},{11,3},{12,4},{13,5},{14,6},{15,7},{0,8},{1,9},... | collective-permute-start | bytes 208904 | tf_op jit(solution)/shard_map/ppermute | solution.py:322
  22.2 1.1 %near_next.1 = (f32[256,256]{1,0:T(8,128)S(1)}, f32[256,256]{1,0:T(8,128)S(1)}) custom-call(f32[4,4,128]{2,1,0:T(4,128)S(1)} %get-tuple-element.35.refs_0_, f32[4,4,128]{2,1,0:T(4,128)S(1)} %get-tuple-element.36.refs_1_, bf16[2048,512]{1,0:T(8,128)(2,1)S(1)} %get-tuple-element.37.refs_2_, bf16[2048,512]{1,0:T(8,128)(2,1)S(1)} %get-tuple-element.38.refs_3_, ...), custom_call_target="tpu_custom_call" | custom-call | flops 402653184 | bytes 2097152 | tf_op jit(solution)/shard_map/near_next/pallas_call | solution.py:374
  23.3 0.0 collective-permute-done.7.refs_6_
  23.3 0.1 collective-permute-start.10
  23.4 0.0 collective-permute-done.4.refs_5_
  23.4 0.0 collective-permute-done.11.refs_7_
  23.4 1.7 %far_first.1 = (f32[256,256]{1,0:T(8,128)S(1)}, f32[256,256]{1,0:T(8,128)S(1)}) custom-call(f32[4,4,128]{2,1,0:T(4,128)S(1)} %get-tuple-element.29.refs_0_, f32[4,4,128]{2,1,0:T(4,128)S(1)} %get-tuple-element.30.refs_1_, bf16[2048,512]{1,0:T(8,128)(2,1)S(1)} %get-tuple-element.31.refs_2_, bf16[2048,512]{1,0:T(8,128)(2,1)S(1)} %get-tuple-element.32.refs_3_, ...), custom_call_target="tpu_custom_call" | custom-call | flops 805306368 | bytes 2097152 | tf_op jit(solution)/shard_map/far_first/pallas_call | solution.py:374
  25.2 0.0 collective-permute-done.10.refs_7_
  25.2 2.7 %far_next.1 = f32[256,512]{1,0:T(8,128)} custom-call(f32[4,4,128]{2,1,0:T(4,128)S(1)} %get-tuple-element.29.refs_0_, f32[4,4,128]{2,1,0:T(4,128)S(1)} %get-tuple-element.30.refs_1_, bf16[2048,512]{1,0:T(8,128)(2,1)S(1)} %get-tuple-element.31.refs_2_, bf16[2048,512]{1,0:T(8,128)(2,1)S(1)} %get-tuple-element.32.refs_3_, ...), custom_call_target="tpu_custom_call" | custom-call | flops 805306368 | bytes 2097152 | tf_op jit(solution)/shard_map/far_next/pallas_call | solution.py:374
  (11 shorter events, 0.1 us)
Async XLA Ops:
  0.8 8.2 %collective-permute-start = (f32[64,128]{1,0:T(8,128)S(1)}, f32[64,128]{1,0:T(8,128)S(1)}, u32[]{:S(2)}, u32[]{:S(2)}) collective-permute-start(f32[64,128]{1,0:T(8,128)S(1)} %bitcast.8), channel_id=1, source_target_pairs={{6,0},{7,1},{4,2},{5,3},{2,4},{3,5},{0,6},{1,7},{14,8},{15,9},{12,... | collective-permute-start | bytes 98312 | tf_op jit(solution)/shard_map/ppermute | solution.py:322
  5.9 4.8 %collective-permute-start.1 = (f32[64,128]{1,0:T(8,128)S(1)}, f32[64,128]{1,0:T(8,128)S(1)}, u32[]{:S(2)}, u32[]{:S(2)}) collective-permute-start(f32[64,128]{1,0:T(8,128)S(1)} %bitcast.9), channel_id=1, source_target_pairs={{4,0},{5,1},{6,2},{7,3},{0,4},{1,5},{2,6},{3,7},{12,8},{13,9},{14,... | collective-permute-start | bytes 98312 | tf_op jit(solution)/shard_map/ppermute | solution.py:322
  5.9 4.8 %collective-permute-start.2 = (f32[64,128]{1,0:T(8,128)S(1)}, f32[64,128]{1,0:T(8,128)S(1)}, u32[]{:S(2)}, u32[]{:S(2)}) collective-permute-start(f32[64,128]{1,0:T(8,128)S(1)} %bitcast.10), channel_id=1, source_target_pairs={{2,0},{3,1},{0,2},{1,3},{6,4},{7,5},{4,6},{5,7},{10,8},{11,9},{8,1... | collective-permute-start | bytes 98312 | tf_op jit(solution)/shard_map/ppermute | solution.py:322
  10.8 5.1 %collective-permute-start.5 = (f32[264,128]{1,0:T(8,128)S(1)}, f32[264,128]{1,0:T(8,128)S(1)}, u32[]{:S(2)}, u32[]{:S(2)}) collective-permute-start(f32[264,128]{1,0:T(8,128)S(1)} %get-tuple-element.65.refs_4_), channel_id=1, source_target_pairs={{16,0},{17,1},{18,2},{19,3},{20,4},{21,5},{22,6},{23,7},{24,8},{25... | collective-permute-start | bytes 405512 | tf_op jit(solution)/shard_map/ppermute | solution.py:322
  12.3 3.5 %collective-permute-start.6 = (f32[264,128]{1,0:T(8,128)S(1)}, f32[264,128]{1,0:T(8,128)S(1)}, u32[]{:S(2)}, u32[]{:S(2)}) collective-permute-start(f32[264,128]{1,0:T(8,128)S(1)} %get-tuple-element.65.refs_4_), channel_id=1, source_target_pairs={{8,0},{9,1},{10,2},{11,3},{12,4},{13,5},{14,6},{15,7},{0,8},{1,9},... | collective-permute-start | bytes 405512 | tf_op jit(solution)/shard_map/ppermute | solution.py:322
  12.3 6.1 %collective-permute-start.3 = (f32[272,128]{1,0:T(8,128)S(1)}, f32[272,128]{1,0:T(8,128)S(1)}, u32[]{:S(2)}, u32[]{:S(2)}) collective-permute-start(f32[272,128]{1,0:T(8,128)S(1)} %constant_dynamic-update-slice_fusion), channel_id=1, source_target_pairs={{1,0},{0,1},{3,2},{2,3},{5,4},{4,5},{7,6},{6,7},{9,8},{8,9},{11,10... | collective-permute-start | bytes 417800 | tf_op jit(solution)/shard_map/ppermute | solution.py:322
  15.9 2.5 %collective-permute-start.8 = (f32[264,128]{1,0:T(8,128)S(1)}, f32[264,128]{1,0:T(8,128)S(1)}, u32[]{:S(2)}, u32[]{:S(2)}) collective-permute-start(f32[264,128]{1,0:T(8,128)S(1)} %collective-permute-done.5.refs_6_), channel_id=1, source_target_pairs={{8,0},{9,1},{10,2},{11,3},{12,4},{13,5},{14,6},{15,7},{0,8},{1,9},... | collective-permute-start | bytes 405512 | tf_op jit(solution)/shard_map/ppermute | solution.py:322
  16.0 5.7 %collective-permute-start.9 = (f32[136,128]{1,0:T(8,128)S(1)}, f32[136,128]{1,0:T(8,128)S(1)}, u32[]{:S(2)}, u32[]{:S(2)}) collective-permute-start(f32[136,128]{1,0:T(8,128)S(1)} %pad_maximum_fusion.1), channel_id=1, source_target_pairs={{1,0},{0,1},{3,2},{2,3},{5,4},{4,5},{7,6},{6,7},{9,8},{8,9},{11,10... | collective-permute-start | bytes 208904 | tf_op jit(solution)/shard_map/ppermute | solution.py:322
  17.6 5.7 %collective-permute-start.7 = (f32[136,128]{1,0:T(8,128)S(1)}, f32[136,128]{1,0:T(8,128)S(1)}, u32[]{:S(2)}, u32[]{:S(2)}) collective-permute-start(f32[136,128]{1,0:T(8,128)S(1)} %pad_maximum_fusion), channel_id=1, source_target_pairs={{1,0},{0,1},{3,2},{2,3},{5,4},{4,5},{7,6},{6,7},{9,8},{8,9},{11,10... | collective-permute-start | bytes 208904 | tf_op jit(solution)/shard_map/ppermute | solution.py:322
  18.4 5.0 %collective-permute-start.4 = (f32[272,128]{1,0:T(8,128)S(1)}, f32[272,128]{1,0:T(8,128)S(1)}, u32[]{:S(2)}, u32[]{:S(2)}) collective-permute-start(f32[272,128]{1,0:T(8,128)S(1)} %collective-permute-done.3.refs_4_), channel_id=1, source_target_pairs={{8,0},{9,1},{10,2},{11,3},{12,4},{13,5},{14,6},{15,7},{0,8},{1,9},... | collective-permute-start | bytes 417800 | tf_op jit(solution)/shard_map/ppermute | solution.py:322
  21.6 1.8 %collective-permute-start.11 = (f32[136,128]{1,0:T(8,128)S(1)}, f32[136,128]{1,0:T(8,128)S(1)}, u32[]{:S(2)}, u32[]{:S(2)}) collective-permute-start(f32[136,128]{1,0:T(8,128)S(1)} %collective-permute-done.9.refs_6_), channel_id=1, source_target_pairs={{8,0},{9,1},{10,2},{11,3},{12,4},{13,5},{14,6},{15,7},{0,8},{1,9},... | collective-permute-start | bytes 208904 | tf_op jit(solution)/shard_map/ppermute | solution.py:322
  23.3 1.9 %collective-permute-start.10 = (f32[136,128]{1,0:T(8,128)S(1)}, f32[136,128]{1,0:T(8,128)S(1)}, u32[]{:S(2)}, u32[]{:S(2)}) collective-permute-start(f32[136,128]{1,0:T(8,128)S(1)} %collective-permute-done.7.refs_6_), channel_id=1, source_target_pairs={{8,0},{9,1},{10,2},{11,3},{12,4},{13,5},{14,6},{15,7},{0,8},{1,9},... | collective-permute-start | bytes 208904 | tf_op jit(solution)/shard_map/ppermute | solution.py:322

commit v17 on v15

--- a/solution.py
+++ b/solution.py
@@ -401,7 +401,7 @@
     )
     column = jnp.concatenate(column + [extras], axis=0)
     depth = 2 * chunks * stations
-    split, middle = steps - steps // 4, steps // 2
+    split = middle = steps // 2
     parts = [(0, middle * depth), (middle * depth, steps * depth)]
     near, layout, far, diagonals = exchange(column, parts)
 

time: 26.3 us -> 26.4 us (level)
  waiting for transfers between devices: 4.11 us -> 4.59 us
  Pallas kernels: 9.41 us -> 9.02 us
    ppermute x12, waiting for transfers between devices: 4.11 us -> 4.59 us  [fetched(): return lax.ppermute(block, ('grp', 'freq'), route)]
    pallas_call x5, Pallas kernels: 9.41 us -> 9.02 us  [call(): pl.pallas_call(kernel, out_shape=out_shape, in_specs=[in_hbm] * len(other...]
  transfers between devices with their start and end apart: 12 -> 12, of which waited for: 4 -> 4; matrix products, arithmetic and copies ran while one was open for 0% -> 0% of each run, Pallas kernels for 28% -> 26%
where the time goes in v17:
time: 26.4 us; the launch traced here: 26.2 us
  starting transfers between devices  11.6 us (44%)
  Pallas kernels  9.02 us (34%)
  waiting for transfers between devices  4.59 us (17%)
  local copies, waits for them, and re-layouts  0.84 us (3%)
    ppermute x12, starting transfers between devices, fetched(): return lax.ppermute(block, ('grp', 'freq'), route)  11.6 us
    pallas_call x5, Pallas kernels, call(): pl.pallas_call(kernel, out_shape=out_shape, in_specs=[in_hbm] * len(other...  9.02 us
    ppermute x12, waiting for transfers between devices, fetched(): return lax.ppermute(block, ('grp', 'freq'), route)  4.59 us
    reshape x2, local copies, waits for them, and re-layouts, per_device(): tiles = spectra.reshape(stations, 2, chunks, LANES).transpose(1, 2, 0, 3)  0.8 us
  transfers between devices with their start and end apart: 12, of which 4 were waited for; matrix products, arithmetic and copies ran while one was open for 0% of the time, Pallas kernels for 26%

profile of v17, /device:TPU:0, one launch (start us, length us, event | category | flops | bytes accessed | tf_op | source)
XLA Modules:
  0.0 26.2 jit_solution(7686159836963981707)
XLA Ops:
  0.0 0.8 %reshape.13 = f32[8,2,4,128]{3,2,1,0:T(4,128)S(1)} reshape(f32[8,2,512]{2,1,0:T(2,128)} %param.3) | data formatting | bytes 65536 | tf_op jit(solution)/shard_map/reshape | solution.py:378
  0.8 5.1 %collective-permute-start = (f32[64,128]{1,0:T(8,128)S(1)}, f32[64,128]{1,0:T(8,128)S(1)}, u32[]{:S(2)}, u32[]{:S(2)}) collective-permute-start(f32[64,128]{1,0:T(8,128)S(1)} %bitcast.8), channel_id=1, source_target_pairs={{6,0},{7,1},{4,2},{5,3},{2,4},{3,5},{0,6},{1,7},{14,8},{15,9},{12,... | collective-permute-start | bytes 98312 | tf_op jit(solution)/shard_map/ppermute | solution.py:314
  5.9 0.0 collective-permute-start.1
  5.9 0.6 %collective-permute-start.2 = (f32[64,128]{1,0:T(8,128)S(1)}, f32[64,128]{1,0:T(8,128)S(1)}, u32[]{:S(2)}, u32[]{:S(2)}) collective-permute-start(f32[64,128]{1,0:T(8,128)S(1)} %bitcast.10), channel_id=1, source_target_pairs={{2,0},{3,1},{0,2},{1,3},{6,4},{7,5},{4,6},{5,7},{10,8},{11,9},{8,1... | collective-permute-start | bytes 98312 | tf_op jit(solution)/shard_map/ppermute | solution.py:314
  6.6 2.4 %tables.1 = (bf16[2048,512]{1,0:T(8,128)(2,1)S(1)}, bf16[2048,512]{1,0:T(8,128)(2,1)S(1)}, f32[4,4,128]{2,1,0:T(4,128)S(1)}, f32[4,4,128]{2,1,0:T(4,128)S(1)}, b...) custom-call(s32[1,2,1,64]{3,2,1,0:T(1,128)} %bitcast.12, ...), custom_call_target="tpu_custom_call" | custom-call | bytes 4194304 | tf_op jit(solution)/shard_map/tables/pallas_call | solution.py:366
  9.0 0.0 collective-permute-done
  9.1 1.7 %collective-permute-done.1 = f32[64,128]{1,0:T(8,128)S(1)} collective-permute-done((f32[64,128]{1,0:T(8,128)S(1)}, f32[64,128]{1,0:T(8,128)S(1)}, u32[]{:S(2)}, u32[]{:S(2)}) %collective-permute-start.1) | collective-permute-done | bytes 32800 | tf_op jit(solution)/shard_map/ppermute | solution.py:314
  10.7 0.0 collective-permute-done.2
  10.8 1.6 %collective-permute-start.5 = (f32[264,128]{1,0:T(8,128)S(1)}, f32[264,128]{1,0:T(8,128)S(1)}, u32[]{:S(2)}, u32[]{:S(2)}) collective-permute-start(f32[264,128]{1,0:T(8,128)S(1)} %get-tuple-element.65.refs_4_), channel_id=1, source_target_pairs={{16,0},{17,1},{18,2},{19,3},{20,4},{21,5},{22,6},{23,7},{24,8},{25... | collective-permute-start | bytes 405512 | tf_op jit(solution)/shard_map/ppermute | solution.py:314
  12.3 0.0 collective-permute-start.6
  12.3 1.5 %collective-permute-start.3 = (f32[272,128]{1,0:T(8,128)S(1)}, f32[272,128]{1,0:T(8,128)S(1)}, u32[]{:S(2)}, u32[]{:S(2)}) collective-permute-start(f32[272,128]{1,0:T(8,128)S(1)} %constant_dynamic-update-slice_fusion), channel_id=1, source_target_pairs={{1,0},{0,1},{3,2},{2,3},{5,4},{4,5},{7,6},{6,7},{9,8},{8,9},{11,10... | collective-permute-start | bytes 417800 | tf_op jit(solution)/shard_map/ppermute | solution.py:314
  13.9 2.0 %collective-permute-done.5.refs_6_ = f32[264,128]{1,0:T(8,128)S(1)} collective-permute-done((f32[264,128]{1,0:T(8,128)S(1)}, f32[264,128]{1,0:T(8,128)S(1)}, u32[]{:S(2)}, u32[]{:S(2)}) %collective-permute-start.5) | collective-permute-done | bytes 135200 | tf_op jit(solution)/shard_map/ppermute | solution.py:314
  15.9 0.0 collective-permute-done.6.refs_5_
  15.9 0.1 collective-permute-start.8
  16.0 1.6 %collective-permute-start.9 = (f32[136,128]{1,0:T(8,128)S(1)}, f32[136,128]{1,0:T(8,128)S(1)}, u32[]{:S(2)}, u32[]{:S(2)}) collective-permute-start(f32[136,128]{1,0:T(8,128)S(1)} %pad_maximum_fusion.1), channel_id=1, source_target_pairs={{1,0},{0,1},{3,2},{2,3},{5,4},{4,5},{7,6},{6,7},{9,8},{8,9},{11,10... | collective-permute-start | bytes 208904 | tf_op jit(solution)/shard_map/ppermute | solution.py:314
  17.6 0.5 %collective-permute-start.7 = (f32[136,128]{1,0:T(8,128)S(1)}, f32[136,128]{1,0:T(8,128)S(1)}, u32[]{:S(2)}, u32[]{:S(2)}) collective-permute-start(f32[136,128]{1,0:T(8,128)S(1)} %pad_maximum_fusion), channel_id=1, source_target_pairs={{1,0},{0,1},{3,2},{2,3},{5,4},{4,5},{7,6},{6,7},{9,8},{8,9},{11,10... | collective-permute-start | bytes 208904 | tf_op jit(solution)/shard_map/ppermute | solution.py:314
  18.1 0.3 %collective-permute-done.3.refs_4_ = f32[272,128]{1,0:T(8,128)S(1)} collective-permute-done((f32[272,128]{1,0:T(8,128)S(1)}, f32[272,128]{1,0:T(8,128)S(1)}, u32[]{:S(2)}, u32[]{:S(2)}) %collective-permute-start.3) | collective-permute-done | bytes 139296 | tf_op jit(solution)/shard_map/ppermute | solution.py:314
  18.4 0.0 collective-permute-start.4
  18.4 0.0 collective-permute-done.8.refs_7_
  18.4 1.9 %near_first.1 = (s32[256,128]{1,0:T(8,128)S(1)}, s32[256,128]{1,0:T(8,128)S(1)}, f32[256,128]{1,0:T(8,128)S(1)}, f32[256,256]{1,0:T(8,128)S(1)}, f32[256,256]{1,0:T(8,128)S(1)}) custom-call(f32[4,4,128]{2,1,0:T(4,128)S(1)} %get-tuple-element.35.refs_0_, f32[4,4,128]{2,1,0:T(4,128)S(1)} %get-tuple-element.36.refs_1_, ...), custom_call_target="tpu_custom_call" | custom-call | flops 805306368 | bytes 2097152 | tf_op jit(solution)/shard_map/near_first/pallas_call | solution.py:366
  20.3 0.5 %collective-permute-done.9.refs_6_ = f32[136,128]{1,0:T(8,128)S(1)} collective-permute-done((f32[136,128]{1,0:T(8,128)S(1)}, f32[136,128]{1,0:T(8,128)S(1)}, u32[]{:S(2)}, u32[]{:S(2)}) %collective-permute-start.9) | collective-permute-done | bytes 69664 | tf_op jit(solution)/shard_map/ppermute | solution.py:314
  20.9 0.0 collective-permute-start.11
  20.9 1.3 %near_next.1 = (f32[256,256]{1,0:T(8,128)S(1)}, f32[256,256]{1,0:T(8,128)S(1)}) custom-call(f32[4,4,128]{2,1,0:T(4,128)S(1)} %get-tuple-element.35.refs_0_, f32[4,4,128]{2,1,0:T(4,128)S(1)} %get-tuple-element.36.refs_1_, bf16[2048,512]{1,0:T(8,128)(2,1)S(1)} %get-tuple-element.37.refs_2_, bf16[2048,512]{1,0:T(8,128)(2,1)S(1)} %get-tuple-element.38.refs_3_, ...), custom_call_target="tpu_custom_call" | custom-call | flops 805306368 | bytes 2097152 | tf_op jit(solution)/shard_map/near_next/pallas_call | solution.py:366
  22.2 0.0 collective-permute-done.7.refs_6_
  22.2 0.5 %collective-permute-start.10 = (f32[136,128]{1,0:T(8,128)S(1)}, f32[136,128]{1,0:T(8,128)S(1)}, u32[]{:S(2)}, u32[]{:S(2)}) collective-permute-start(f32[136,128]{1,0:T(8,128)S(1)} %collective-permute-done.7.refs_6_), channel_id=1, source_target_pairs={{8,0},{9,1},{10,2},{11,3},{12,4},{13,5},{14,6},{15,7},{0,8},{1,9},... | collective-permute-start | bytes 208904 | tf_op jit(solution)/shard_map/ppermute | solution.py:314
  22.7 0.0 collective-permute-done.4.refs_5_
  22.7 0.0 collective-permute-done.11.refs_7_
  22.7 1.3 %far_first.1 = (f32[256,256]{1,0:T(8,128)S(1)}, f32[256,256]{1,0:T(8,128)S(1)}) custom-call(f32[4,4,128]{2,1,0:T(4,128)S(1)} %get-tuple-element.29.refs_0_, f32[4,4,128]{2,1,0:T(4,128)S(1)} %get-tuple-element.30.refs_1_, bf16[2048,512]{1,0:T(8,128)(2,1)S(1)} %get-tuple-element.31.refs_2_, bf16[2048,512]{1,0:T(8,128)(2,1)S(1)} %get-tuple-element.32.refs_3_, ...), custom_call_target="tpu_custom_call" | custom-call | flops 805306368 | bytes 2097152 | tf_op jit(solution)/shard_map/far_first/pallas_call | solution.py:366
  24.0 0.0 collective-permute-done.10.refs_7_
  24.0 2.2 %far_next.1 = f32[256,512]{1,0:T(8,128)} custom-call(f32[4,4,128]{2,1,0:T(4,128)S(1)} %get-tuple-element.29.refs_0_, f32[4,4,128]{2,1,0:T(4,128)S(1)} %get-tuple-element.30.refs_1_, bf16[2048,512]{1,0:T(8,128)(2,1)S(1)} %get-tuple-element.31.refs_2_, bf16[2048,512]{1,0:T(8,128)(2,1)S(1)} %get-tuple-element.32.refs_3_, ...), custom_call_target="tpu_custom_call" | custom-call | flops 805306368 | bytes 2097152 | tf_op jit(solution)/shard_map/far_next/pallas_call | solution.py:366
  (11 shorter events, 0.1 us)
Async XLA Ops:
  0.8 8.2 %collective-permute-start = (f32[64,128]{1,0:T(8,128)S(1)}, f32[64,128]{1,0:T(8,128)S(1)}, u32[]{:S(2)}, u32[]{:S(2)}) collective-permute-start(f32[64,128]{1,0:T(8,128)S(1)} %bitcast.8), channel_id=1, source_target_pairs={{6,0},{7,1},{4,2},{5,3},{2,4},{3,5},{0,6},{1,7},{14,8},{15,9},{12,... | collective-permute-start | bytes 98312 | tf_op jit(solution)/shard_map/ppermute | solution.py:314
  5.9 4.8 %collective-permute-start.1 = (f32[64,128]{1,0:T(8,128)S(1)}, f32[64,128]{1,0:T(8,128)S(1)}, u32[]{:S(2)}, u32[]{:S(2)}) collective-permute-start(f32[64,128]{1,0:T(8,128)S(1)} %bitcast.9), channel_id=1, source_target_pairs={{4,0},{5,1},{6,2},{7,3},{0,4},{1,5},{2,6},{3,7},{12,8},{13,9},{14,... | collective-permute-start | bytes 98312 | tf_op jit(solution)/shard_map/ppermute | solution.py:314
  5.9 4.8 %collective-permute-start.2 = (f32[64,128]{1,0:T(8,128)S(1)}, f32[64,128]{1,0:T(8,128)S(1)}, u32[]{:S(2)}, u32[]{:S(2)}) collective-permute-start(f32[64,128]{1,0:T(8,128)S(1)} %bitcast.10), channel_id=1, source_target_pairs={{2,0},{3,1},{0,2},{1,3},{6,4},{7,5},{4,6},{5,7},{10,8},{11,9},{8,1... | collective-permute-start | bytes 98312 | tf_op jit(solution)/shard_map/ppermute | solution.py:314
  10.8 5.1 %collective-permute-start.5 = (f32[264,128]{1,0:T(8,128)S(1)}, f32[264,128]{1,0:T(8,128)S(1)}, u32[]{:S(2)}, u32[]{:S(2)}) collective-permute-start(f32[264,128]{1,0:T(8,128)S(1)} %get-tuple-element.65.refs_4_), channel_id=1, source_target_pairs={{16,0},{17,1},{18,2},{19,3},{20,4},{21,5},{22,6},{23,7},{24,8},{25... | collective-permute-start | bytes 405512 | tf_op jit(solution)/shard_map/ppermute | solution.py:314
  12.3 3.5 %collective-permute-start.6 = (f32[264,128]{1,0:T(8,128)S(1)}, f32[264,128]{1,0:T(8,128)S(1)}, u32[]{:S(2)}, u32[]{:S(2)}) collective-permute-start(f32[264,128]{1,0:T(8,128)S(1)} %get-tuple-element.65.refs_4_), channel_id=1, source_target_pairs={{8,0},{9,1},{10,2},{11,3},{12,4},{13,5},{14,6},{15,7},{0,8},{1,9},... | collective-permute-start | bytes 405512 | tf_op jit(solution)/shard_map/ppermute | solution.py:314
  12.3 6.1 %collective-permute-start.3 = (f32[272,128]{1,0:T(8,128)S(1)}, f32[272,128]{1,0:T(8,128)S(1)}, u32[]{:S(2)}, u32[]{:S(2)}) collective-permute-start(f32[272,128]{1,0:T(8,128)S(1)} %constant_dynamic-update-slice_fusion), channel_id=1, source_target_pairs={{1,0},{0,1},{3,2},{2,3},{5,4},{4,5},{7,6},{6,7},{9,8},{8,9},{11,10... | collective-permute-start | bytes 417800 | tf_op jit(solution)/shard_map/ppermute | solution.py:314
  15.9 2.5 %collective-permute-start.8 = (f32[264,128]{1,0:T(8,128)S(1)}, f32[264,128]{1,0:T(8,128)S(1)}, u32[]{:S(2)}, u32[]{:S(2)}) collective-permute-start(f32[264,128]{1,0:T(8,128)S(1)} %collective-permute-done.5.refs_6_), channel_id=1, source_target_pairs={{8,0},{9,1},{10,2},{11,3},{12,4},{13,5},{14,6},{15,7},{0,8},{1,9},... | collective-permute-start | bytes 405512 | tf_op jit(solution)/shard_map/ppermute | solution.py:314
  16.0 4.9 %collective-permute-start.9 = (f32[136,128]{1,0:T(8,128)S(1)}, f32[136,128]{1,0:T(8,128)S(1)}, u32[]{:S(2)}, u32[]{:S(2)}) collective-permute-start(f32[136,128]{1,0:T(8,128)S(1)} %pad_maximum_fusion.1), channel_id=1, source_target_pairs={{1,0},{0,1},{3,2},{2,3},{5,4},{4,5},{7,6},{6,7},{9,8},{8,9},{11,10... | collective-permute-start | bytes 208904 | tf_op jit(solution)/shard_map/ppermute | solution.py:314
  17.6 4.6 %collective-permute-start.7 = (f32[136,128]{1,0:T(8,128)S(1)}, f32[136,128]{1,0:T(8,128)S(1)}, u32[]{:S(2)}, u32[]{:S(2)}) collective-permute-start(f32[136,128]{1,0:T(8,128)S(1)} %pad_maximum_fusion), channel_id=1, source_target_pairs={{1,0},{0,1},{3,2},{2,3},{5,4},{4,5},{7,6},{6,7},{9,8},{8,9},{11,10... | collective-permute-start | bytes 208904 | tf_op jit(solution)/shard_map/ppermute | solution.py:314
  18.4 4.3 %collective-permute-start.4 = (f32[272,128]{1,0:T(8,128)S(1)}, f32[272,128]{1,0:T(8,128)S(1)}, u32[]{:S(2)}, u32[]{:S(2)}) collective-permute-start(f32[272,128]{1,0:T(8,128)S(1)} %collective-permute-done.3.refs_4_), channel_id=1, source_target_pairs={{8,0},{9,1},{10,2},{11,3},{12,4},{13,5},{14,6},{15,7},{0,8},{1,9},... | collective-permute-start | bytes 417800 | tf_op jit(solution)/shard_map/ppermute | solution.py:314
  20.9 1.9 %collective-permute-start.11 = (f32[136,128]{1,0:T(8,128)S(1)}, f32[136,128]{1,0:T(8,128)S(1)}, u32[]{:S(2)}, u32[]{:S(2)}) collective-permute-start(f32[136,128]{1,0:T(8,128)S(1)} %collective-permute-done.9.refs_6_), channel_id=1, source_target_pairs={{8,0},{9,1},{10,2},{11,3},{12,4},{13,5},{14,6},{15,7},{0,8},{1,9},... | collective-permute-start | bytes 208904 | tf_op jit(solution)/shard_map/ppermute | solution.py:314
  22.2 1.8 %collective-permute-start.10 = (f32[136,128]{1,0:T(8,128)S(1)}, f32[136,128]{1,0:T(8,128)S(1)}, u32[]{:S(2)}, u32[]{:S(2)}) collective-permute-start(f32[136,128]{1,0:T(8,128)S(1)} %collective-permute-done.7.refs_6_), channel_id=1, source_target_pairs={{8,0},{9,1},{10,2},{11,3},{12,4},{13,5},{14,6},{15,7},{0,8},{1,9},... | collective-permute-start | bytes 208904 | tf_op jit(solution)/shard_map/ppermute | solution.py:314

commit v18 on v17

--- a/solution.py
+++ b/solution.py
@@ -325,7 +325,7 @@
     beside = fetched(longer(column), 0, 1)
     across, core = lax.optimization_barrier((across, core))
     near = [column, core, across, fetched(across, 1, 0)]
-    diagonals = [[fetched(longer(across[start:stop]), 0, 1)] for start, stop in parts]
+    diagonals = [[fetched(across[start:stop], 0, 1)] for start, stop in parts]
     far = [beside, fetched(beside, 1, 0)]
     return near, [(place, 0, place) for place in range(4)], far, diagonals
 

time: 26.4 us -> 26.1 us (0.989)
  no operation moved by 1% of the time
where the time goes in v18:
time: 26.1 us; the launch traced here: 26 us
  starting transfers between devices  11.5 us (44%)
  Pallas kernels  9.02 us (35%)
  waiting for transfers between devices  4.49 us (17%)
  local copies, waits for them, and re-layouts  0.84 us (3%)
    ppermute x12, starting transfers between devices, fetched(): return lax.ppermute(block, ('grp', 'freq'), route)  11.5 us
    pallas_call x5, Pallas kernels, call(): pl.pallas_call(kernel, out_shape=out_shape, in_specs=[in_hbm] * len(other...  9.02 us
    ppermute x12, waiting for transfers between devices, fetched(): return lax.ppermute(block, ('grp', 'freq'), route)  4.49 us
    reshape x2, local copies, waits for them, and re-layouts, per_device(): tiles = spectra.reshape(stations, 2, chunks, LANES).transpose(1, 2, 0, 3)  0.8 us
  transfers between devices with their start and end apart: 12, of which 4 were waited for; matrix products, arithmetic and copies ran while one was open for 0% of the time, Pallas kernels for 26%

profile of v18, /device:TPU:0, one launch (start us, length us, event | category | flops | bytes accessed | tf_op | source)
XLA Modules:
  0.0 26.0 jit_solution(14061978384196642393)
XLA Ops:
  0.0 0.8 %reshape.13 = f32[8,2,4,128]{3,2,1,0:T(4,128)S(1)} reshape(f32[8,2,512]{2,1,0:T(2,128)} %param.3) | data formatting | bytes 65536 | tf_op jit(solution)/shard_map/reshape | solution.py:378
  0.8 5.1 %collective-permute-start = (f32[64,128]{1,0:T(8,128)S(1)}, f32[64,128]{1,0:T(8,128)S(1)}, u32[]{:S(2)}, u32[]{:S(2)}) collective-permute-start(f32[64,128]{1,0:T(8,128)S(1)} %bitcast.8), channel_id=1, source_target_pairs={{6,0},{7,1},{4,2},{5,3},{2,4},{3,5},{0,6},{1,7},{14,8},{15,9},{12,... | collective-permute-start | bytes 98312 | tf_op jit(solution)/shard_map/ppermute | solution.py:314
  5.9 0.0 collective-permute-start.1
  5.9 0.6 %collective-permute-start.2 = (f32[64,128]{1,0:T(8,128)S(1)}, f32[64,128]{1,0:T(8,128)S(1)}, u32[]{:S(2)}, u32[]{:S(2)}) collective-permute-start(f32[64,128]{1,0:T(8,128)S(1)} %bitcast.10), channel_id=1, source_target_pairs={{2,0},{3,1},{0,2},{1,3},{6,4},{7,5},{4,6},{5,7},{10,8},{11,9},{8,1... | collective-permute-start | bytes 98312 | tf_op jit(solution)/shard_map/ppermute | solution.py:314
  6.6 2.4 %tables.1 = (bf16[2048,512]{1,0:T(8,128)(2,1)S(1)}, bf16[2048,512]{1,0:T(8,128)(2,1)S(1)}, f32[4,4,128]{2,1,0:T(4,128)S(1)}, f32[4,4,128]{2,1,0:T(4,128)S(1)}, b...) custom-call(s32[1,2,1,64]{3,2,1,0:T(1,128)} %bitcast.12, ...), custom_call_target="tpu_custom_call" | custom-call | bytes 4194304 | tf_op jit(solution)/shard_map/tables/pallas_call | solution.py:366
  9.0 0.0 collective-permute-done
  9.1 1.7 %collective-permute-done.1 = f32[64,128]{1,0:T(8,128)S(1)} collective-permute-done((f32[64,128]{1,0:T(8,128)S(1)}, f32[64,128]{1,0:T(8,128)S(1)}, u32[]{:S(2)}, u32[]{:S(2)}) %collective-permute-start.1) | collective-permute-done | bytes 32800 | tf_op jit(solution)/shard_map/ppermute | solution.py:314
  10.7 0.0 collective-permute-done.2
  10.8 1.6 %collective-permute-start.5 = (f32[264,128]{1,0:T(8,128)S(1)}, f32[264,128]{1,0:T(8,128)S(1)}, u32[]{:S(2)}, u32[]{:S(2)}) collective-permute-start(f32[264,128]{1,0:T(8,128)S(1)} %get-tuple-element.63.refs_4_), channel_id=1, source_target_pairs={{16,0},{17,1},{18,2},{19,3},{20,4},{21,5},{22,6},{23,7},{24,8},{25... | collective-permute-start | bytes 405512 | tf_op jit(solution)/shard_map/ppermute | solution.py:314
  12.3 0.0 collective-permute-start.6
  12.3 1.5 %collective-permute-start.3 = (f32[272,128]{1,0:T(8,128)S(1)}, f32[272,128]{1,0:T(8,128)S(1)}, u32[]{:S(2)}, u32[]{:S(2)}) collective-permute-start(f32[272,128]{1,0:T(8,128)S(1)} %constant_dynamic-update-slice_fusion), channel_id=1, source_target_pairs={{1,0},{0,1},{3,2},{2,3},{5,4},{4,5},{7,6},{6,7},{9,8},{8,9},{11,10... | collective-permute-start | bytes 417800 | tf_op jit(solution)/shard_map/ppermute | solution.py:314
  13.9 2.0 %collective-permute-done.5.refs_6_ = f32[264,128]{1,0:T(8,128)S(1)} collective-permute-done((f32[264,128]{1,0:T(8,128)S(1)}, f32[264,128]{1,0:T(8,128)S(1)}, u32[]{:S(2)}, u32[]{:S(2)}) %collective-permute-start.5) | collective-permute-done | bytes 135200 | tf_op jit(solution)/shard_map/ppermute | solution.py:314
  15.9 0.0 collective-permute-done.6.refs_5_
  15.9 0.0 collective-permute-start.8
  15.9 1.6 %collective-permute-start.9 = (f32[128,128]{1,0:T(8,128)S(1)}, f32[128,128]{1,0:T(8,128)S(1)}, u32[]{:S(2)}, u32[]{:S(2)}) collective-permute-start(f32[128,128]{1,0:T(8,128)S(1)} %get-tuple-element.53), channel_id=1, source_target_pairs={{1,0},{0,1},{3,2},{2,3},{5,4},{4,5},{7,6},{6,7},{9,8},{8,9},{11,10... | collective-permute-start | bytes 196616 | tf_op jit(solution)/shard_map/ppermute | solution.py:314
  17.5 0.5 %collective-permute-start.7 = (f32[128,128]{1,0:T(8,128)S(1)}, f32[128,128]{1,0:T(8,128)S(1)}, u32[]{:S(2)}, u32[]{:S(2)}) collective-permute-start(f32[128,128]{1,0:T(8,128)S(1)} %get-tuple-element.54), channel_id=1, source_target_pairs={{1,0},{0,1},{3,2},{2,3},{5,4},{4,5},{7,6},{6,7},{9,8},{8,9},{11,10... | collective-permute-start | bytes 196616 | tf_op jit(solution)/shard_map/ppermute | solution.py:314
  18.0 0.5 %collective-permute-done.3.refs_4_ = f32[272,128]{1,0:T(8,128)S(1)} collective-permute-done((f32[272,128]{1,0:T(8,128)S(1)}, f32[272,128]{1,0:T(8,128)S(1)}, u32[]{:S(2)}, u32[]{:S(2)}) %collective-permute-start.3) | collective-permute-done | bytes 139296 | tf_op jit(solution)/shard_map/ppermute | solution.py:314
  18.4 0.0 collective-permute-start.4
  18.4 0.0 collective-permute-done.8.refs_7_
  18.4 1.9 %near_first.1 = (s32[256,128]{1,0:T(8,128)S(1)}, s32[256,128]{1,0:T(8,128)S(1)}, f32[256,128]{1,0:T(8,128)S(1)}, f32[256,256]{1,0:T(8,128)S(1)}, f32[256,256]{1,0:T(8,128)S(1)}) custom-call(f32[4,4,128]{2,1,0:T(4,128)S(1)} %get-tuple-element.35.refs_0_, f32[4,4,128]{2,1,0:T(4,128)S(1)} %get-tuple-element.36.refs_1_, ...), custom_call_target="tpu_custom_call" | custom-call | flops 805306368 | bytes 2097152 | tf_op jit(solution)/shard_map/near_first/pallas_call | solution.py:366
  20.3 0.3 %collective-permute-done.9.refs_6_ = f32[128,128]{1,0:T(8,128)S(1)} collective-permute-done((f32[128,128]{1,0:T(8,128)S(1)}, f32[128,128]{1,0:T(8,128)S(1)}, u32[]{:S(2)}, u32[]{:S(2)}) %collective-permute-start.9) | collective-permute-done | bytes 65568 | tf_op jit(solution)/shard_map/ppermute | solution.py:314
  20.6 0.3 collective-permute-start.11
  20.9 1.3 %near_next.1 = (f32[256,256]{1,0:T(8,128)S(1)}, f32[256,256]{1,0:T(8,128)S(1)}) custom-call(f32[4,4,128]{2,1,0:T(4,128)S(1)} %get-tuple-element.35.refs_0_, f32[4,4,128]{2,1,0:T(4,128)S(1)} %get-tuple-element.36.refs_1_, bf16[2048,512]{1,0:T(8,128)(2,1)S(1)} %get-tuple-element.37.refs_2_, bf16[2048,512]{1,0:T(8,128)(2,1)S(1)} %get-tuple-element.38.refs_3_, ...), custom_call_target="tpu_custom_call" | custom-call | flops 805306368 | bytes 2097152 | tf_op jit(solution)/shard_map/near_next/pallas_call | solution.py:366
  22.2 0.0 collective-permute-done.7.refs_6_
  22.2 0.3 %collective-permute-start.10 = (f32[128,128]{1,0:T(8,128)S(1)}, f32[128,128]{1,0:T(8,128)S(1)}, u32[]{:S(2)}, u32[]{:S(2)}) collective-permute-start(f32[128,128]{1,0:T(8,128)S(1)} %collective-permute-done.7.refs_6_), channel_id=1, source_target_pairs={{8,0},{9,1},{10,2},{11,3},{12,4},{13,5},{14,6},{15,7},{0,8},{1,9},... | collective-permute-start | bytes 196616 | tf_op jit(solution)/shard_map/ppermute | solution.py:314
  22.5 0.0 collective-permute-done.4.refs_5_
  22.5 0.0 collective-permute-done.11.refs_7_
  22.5 1.3 %far_first.1 = (f32[256,256]{1,0:T(8,128)S(1)}, f32[256,256]{1,0:T(8,128)S(1)}) custom-call(f32[4,4,128]{2,1,0:T(4,128)S(1)} %get-tuple-element.29.refs_0_, f32[4,4,128]{2,1,0:T(4,128)S(1)} %get-tuple-element.30.refs_1_, bf16[2048,512]{1,0:T(8,128)(2,1)S(1)} %get-tuple-element.31.refs_2_, bf16[2048,512]{1,0:T(8,128)(2,1)S(1)} %get-tuple-element.32.refs_3_, ...), custom_call_target="tpu_custom_call" | custom-call | flops 805306368 | bytes 2097152 | tf_op jit(solution)/shard_map/far_first/pallas_call | solution.py:366
  23.8 0.0 collective-permute-done.10.refs_7_
  23.8 2.2 %far_next.1 = f32[256,512]{1,0:T(8,128)} custom-call(f32[4,4,128]{2,1,0:T(4,128)S(1)} %get-tuple-element.29.refs_0_, f32[4,4,128]{2,1,0:T(4,128)S(1)} %get-tuple-element.30.refs_1_, bf16[2048,512]{1,0:T(8,128)(2,1)S(1)} %get-tuple-element.31.refs_2_, bf16[2048,512]{1,0:T(8,128)(2,1)S(1)} %get-tuple-element.32.refs_3_, ...), custom_call_target="tpu_custom_call" | custom-call | flops 805306368 | bytes 2097152 | tf_op jit(solution)/shard_map/far_next/pallas_call | solution.py:366
  (8 shorter events, 0.1 us)
Async XLA Ops:
  0.8 8.2 %collective-permute-start = (f32[64,128]{1,0:T(8,128)S(1)}, f32[64,128]{1,0:T(8,128)S(1)}, u32[]{:S(2)}, u32[]{:S(2)}) collective-permute-start(f32[64,128]{1,0:T(8,128)S(1)} %bitcast.8), channel_id=1, source_target_pairs={{6,0},{7,1},{4,2},{5,3},{2,4},{3,5},{0,6},{1,7},{14,8},{15,9},{12,... | collective-permute-start | bytes 98312 | tf_op jit(solution)/shard_map/ppermute | solution.py:314
  5.9 4.8 %collective-permute-start.1 = (f32[64,128]{1,0:T(8,128)S(1)}, f32[64,128]{1,0:T(8,128)S(1)}, u32[]{:S(2)}, u32[]{:S(2)}) collective-permute-start(f32[64,128]{1,0:T(8,128)S(1)} %bitcast.9), channel_id=1, source_target_pairs={{4,0},{5,1},{6,2},{7,3},{0,4},{1,5},{2,6},{3,7},{12,8},{13,9},{14,... | collective-permute-start | bytes 98312 | tf_op jit(solution)/shard_map/ppermute | solution.py:314
  5.9 4.8 %collective-permute-start.2 = (f32[64,128]{1,0:T(8,128)S(1)}, f32[64,128]{1,0:T(8,128)S(1)}, u32[]{:S(2)}, u32[]{:S(2)}) collective-permute-start(f32[64,128]{1,0:T(8,128)S(1)} %bitcast.10), channel_id=1, source_target_pairs={{2,0},{3,1},{0,2},{1,3},{6,4},{7,5},{4,6},{5,7},{10,8},{11,9},{8,1... | collective-permute-start | bytes 98312 | tf_op jit(solution)/shard_map/ppermute | solution.py:314
  10.8 5.1 %collective-permute-start.5 = (f32[264,128]{1,0:T(8,128)S(1)}, f32[264,128]{1,0:T(8,128)S(1)}, u32[]{:S(2)}, u32[]{:S(2)}) collective-permute-start(f32[264,128]{1,0:T(8,128)S(1)} %get-tuple-element.63.refs_4_), channel_id=1, source_target_pairs={{16,0},{17,1},{18,2},{19,3},{20,4},{21,5},{22,6},{23,7},{24,8},{25... | collective-permute-start | bytes 405512 | tf_op jit(solution)/shard_map/ppermute | solution.py:314
  12.3 3.5 %collective-permute-start.6 = (f32[264,128]{1,0:T(8,128)S(1)}, f32[264,128]{1,0:T(8,128)S(1)}, u32[]{:S(2)}, u32[]{:S(2)}) collective-permute-start(f32[264,128]{1,0:T(8,128)S(1)} %get-tuple-element.63.refs_4_), channel_id=1, source_target_pairs={{8,0},{9,1},{10,2},{11,3},{12,4},{13,5},{14,6},{15,7},{0,8},{1,9},... | collective-permute-start | bytes 405512 | tf_op jit(solution)/shard_map/ppermute | solution.py:314
  12.3 6.1 %collective-permute-start.3 = (f32[272,128]{1,0:T(8,128)S(1)}, f32[272,128]{1,0:T(8,128)S(1)}, u32[]{:S(2)}, u32[]{:S(2)}) collective-permute-start(f32[272,128]{1,0:T(8,128)S(1)} %constant_dynamic-update-slice_fusion), channel_id=1, source_target_pairs={{1,0},{0,1},{3,2},{2,3},{5,4},{4,5},{7,6},{6,7},{9,8},{8,9},{11,10... | collective-permute-start | bytes 417800 | tf_op jit(solution)/shard_map/ppermute | solution.py:314
  15.9 2.6 %collective-permute-start.8 = (f32[264,128]{1,0:T(8,128)S(1)}, f32[264,128]{1,0:T(8,128)S(1)}, u32[]{:S(2)}, u32[]{:S(2)}) collective-permute-start(f32[264,128]{1,0:T(8,128)S(1)} %collective-permute-done.5.refs_6_), channel_id=1, source_target_pairs={{8,0},{9,1},{10,2},{11,3},{12,4},{13,5},{14,6},{15,7},{0,8},{1,9},... | collective-permute-start | bytes 405512 | tf_op jit(solution)/shard_map/ppermute | solution.py:314
  15.9 4.8 %collective-permute-start.9 = (f32[128,128]{1,0:T(8,128)S(1)}, f32[128,128]{1,0:T(8,128)S(1)}, u32[]{:S(2)}, u32[]{:S(2)}) collective-permute-start(f32[128,128]{1,0:T(8,128)S(1)} %get-tuple-element.53), channel_id=1, source_target_pairs={{1,0},{0,1},{3,2},{2,3},{5,4},{4,5},{7,6},{6,7},{9,8},{8,9},{11,10... | collective-permute-start | bytes 196616 | tf_op jit(solution)/shard_map/ppermute | solution.py:314
  17.5 4.7 %collective-permute-start.7 = (f32[128,128]{1,0:T(8,128)S(1)}, f32[128,128]{1,0:T(8,128)S(1)}, u32[]{:S(2)}, u32[]{:S(2)}) collective-permute-start(f32[128,128]{1,0:T(8,128)S(1)} %get-tuple-element.54), channel_id=1, source_target_pairs={{1,0},{0,1},{3,2},{2,3},{5,4},{4,5},{7,6},{6,7},{9,8},{8,9},{11,10... | collective-permute-start | bytes 196616 | tf_op jit(solution)/shard_map/ppermute | solution.py:314
  18.4 4.1 %collective-permute-start.4 = (f32[272,128]{1,0:T(8,128)S(1)}, f32[272,128]{1,0:T(8,128)S(1)}, u32[]{:S(2)}, u32[]{:S(2)}) collective-permute-start(f32[272,128]{1,0:T(8,128)S(1)} %collective-permute-done.3.refs_4_), channel_id=1, source_target_pairs={{8,0},{9,1},{10,2},{11,3},{12,4},{13,5},{14,6},{15,7},{0,8},{1,9},... | collective-permute-start | bytes 417800 | tf_op jit(solution)/shard_map/ppermute | solution.py:314
  20.6 1.9 %collective-permute-start.11 = (f32[128,128]{1,0:T(8,128)S(1)}, f32[128,128]{1,0:T(8,128)S(1)}, u32[]{:S(2)}, u32[]{:S(2)}) collective-permute-start(f32[128,128]{1,0:T(8,128)S(1)} %collective-permute-done.9.refs_6_), channel_id=1, source_target_pairs={{8,0},{9,1},{10,2},{11,3},{12,4},{13,5},{14,6},{15,7},{0,8},{1,9},... | collective-permute-start | bytes 196616 | tf_op jit(solution)/shard_map/ppermute | solution.py:314
  22.2 1.6 %collective-permute-start.10 = (f32[128,128]{1,0:T(8,128)S(1)}, f32[128,128]{1,0:T(8,128)S(1)}, u32[]{:S(2)}, u32[]{:S(2)}) collective-permute-start(f32[128,128]{1,0:T(8,128)S(1)} %collective-permute-done.7.refs_6_), channel_id=1, source_target_pairs={{8,0},{9,1},{10,2},{11,3},{12,4},{13,5},{14,6},{15,7},{0,8},{1,9},... | collective-permute-start | bytes 196616 | tf_op jit(solution)/shard_map/ppermute | solution.py:314
